TPU v7x, 32 devices: a whole 2x2x4 slice. The times are simulated.
32 devices in a mesh: groups: 2 (over x), tp: 8 (over z, y), section: 2 (over core).
Axes of the slice: x: 2, y: 2, z: 4, core: 2. Of those that a mesh axis runs over, the one named last changes fastest.
Arguments:
- hidden: bfloat16 [2, 64, 8192], P(None, 'groups', ('tp', 'section')), parts along dimension 1, may hold values from -16 to 16
- norm_gain: float32 [8192], replicated, may hold values from 0.25 to 1.75
- w_query: bfloat16 [8192, 8192], P(None, ('tp', 'section')), may hold values from -0.0625 to 0.0625
- key_value_weight: bfloat16 [8192, 2048], P(('tp', 'section')), may hold values from -0.09375 to 0.09375
- w_output: bfloat16 [8192, 8192], P(('tp', 'section')), may hold values from -0.0625 to 0.0625
- prompt_cache_pages: bfloat16 [512, 16, 2048], P(('groups', 'tp', 'section')), parts along dimension 0, may hold values from -4 to 4
- per_page_scales: bfloat16 [512, 16], P(('groups', 'tp', 'section')), parts along dimension 0, may hold values from 0.5 to 100
- lengths: int32 [8], P('groups'), parts along dimension 0, may hold values from 1 to 512, as said below
- block_table: int32 [8, 32], P('groups'), parts along dimension 0, may hold values from 0 to 255, as said below
Outputs:
- layer_out: bfloat16 [2, 64, 8192], P(None, 'groups', ('tp', 'section')), parts along dimension 1
There are 2 independent parts, one for each index of `groups`. A program takes and returns all parts, laid end to end along the dimension named above; an argument that names none is the same for every part. Nothing has to cross between parts.
Inputs may be any that keep to these rules, and one draw needn't show every extreme that they name: `lengths`: one request has exactly 512 tokens. `block_table`: entry i of request r lies among the 16 pages of device r * 4 + i % 4 of the group (pages numbered device by device in the order of tp+section); entries on one device use distinct pages.
All inputs are finite; a program needn't handle non-finite values.
Results may differ from a plain program's by a relative error of at most 0.004.
The roundings to bfloat16 on the way count: a program that leaves them out, or rounds other values in their place, can miss the bound.
Values may be sent and summed in bfloat16 or wider, within the bound.
No kernel may reach another device: no remote copies, remote signals or barrier semaphores. Data moves between devices by JAX's collectives and lax.ppermute only.
A program may use at most 128 MiB of HBM per device.

v0:
```python
import jax
import jax.numpy as jnp
from jax import lax
from jax.sharding import PartitionSpec as P

QUERY_HEADS = 64
KEY_VALUE_HEADS = 8
HEAD_SIZE = 128
GROUP_REQUESTS = 4
SAMPLES = 8
PAGE_TOKENS = 16


theta_base = 500000.0
eps_norm = 1e-05


def rotate(vectors, positions):
    half = vectors.shape[-1] // 2
    freqs = jnp.exp(
        -jnp.log(theta_base) * jnp.arange(half, dtype=jnp.float32) * (2.0 / vectors.shape[-1])
    )
    angles = positions.astype(jnp.float32)[..., None] * freqs
    cosine = jnp.cos(angles)
    sine = jnp.sin(angles)
    first = vectors[..., :half]
    second = vectors[..., half:]
    return jnp.concatenate(
        [first * cosine - second * sine, second * cosine + first * sine], axis=-1
    )


def normalize(rows, gain):
    wide = rows.astype(jnp.float32)
    scale = lax.rsqrt(jnp.mean(wide * wide, axis=-1, keepdims=True) + eps_norm)
    return (wide * scale * gain).astype(jnp.bfloat16)


def project(whole, norm_gain, w_query, key_value_weight, positions, device):
    normalized_input = normalize(whole, norm_gain)
    width = key_value_weight.shape[0]
    mine = lax.dynamic_slice_in_dim(normalized_input, device * width, width, 1)
    query = jnp.dot(normalized_input, w_query, preferred_element_type=jnp.float32)
    query = query.reshape(query.shape[0], -1, HEAD_SIZE)
    query = rotate(query, positions[:, None]).astype(jnp.bfloat16)
    partial_pair = jnp.dot(mine, key_value_weight, preferred_element_type=jnp.float32)
    return (query, partial_pair)


def new_entry(summed_output, positions, head_number):
    key_value_pair = summed_output.reshape(summed_output.shape[0], KEY_VALUE_HEADS, 2, HEAD_SIZE)
    picked_entries = lax.dynamic_index_in_dim(key_value_pair, head_number, 1, keepdims=False)
    fresh_key = rotate(picked_entries[:, 0], positions).astype(jnp.bfloat16)
    fresh_value = picked_entries[:, 1].astype(jnp.bfloat16)
    return (fresh_key, fresh_value)


def attend(query, keys, values, visible, fresh_keys, fresh_values):
    rows, heads, width = query.shape
    requests = keys.shape[0]
    span = keys.shape[1]
    grouped = query.reshape(requests, rows // requests, heads, width)
    factor = width ** (-0.5)
    prompt = (
        jnp.einsum("rsjd,rtd->rsjt", grouped, keys, preferred_element_type=jnp.float32) * factor
    )
    prompt = jnp.where(visible[:, None, None, :], prompt, -jnp.inf).reshape(rows, heads, span)
    own = (
        jnp.stack(
            [
                jnp.einsum("bjd,bd->bj", query, fresh, preferred_element_type=jnp.float32)
                for fresh in fresh_keys
            ],
            axis=-1,
        )
        * factor
    )
    scores = jnp.concatenate([prompt, own], axis=-1)
    highest = jnp.max(scores, axis=-1, keepdims=True)
    weights = jnp.exp(scores - highest)
    weights = (weights / jnp.sum(weights, axis=-1, keepdims=True)).astype(jnp.bfloat16)
    spread = weights[..., :span].reshape(requests, rows // requests, heads, span)
    mixed = jnp.einsum(
        "rsjt,rtd->rsjd", spread, values, preferred_element_type=jnp.float32
    ).reshape(rows, heads, width)
    for index, fresh in enumerate(fresh_values):
        mixed = (
            mixed
            + weights[..., span + index].astype(jnp.float32)[..., None]
            * fresh.astype(jnp.float32)[:, None, :]
        )
    return mixed.reshape(rows, heads * width).astype(jnp.bfloat16)


def shards(
    hidden,
    norm_gain,
    w_query,
    key_value_weight,
    w_output,
    prompt_cache_pages,
    per_page_scales,
    lengths,
    block_table,
):
    shard_devices = lax.axis_size(("tp", "section"))
    device = lax.axis_index(("tp", "section"))
    heads_here = w_query.shape[1] // HEAD_SIZE
    request_group = QUERY_HEADS // KEY_VALUE_HEADS
    head_number = device * heads_here // request_group
    blocks = block_table.shape[1]
    token_count = prompt_cache_pages.shape[0]
    query_group_factor = shard_devices // KEY_VALUE_HEADS
    send_codes = jnp.repeat(
        jnp.moveaxis(
            prompt_cache_pages.reshape(token_count, PAGE_TOKENS, KEY_VALUE_HEADS, 2 * HEAD_SIZE),
            2,
            0,
        ),
        query_group_factor,
        axis=0,
    )
    send_scales = jnp.repeat(
        jnp.moveaxis(per_page_scales.reshape(token_count, KEY_VALUE_HEADS, 2), 1, 0),
        query_group_factor,
        axis=0,
    )
    got_codes, got_scales = (
        lax.all_to_all(send_codes, ("tp", "section"), split_axis=0, concat_axis=0, tiled=True),
        lax.all_to_all(send_scales, ("tp", "section"), split_axis=0, concat_axis=0, tiled=True),
    )
    flattened_page_table = block_table.reshape(-1)
    block_codes = jnp.take(
        got_codes.reshape((shard_devices * token_count, PAGE_TOKENS, 2 * HEAD_SIZE)),
        flattened_page_table,
        axis=0,
    )
    block_scales = jnp.take(
        got_scales.reshape((shard_devices * token_count, 2)), flattened_page_table, axis=0
    )
    block_codes = block_codes.reshape((GROUP_REQUESTS, blocks, PAGE_TOKENS, 2, HEAD_SIZE))
    block_scales = block_scales.reshape((GROUP_REQUESTS, blocks, 1, 2, 1))
    cache_pool = (block_codes.astype(jnp.float32) * block_scales.astype(jnp.float32)).astype(
        jnp.bfloat16
    )
    cache_pool = cache_pool.reshape((GROUP_REQUESTS, blocks * PAGE_TOKENS, 2, HEAD_SIZE))
    keys = cache_pool[:, :, 0]
    values = cache_pool[:, :, 1]
    visible = jnp.arange(blocks * PAGE_TOKENS)[None, :] < lengths[:, None]
    base_positions = jnp.repeat(lengths, SAMPLES)
    fresh_keys = []
    fresh_values = []
    results = []
    for step in range(2):
        positions = base_positions + step
        whole = lax.all_gather(hidden[step], ("tp", "section"), axis=1, tiled=True)
        query, partial_pair = project(
            whole, norm_gain, w_query, key_value_weight, positions, device
        )
        summed_output = lax.psum(partial_pair, ("tp", "section"))
        fresh_key, fresh_value = new_entry(summed_output, positions, head_number)
        fresh_keys.append(fresh_key)
        fresh_values.append(fresh_value)
        mixed = attend(query, keys, values, visible, fresh_keys, fresh_values)
        term = jnp.dot(mixed, w_output, preferred_element_type=jnp.float32)
        reduced = lax.psum_scatter(term, ("tp", "section"), scatter_dimension=1, tiled=True)
        results.append((reduced + hidden[step].astype(jnp.float32)).astype(jnp.bfloat16))
    return jnp.stack(results)


def solution(mesh):
    placed = (
        P(None, "groups", ("tp", "section")),
        P(),
        P(None, ("tp", "section")),
        P(("tp", "section"), None),
        P(("tp", "section"), None),
        P(("groups", "tp", "section"), None, None),
        P(("groups", "tp", "section"), None),
        P("groups"),
        P("groups", None),
    )
    return jax.shard_map(
        shards,
        mesh=mesh,
        in_specs=placed,
        out_specs=P(None, "groups", ("tp", "section")),
        check_vma=False,
    )
```

profile of v0, /device:TPU:0, one launch (start us, length us, event | category | flops | bytes accessed | tf_op | source)
XLA Modules:
  0.0 330.3 jit_solution(6160967564357402887)
XLA Ops:
  8.1 7.4 %all-to-all-start.1 = ((bf16[16,16,2]{1,2,0:T(2,128)(2,1)}), bf16[16,16,2]{1,2,0:T(2,128)(2,1)S(1)}, u32[]{:S(2)}, u32[]{:S(2)}) async-start(bf16[16,16,2]{1,2,0:T(2,128)(2,1)} %bitcast.10), calls=%async_computation.1 | async-start | bytes 16384 | tf_op jit(solution)/shard_map/all_to_all | solution.py:130
  16.3 23.2 %all-gather = bf16[1,32,8192]{2,1,0:T(8,128)(2,1)S(1)} all-gather(bf16[1,32,512]{2,1,0:T(8,128)(2,1)S(1)} %get-tuple-element.19), channel_id=2, replica_groups=mesh['groups'=2,'tp'=8,'section'=2] {'tp','section'}, dimensions={2}, use_global_device_ids=true | all-gather | bytes 557056 | tf_op jit(solution)/shard_map/all_gather | solution.py:156
  40.6 18.9 %all-gather.1 = bf16[1,32,8192]{2,1,0:T(8,128)(2,1)S(1)} all-gather(bf16[1,32,512]{2,1,0:T(8,128)(2,1)S(1)} %get-tuple-element.20), channel_id=3, replica_groups=mesh['groups'=2,'tp'=8,'section'=2] {'tp','section'}, dimensions={2}, use_global_device_ids=true | all-gather | bytes 557056 | tf_op jit(solution)/shard_map/all_gather | solution.py:156
  60.5 1.5 fusion.11
  62.0 1.2 fusion.39
  63.2 1.2 reshape.355
  65.2 1.2 fusion.41
  66.3 1.2 reshape.350
  68.4 4.9 %fusion.82 = f32[32,512]{1,0:T(8,128)S(1)} fusion(bf16[32,8192]{1,0:T(8,128)(2,1)S(1)} %get-tuple-element.23, bf16[8192,512]{1,0:T(8,128)(2,1)} %param.11), kind=kOutput, calls=%fused_computation.141 | convolution fusion | flops 268435456 | bytes 8978432 | tf_op jit(solution)/shard_map/dot_general | solution.py:43
  73.3 5.0 %fusion.83 = f32[32,512]{1,0:T(8,128)S(1)} fusion(bf16[32,8192]{1,0:T(8,128)(2,1)S(1)} %get-tuple-element.24, bf16[8192,512]{1,0:T(8,128)(2,1)} %param.11), kind=kOutput, calls=%fused_computation.142 | convolution fusion | flops 268435456 | bytes 8978432 | tf_op jit(solution)/shard_map/dot_general | solution.py:43
  79.7 1.5 broadcast_in_dim.83
  81.2 4.4 %all-to-all-start = ((bf16[16,16,16,256]{3,2,1,0:T(8,128)(2,1)}), bf16[16,16,16,256]{3,2,1,0:T(8,128)(2,1)}, u32[]{:S(2)}, u32[]{:S(2)}) async-start(bf16[16,16,16,256]{3,2,1,0:T(8,128)(2,1)} %bitcast.165), calls=%async_computation | async-start | bytes 4194304 | tf_op jit(solution)/shard_map/all_to_all | solution.py:129
  88.3 90.0 %all-reduce.3.cloned.1.call-done = (f32[32,8,2,128]{3,0,2,1:T(8,128)}, f32[32,8,2,128]{3,0,2,1:T(8,128)}) async-done(((f32[32,8,2,128]{3,0,2,1:T(8,128)}, f32[32,8,2,128]{3,0,2,1:T(8,128)}), (f32[32,8,2,128]{3,0,2,1:T(8,128)}, f32[32,8,2,128]{3,0,2,1:T(8,128)})) %all-reduce.3.cloned.1.call-update) | async-done | bytes 524304 | tf_op jit(solution)/shard_map/psum | solution.py:160
  181.4 1.2 fusion.75
  182.6 2.4 gather_fusion
  185.0 1.1 gather.13
  186.1 2.0 multiply_convert_fusion
  189.3 1.3 fusion.56
  191.4 1.3 divide_convert_fusion.1
  194.9 1.5 divide_convert_fusion
  197.5 6.1 %fusion.8 = f32[32,8192]{1,0:T(8,128)} fusion(bf16[512,8192]{1,0:T(8,128)(2,1)} %param.13, bf16[4,512,2,128]{3,1,0,2:T(8,128)(2,1)S(1)} %multiply_convert_fusion, f32[4,8,4,128]{3,2,1,0:T(4,128)S(1)} %bitcast.175, bf16[32,4,513]{2,0,1:T(8,128)(2,1)} %copy-done.6), kind=kOutput, calls=%fused_computation.19 | convolution fusion | flops 285245440 | bytes 10158080 | tf_op jit(solution)/shard_map/dot_general | solution.py:165
  204.9 6.2 %fusion.7 = f32[32,8192]{1,0:T(8,128)} fusion(bf16[512,8192]{1,0:T(8,128)(2,1)} %param.13, bf16[4,512,2,128]{3,1,0,2:T(8,128)(2,1)S(1)} %multiply_convert_fusion, f32[4,8,4,128]{3,2,1,0:T(4,128)S(1)} %bitcast.173, f32[4,8,4,128]{3,2,1,0:T(4,128)S(1)} %bitcast.174, bf16[32,4,514]{2,0,1:T(8,128)(2,1)} %copy-done.5), kind=kOutput, calls=%fused_computation.18 | convolution fusion | flops 285261824 | bytes 10223616 | tf_op jit(solution)/shard_map/dot_general | solution.py:165
  211.1 50.7 %reduce-scatter.3.cloned.1.call-done = f32[32,512]{1,0:T(8,128)} async-done(((f32[32,8192]{1,0:T(8,128)}), f32[32,512]{1,0:T(8,128)}) %reduce-scatter.3.cloned.1.call-update) | async-done | bytes 65552 | tf_op jit(solution)/shard_map/reduce_scatter | solution.py:166
  261.7 60.5 %reduce-scatter.5.cloned.1.call-done = f32[32,512]{1,0:T(8,128)} async-done(((f32[32,8192]{1,0:T(8,128)}), f32[32,512]{1,0:T(8,128)}) %reduce-scatter.5.cloned.1.call-update) | async-done | bytes 65552 | tf_op jit(solution)/shard_map/reduce_scatter | solution.py:166
  (108 shorter events, 21.0 us)
Async XLA Ops:
  6.5 55.5 %copy-start = (bf16[512,2048]{1,0:T(8,128)(2,1)S(1)}, bf16[512,2048]{1,0:T(8,128)(2,1)}, u32[]{:S(2)}) copy-start(bf16[512,2048]{1,0:T(8,128)(2,1)} %param.12) | copy-start | bytes 6291460
  6.5 61.8 %copy-start.8 = (s32[4,32]{1,0:T(4,128)S(1)}, s32[4,32]{1,0:T(4,128)}, u32[]{:S(2)}) copy-start(s32[4,32]{1,0:T(4,128)} %param.17) | copy-start | bytes 1540
  8.1 71.6 %all-to-all-start.1 = ((bf16[16,16,2]{1,2,0:T(2,128)(2,1)}), bf16[16,16,2]{1,2,0:T(2,128)(2,1)S(1)}, u32[]{:S(2)}, u32[]{:S(2)}) async-start(bf16[16,16,2]{1,2,0:T(2,128)(2,1)} %bitcast.10), calls=%async_computation.1 | async-start | bytes 16384 | tf_op jit(solution)/shard_map/all_to_all | solution.py:130
  15.5 162.8 %all-reduce.3.cloned.1.call-start = ((), (), s32[]{:S(2)}) async-start(), calls=%async_computation.6 | async-start | bytes 1048576 | tf_op jit(solution)/shard_map/psum | solution.py:160
  39.5 0.8 copy-start.1
  59.4 0.8 copy-start.2
  73.3 5.0 %copy-start.3 = (bf16[16,16,2048]{2,1,0:T(8,128)(2,1)S(1)}, bf16[16,16,2048]{2,1,0:T(8,128)(2,1)}, u32[]{:S(2)}) copy-start(bf16[16,16,2048]{2,1,0:T(8,128)(2,1)} %param.14) | copy-start | bytes 3145732
  73.3 5.5 %copy-start.10 = (s32[4]{0:T(128)S(1)}, s32[4]{0:T(128)}, u32[]{:S(2)}) copy-start(s32[4]{0:T(128)} %param.16) | copy-start | bytes 52
  79.4 99.9 %copy-start.9 = (s32[1024]{0:T(1024)}, s32[1024]{0:T(1024)S(1)}, u32[]{:S(2)}) copy-start(s32[1024]{0:T(1024)S(1)} %pad_clamp_fusion) | copy-start | bytes 12292
  81.2 101.4 %all-to-all-start = ((bf16[16,16,16,256]{3,2,1,0:T(8,128)(2,1)}), bf16[16,16,16,256]{3,2,1,0:T(8,128)(2,1)}, u32[]{:S(2)}, u32[]{:S(2)}) async-start(bf16[16,16,16,256]{3,2,1,0:T(8,128)(2,1)} %bitcast.165), calls=%async_computation | async-start | bytes 4194304 | tf_op jit(solution)/shard_map/all_to_all | solution.py:129
  85.7 176.0 %reduce-scatter.3.cloned.1.call-start = ((), (), s32[]{:S(2)}) async-start(), calls=%async_computation.4 | async-start | bytes 1114112 | tf_op jit(solution)/shard_map/reduce_scatter | solution.py:166
  179.1 0.6 copy-start.7
  192.7 1.4 copy-start.6
  196.4 0.7 copy-start.5
  203.7 118.6 %copy-start.4 = (bf16[2,32,512]{2,1,0:T(8,128)(2,1)S(1)}, bf16[2,32,512]{2,1,0:T(8,128)(2,1)}, u32[]{:S(2)}) copy-start(bf16[2,32,512]{2,1,0:T(8,128)(2,1)} %param.9) | copy-start | bytes 196612
  203.7 118.6 %reduce-scatter.5.cloned.1.call-start = ((), (), s32[]{:S(2)}) async-start(), calls=%async_computation.5 | async-start | bytes 1114112 | tf_op jit(solution)/shard_map/reduce_scatter | solution.py:166
  323.2 0.6 copy-start.11
Sparse Core Ops, SparseCore 0:
  68.4 109.8 all-reduce.2
  203.8 57.8 reduce-scatter.2
  265.8 56.4 reduce-scatter.4
where the time goes:
time: 331 us; the launch traced here: 330 us
  waiting for transfers between devices  201 us (61%)
  blocking collectives  42.1 us (13%)
  matrix products  27.1 us (8%)
  local copies, waits for them, and re-layouts  21.3 us (6%)
  between operations  13.5 us (4%)
  other arithmetic  13.2 us (4%)
  starting transfers between devices  11.9 us (4%)
    reduce_scatter x2, waiting for transfers between devices, shards(): lax.psum_scatter(term, ('tp', 'section'), scatter_dimension=1, tiled=True)  111 us
    psum x1, waiting for transfers between devices, shards(): summed_output = lax.psum(partial_pair, ('tp', 'section'))  90 us
    all_gather x2, blocking collectives, shards(): whole = lax.all_gather(hidden[step], ('tp', 'section'), axis=1, tiled=True)  42.1 us
    dot_general x2, matrix products, shards(): term = jnp.dot(mixed, w_output, preferred_element_type=jnp.float32)  12.3 us
    dot_general x2, matrix products, project(): jnp.dot(normalized_input, w_query, preferred_element_type=jnp.float32)  9.9 us
    all_to_all x1, starting transfers between devices, shards(): lax.all_to_all(send_scales, ('tp', 'section'), split_axis=0, concat_axis=...  7.39 us
  transfers between devices with their start and end apart: 5, of which 3 were waited for; matrix products, arithmetic and copies ran while one was open for 11% of the time, Pallas kernels for 0%

commit v1 on v0

v1 whole, which is shorter than its diff:
```python
import functools

import jax
import jax.numpy as jnp
import numpy as np
from jax import lax
from jax.experimental import pallas as pl
from jax.experimental.pallas import tpu as pltpu
from jax.sharding import Mesh
from jax.sharding import PartitionSpec as P

QUERY_HEADS = 64
KEY_VALUE_HEADS = 8
HEAD_SIZE = 128
GROUP_REQUESTS = 4
SAMPLES = 8
PAGE_TOKENS = 16
STEPS = 2
ROWS = STEPS * SAMPLES
PAIR = 2 * HEAD_SIZE
DEVICES = ("req", "sub", "section")
PLANE = ("sub", "section")

theta_base = 500000.0
eps_norm = 1e-05
VMEM = 48 * 2**20


def params(**more):
    return pltpu.CompilerParams(vmem_limit_bytes=VMEM, **more)


def whole_spec(shape):
    return pl.BlockSpec(shape, lambda *_: (0,) * len(shape))


def turn(vectors, cosine, sine):
    return vectors * cosine + pltpu.roll(vectors, HEAD_SIZE // 2, vectors.ndim - 1) * sine


def pages_kernel(table, place, scales, page_ref, out_ref):
    e = pl.program_id(0)
    targets, heads = out_ref.shape[0], out_ref.shape[1]
    page = table[place[0], e * targets + place[1]] - place[2]
    repeats = targets * heads // KEY_VALUE_HEADS
    for target in range(targets):
        for h in range(heads):
            head = (target * heads) // repeats + h if repeats > 1 else target * heads + h
            for part in range(2):
                c = head * 2 + part
                block = page_ref[0, :, c * HEAD_SIZE : (c + 1) * HEAD_SIZE].astype(jnp.float32)
                out_ref[target, h, :, part * HEAD_SIZE : (part + 1) * HEAD_SIZE] = (
                    block * scales[page, c]
                ).astype(jnp.bfloat16)


def used_pages(pages, scales, table, place, targets, heads):
    entries = table.shape[1] // targets
    return pl.pallas_call(
        pages_kernel,
        grid_spec=pltpu.PrefetchScalarGridSpec(
            num_scalar_prefetch=3,
            grid=(entries,),
            in_specs=[
                pl.BlockSpec(
                    (1, PAGE_TOKENS, pages.shape[2]),
                    lambda e, table, place, scales: (
                        table[place[0], e * targets + place[1]] - place[2],
                        0,
                        0,
                    ),
                )
            ],
            out_specs=pl.BlockSpec(
                (targets, heads, PAGE_TOKENS, PAIR), lambda e, *_: (0, 0, e, 0)
            ),
        ),
        out_shape=jax.ShapeDtypeStruct(
            (targets, heads, entries * PAGE_TOKENS, PAIR), jnp.bfloat16
        ),
        compiler_params=params(),
        name="used_pages",
    )(table, place, scales.astype(jnp.float32), pages)


def norm_kernel(place, x_ref, gain_ref, weight_ref, normed_ref, pair_ref):
    blocks, rows, width = x_ref.shape
    total = jnp.zeros((rows, width), jnp.float32)
    for i in range(blocks):
        x = x_ref[i].astype(jnp.float32)
        total += x * x
    mean = jnp.sum(total, axis=-1, keepdims=True) / (blocks * width)
    scale = lax.rsqrt(mean + eps_norm)
    for i in range(blocks):
        x = x_ref[i].astype(jnp.float32)
        normed_ref[i] = (x * scale * gain_ref[i]).astype(jnp.bfloat16)
    mine = normed_ref[place[0]]
    requests, targets, _, wide = pair_ref.shape
    repeats = targets * wide // weight_ref.shape[1]
    for t in range(0, targets, repeats):
        first = (t // repeats) * wide
        part = jnp.dot(
            mine, weight_ref[:, first : first + wide], preferred_element_type=jnp.float32
        )
        for r in range(requests):
            for c in range(repeats):
                pair_ref[r, t + c] = part[r * ROWS : (r + 1) * ROWS]


def norm_and_pairs(x, gain, weight, device, targets, heads):
    blocks, rows, width = x.shape
    shapes = [
        jax.ShapeDtypeStruct((blocks, rows, width), jnp.bfloat16),
        jax.ShapeDtypeStruct((GROUP_REQUESTS, targets, ROWS, heads * PAIR), jnp.float32),
    ]
    return pl.pallas_call(
        norm_kernel,
        in_specs=[pl.BlockSpec(memory_space=pltpu.SMEM)]
        + [pl.BlockSpec(memory_space=pltpu.VMEM)] * 3,
        out_specs=[pl.BlockSpec(memory_space=pltpu.VMEM)] * 2,
        out_shape=shapes,
        compiler_params=params(),
        name="norm_and_pairs",
    )(device, x, gain.reshape(blocks, 1, width), weight)


def query_kernel(x_ref, weight_ref, cos_ref, sin_ref, out_ref, total):
    i = pl.program_id(0)

    @pl.when(i == 0)
    def _():
        total[...] = jnp.zeros_like(total)

    total[...] += jnp.dot(x_ref[0], weight_ref[...], preferred_element_type=jnp.float32)

    @pl.when(i == pl.num_programs(0) - 1)
    def _():
        for head in range(total.shape[1] // HEAD_SIZE):
            part = slice(head * HEAD_SIZE, (head + 1) * HEAD_SIZE)
            out_ref[:, part] = turn(total[:, part], cos_ref[...], sin_ref[...]).astype(
                jnp.bfloat16
            )


def queries(normed, weight, cosine, sine):
    blocks, rows, width = normed.shape
    columns = weight.shape[1]
    return pl.pallas_call(
        query_kernel,
        grid=(blocks,),
        in_specs=[
            pl.BlockSpec((1, rows, width), lambda i: (i, 0, 0)),
            pl.BlockSpec((width, columns), lambda i: (i, 0)),
            whole_spec(cosine.shape),
            whole_spec(sine.shape),
        ],
        out_specs=whole_spec((rows, columns)),
        out_shape=jax.ShapeDtypeStruct((rows, columns), jnp.bfloat16),
        scratch_shapes=[pltpu.VMEM((rows, columns), jnp.float32)],
        compiler_params=params(),
        name="queries",
    )(normed, weight, cosine, sine)


def attend_kernel(place, q_ref, cache_ref, pair_ref, cos_ref, sin_ref, out_ref):
    r, length = place[0], place[1]
    sources, heads, span, _ = cache_ref.shape
    quarter = q_ref.shape[2] // HEAD_SIZE
    parts = GROUP_REQUESTS // heads
    tokens = sources * span
    pairs = pair_ref[0]
    for i in range(1, pair_ref.shape[0]):
        pairs = pairs + pair_ref[i]
    column = lax.broadcasted_iota(jnp.int32, (1, tokens), 1)
    source, inside = column // span, column % span
    position = (inside // PAGE_TOKENS * sources + source) * PAGE_TOKENS + inside % PAGE_TOKENS
    visible = position < length
    count = parts * quarter * ROWS
    row = lax.broadcasted_iota(jnp.int32, (count, ROWS), 0) % ROWS
    other = lax.broadcasted_iota(jnp.int32, (count, ROWS), 1)
    own_visible = (row % SAMPLES == other % SAMPLES) & (other // SAMPLES <= row // SAMPLES)
    factor = HEAD_SIZE ** (-0.5)
    for h in range(heads):
        keys = cache_ref[:, h, :, :HEAD_SIZE].reshape(tokens, HEAD_SIZE)
        values = cache_ref[:, h, :, HEAD_SIZE:].reshape(tokens, HEAD_SIZE)
        new_key = turn(
            pairs[:, h * PAIR : h * PAIR + HEAD_SIZE], cos_ref[...], sin_ref[...]
        ).astype(jnp.bfloat16)
        new_value = pairs[:, h * PAIR + HEAD_SIZE : (h + 1) * PAIR].astype(jnp.bfloat16)
        slots = [lax.rem(r - k + GROUP_REQUESTS, GROUP_REQUESTS) for k in range(h * parts, (h + 1) * parts)]
        query = jnp.concatenate(
            [
                q_ref[slot, :, head * HEAD_SIZE : (head + 1) * HEAD_SIZE]
                for slot in slots
                for head in range(quarter)
            ],
            axis=0,
        )
        contract = (((1,), (1,)), ((), ()))
        scores = lax.dot_general(query, keys, contract, preferred_element_type=jnp.float32)
        scores = jnp.where(visible, scores * factor, -jnp.inf)
        own = lax.dot_general(query, new_key, contract, preferred_element_type=jnp.float32)
        own = jnp.where(own_visible, own * factor, -jnp.inf)
        highest = jnp.maximum(
            jnp.max(scores, axis=-1, keepdims=True), jnp.max(own, axis=-1, keepdims=True)
        )
        scores = jnp.exp(scores - highest)
        own = jnp.exp(own - highest)
        total = jnp.sum(scores, axis=-1, keepdims=True) + jnp.sum(own, axis=-1, keepdims=True)
        mixed = jnp.dot(
            (scores / total).astype(jnp.bfloat16), values, preferred_element_type=jnp.float32
        ) + jnp.dot(
            (own / total).astype(jnp.bfloat16), new_value, preferred_element_type=jnp.float32
        )
        mixed = mixed.astype(jnp.bfloat16)
        for i, slot in enumerate(slots):
            for head in range(quarter):
                first = (i * quarter + head) * ROWS
                out_ref[slot, :, head * HEAD_SIZE : (head + 1) * HEAD_SIZE] = mixed[
                    first : first + ROWS
                ]


def attend(query, cache, pairs, cosine, sine, place):
    return pl.pallas_call(
        attend_kernel,
        in_specs=[pl.BlockSpec(memory_space=pltpu.SMEM)]
        + [pl.BlockSpec(memory_space=pltpu.VMEM)] * 5,
        out_specs=pl.BlockSpec(memory_space=pltpu.VMEM),
        out_shape=jax.ShapeDtypeStruct(query.shape, jnp.bfloat16),
        compiler_params=params(),
        name="attend",
    )(place, query, cache, pairs, cosine, sine)


def output_kernel(x_ref, weight_ref, out_ref):
    out_ref[0] = jnp.dot(x_ref[...], weight_ref[...], preferred_element_type=jnp.float32)


def outputs(mixed, weight, blocks):
    rows, depth = mixed.shape
    width = weight.shape[1] // blocks
    return pl.pallas_call(
        output_kernel,
        grid=(blocks,),
        in_specs=[whole_spec((rows, depth)), pl.BlockSpec((depth, width), lambda i: (0, i))],
        out_specs=pl.BlockSpec((1, rows, width), lambda i: (i, 0, 0)),
        out_shape=jax.ShapeDtypeStruct((blocks, rows, width), jnp.float32),
        compiler_params=params(),
        name="outputs",
    )(mixed, weight)


def shards(
    hidden,
    norm_gain,
    w_query,
    key_value_weight,
    w_output,
    prompt_cache_pages,
    per_page_scales,
    lengths,
    block_table,
):
    devices = lax.axis_size(DEVICES)
    targets = lax.axis_size(PLANE)
    heads = max(1, KEY_VALUE_HEADS // targets)
    device = lax.axis_index(DEVICES)
    request = lax.axis_index("req")
    spot = lax.axis_index(PLANE)
    width = hidden.shape[2]

    rows = hidden.reshape(STEPS, GROUP_REQUESTS, SAMPLES, width)
    rows = jnp.swapaxes(rows, 0, 1).reshape(GROUP_REQUESTS * ROWS, width)
    gathered = lax.all_to_all(
        jnp.broadcast_to(rows[None], (devices,) + rows.shape), DEVICES, 0, 0, tiled=True
    )

    place = jnp.stack([request, spot, device * prompt_cache_pages.shape[0]]).astype(jnp.int32)
    send = used_pages(prompt_cache_pages, per_page_scales, block_table, place, targets, heads)
    cache = lax.all_to_all(send, PLANE, 0, 0, tiled=True)

    half = HEAD_SIZE // 2
    freqs = jnp.exp(
        -jnp.log(theta_base) * jnp.arange(half, dtype=jnp.float32) * (2.0 / HEAD_SIZE)
    )
    positions = (lengths[:, None] + jnp.arange(STEPS)[None, :]).astype(jnp.float32)
    angles = positions[..., None] * freqs
    cosine, sine = jnp.cos(angles), jnp.sin(angles)
    cosine = jnp.concatenate([cosine, cosine], axis=-1)
    sine = jnp.concatenate([-sine, sine], axis=-1)
    cosine = jnp.repeat(cosine, SAMPLES, axis=1)
    sine = jnp.repeat(sine, SAMPLES, axis=1)
    my_cosine = lax.dynamic_index_in_dim(cosine, request, 0, keepdims=False)
    my_sine = lax.dynamic_index_in_dim(sine, request, 0, keepdims=False)
    cosine = cosine.reshape(-1, HEAD_SIZE)
    sine = sine.reshape(-1, HEAD_SIZE)

    normed, pairs = norm_and_pairs(
        gathered, norm_gain, key_value_weight, device[None].astype(jnp.int32), targets, heads
    )
    pairs = lax.all_to_all(
        pairs.reshape(devices, ROWS, heads * PAIR), DEVICES, 0, 0, tiled=True
    )

    query = queries(normed, w_query, cosine, sine)
    query = query.reshape(GROUP_REQUESTS, ROWS, -1)
    group, member = device // GROUP_REQUESTS, device % GROUP_REQUESTS
    got = []
    for s in range(GROUP_REQUESTS):
        there = [
            (d, (d % GROUP_REQUESTS + s) % GROUP_REQUESTS * targets + d // GROUP_REQUESTS)
            for d in range(devices)
        ]
        block = lax.dynamic_index_in_dim(
            query, (member + s) % GROUP_REQUESTS, 0, keepdims=False
        )
        got.append(lax.ppermute(block, DEVICES, there))
    query = jnp.stack(got)

    my_length = lax.dynamic_index_in_dim(lengths, request, 0, keepdims=False)
    mixed = attend(
        query,
        cache,
        pairs,
        my_cosine,
        my_sine,
        jnp.stack([request, my_length]).astype(jnp.int32),
    )
    got = []
    for s in range(GROUP_REQUESTS):
        back = [
            ((d % GROUP_REQUESTS + s) % GROUP_REQUESTS * targets + d // GROUP_REQUESTS, d)
            for d in range(devices)
        ]
        got.append(lax.ppermute(mixed[s], DEVICES, back))
    mixed = jnp.stack(got)
    mixed = jnp.take(
        mixed, (jnp.arange(GROUP_REQUESTS) - member) % GROUP_REQUESTS, axis=0
    ).reshape(GROUP_REQUESTS * ROWS, -1)

    terms = outputs(mixed, w_output, devices)
    terms = lax.all_to_all(terms, DEVICES, 0, 0, tiled=True)
    result = jnp.sum(terms, axis=0) + rows.astype(jnp.float32)
    result = result.astype(jnp.bfloat16).reshape(GROUP_REQUESTS, STEPS, SAMPLES, width)
    return jnp.swapaxes(result, 0, 1).reshape(hidden.shape)


def solution(mesh):
    groups, tp, section = mesh.devices.shape
    finer = Mesh(
        mesh.devices.reshape(groups, GROUP_REQUESTS, tp // GROUP_REQUESTS, section),
        ("groups",) + DEVICES,
    )
    placed = (
        P(None, "groups", DEVICES),
        P(),
        P(None, DEVICES),
        P(DEVICES, None),
        P(DEVICES, None),
        P(("groups",) + DEVICES, None, None),
        P(("groups",) + DEVICES, None),
        P("groups"),
        P("groups", None),
    )
    return jax.shard_map(
        shards,
        mesh=finer,
        in_specs=placed,
        out_specs=P(None, "groups", DEVICES),
        check_vma=False,
    )
```

time: 331 us -> 155 us (0.47)
  waiting for transfers between devices: 201 us -> 26.9 us
  Pallas kernels: 0 us -> 27.5 us
  matrix products: 27.1 us -> 0 us
  starting transfers between devices: 11.9 us -> 35.7 us
  local copies, waits for them, and re-layouts: 21.3 us -> 7.72 us
  between operations: 13.5 us -> 0.34 us
  blocking collectives: 42.1 us -> 51.9 us
  other arithmetic: 13.2 us -> 3.8 us
    reduce_scatter x2 -> x0, waiting for transfers between devices: 111 us -> none  [shards(): lax.psum_scatter(term, ('tp', 'section'), scatter_dimension=1, tiled=True)]
    psum x1 -> x0, waiting for transfers between devices: 90 us -> none  [shards(): summed_output = lax.psum(partial_pair, ('tp', 'section'))]
    all_to_all x0 -> x1, blocking collectives: none -> 51.9 us  [shards(): terms = lax.all_to_all(terms, DEVICES, 0, 0, tiled=True)]
    all_gather x2 -> x0, blocking collectives: 42.1 us -> none  [shards(): whole = lax.all_gather(hidden[step], ('tp', 'section'), axis=1, tiled=True)]
    pallas_call x0 -> x5, Pallas kernels: none -> 27.5 us  [the longest x1 10.7 us: queries(): pl.pallas_call(query_kernel, grid=(blocks,), in_specs=[pl.BlockSpec((1, r...]
    dot_general x11 -> x0, matrix products: 27.1 us -> none  [the longest x2 12.3 us: shards(): term = jnp.dot(mixed, w_output, preferred_element_type=jnp.float32)]
    all_to_all x2 -> x3, waiting for transfers between devices: 0.01 us -> 23.6 us  [the longest x1 17.3 us: shards(): lax.all_to_all(jnp.broadcast_to(rows[None], (devices,) + rows.shape), DEV...]
    ppermute x0 -> x8, starting transfers between devices: none -> 18 us  [the longest x4 9.13 us: shards(): got.append(lax.ppermute(mixed[s], DEVICES, back))]
  transfers between devices with their start and end apart: 5 -> 11, of which waited for: 3 -> 4; matrix products, arithmetic and copies ran while one was open for 11% -> 1% of each run, Pallas kernels for 0% -> 10%
where the time goes in v1:
time: 155 us; the launch traced here: 154 us
  blocking collectives  51.9 us (33%)
  starting transfers between devices  35.7 us (23%)
  Pallas kernels  27.5 us (18%)
  waiting for transfers between devices  26.9 us (17%)
  local copies, waits for them, and re-layouts  7.72 us (5%)
  other arithmetic  3.8 us (2%)
    all_to_all x1, blocking collectives, shards(): terms = lax.all_to_all(terms, DEVICES, 0, 0, tiled=True)  51.9 us
    all_to_all x1, waiting for transfers between devices, shards(): lax.all_to_all(jnp.broadcast_to(rows[None], (devices,) + rows.shape), DEV...  17.3 us
    pallas_call x1, Pallas kernels, queries(): pl.pallas_call(query_kernel, grid=(blocks,), in_specs=[pl.BlockSpec((1, r...  10.7 us
    pallas_call x1, Pallas kernels, outputs(): pl.pallas_call(output_kernel, grid=(blocks,), in_specs=[whole_spec((rows,...  10.5 us
    ppermute x4, starting transfers between devices, shards(): got.append(lax.ppermute(mixed[s], DEVICES, back))  9.13 us
    ppermute x4, starting transfers between devices, shards(): got.append(lax.ppermute(block, DEVICES, there))  8.9 us
    all_to_all x1, starting transfers between devices, shards(): lax.all_to_all(jnp.broadcast_to(rows[None], (devices,) + rows.shape), DEV...  7.52 us
    all_to_all x1, waiting for transfers between devices, shards(): cache = lax.all_to_all(send, PLANE, 0, 0, tiled=True)  6.37 us
  transfers between devices with their start and end apart: 11, of which 4 were waited for; matrix products, arithmetic and copies ran while one was open for 1% of the time, Pallas kernels for 10%

profile of v1, /device:TPU:0, one launch (start us, length us, event | category | flops | bytes accessed | tf_op | source)
XLA Modules:
  0.0 153.9 jit_solution(5485429046605839238)
XLA Ops:
  0.0 0.9 copy.12
  0.9 1.1 broadcast_in_dim.39
  2.0 7.5 %all-to-all-start = ((bf16[16,64,512]{2,1,0:T(8,128)(2,1)}), bf16[16,64,512]{2,1,0:T(8,128)(2,1)S(1)}, u32[]{:S(2)}, u32[]{:S(2)}) async-start(bf16[16,64,512]{2,1,0:T(8,128)(2,1)} %broadcast_in_dim.39), calls=%async_computation | async-start | bytes 2097152 | tf_op jit(solution)/shard_map/all_to_all | solution.py:275
  10.4 1.2 copy-done.3
  11.7 3.4 %used_pages.1 = bf16[4,2,128,256]{3,2,1,0:T(8,128)(2,1)} custom-call(s32[4,32]{1,0:T(4,128)S(1)} %copy-done.6, s32[3]{0:T(128)S(1)} %pad_add_fusion.1.place, f32[16,16]{1,0:T(8,128)S(1)} %convert_element_type.19.scales, bf16[16,16,2048]{2,1,0:T(8,128)(2,1)S(1)} %copy-done.3), custom_call_target="tpu_custom_call" | custom-call | tf_op jit(solution)/shard_map/used_pages/pallas_call | solution.py:59
  15.2 17.3 %all-to-all-done.x_ref = bf16[16,64,512]{2,1,0:T(8,128)(2,1)S(1)} async-done(((bf16[16,64,512]{2,1,0:T(8,128)(2,1)}), bf16[16,64,512]{2,1,0:T(8,128)(2,1)S(1)}, u32[]{:S(2)}, u32[]{:S(2)}) %all-to-all-start) | async-done | bytes 1048608 | tf_op jit(solution)/shard_map/all_to_all | solution.py:275
  32.5 4.1 %all-to-all-start.1 = ((bf16[4,2,128,256]{3,2,1,0:T(8,128)(2,1)}), bf16[4,2,128,256]{3,2,1,0:T(8,128)(2,1)}, u32[]{:S(2)}, u32[]{:S(2)}) async-start(bf16[4,2,128,256]{3,2,1,0:T(8,128)(2,1)} %used_pages.1), calls=%async_computation.1 | async-start | bytes 1048576 | tf_op jit(solution)/shard_map/all_to_all | solution.py:281
  36.9 0.9 norm_and_pairs.1
  37.8 1.0 copy-done.1
  39.6 6.4 %all-to-all-done.1.cache_ref = bf16[4,2,128,256]{3,2,1,0:T(8,128)(2,1)} async-done(((bf16[4,2,128,256]{3,2,1,0:T(8,128)(2,1)}), bf16[4,2,128,256]{3,2,1,0:T(8,128)(2,1)}, u32[]{:S(2)}, u32[]{:S(2)}) %all-to-all-start.1) | async-done | bytes 524320 | tf_op jit(solution)/shard_map/all_to_all | solution.py:281
  45.9 6.0 %all-to-all-start.2 = ((f32[16,16,512]{2,1,0:T(8,128)}), f32[16,16,512]{2,1,0:T(8,128)S(1)}, u32[]{:S(2)}, u32[]{:S(2)}) async-start(f32[16,16,512]{2,1,0:T(8,128)} %bitcast.55), calls=%async_computation.2 | async-start | bytes 1048576 | tf_op jit(solution)/shard_map/all_to_all | solution.py:302
  52.1 1.2 copy-done.2
  53.3 10.7 %queries.1 = bf16[64,512]{1,0:T(8,128)(2,1)S(1)} custom-call(bf16[16,64,512]{2,1,0:T(8,128)(2,1)S(1)} %copy-done.2, bf16[8192,512]{1,0:T(8,128)(2,1)} %weight_ref.4, f32[64,128]{1,0:T(8,128)S(1)} %bitcast.57, f32[64,128]{1,0:T(8,128)S(1)} %bitcast.58), custom_call_target="tpu_custom_call" | custom-call | tf_op jit(solution)/shard_map/queries/pallas_call | solution.py:148
  64.7 6.2 %collective-permute-start.3 = (bf16[16,512]{1,0:T(8,128)(2,1)S(1)}, bf16[16,512]{1,0:T(8,128)(2,1)S(1)}, u32[]{:S(2)}, u32[]{:S(2)}) collective-permute-start(bf16[16,512]{1,0:T(8,128)(2,1)S(1)} %get-tuple-element.14), channel_id=1, source_target_pairs={{0,12},{1,0},{2,4},{3,8},{4,13},{5,1},{6,5},{7,9},{8,14},{9,2},{10... | collective-permute-start | bytes 49160 | tf_op jit(solution)/shard_map/ppermute | solution.py:318
  71.5 1.4 collective-permute-start.1
  73.7 1.3 collective-permute-done.2
  75.1 2.0 %attend.1 = bf16[4,16,512]{2,1,0:T(8,128)(2,1)S(1)} custom-call(s32[2]{0:T(128)S(1)} %pad_add_fusion.place, bf16[4,16,512]{2,1,0:T(8,128)(2,1)S(1)} %pad_maximum_fusion.q_ref, bf16[4,2,128,256]{3,2,1,0:T(8,128)(2,1)} %all-to-all-done.1.cache_ref, f32[16,16,512]{2,1,0:T(8,128)S(1)} %all-to-all-done.2.pair_ref, f32[16,128]{1,0:T(8,128)S(1)} %get-tuple-element.21.cos_ref, ...), custom_call_target="tpu_custom_call" | custom-call | tf_op jit(solution)/shard_map/attend/pallas_call | solution.py:225
  77.8 3.1 %collective-permute-start.7 = (bf16[16,512]{1,0:T(8,128)(2,1)S(1)}, bf16[16,512]{1,0:T(8,128)(2,1)S(1)}, u32[]{:S(2)}, u32[]{:S(2)}) collective-permute-start(bf16[16,512]{1,0:T(8,128)(2,1)S(1)} %get-tuple-element.10), channel_id=1, source_target_pairs={{12,0},{0,1},{4,2},{8,3},{13,4},{1,5},{5,6},{9,7},{14,8},{2,9},{6,... | collective-permute-start | bytes 49160 | tf_op jit(solution)/shard_map/ppermute | solution.py:336
  80.9 2.7 %collective-permute-start.6 = (bf16[16,512]{1,0:T(8,128)(2,1)S(1)}, bf16[16,512]{1,0:T(8,128)(2,1)S(1)}, u32[]{:S(2)}, u32[]{:S(2)}) collective-permute-start(bf16[16,512]{1,0:T(8,128)(2,1)S(1)} %get-tuple-element.11), channel_id=1, source_target_pairs={{8,0},{12,1},{0,2},{4,3},{9,4},{13,5},{1,6},{5,7},{10,8},{14,9},{2... | collective-permute-start | bytes 49160 | tf_op jit(solution)/shard_map/ppermute | solution.py:336
  83.5 2.7 %collective-permute-start.5 = (bf16[16,512]{1,0:T(8,128)(2,1)S(1)}, bf16[16,512]{1,0:T(8,128)(2,1)S(1)}, u32[]{:S(2)}, u32[]{:S(2)}) collective-permute-start(bf16[16,512]{1,0:T(8,128)(2,1)S(1)} %get-tuple-element.12), channel_id=1, source_target_pairs={{4,0},{8,1},{12,2},{0,3},{5,4},{9,5},{13,6},{1,7},{6,8},{10,9},{14... | collective-permute-start | bytes 49160 | tf_op jit(solution)/shard_map/ppermute | solution.py:336
  86.4 1.9 %collective-permute-done.6 = bf16[16,512]{1,0:T(8,128)(2,1)S(1)} collective-permute-done((bf16[16,512]{1,0:T(8,128)(2,1)S(1)}, bf16[16,512]{1,0:T(8,128)(2,1)S(1)}, u32[]{:S(2)}, u32[]{:S(2)}) %collective-permute-start.6) | collective-permute-done | bytes 16416 | tf_op jit(solution)/shard_map/ppermute | solution.py:336
  89.0 10.5 %outputs.1 = f32[16,64,512]{2,1,0:T(8,128)S(1)} custom-call(bf16[64,512]{1,0:T(8,128)(2,1)S(1)} %bitcast_select_fusion.x_ref, bf16[512,8192]{1,0:T(8,128)(2,1)} %weight_ref.5), custom_call_target="tpu_custom_call" | custom-call | tf_op jit(solution)/shard_map/outputs/pallas_call | solution.py:243
  99.5 51.9 %all_to_all.20 = f32[16,64,512]{2,1,0:T(8,128)} all-to-all(f32[16,64,512]{2,1,0:T(8,128)S(1)} %outputs.1), channel_id=1, replica_groups=mesh['groups'=2,'req'=4,'sub'=2,'section'=2] {'req','sub','section'}, dimensions={0} | all-to-all | bytes 4194304 | tf_op jit(solution)/shard_map/all_to_all | solution.py:343
  151.5 1.8 %reduce_sum.11 = f32[64,512]{1,0:T(8,128)S(1)} reduce(f32[16,64,512]{2,1,0:T(8,128)} %all_to_all.20, f32[]{:T(128)} %constant.95.clone.1), dimensions={0}, to_apply=%region_0.1 | reduce | flops 491520 | bytes 2228228 | tf_op jit(solution)/shard_map/reduce_sum | solution.py:344
  (53 shorter events, 6.2 us)
Async XLA Ops:
  0.0 9.6 %copy-start.8 = (bf16[16,16]{1,0:T(8,128)(2,1)S(1)}, bf16[16,16]{1,0:T(8,128)(2,1)}, u32[]{:S(2)}) copy-start(bf16[16,16]{1,0:T(8,128)(2,1)} %param.15) | copy-start | bytes 1540
  0.0 9.7 %copy-start.9 = (s32[4]{0:T(128)S(1)}, s32[4]{0:T(128)}, u32[]{:S(2)}) copy-start(s32[4]{0:T(128)} %param.16) | copy-start | bytes 52
  0.0 10.4 %copy-start.6 = (s32[4,32]{1,0:T(4,128)S(1)}, s32[4,32]{1,0:T(4,128)}, u32[]{:S(2)}) copy-start(s32[4,32]{1,0:T(4,128)} %table.1) | copy-start | bytes 1540
  2.0 34.8 %copy-start = (bf16[512,2048]{1,0:T(8,128)(2,1)S(1)}, bf16[512,2048]{1,0:T(8,128)(2,1)}, u32[]{:S(2)}) copy-start(bf16[512,2048]{1,0:T(8,128)(2,1)} %weight_ref.3) | copy-start | bytes 6291460
  2.0 34.8 %copy-start.5 = (f32[8192]{0:T(1024)S(1)}, f32[8192]{0:T(1024)}, u32[]{:S(2)}) copy-start(f32[8192]{0:T(1024)} %param.10) | copy-start | bytes 98308
  2.0 30.5 %all-to-all-start = ((bf16[16,64,512]{2,1,0:T(8,128)(2,1)}), bf16[16,64,512]{2,1,0:T(8,128)(2,1)S(1)}, u32[]{:S(2)}, u32[]{:S(2)}) async-start(bf16[16,64,512]{2,1,0:T(8,128)(2,1)} %broadcast_in_dim.39), calls=%async_computation | async-start | bytes 2097152 | tf_op jit(solution)/shard_map/all_to_all | solution.py:275
  10.4 1.2 copy-start.3
  32.5 13.5 %all-to-all-start.1 = ((bf16[4,2,128,256]{3,2,1,0:T(8,128)(2,1)}), bf16[4,2,128,256]{3,2,1,0:T(8,128)(2,1)}, u32[]{:S(2)}, u32[]{:S(2)}) async-start(bf16[4,2,128,256]{3,2,1,0:T(8,128)(2,1)} %used_pages.1), calls=%async_computation.1 | async-start | bytes 1048576 | tf_op jit(solution)/shard_map/all_to_all | solution.py:281
  37.8 1.0 copy-start.1
  38.8 0.8 copy-start.4
  45.9 29.1 %all-to-all-start.2 = ((f32[16,16,512]{2,1,0:T(8,128)}), f32[16,16,512]{2,1,0:T(8,128)S(1)}, u32[]{:S(2)}, u32[]{:S(2)}) async-start(f32[16,16,512]{2,1,0:T(8,128)} %bitcast.55), calls=%async_computation.2 | async-start | bytes 1048576 | tf_op jit(solution)/shard_map/all_to_all | solution.py:302
  52.1 1.2 copy-start.2
  64.0 9.7 %collective-permute-start = (bf16[16,512]{1,0:T(8,128)(2,1)S(1)}, bf16[16,512]{1,0:T(8,128)(2,1)S(1)}, u32[]{:S(2)}, u32[]{:S(2)}) collective-permute-start(bf16[16,512]{1,0:T(8,128)(2,1)S(1)} %get-tuple-element.13), channel_id=1, source_target_pairs={{0,0},{1,4},{2,8},{3,12},{4,1},{5,5},{6,9},{7,13},{8,2},{9,6},{10,... | collective-permute-start | bytes 49160 | tf_op jit(solution)/shard_map/ppermute | solution.py:318
  64.7 9.0 %collective-permute-start.3 = (bf16[16,512]{1,0:T(8,128)(2,1)S(1)}, bf16[16,512]{1,0:T(8,128)(2,1)S(1)}, u32[]{:S(2)}, u32[]{:S(2)}) collective-permute-start(bf16[16,512]{1,0:T(8,128)(2,1)S(1)} %get-tuple-element.14), channel_id=1, source_target_pairs={{0,12},{1,0},{2,4},{3,8},{4,13},{5,1},{6,5},{7,9},{8,14},{9,2},{10... | collective-permute-start | bytes 49160 | tf_op jit(solution)/shard_map/ppermute | solution.py:318
  70.9 4.1 %collective-permute-start.2 = (bf16[16,512]{1,0:T(8,128)(2,1)S(1)}, bf16[16,512]{1,0:T(8,128)(2,1)S(1)}, u32[]{:S(2)}, u32[]{:S(2)}) collective-permute-start(bf16[16,512]{1,0:T(8,128)(2,1)S(1)} %get-tuple-element.15), channel_id=1, source_target_pairs={{0,8},{1,12},{2,0},{3,4},{4,9},{5,13},{6,1},{7,5},{8,10},{9,14},{1... | collective-permute-start | bytes 49160 | tf_op jit(solution)/shard_map/ppermute | solution.py:318
  71.5 3.5 %collective-permute-start.1 = (bf16[16,512]{1,0:T(8,128)(2,1)S(1)}, bf16[16,512]{1,0:T(8,128)(2,1)S(1)}, u32[]{:S(2)}, u32[]{:S(2)}) collective-permute-start(bf16[16,512]{1,0:T(8,128)(2,1)S(1)} %get-tuple-element.16), channel_id=1, source_target_pairs={{0,4},{1,8},{2,12},{3,0},{4,5},{5,9},{6,13},{7,1},{8,6},{9,10},{10... | collective-permute-start | bytes 49160 | tf_op jit(solution)/shard_map/ppermute | solution.py:318
  77.1 9.3 %collective-permute-start.4 = (bf16[16,512]{1,0:T(8,128)(2,1)S(1)}, bf16[16,512]{1,0:T(8,128)(2,1)S(1)}, u32[]{:S(2)}, u32[]{:S(2)}) collective-permute-start(bf16[16,512]{1,0:T(8,128)(2,1)S(1)} %get-tuple-element.9), channel_id=1, source_target_pairs={{0,0},{4,1},{8,2},{12,3},{1,4},{5,5},{9,6},{13,7},{2,8},{6,9},{10,... | collective-permute-start | bytes 49160 | tf_op jit(solution)/shard_map/ppermute | solution.py:336
  77.8 8.7 %collective-permute-start.7 = (bf16[16,512]{1,0:T(8,128)(2,1)S(1)}, bf16[16,512]{1,0:T(8,128)(2,1)S(1)}, u32[]{:S(2)}, u32[]{:S(2)}) collective-permute-start(bf16[16,512]{1,0:T(8,128)(2,1)S(1)} %get-tuple-element.10), channel_id=1, source_target_pairs={{12,0},{0,1},{4,2},{8,3},{13,4},{1,5},{5,6},{9,7},{14,8},{2,9},{6,... | collective-permute-start | bytes 49160 | tf_op jit(solution)/shard_map/ppermute | solution.py:336
  80.9 7.5 %collective-permute-start.6 = (bf16[16,512]{1,0:T(8,128)(2,1)S(1)}, bf16[16,512]{1,0:T(8,128)(2,1)S(1)}, u32[]{:S(2)}, u32[]{:S(2)}) collective-permute-start(bf16[16,512]{1,0:T(8,128)(2,1)S(1)} %get-tuple-element.11), channel_id=1, source_target_pairs={{8,0},{12,1},{0,2},{4,3},{9,4},{13,5},{1,6},{5,7},{10,8},{14,9},{2... | collective-permute-start | bytes 49160 | tf_op jit(solution)/shard_map/ppermute | solution.py:336
  83.5 4.9 %collective-permute-start.5 = (bf16[16,512]{1,0:T(8,128)(2,1)S(1)}, bf16[16,512]{1,0:T(8,128)(2,1)S(1)}, u32[]{:S(2)}, u32[]{:S(2)}) collective-permute-start(bf16[16,512]{1,0:T(8,128)(2,1)S(1)} %get-tuple-element.12), channel_id=1, source_target_pairs={{4,0},{8,1},{12,2},{0,3},{5,4},{9,5},{13,6},{1,7},{6,8},{10,9},{14... | collective-permute-start | bytes 49160 | tf_op jit(solution)/shard_map/ppermute | solution.py:336
  151.5 1.8 %copy-start.7 = (bf16[2,32,512]{2,1,0:T(8,128)(2,1)S(1)}, bf16[2,32,512]{2,1,0:T(8,128)(2,1)}, u32[]{:S(2)}) copy-start(bf16[2,32,512]{2,1,0:T(8,128)(2,1)} %param.9) | copy-start | bytes 196612

commit v2 on v1

v2 whole, which is shorter than its diff:
```python
import jax
import jax.numpy as jnp
from jax import lax
from jax.experimental import pallas as pl
from jax.experimental.pallas import tpu as pltpu
from jax.sharding import Mesh
from jax.sharding import PartitionSpec as P

QUERY_HEADS = 64
KEY_VALUE_HEADS = 8
HEAD_SIZE = 128
GROUP_REQUESTS = 4
SAMPLES = 8
PAGE_TOKENS = 16
STEPS = 2
ROWS = STEPS * SAMPLES
PAIR = 2 * HEAD_SIZE
DEVICES = ("req", "sub", "section")
PLANE = ("sub", "section")
CHIPS = ("req", "sub")

theta_base = 500000.0
eps_norm = 1e-05
VMEM = 16 * 2**20


def params(**more):
    return pltpu.CompilerParams(vmem_limit_bytes=VMEM, **more)


def whole_spec(shape):
    return pl.BlockSpec(shape, lambda *_: (0,) * len(shape))


def turn(vectors, cosine, sine):
    return vectors * cosine + pltpu.roll(vectors, HEAD_SIZE // 2, vectors.ndim - 1) * sine


def pages_kernel(table, place, scales, page_ref, *out_refs):
    e = pl.program_id(0)
    targets, heads = len(out_refs), out_refs[0].shape[0]
    page = table[place[0], e * targets + place[1]] - place[2]
    repeats = targets * heads // KEY_VALUE_HEADS
    for shift, out_ref in enumerate(out_refs):
        first = lax.rem(place[1] + shift, targets) * heads // repeats
        for h in range(heads):
            for part in range(2):
                c = (first + h) * 2 + part
                columns = pl.ds(pl.multiple_of(c * HEAD_SIZE, HEAD_SIZE), HEAD_SIZE)
                block = page_ref[0, :, columns].astype(jnp.float32)
                out_ref[h, :, part * HEAD_SIZE : (part + 1) * HEAD_SIZE] = (
                    block * scales[page, c]
                ).astype(jnp.bfloat16)


def used_pages(pages, scales, table, place, targets, heads):
    entries = table.shape[1] // targets
    return pl.pallas_call(
        pages_kernel,
        grid_spec=pltpu.PrefetchScalarGridSpec(
            num_scalar_prefetch=3,
            grid=(entries,),
            in_specs=[
                pl.BlockSpec(
                    (1, PAGE_TOKENS, pages.shape[2]),
                    lambda e, table, place, scales: (
                        table[place[0], e * targets + place[1]] - place[2],
                        0,
                        0,
                    ),
                )
            ],
            out_specs=[
                pl.BlockSpec((heads, PAGE_TOKENS, PAIR), lambda e, *_: (0, e, 0))
            ]
            * targets,
        ),
        out_shape=[
            jax.ShapeDtypeStruct((heads, entries * PAGE_TOKENS, PAIR), jnp.bfloat16)
        ]
        * targets,
        compiler_params=params(),
        name="used_pages",
    )(table, place, scales.astype(jnp.float32), pages)


def pairs_kernel(place, mine_ref, other_ref, rows_ref, gain_ref, weight_ref, scale_ref, pair_ref):
    blocks, rows, width = mine_ref.shape
    total = jnp.zeros((rows, width), jnp.float32)
    for ref in (mine_ref, other_ref):
        for i in range(blocks):
            x = ref[i].astype(jnp.float32)
            total += x * x
    mean = jnp.sum(total, axis=-1, keepdims=True) / (2 * blocks * width)
    scale = lax.rsqrt(mean + eps_norm)
    scale_ref[...] = jnp.broadcast_to(scale, scale_ref.shape)
    x = rows_ref[...].astype(jnp.float32)
    mine = (x * scale * gain_ref[place[0]]).astype(jnp.bfloat16)
    requests, targets, _, wide = pair_ref.shape
    repeats = targets * wide // weight_ref.shape[1]
    for t in range(0, targets, repeats):
        first = (t // repeats) * wide
        part = jnp.dot(
            mine, weight_ref[:, first : first + wide], preferred_element_type=jnp.float32
        )
        for r in range(requests):
            for step in range(STEPS):
                first = (step * requests + r) * SAMPLES
                for c in range(repeats):
                    pair_ref[r, t + c, step * SAMPLES : (step + 1) * SAMPLES] = part[
                        first : first + SAMPLES
                    ]


def scale_and_pairs(mine, other, rows, gain, weight, device, targets, heads):
    blocks, count, width = mine.shape
    shapes = [
        jax.ShapeDtypeStruct((count, HEAD_SIZE), jnp.float32),
        jax.ShapeDtypeStruct((GROUP_REQUESTS, targets, ROWS, heads * PAIR), jnp.float32),
    ]
    return pl.pallas_call(
        pairs_kernel,
        in_specs=[pl.BlockSpec(memory_space=pltpu.SMEM)]
        + [pl.BlockSpec(memory_space=pltpu.VMEM)] * 5,
        out_specs=[pl.BlockSpec(memory_space=pltpu.VMEM)] * 2,
        out_shape=shapes,
        compiler_params=params(),
        name="scale_and_pairs",
    )(device, mine, other, rows, gain, weight)


def query_kernel(
    place, mine_ref, other_ref, scale_ref, gain_ref, weight_ref, cos_ref, sin_ref, out_ref
):
    blocks, rows, width = mine_ref.shape
    columns = weight_ref.shape[1]
    scale = scale_ref[:, :1]
    total = jnp.zeros((rows, columns), jnp.float32)
    for i in range(blocks):
        for ref, core in ((mine_ref, place[1]), (other_ref, 1 - place[1])):
            block = 2 * i + core
            x = ref[i].astype(jnp.float32)
            x = (x * scale * gain_ref[block]).astype(jnp.bfloat16)
            depth = pl.ds(pl.multiple_of(block * width, width), width)
            total += jnp.dot(x, weight_ref[depth, :], preferred_element_type=jnp.float32)
    for head in range(columns // HEAD_SIZE):
        part = slice(head * HEAD_SIZE, (head + 1) * HEAD_SIZE)
        turned = turn(total[:, part], cos_ref[...], sin_ref[...])
        for r in range(GROUP_REQUESTS):
            first, second = r * SAMPLES, (GROUP_REQUESTS + r) * SAMPLES
            out_ref[r, :, part] = jnp.concatenate(
                [turned[first : first + SAMPLES], turned[second : second + SAMPLES]], axis=0
            ).astype(jnp.bfloat16)


def queries(place, mine, other, scale, gain, weight, cosine, sine):
    columns = weight.shape[1]
    return pl.pallas_call(
        query_kernel,
        in_specs=[pl.BlockSpec(memory_space=pltpu.SMEM)]
        + [pl.BlockSpec(memory_space=pltpu.VMEM)] * 7,
        out_specs=pl.BlockSpec(memory_space=pltpu.VMEM),
        out_shape=jax.ShapeDtypeStruct((GROUP_REQUESTS, ROWS, columns), jnp.bfloat16),
        compiler_params=params(),
        name="queries",
    )(place, mine, other, scale, gain, weight, cosine, sine)


def attend_kernel(place, *refs):
    r, length, spot = place[0], place[1], place[2]
    q_refs = refs[:GROUP_REQUESTS]
    out_refs = refs[-GROUP_REQUESTS:]
    pair_ref, cos_ref, sin_ref = refs[GROUP_REQUESTS : GROUP_REQUESTS + 3]
    cache_refs = refs[GROUP_REQUESTS + 3 : -GROUP_REQUESTS]
    sources = len(cache_refs)
    heads, span, _ = cache_refs[0].shape
    quarter = q_refs[0].shape[1] // HEAD_SIZE
    parts = GROUP_REQUESTS // heads
    tokens = sources * span
    pairs = pair_ref[0]
    for i in range(1, pair_ref.shape[0]):
        pairs = pairs + pair_ref[i]
    column = lax.broadcasted_iota(jnp.int32, (1, tokens), 1)
    shift, inside = column // span, column % span
    source = (spot - shift + sources) % sources
    position = (inside // PAGE_TOKENS * sources + source) * PAGE_TOKENS + inside % PAGE_TOKENS
    visible = position < length
    count = GROUP_REQUESTS * quarter * ROWS
    row = lax.broadcasted_iota(jnp.int32, (count, ROWS), 0) % ROWS
    other = lax.broadcasted_iota(jnp.int32, (count, ROWS), 1)
    own_visible = (row % SAMPLES == other % SAMPLES) & (other // SAMPLES <= row // SAMPLES)
    query = jnp.concatenate(
        [
            ref[:, head * HEAD_SIZE : (head + 1) * HEAD_SIZE]
            for ref in q_refs
            for head in range(quarter)
        ],
        axis=0,
    )
    block = quarter * ROWS
    factor = HEAD_SIZE ** (-0.5)
    contract = (((1,), (1,)), ((), ()))
    result = None
    for h in range(heads):
        keys = jnp.concatenate([ref[h, :, :HEAD_SIZE] for ref in cache_refs], axis=0)
        values = jnp.concatenate([ref[h, :, HEAD_SIZE:] for ref in cache_refs], axis=0)
        new_key = turn(
            pairs[:, h * PAIR : h * PAIR + HEAD_SIZE], cos_ref[...], sin_ref[...]
        ).astype(jnp.bfloat16)
        new_value = pairs[:, h * PAIR + HEAD_SIZE : (h + 1) * PAIR].astype(jnp.bfloat16)
        scores = lax.dot_general(query, keys, contract, preferred_element_type=jnp.float32)
        scores = jnp.where(visible, scores * factor, -jnp.inf)
        own = lax.dot_general(query, new_key, contract, preferred_element_type=jnp.float32)
        own = jnp.where(own_visible, own * factor, -jnp.inf)
        highest = jnp.maximum(
            jnp.max(scores, axis=-1, keepdims=True), jnp.max(own, axis=-1, keepdims=True)
        )
        scores = jnp.exp(scores - highest)
        own = jnp.exp(own - highest)
        total = jnp.sum(scores, axis=-1, keepdims=True) + jnp.sum(own, axis=-1, keepdims=True)
        mixed = jnp.dot(
            (scores / total).astype(jnp.bfloat16), values, preferred_element_type=jnp.float32
        ) + jnp.dot(
            (own / total).astype(jnp.bfloat16), new_value, preferred_element_type=jnp.float32
        )
        if result is None:
            result = mixed
        else:
            slot = lax.broadcasted_iota(jnp.int32, (count, 1), 0) // block
            source = (r - slot + GROUP_REQUESTS) % GROUP_REQUESTS
            result = jnp.where(source // parts == h, mixed, result)
    result = result.astype(jnp.bfloat16)
    for slot, out_ref in enumerate(out_refs):
        for head in range(quarter):
            first = slot * block + head * ROWS
            out_ref[:, head * HEAD_SIZE : (head + 1) * HEAD_SIZE] = result[first : first + ROWS]


def attend(place, query, pairs, cosine, sine, cache):
    shape = jax.ShapeDtypeStruct(query[0].shape, jnp.bfloat16)
    return pl.pallas_call(
        attend_kernel,
        in_specs=[pl.BlockSpec(memory_space=pltpu.SMEM)]
        + [pl.BlockSpec(memory_space=pltpu.VMEM)] * (len(query) + 3 + len(cache)),
        out_specs=[pl.BlockSpec(memory_space=pltpu.VMEM)] * GROUP_REQUESTS,
        out_shape=[shape] * GROUP_REQUESTS,
        compiler_params=params(),
        name="attend",
    )(place, *query, pairs, cosine, sine, *cache)


def output_kernel(place, *refs):
    x_refs, weight_ref, out_ref = refs[:GROUP_REQUESTS], refs[-2], refs[-1]
    blocks, rows, width = out_ref.shape
    order = [lax.rem(r - place[0] + GROUP_REQUESTS, GROUP_REQUESTS) for r in range(GROUP_REQUESTS)]
    x = jnp.stack([ref[...] for ref in x_refs])
    pieces = []
    for r in range(GROUP_REQUESTS):
        piece = x[0]
        for s in range(1, GROUP_REQUESTS):
            piece = jnp.where(order[r] == s, x[s], piece)
        pieces.append(piece)
    x = jnp.concatenate(pieces, axis=0)
    for i in range(blocks):
        columns = pl.ds(pl.multiple_of((2 * i + place[1]) * width, width), width)
        part = jnp.dot(x, weight_ref[:, columns], preferred_element_type=jnp.float32)
        for r in range(GROUP_REQUESTS):
            for step in range(STEPS):
                source = r * ROWS + step * SAMPLES
                target = (step * GROUP_REQUESTS + r) * SAMPLES
                out_ref[i, target : target + SAMPLES] = part[source : source + SAMPLES]


def outputs(place, mixed, weight, blocks):
    rows = GROUP_REQUESTS * ROWS
    width = weight.shape[1] // (2 * blocks)
    return pl.pallas_call(
        output_kernel,
        in_specs=[pl.BlockSpec(memory_space=pltpu.SMEM)]
        + [pl.BlockSpec(memory_space=pltpu.VMEM)] * (GROUP_REQUESTS + 1),
        out_specs=pl.BlockSpec(memory_space=pltpu.VMEM),
        out_shape=jax.ShapeDtypeStruct((blocks, rows, width), jnp.float32),
        compiler_params=params(),
        name="outputs",
    )(place, *mixed, weight)


def fold_core_kernel(place, mine_ref, got_ref, *out_refs):
    subs = len(out_refs)
    for shift, out_ref in enumerate(out_refs):
        sub = lax.rem(place[0] + shift, subs)
        for i in range(GROUP_REQUESTS):
            block = i * subs + sub
            out_ref[i] = mine_ref[block] + got_ref[block]


def fold_core(place, mine, got, subs):
    shape = jax.ShapeDtypeStruct((GROUP_REQUESTS,) + mine.shape[1:], jnp.float32)
    return pl.pallas_call(
        fold_core_kernel,
        in_specs=[pl.BlockSpec(memory_space=pltpu.SMEM)]
        + [pl.BlockSpec(memory_space=pltpu.VMEM)] * 2,
        out_specs=[pl.BlockSpec(memory_space=pltpu.VMEM)] * subs,
        out_shape=[shape] * subs,
        compiler_params=params(),
        name="fold_core",
    )(place, mine, got)


def fold_sub_kernel(place, *refs):
    in_refs, out_refs = refs[:-GROUP_REQUESTS], refs[-GROUP_REQUESTS:]
    for shift, out_ref in enumerate(out_refs):
        block = lax.rem(place[0] + shift, GROUP_REQUESTS)
        total = in_refs[0][block]
        for ref in in_refs[1:]:
            total = total + ref[block]
        out_ref[...] = total


def fold_sub(place, parts):
    shape = jax.ShapeDtypeStruct(parts[0].shape[1:], jnp.float32)
    return pl.pallas_call(
        fold_sub_kernel,
        in_specs=[pl.BlockSpec(memory_space=pltpu.SMEM)]
        + [pl.BlockSpec(memory_space=pltpu.VMEM)] * len(parts),
        out_specs=[pl.BlockSpec(memory_space=pltpu.VMEM)] * GROUP_REQUESTS,
        out_shape=[shape] * GROUP_REQUESTS,
        compiler_params=params(),
        name="fold_sub",
    )(place, *parts)


def finish_kernel(rows_ref, *refs):
    total = refs[0][...]
    for ref in refs[1:-1]:
        total = total + ref[...]
    refs[-1][...] = (total + rows_ref[...].astype(jnp.float32)).astype(jnp.bfloat16)


def finish(rows, parts):
    return pl.pallas_call(
        finish_kernel,
        in_specs=[pl.BlockSpec(memory_space=pltpu.VMEM)] * (1 + len(parts)),
        out_specs=pl.BlockSpec(memory_space=pltpu.VMEM),
        out_shape=jax.ShapeDtypeStruct(rows.shape, jnp.bfloat16),
        compiler_params=params(),
        name="finish",
    )(rows, *parts)


def passed(array, axis, shift):
    size = lax.axis_size(axis)
    return lax.ppermute(array, axis, [(i, (i + shift) % size) for i in range(size)])


def scalars(*values):
    return jnp.stack(values).astype(jnp.int32)


def shards(
    hidden,
    norm_gain,
    w_query,
    key_value_weight,
    w_output,
    prompt_cache_pages,
    per_page_scales,
    lengths,
    block_table,
):
    devices = lax.axis_size(DEVICES)
    targets = lax.axis_size(PLANE)
    subs = lax.axis_size("sub")
    chips = devices // 2
    heads = max(1, KEY_VALUE_HEADS // targets)
    device = lax.axis_index(DEVICES)
    request = lax.axis_index("req")
    sub = lax.axis_index("sub")
    core = lax.axis_index("section")
    spot = lax.axis_index(PLANE)
    group, member = device // GROUP_REQUESTS, device % GROUP_REQUESTS
    width = hidden.shape[2]

    rows = hidden.reshape(GROUP_REQUESTS * ROWS, width)
    mine = lax.all_to_all(
        jnp.broadcast_to(rows[None], (chips,) + rows.shape), CHIPS, 0, 0, tiled=True
    )
    other = passed(mine, "section", 1)

    place = scalars(request, spot, device * prompt_cache_pages.shape[0])
    send = used_pages(prompt_cache_pages, per_page_scales, block_table, place, targets, heads)
    cache = [send[0]]
    for s in range(1, targets):
        there = [(d, (d + s) % targets) for d in range(targets)]
        cache.append(lax.ppermute(send[s], PLANE, there))

    half = HEAD_SIZE // 2
    freqs = jnp.exp(
        -jnp.log(theta_base) * jnp.arange(half, dtype=jnp.float32) * (2.0 / HEAD_SIZE)
    )
    positions = (lengths[None, :] + jnp.arange(STEPS)[:, None]).astype(jnp.float32)
    angles = positions[..., None] * freqs
    cosine, sine = jnp.cos(angles), jnp.sin(angles)
    cosine = jnp.repeat(jnp.concatenate([cosine, cosine], axis=-1)[:, :, None], SAMPLES, axis=2)
    sine = jnp.repeat(jnp.concatenate([-sine, sine], axis=-1)[:, :, None], SAMPLES, axis=2)
    my_cosine = lax.dynamic_index_in_dim(cosine, request, 1, keepdims=False)
    my_sine = lax.dynamic_index_in_dim(sine, request, 1, keepdims=False)

    gain = norm_gain.reshape(devices, 1, width)
    scale, pairs = scale_and_pairs(
        mine, other, rows, gain, key_value_weight, scalars(device), targets, heads
    )
    pairs = lax.all_to_all(
        pairs.reshape(devices, ROWS, heads * PAIR), DEVICES, 0, 0, tiled=True
    )

    query = queries(
        scalars(device, core),
        mine,
        other,
        scale,
        gain,
        w_query,
        cosine.reshape(-1, HEAD_SIZE),
        sine.reshape(-1, HEAD_SIZE),
    )
    got = []
    for s in range(GROUP_REQUESTS):
        there = [
            (d, (d % GROUP_REQUESTS + s) % GROUP_REQUESTS * targets + d // GROUP_REQUESTS)
            for d in range(devices)
        ]
        block = lax.dynamic_index_in_dim(
            query, (member + s) % GROUP_REQUESTS, 0, keepdims=False
        )
        got.append(lax.ppermute(block, DEVICES, there))

    my_length = lax.dynamic_index_in_dim(lengths, request, 0, keepdims=False)
    mixed = attend(
        scalars(request, my_length, spot),
        got,
        pairs,
        my_cosine.reshape(ROWS, HEAD_SIZE),
        my_sine.reshape(ROWS, HEAD_SIZE),
        cache,
    )
    got = []
    for s in range(GROUP_REQUESTS):
        back = [
            ((d % GROUP_REQUESTS + s) % GROUP_REQUESTS * targets + d // GROUP_REQUESTS, d)
            for d in range(devices)
        ]
        got.append(lax.ppermute(mixed[s], DEVICES, back))

    away = outputs(scalars(member, 1 - core), got, w_output, chips)
    arrived = passed(away, "section", 1)
    kept = outputs(scalars(member, core), got, w_output, chips)
    parts = fold_core(scalars(sub), kept, arrived, subs)
    parts = [parts[0]] + [passed(parts[s], "sub", s) for s in range(1, subs)]
    parts = fold_sub(scalars(request), parts)
    parts = [parts[0]] + [passed(parts[s], "req", s) for s in range(1, GROUP_REQUESTS)]
    return finish(rows, parts).reshape(hidden.shape)


def solution(mesh):
    groups, tp, section = mesh.devices.shape
    finer = Mesh(
        mesh.devices.reshape(groups, GROUP_REQUESTS, tp // GROUP_REQUESTS, section),
        ("groups",) + DEVICES,
    )
    placed = (
        P(None, "groups", DEVICES),
        P(),
        P(None, DEVICES),
        P(DEVICES, None),
        P(DEVICES, None),
        P(("groups",) + DEVICES, None, None),
        P(("groups",) + DEVICES, None),
        P("groups"),
        P("groups", None),
    )
    return jax.shard_map(
        shards,
        mesh=finer,
        in_specs=placed,
        out_specs=P(None, "groups", DEVICES),
        check_vma=False,
    )
```

time: 155 us -> 108 us (0.70)
  blocking collectives: 51.9 us -> 0 us
  Pallas kernels: 27.5 us -> 10.5 us
  local copies, waits for them, and re-layouts: 7.72 us -> 18.9 us
  starting transfers between devices: 35.7 us -> 43.3 us
  waiting for transfers between devices: 26.9 us -> 31.7 us
    all_to_all x1 -> x0, blocking collectives: 51.9 us -> none  [shards(): terms = lax.all_to_all(terms, DEVICES, 0, 0, tiled=True)]
    ppermute x0 -> x9, waiting for transfers between devices: none -> 22.7 us  [the longest x6 22.7 us: passed(): lax.ppermute(array, axis, [(i, (i + shift) % size) for i in range(size)])]
    all_to_all x2 -> x1, waiting for transfers between devices: 23.6 us -> 6.81 us  [shards(): lax.all_to_all(jnp.broadcast_to(rows[None], (chips,) + rows.shape), CHIPS...]
    pallas_call x3 -> x7, Pallas kernels: 22 us -> 7.36 us  [the longest x2 2.76 us: outputs(): pl.pallas_call(output_kernel, in_specs=[pl.BlockSpec(memory_space=pltpu.S...]
    ppermute x0 -> x9, starting transfers between devices: none -> 13.2 us  [the longest x6 9.62 us: passed(): lax.ppermute(array, axis, [(i, (i + shift) % size) for i in range(size)])]
    unnamed x20, local copies, waits for them, and re-layouts: 4.28 us -> 16 us
    all_to_all x2 -> x1, starting transfers between devices: 11.6 us -> 7.28 us  [shards(): lax.all_to_all(jnp.broadcast_to(rows[None], (chips,) + rows.shape), CHIPS...]
    all_to_all x1, starting transfers between devices: 6.02 us -> 3.78 us  [shards(): lax.all_to_all(pairs.reshape(devices, ROWS, heads * PAIR), DEVICES, 0, 0,...]
  transfers between devices with their start and end apart: 11 -> 19, of which waited for: 4 -> 7; matrix products, arithmetic and copies ran while one was open for 1% -> 4% of each run, Pallas kernels for 10% -> 6%
where the time goes in v2:
time: 108 us; the launch traced here: 107 us
  starting transfers between devices  43.3 us (40%)
  waiting for transfers between devices  31.7 us (29%)
  local copies, waits for them, and re-layouts  18.9 us (17%)
  Pallas kernels  10.5 us (10%)
  other arithmetic  2.58 us (2%)
    ppermute x6, waiting for transfers between devices, passed(): lax.ppermute(array, axis, [(i, (i + shift) % size) for i in range(size)])  22.7 us
    unnamed x20, local copies, waits for them, and re-layouts  16 us
    ppermute x4, starting transfers between devices, shards(): got.append(lax.ppermute(block, DEVICES, there))  9.8 us
    ppermute x6, starting transfers between devices, passed(): lax.ppermute(array, axis, [(i, (i + shift) % size) for i in range(size)])  9.62 us
    ppermute x4, starting transfers between devices, shards(): got.append(lax.ppermute(mixed[s], DEVICES, back))  9.29 us
    all_to_all x1, starting transfers between devices, shards(): lax.all_to_all(jnp.broadcast_to(rows[None], (chips,) + rows.shape), CHIPS...  7.28 us
    all_to_all x1, waiting for transfers between devices, shards(): lax.all_to_all(jnp.broadcast_to(rows[None], (chips,) + rows.shape), CHIPS...  6.81 us
    all_to_all x1, starting transfers between devices, shards(): lax.all_to_all(pairs.reshape(devices, ROWS, heads * PAIR), DEVICES, 0, 0,...  3.78 us
  transfers between devices with their start and end apart: 19, of which 7 were waited for; matrix products, arithmetic and copies ran while one was open for 4% of the time, Pallas kernels for 6%

profile of v2, /device:TPU:0, one launch (start us, length us, event | category | flops | bytes accessed | tf_op | source)
XLA Modules:
  0.0 107.2 jit_solution(9674808991333801274)
XLA Ops:
  0.0 1.7 %broadcast_in_dim.6 = bf16[8,64,512]{2,1,0:T(8,128)(2,1)} broadcast(bf16[64,512]{1,0:T(8,128)(2,1)} %bitcast.28), dimensions={1,2} | broadcast | bytes 589824 | tf_op jit(solution)/shard_map/broadcast_in_dim | solution.py:386
  1.7 7.3 %all-to-all-start = ((bf16[8,64,512]{2,1,0:T(8,128)(2,1)}), bf16[8,64,512]{2,1,0:T(8,128)(2,1)S(1)}, u32[]{:S(2)}, u32[]{:S(2)}) async-start(bf16[8,64,512]{2,1,0:T(8,128)(2,1)} %broadcast_in_dim.6), calls=%async_computation | async-start | bytes 1048576 | tf_op jit(solution)/shard_map/all_to_all | solution.py:385
  11.6 1.5 %used_pages.1 = (bf16[2,128,256]{2,1,0:T(8,128)(2,1)S(1)}, bf16[2,128,256]{2,1,0:T(8,128)(2,1)S(1)}, bf16[2,128,256]{2,1,0:T(8,128)(2,1)S(1)}, bf16[2,128,256]{2,1,0:T(8,128)(2,1)S(1)}) custom-call(s32[4,32]{1,0:T(4,128)S(1)} %copy-done.9, s32[3]{0:T(128)S(1)} %pad_add_fusion.2.place, f32[16,16]{1,0:T(8,128)S(1)} %convert_element_type.11.scales, ...), custom_call_target="tpu_custom_call" | custom-call | tf_op jit(solution)/shard_map/used_pages/pallas_call | solution.py:58
  13.2 2.1 %collective-permute-start.6 = (bf16[2,128,256]{2,1,0:T(8,128)(2,1)S(1)}, bf16[2,128,256]{2,1,0:T(8,128)(2,1)S(1)}, u32[]{:S(2)}, u32[]{:S(2)}) collective-permute-start(bf16[2,128,256]{2,1,0:T(8,128)(2,1)S(1)} %get-tuple-element.25), channel_id=1, source_target_pairs={{0,2},{1,3},{2,0},{3,1},{4,6},{5,7},{6,4},{7,5},{8,10},{9,11},{10,... | collective-permute-start | bytes 393224 | tf_op jit(solution)/shard_map/ppermute | solution.py:395
  15.2 1.4 %collective-permute-start.7 = (bf16[2,128,256]{2,1,0:T(8,128)(2,1)S(1)}, bf16[2,128,256]{2,1,0:T(8,128)(2,1)S(1)}, u32[]{:S(2)}, u32[]{:S(2)}) collective-permute-start(bf16[2,128,256]{2,1,0:T(8,128)(2,1)S(1)} %get-tuple-element.26), channel_id=1, source_target_pairs={{0,3},{1,0},{2,1},{3,2},{4,7},{5,4},{6,5},{7,6},{8,11},{9,8},{10,9... | collective-permute-start | bytes 393224 | tf_op jit(solution)/shard_map/ppermute | solution.py:395
  16.6 6.8 %all-to-all-done.mine_ref = bf16[8,64,512]{2,1,0:T(8,128)(2,1)S(1)} async-done(((bf16[8,64,512]{2,1,0:T(8,128)(2,1)}), bf16[8,64,512]{2,1,0:T(8,128)(2,1)S(1)}, u32[]{:S(2)}, u32[]{:S(2)}) %all-to-all-start) | async-done | bytes 524320 | tf_op jit(solution)/shard_map/all_to_all | solution.py:385
  25.4 1.6 %copy-done.3 = bf16[512,2048]{1,0:T(8,128)(2,1)S(1)} copy-done((bf16[512,2048]{1,0:T(8,128)(2,1)S(1)}, bf16[512,2048]{1,0:T(8,128)(2,1)}, u32[]{:S(2)}) %copy-start.3) | copy-done | bytes 2097176
  28.5 1.5 %scale_and_pairs.1 = (f32[64,128]{1,0:T(8,128)S(1)}, f32[4,4,16,512]{3,2,1,0:T(8,128)}) custom-call(s32[1]{0:T(128)} %bitcast.6.place, bf16[8,64,512]{2,1,0:T(8,128)(2,1)S(1)} %all-to-all-done.mine_ref, bf16[8,64,512]{2,1,0:T(8,128)(2,1)S(1)} %collective-permute-done.other_ref, bf16[64,512]{1,0:T(8,128)(2,1)S(1)} %bitcast.29, f32[16,1,512]{2,1,0:T(1,128)S(1)} %bitcast.31, ...), custom_call_target="tpu_custom_call" | custom-call | tf_op jit(solution)/shard_map/scale_and_pairs/pallas_call | solution.py:121
  30.0 3.8 %all-to-all-start.1 = ((f32[16,16,512]{2,1,0:T(8,128)}), f32[16,16,512]{2,1,0:T(8,128)S(1)}, u32[]{:S(2)}, u32[]{:S(2)}) async-start(f32[16,16,512]{2,1,0:T(8,128)} %bitcast.14), calls=%async_computation.1 | async-start | bytes 1048576 | tf_op jit(solution)/shard_map/all_to_all | solution.py:413
  35.3 3.4 %copy-done.2 = bf16[8192,512]{1,0:T(8,128)(2,1)S(1)} copy-done((bf16[8192,512]{1,0:T(8,128)(2,1)S(1)}, bf16[8192,512]{1,0:T(8,128)(2,1)}, u32[]{:S(2)}) %copy-start.2) | copy-done | bytes 8388632
  39.4 2.3 %queries.1 = bf16[4,16,512]{2,1,0:T(8,128)(2,1)S(1)} custom-call(s32[2]{0:T(128)S(1)} %pad_add_fusion.1.place, bf16[8,64,512]{2,1,0:T(8,128)(2,1)S(1)} %all-to-all-done.mine_ref, bf16[8,64,512]{2,1,0:T(8,128)(2,1)S(1)} %collective-permute-done.other_ref, f32[64,128]{1,0:T(8,128)S(1)} %get-tuple-element.21.scale_ref, f32[16,1,512]{2,1,0:T(1,128)S(1)} %bitcast.32, ...), custom_call_target="tpu_custom_call" | custom-call | tf_op jit(solution)/shard_map/queries/pallas_call | solution.py:158
  42.4 3.3 %collective-permute-start.2 = (bf16[16,512]{1,0:T(8,128)(2,1)S(1)}, bf16[16,512]{1,0:T(8,128)(2,1)S(1)}, u32[]{:S(2)}, u32[]{:S(2)}) collective-permute-start(bf16[16,512]{1,0:T(8,128)(2,1)S(1)} %get-tuple-element.39), channel_id=1, source_target_pairs={{0,4},{1,8},{2,12},{3,0},{4,5},{5,9},{6,13},{7,1},{8,6},{9,10},{10... | collective-permute-start | bytes 49160 | tf_op jit(solution)/shard_map/ppermute | solution.py:436
  45.8 3.5 %collective-permute-start.3 = (bf16[16,512]{1,0:T(8,128)(2,1)S(1)}, bf16[16,512]{1,0:T(8,128)(2,1)S(1)}, u32[]{:S(2)}, u32[]{:S(2)}) collective-permute-start(bf16[16,512]{1,0:T(8,128)(2,1)S(1)} %get-tuple-element.38), channel_id=1, source_target_pairs={{0,8},{1,12},{2,0},{3,4},{4,9},{5,13},{6,1},{7,5},{8,10},{9,14},{1... | collective-permute-start | bytes 49160 | tf_op jit(solution)/shard_map/ppermute | solution.py:436
  49.2 2.3 %collective-permute-start.4 = (bf16[16,512]{1,0:T(8,128)(2,1)S(1)}, bf16[16,512]{1,0:T(8,128)(2,1)S(1)}, u32[]{:S(2)}, u32[]{:S(2)}) collective-permute-start(bf16[16,512]{1,0:T(8,128)(2,1)S(1)} %get-tuple-element.37), channel_id=1, source_target_pairs={{0,12},{1,0},{2,4},{3,8},{4,13},{5,1},{6,5},{7,9},{8,14},{9,2},{10... | collective-permute-start | bytes 49160 | tf_op jit(solution)/shard_map/ppermute | solution.py:436
  53.0 1.7 %attend.1 = (bf16[16,512]{1,0:T(8,128)(2,1)S(1)}, bf16[16,512]{1,0:T(8,128)(2,1)S(1)}, bf16[16,512]{1,0:T(8,128)(2,1)S(1)}, bf16[16,512]{1,0:T(8,128)(2,1)S(1)}) custom-call(s32[3]{0:T(128)S(1)} %pad_add_fusion.place, bf16[16,512]{1,0:T(8,128)(2,1)S(1)} %collective-permute-done.1.refs_0_, bf16[16,512]{1,0:T(8,128)(2,1)S(1)} %collective-permute-done.2.refs_1_, ...), custom_call_target="tpu_custom_call" | custom-call | tf_op jit(solution)/shard_map/attend/pallas_call | solution.py:241
  54.7 2.3 %collective-permute-start.10 = (bf16[16,512]{1,0:T(8,128)(2,1)S(1)}, bf16[16,512]{1,0:T(8,128)(2,1)S(1)}, u32[]{:S(2)}, u32[]{:S(2)}) collective-permute-start(bf16[16,512]{1,0:T(8,128)(2,1)S(1)} %get-tuple-element.29), channel_id=1, source_target_pairs={{8,0},{12,1},{0,2},{4,3},{9,4},{13,5},{1,6},{5,7},{10,8},{14,9},{2... | collective-permute-start | bytes 49160 | tf_op jit(solution)/shard_map/ppermute | solution.py:453
  57.7 6.3 %collective-permute-start.9 = (bf16[16,512]{1,0:T(8,128)(2,1)S(1)}, bf16[16,512]{1,0:T(8,128)(2,1)S(1)}, u32[]{:S(2)}, u32[]{:S(2)}) collective-permute-start(bf16[16,512]{1,0:T(8,128)(2,1)S(1)} %get-tuple-element.28), channel_id=1, source_target_pairs={{4,0},{8,1},{12,2},{0,3},{5,4},{9,5},{13,6},{1,7},{6,8},{10,9},{14... | collective-permute-start | bytes 49160 | tf_op jit(solution)/shard_map/ppermute | solution.py:453
  65.5 3.4 %copy-done = bf16[512,8192]{1,0:T(8,128)(2,1)S(1)} copy-done((bf16[512,8192]{1,0:T(8,128)(2,1)S(1)}, bf16[512,8192]{1,0:T(8,128)(2,1)}, u32[]{:S(2)}) %copy-start) | copy-done | bytes 8388632
  70.4 3.4 %copy-done.1 = bf16[512,8192]{1,0:T(8,128)(2,1)S(1)} copy-done((bf16[512,8192]{1,0:T(8,128)(2,1)S(1)}, bf16[512,8192]{1,0:T(8,128)(2,1)}, u32[]{:S(2)}) %copy-start.1) | copy-done | bytes 8388632
  75.3 5.7 %collective-permute-start.13 = (f32[4,64,512]{2,1,0:T(8,128)S(1)}, f32[4,64,512]{2,1,0:T(8,128)S(1)}, u32[]{:S(2)}, u32[]{:S(2)}) collective-permute-start(f32[4,64,512]{2,1,0:T(8,128)S(1)} %get-tuple-element.32), channel_id=1, source_target_pairs={{0,2},{2,0},{1,3},{3,1},{4,6},{6,4},{5,7},{7,5},{8,10},{10,8},{9,1... | collective-permute-start | bytes 1572872 | tf_op jit(solution)/shard_map/ppermute | solution.py:353
  81.0 12.6 %collective-permute-done.13.refs_1_ = f32[4,64,512]{2,1,0:T(8,128)S(1)} collective-permute-done((f32[4,64,512]{2,1,0:T(8,128)S(1)}, f32[4,64,512]{2,1,0:T(8,128)S(1)}, u32[]{:S(2)}, u32[]{:S(2)}) %collective-permute-start.13) | collective-permute-done | bytes 524320 | tf_op jit(solution)/shard_map/ppermute | solution.py:353
  94.3 3.3 %collective-permute-start.16 = (f32[64,512]{1,0:T(8,128)S(1)}, f32[64,512]{1,0:T(8,128)S(1)}, u32[]{:S(2)}, u32[]{:S(2)}) collective-permute-start(f32[64,512]{1,0:T(8,128)S(1)} %get-tuple-element.36), channel_id=1, source_target_pairs={{0,12},{4,0},{8,4},{12,8},{1,13},{5,1},{9,5},{13,9},{2,14},{6,2},{... | collective-permute-start | bytes 393224 | tf_op jit(solution)/shard_map/ppermute | solution.py:353
  97.5 4.4 %collective-permute-done.14.refs_1_ = f32[64,512]{1,0:T(8,128)S(1)} collective-permute-done((f32[64,512]{1,0:T(8,128)S(1)}, f32[64,512]{1,0:T(8,128)S(1)}, u32[]{:S(2)}, u32[]{:S(2)}) %collective-permute-start.14) | collective-permute-done | bytes 131104 | tf_op jit(solution)/shard_map/ppermute | solution.py:353
  101.9 4.6 %collective-permute-done.15.refs_2_ = f32[64,512]{1,0:T(8,128)S(1)} collective-permute-done((f32[64,512]{1,0:T(8,128)S(1)}, f32[64,512]{1,0:T(8,128)S(1)}, u32[]{:S(2)}, u32[]{:S(2)}) %collective-permute-start.15) | collective-permute-done | bytes 131104 | tf_op jit(solution)/shard_map/ppermute | solution.py:353
  (61 shorter events, 17.1 us)
Async XLA Ops:
  1.7 21.8 %all-to-all-start = ((bf16[8,64,512]{2,1,0:T(8,128)(2,1)}), bf16[8,64,512]{2,1,0:T(8,128)(2,1)S(1)}, u32[]{:S(2)}, u32[]{:S(2)}) async-start(bf16[8,64,512]{2,1,0:T(8,128)(2,1)} %broadcast_in_dim.6), calls=%async_computation | async-start | bytes 1048576 | tf_op jit(solution)/shard_map/all_to_all | solution.py:385
  13.1 32.7 %collective-permute-start.5 = (bf16[2,128,256]{2,1,0:T(8,128)(2,1)S(1)}, bf16[2,128,256]{2,1,0:T(8,128)(2,1)S(1)}, u32[]{:S(2)}, u32[]{:S(2)}) collective-permute-start(bf16[2,128,256]{2,1,0:T(8,128)(2,1)S(1)} %get-tuple-element.24), channel_id=1, source_target_pairs={{0,1},{1,2},{2,3},{3,0},{4,5},{5,6},{6,7},{7,4},{8,9},{9,10},{10,1... | collective-permute-start | bytes 393224 | tf_op jit(solution)/shard_map/ppermute | solution.py:395
  13.2 36.1 %collective-permute-start.6 = (bf16[2,128,256]{2,1,0:T(8,128)(2,1)S(1)}, bf16[2,128,256]{2,1,0:T(8,128)(2,1)S(1)}, u32[]{:S(2)}, u32[]{:S(2)}) collective-permute-start(bf16[2,128,256]{2,1,0:T(8,128)(2,1)S(1)} %get-tuple-element.25), channel_id=1, source_target_pairs={{0,2},{1,3},{2,0},{3,1},{4,6},{5,7},{6,4},{7,5},{8,10},{9,11},{10,... | collective-permute-start | bytes 393224 | tf_op jit(solution)/shard_map/ppermute | solution.py:395
  15.2 37.0 %collective-permute-start.7 = (bf16[2,128,256]{2,1,0:T(8,128)(2,1)S(1)}, bf16[2,128,256]{2,1,0:T(8,128)(2,1)S(1)}, u32[]{:S(2)}, u32[]{:S(2)}) collective-permute-start(bf16[2,128,256]{2,1,0:T(8,128)(2,1)S(1)} %get-tuple-element.26), channel_id=1, source_target_pairs={{0,3},{1,0},{2,1},{3,2},{4,7},{5,4},{6,5},{7,6},{8,11},{9,8},{10,9... | collective-permute-start | bytes 393224 | tf_op jit(solution)/shard_map/ppermute | solution.py:395
  23.4 1.9 %collective-permute-start = (bf16[8,64,512]{2,1,0:T(8,128)(2,1)S(1)}, bf16[8,64,512]{2,1,0:T(8,128)(2,1)S(1)}, u32[]{:S(2)}, u32[]{:S(2)}) collective-permute-start(bf16[8,64,512]{2,1,0:T(8,128)(2,1)S(1)} %all-to-all-done.mine_ref), channel_id=1, source_target_pairs={{0,1},{1,0},{2,3},{3,2},{4,5},{5,4},{6,7},{7,6},{8,9},{9,8},{10,11... | collective-permute-start | bytes 1572872 | tf_op jit(solution)/shard_map/ppermute | solution.py:353
  25.4 1.6 %copy-start.3 = (bf16[512,2048]{1,0:T(8,128)(2,1)S(1)}, bf16[512,2048]{1,0:T(8,128)(2,1)}, u32[]{:S(2)}) copy-start(bf16[512,2048]{1,0:T(8,128)(2,1)} %weight_ref.2) | copy-start | bytes 6291460
  30.0 23.0 %all-to-all-start.1 = ((f32[16,16,512]{2,1,0:T(8,128)}), f32[16,16,512]{2,1,0:T(8,128)S(1)}, u32[]{:S(2)}, u32[]{:S(2)}) async-start(f32[16,16,512]{2,1,0:T(8,128)} %bitcast.14), calls=%async_computation.1 | async-start | bytes 1048576 | tf_op jit(solution)/shard_map/all_to_all | solution.py:413
  35.3 3.4 %copy-start.2 = (bf16[8192,512]{1,0:T(8,128)(2,1)S(1)}, bf16[8192,512]{1,0:T(8,128)(2,1)}, u32[]{:S(2)}) copy-start(bf16[8192,512]{1,0:T(8,128)(2,1)} %weight_ref.3) | copy-start | bytes 25165828
  41.7 10.5 %collective-permute-start.1 = (bf16[16,512]{1,0:T(8,128)(2,1)S(1)}, bf16[16,512]{1,0:T(8,128)(2,1)S(1)}, u32[]{:S(2)}, u32[]{:S(2)}) collective-permute-start(bf16[16,512]{1,0:T(8,128)(2,1)S(1)} %get-tuple-element.40), channel_id=1, source_target_pairs={{0,0},{1,4},{2,8},{3,12},{4,1},{5,5},{6,9},{7,13},{8,2},{9,6},{10,... | collective-permute-start | bytes 49160 | tf_op jit(solution)/shard_map/ppermute | solution.py:436
  42.4 9.8 %collective-permute-start.2 = (bf16[16,512]{1,0:T(8,128)(2,1)S(1)}, bf16[16,512]{1,0:T(8,128)(2,1)S(1)}, u32[]{:S(2)}, u32[]{:S(2)}) collective-permute-start(bf16[16,512]{1,0:T(8,128)(2,1)S(1)} %get-tuple-element.39), channel_id=1, source_target_pairs={{0,4},{1,8},{2,12},{3,0},{4,5},{5,9},{6,13},{7,1},{8,6},{9,10},{10... | collective-permute-start | bytes 49160 | tf_op jit(solution)/shard_map/ppermute | solution.py:436
  45.8 6.5 %collective-permute-start.3 = (bf16[16,512]{1,0:T(8,128)(2,1)S(1)}, bf16[16,512]{1,0:T(8,128)(2,1)S(1)}, u32[]{:S(2)}, u32[]{:S(2)}) collective-permute-start(bf16[16,512]{1,0:T(8,128)(2,1)S(1)} %get-tuple-element.38), channel_id=1, source_target_pairs={{0,8},{1,12},{2,0},{3,4},{4,9},{5,13},{6,1},{7,5},{8,10},{9,14},{1... | collective-permute-start | bytes 49160 | tf_op jit(solution)/shard_map/ppermute | solution.py:436
  49.2 3.8 %collective-permute-start.4 = (bf16[16,512]{1,0:T(8,128)(2,1)S(1)}, bf16[16,512]{1,0:T(8,128)(2,1)S(1)}, u32[]{:S(2)}, u32[]{:S(2)}) collective-permute-start(bf16[16,512]{1,0:T(8,128)(2,1)S(1)} %get-tuple-element.37), channel_id=1, source_target_pairs={{0,12},{1,0},{2,4},{3,8},{4,13},{5,1},{6,5},{7,9},{8,14},{9,2},{10... | collective-permute-start | bytes 49160 | tf_op jit(solution)/shard_map/ppermute | solution.py:436
  54.7 9.4 %collective-permute-start.10 = (bf16[16,512]{1,0:T(8,128)(2,1)S(1)}, bf16[16,512]{1,0:T(8,128)(2,1)S(1)}, u32[]{:S(2)}, u32[]{:S(2)}) collective-permute-start(bf16[16,512]{1,0:T(8,128)(2,1)S(1)} %get-tuple-element.29), channel_id=1, source_target_pairs={{8,0},{12,1},{0,2},{4,3},{9,4},{13,5},{1,6},{5,7},{10,8},{14,9},{2... | collective-permute-start | bytes 49160 | tf_op jit(solution)/shard_map/ppermute | solution.py:453
  57.1 7.1 %collective-permute-start.11 = (bf16[16,512]{1,0:T(8,128)(2,1)S(1)}, bf16[16,512]{1,0:T(8,128)(2,1)S(1)}, u32[]{:S(2)}, u32[]{:S(2)}) collective-permute-start(bf16[16,512]{1,0:T(8,128)(2,1)S(1)} %get-tuple-element.30), channel_id=1, source_target_pairs={{12,0},{0,1},{4,2},{8,3},{13,4},{1,5},{5,6},{9,7},{14,8},{2,9},{6,... | collective-permute-start | bytes 49160 | tf_op jit(solution)/shard_map/ppermute | solution.py:453
  57.1 7.1 %collective-permute-start.8 = (bf16[16,512]{1,0:T(8,128)(2,1)S(1)}, bf16[16,512]{1,0:T(8,128)(2,1)S(1)}, u32[]{:S(2)}, u32[]{:S(2)}) collective-permute-start(bf16[16,512]{1,0:T(8,128)(2,1)S(1)} %get-tuple-element.27), channel_id=1, source_target_pairs={{0,0},{4,1},{8,2},{12,3},{1,4},{5,5},{9,6},{13,7},{2,8},{6,9},{10,... | collective-permute-start | bytes 49160 | tf_op jit(solution)/shard_map/ppermute | solution.py:453
  57.7 7.8 %collective-permute-start.9 = (bf16[16,512]{1,0:T(8,128)(2,1)S(1)}, bf16[16,512]{1,0:T(8,128)(2,1)S(1)}, u32[]{:S(2)}, u32[]{:S(2)}) collective-permute-start(bf16[16,512]{1,0:T(8,128)(2,1)S(1)} %get-tuple-element.28), channel_id=1, source_target_pairs={{4,0},{8,1},{12,2},{0,3},{5,4},{9,5},{13,6},{1,7},{6,8},{10,9},{14... | collective-permute-start | bytes 49160 | tf_op jit(solution)/shard_map/ppermute | solution.py:453
  65.5 3.4 %copy-start = (bf16[512,8192]{1,0:T(8,128)(2,1)S(1)}, bf16[512,8192]{1,0:T(8,128)(2,1)}, u32[]{:S(2)}) copy-start(bf16[512,8192]{1,0:T(8,128)(2,1)} %refs_4_.3) | copy-start | bytes 25165828
  68.9 37.7 %copy-start.6 = (bf16[2,32,512]{2,1,0:T(8,128)(2,1)S(1)}, bf16[2,32,512]{2,1,0:T(8,128)(2,1)}, u32[]{:S(2)}) copy-start(bf16[2,32,512]{2,1,0:T(8,128)(2,1)} %param.9) | copy-start | bytes 196612
  70.2 4.9 %collective-permute-start.12 = (f32[8,64,512]{2,1,0:T(8,128)S(1)}, f32[8,64,512]{2,1,0:T(8,128)S(1)}, u32[]{:S(2)}, u32[]{:S(2)}) collective-permute-start(f32[8,64,512]{2,1,0:T(8,128)S(1)} %outputs.3), channel_id=1, source_target_pairs={{0,1},{1,0},{2,3},{3,2},{4,5},{5,4},{6,7},{7,6},{8,9},{9,8},{10,11... | collective-permute-start | bytes 3145736 | tf_op jit(solution)/shard_map/ppermute | solution.py:353
  70.4 3.4 %copy-start.1 = (bf16[512,8192]{1,0:T(8,128)(2,1)S(1)}, bf16[512,8192]{1,0:T(8,128)(2,1)}, u32[]{:S(2)}) copy-start(bf16[512,8192]{1,0:T(8,128)(2,1)} %refs_4_.3) | copy-start | bytes 25165828
  75.3 18.3 %collective-permute-start.13 = (f32[4,64,512]{2,1,0:T(8,128)S(1)}, f32[4,64,512]{2,1,0:T(8,128)S(1)}, u32[]{:S(2)}, u32[]{:S(2)}) collective-permute-start(f32[4,64,512]{2,1,0:T(8,128)S(1)} %get-tuple-element.32), channel_id=1, source_target_pairs={{0,2},{2,0},{1,3},{3,1},{4,6},{6,4},{5,7},{7,5},{8,10},{10,8},{9,1... | collective-permute-start | bytes 1572872 | tf_op jit(solution)/shard_map/ppermute | solution.py:353
  93.6 8.3 %collective-permute-start.14 = (f32[64,512]{1,0:T(8,128)S(1)}, f32[64,512]{1,0:T(8,128)S(1)}, u32[]{:S(2)}, u32[]{:S(2)}) collective-permute-start(f32[64,512]{1,0:T(8,128)S(1)} %get-tuple-element.34), channel_id=1, source_target_pairs={{0,4},{4,8},{8,12},{12,0},{1,5},{5,9},{9,13},{13,1},{2,6},{6,10},{... | collective-permute-start | bytes 393224 | tf_op jit(solution)/shard_map/ppermute | solution.py:353
  93.7 12.8 %collective-permute-start.15 = (f32[64,512]{1,0:T(8,128)S(1)}, f32[64,512]{1,0:T(8,128)S(1)}, u32[]{:S(2)}, u32[]{:S(2)}) collective-permute-start(f32[64,512]{1,0:T(8,128)S(1)} %get-tuple-element.35), channel_id=1, source_target_pairs={{0,8},{4,12},{8,0},{12,4},{1,9},{5,13},{9,1},{13,5},{2,10},{6,14},... | collective-permute-start | bytes 393224 | tf_op jit(solution)/shard_map/ppermute | solution.py:353
  94.3 12.3 %collective-permute-start.16 = (f32[64,512]{1,0:T(8,128)S(1)}, f32[64,512]{1,0:T(8,128)S(1)}, u32[]{:S(2)}, u32[]{:S(2)}) collective-permute-start(f32[64,512]{1,0:T(8,128)S(1)} %get-tuple-element.36), channel_id=1, source_target_pairs={{0,12},{4,0},{8,4},{12,8},{1,13},{5,1},{9,5},{13,9},{2,14},{6,2},{... | collective-permute-start | bytes 393224 | tf_op jit(solution)/shard_map/ppermute | solution.py:353
  (5 other events, 4.3 us)

commit v3 on v2

--- a/solution.py
+++ b/solution.py
@@ -15,6 +15,8 @@
 STEPS = 2
 ROWS = STEPS * SAMPLES
 PAIR = 2 * HEAD_SIZE
+LANES = 128
+TAIL = 16
 DEVICES = ("req", "sub", "section")
 PLANE = ("sub", "section")
 CHIPS = ("req", "sub")
@@ -34,6 +36,31 @@
 
 def turn(vectors, cosine, sine):
     return vectors * cosine + pltpu.roll(vectors, HEAD_SIZE // 2, vectors.ndim - 1) * sine
+
+
+def stage_kernel(*refs):
+    half = (len(refs) - 1) // 2
+    copies = [
+        pltpu.make_async_copy(refs[i], refs[half + i], refs[-1].at[i]) for i in range(half)
+    ]
+    for copy in copies:
+        copy.start()
+    for copy in copies:
+        copy.wait()
+
+
+def staged(*arrays):
+    size = sum(array.size * array.dtype.itemsize for array in arrays)
+    return pl.pallas_call(
+        stage_kernel,
+        in_specs=[pl.BlockSpec(memory_space=pltpu.HBM)] * len(arrays),
+        out_specs=[pl.BlockSpec(memory_space=pltpu.VMEM)] * len(arrays),
+        out_shape=[jax.ShapeDtypeStruct(array.shape, array.dtype) for array in arrays],
+        scratch_shapes=[pltpu.SemaphoreType.DMA((len(arrays),))],
+        compiler_params=pltpu.CompilerParams(vmem_limit_bytes=30 * 2**20),
+        cost_estimate=pl.CostEstimate(flops=0, bytes_accessed=2 * size, transcendentals=0),
+        name="staged",
+    )(*arrays)
 
 
 def pages_kernel(table, place, scales, page_ref, *out_refs):
@@ -285,67 +312,123 @@
     )(place, *mixed, weight)
 
 
-def fold_core_kernel(place, mine_ref, got_ref, *out_refs):
-    subs = len(out_refs)
-    for shift, out_ref in enumerate(out_refs):
+def pieces_of(block):
+    return [block[:, c : c + LANES] for c in range(0, block.shape[1], LANES)]
+
+
+def encode(out_ref, pieces):
+    rows = pieces[0].shape[0]
+    peak = jnp.abs(pieces[0])
+    for piece in pieces[1:]:
+        peak = jnp.maximum(peak, jnp.abs(piece))
+    peak = jnp.maximum(jnp.max(peak, axis=0, keepdims=True), 1e-30)
+    exponent = jnp.floor(jnp.log2(peak)) - 14.0
+    inverse = jnp.exp2(-exponent)
+    for i, piece in enumerate(pieces):
+        code = jnp.clip(jnp.floor(piece * inverse + 0.5), -32767.0, 32767.0)
+        out_ref[i * rows : (i + 1) * rows] = code.astype(jnp.int32).astype(jnp.int16)
+    out_ref[len(pieces) * rows :] = (
+        jnp.broadcast_to(exponent, (TAIL, LANES)).astype(jnp.int32).astype(jnp.int16)
+    )
+
+
+def step_of(ref):
+    tail = ref[ref.shape[0] - TAIL :].astype(jnp.int32).astype(jnp.float32)
+    return jnp.exp2(tail[:1])
+
+
+def decoded(ref, first, rows, step):
+    return ref[pl.ds(first, rows)].astype(jnp.int32).astype(jnp.float32) * step
+
+
+def fold_core_kernel(place, mine_ref, got_ref, kept_ref, *out_refs):
+    subs = 1 + len(out_refs)
+    for shift in range(subs):
         sub = lax.rem(place[0] + shift, subs)
+        pieces = []
         for i in range(GROUP_REQUESTS):
-            block = i * subs + sub
-            out_ref[i] = mine_ref[block] + got_ref[block]
+            block = mine_ref[i * subs + sub] + got_ref[i * subs + sub]
+            if shift == 0:
+                kept_ref[i] = block
+            pieces += pieces_of(block)
+        if shift:
+            encode(out_refs[shift - 1], pieces)
 
 
 def fold_core(place, mine, got, subs):
-    shape = jax.ShapeDtypeStruct((GROUP_REQUESTS,) + mine.shape[1:], jnp.float32)
+    _, rows, width = mine.shape
+    kept = jax.ShapeDtypeStruct((GROUP_REQUESTS, rows, width), jnp.float32)
+    sent = jax.ShapeDtypeStruct(
+        (GROUP_REQUESTS * width // LANES * rows + TAIL, LANES), jnp.int16
+    )
     return pl.pallas_call(
         fold_core_kernel,
         in_specs=[pl.BlockSpec(memory_space=pltpu.SMEM)]
         + [pl.BlockSpec(memory_space=pltpu.VMEM)] * 2,
         out_specs=[pl.BlockSpec(memory_space=pltpu.VMEM)] * subs,
-        out_shape=[shape] * subs,
+        out_shape=[kept] + [sent] * (subs - 1),
         compiler_params=params(),
         name="fold_core",
     )(place, mine, got)
 
 
-def fold_sub_kernel(place, *refs):
-    in_refs, out_refs = refs[:-GROUP_REQUESTS], refs[-GROUP_REQUESTS:]
-    for shift, out_ref in enumerate(out_refs):
+def fold_sub_kernel(place, kept_ref, *refs):
+    in_refs, total_ref, out_refs = (
+        refs[:-GROUP_REQUESTS],
+        refs[-GROUP_REQUESTS],
+        refs[1 - GROUP_REQUESTS :],
+    )
+    _, rows, width = kept_ref.shape
+    steps = [step_of(ref) for ref in in_refs]
+    for shift in range(GROUP_REQUESTS):
         block = lax.rem(place[0] + shift, GROUP_REQUESTS)
-        total = in_refs[0][block]
-        for ref in in_refs[1:]:
-            total = total + ref[block]
-        out_ref[...] = total
-
-
-def fold_sub(place, parts):
-    shape = jax.ShapeDtypeStruct(parts[0].shape[1:], jnp.float32)
+        pieces = pieces_of(kept_ref[block])
+        for c in range(len(pieces)):
+            first = pl.multiple_of((block * len(pieces) + c) * rows, rows)
+            for ref, step in zip(in_refs, steps):
+                pieces[c] = pieces[c] + decoded(ref, first, rows, step)
+        if shift:
+            encode(out_refs[shift - 1], pieces)
+        else:
+            for c, piece in enumerate(pieces):
+                total_ref[:, c * LANES : (c + 1) * LANES] = piece
+
+
+def fold_sub(place, kept, parts):
+    _, rows, width = kept.shape
+    total = jax.ShapeDtypeStruct((rows, width), jnp.float32)
+    sent = jax.ShapeDtypeStruct((width // LANES * rows + TAIL, LANES), jnp.int16)
     return pl.pallas_call(
         fold_sub_kernel,
         in_specs=[pl.BlockSpec(memory_space=pltpu.SMEM)]
-        + [pl.BlockSpec(memory_space=pltpu.VMEM)] * len(parts),
+        + [pl.BlockSpec(memory_space=pltpu.VMEM)] * (1 + len(parts)),
         out_specs=[pl.BlockSpec(memory_space=pltpu.VMEM)] * GROUP_REQUESTS,
-        out_shape=[shape] * GROUP_REQUESTS,
+        out_shape=[total] + [sent] * (GROUP_REQUESTS - 1),
         compiler_params=params(),
         name="fold_sub",
-    )(place, *parts)
-
-
-def finish_kernel(rows_ref, *refs):
-    total = refs[0][...]
-    for ref in refs[1:-1]:
-        total = total + ref[...]
-    refs[-1][...] = (total + rows_ref[...].astype(jnp.float32)).astype(jnp.bfloat16)
-
-
-def finish(rows, parts):
+    )(place, kept, *parts)
+
+
+def finish_kernel(rows_ref, total_ref, *refs):
+    rows = rows_ref.shape[0]
+    steps = [step_of(ref) for ref in refs[:-1]]
+    for c in range(rows_ref.shape[1] // LANES):
+        part = slice(c * LANES, (c + 1) * LANES)
+        total = total_ref[:, part]
+        for ref, step in zip(refs[:-1], steps):
+            total = total + decoded(ref, c * rows, rows, step)
+        refs[-1][:, part] = (total + rows_ref[:, part].astype(jnp.float32)).astype(jnp.bfloat16)
+
+
+def finish(rows, total, parts):
     return pl.pallas_call(
         finish_kernel,
-        in_specs=[pl.BlockSpec(memory_space=pltpu.VMEM)] * (1 + len(parts)),
+        in_specs=[pl.BlockSpec(memory_space=pltpu.VMEM)] * (2 + len(parts)),
         out_specs=pl.BlockSpec(memory_space=pltpu.VMEM),
         out_shape=jax.ShapeDtypeStruct(rows.shape, jnp.bfloat16),
         compiler_params=params(),
         name="finish",
-    )(rows, *parts)
+    )(rows, total, *parts)
 
 
 def passed(array, axis, shift):
@@ -406,7 +489,9 @@
     my_cosine = lax.dynamic_index_in_dim(cosine, request, 1, keepdims=False)
     my_sine = lax.dynamic_index_in_dim(sine, request, 1, keepdims=False)
 
-    gain = norm_gain.reshape(devices, 1, width)
+    rows, gain, key_value_weight, w_query, w_output = staged(
+        rows, norm_gain.reshape(devices, 1, width), key_value_weight, w_query, w_output
+    )
     scale, pairs = scale_and_pairs(
         mine, other, rows, gain, key_value_weight, scalars(device), targets, heads
     )
@@ -455,11 +540,11 @@
     away = outputs(scalars(member, 1 - core), got, w_output, chips)
     arrived = passed(away, "section", 1)
     kept = outputs(scalars(member, core), got, w_output, chips)
-    parts = fold_core(scalars(sub), kept, arrived, subs)
-    parts = [parts[0]] + [passed(parts[s], "sub", s) for s in range(1, subs)]
-    parts = fold_sub(scalars(request), parts)
-    parts = [parts[0]] + [passed(parts[s], "req", s) for s in range(1, GROUP_REQUESTS)]
-    return finish(rows, parts).reshape(hidden.shape)
+    kept, *parts = fold_core(scalars(sub), kept, arrived, subs)
+    parts = [passed(part, "sub", s + 1) for s, part in enumerate(parts)]
+    total, *parts = fold_sub(scalars(request), kept, parts)
+    parts = [passed(part, "req", s + 1) for s, part in enumerate(parts)]
+    return finish(rows, total, parts).reshape(hidden.shape)
 
 
 def solution(mesh):

time: 108 us -> 104 us (0.963)
  waiting for transfers between devices: 31.7 us -> 16.3 us
  Pallas kernels: 10.5 us -> 18.7 us
  local copies, waits for them, and re-layouts: 18.9 us -> 21.5 us
    ppermute x6, waiting for transfers between devices: 22.7 us -> 14.2 us  [passed(): lax.ppermute(array, axis, [(i, (i + shift) % size) for i in range(size)])]
    all_to_all x1, waiting for transfers between devices: 6.81 us -> 0.01 us  [shards(): lax.all_to_all(jnp.broadcast_to(rows[None], (chips,) + rows.shape), CHIPS...]
    pallas_call x0 -> x1, Pallas kernels: none -> 6.05 us  [staged(): pl.pallas_call(stage_kernel, in_specs=[pl.BlockSpec(memory_space=pltpu.HB...]
    unnamed x20 -> x22, local copies, waits for them, and re-layouts: 16 us -> 19.2 us
    pallas_call x1, Pallas kernels: 1.46 us -> 3.62 us  [used_pages(): pl.pallas_call(pages_kernel, grid_spec=pltpu.PrefetchScalarGridSpec(num_s...]
  transfers between devices with their start and end apart: 19 -> 19, of which waited for: 7 -> 7; matrix products, arithmetic and copies ran while one was open for 4% -> 3% of each run, Pallas kernels for 6% -> 14%
where the time goes in v3:
time: 104 us; the launch traced here: 103 us
  starting transfers between devices  44.1 us (42%)
  local copies, waits for them, and re-layouts  21.5 us (21%)
  Pallas kernels  18.7 us (18%)
  waiting for transfers between devices  16.3 us (16%)
  other arithmetic  1.99 us (2%)
    unnamed x22, local copies, waits for them, and re-layouts  19.2 us
    ppermute x6, waiting for transfers between devices, passed(): lax.ppermute(array, axis, [(i, (i + shift) % size) for i in range(size)])  14.2 us
    ppermute x4, starting transfers between devices, shards(): got.append(lax.ppermute(block, DEVICES, there))  9.8 us
    ppermute x6, starting transfers between devices, passed(): lax.ppermute(array, axis, [(i, (i + shift) % size) for i in range(size)])  9.62 us
    ppermute x4, starting transfers between devices, shards(): got.append(lax.ppermute(mixed[s], DEVICES, back))  9.29 us
    all_to_all x1, starting transfers between devices, shards(): lax.all_to_all(jnp.broadcast_to(rows[None], (chips,) + rows.shape), CHIPS...  7.28 us
    pallas_call x1, Pallas kernels, staged(): pl.pallas_call(stage_kernel, in_specs=[pl.BlockSpec(memory_space=pltpu.HB...  6.05 us
    all_to_all x1, starting transfers between devices, shards(): lax.all_to_all(pairs.reshape(devices, ROWS, heads * PAIR), DEVICES, 0, 0,...  4.65 us
  transfers between devices with their start and end apart: 19, of which 7 were waited for; matrix products, arithmetic and copies ran while one was open for 3% of the time, Pallas kernels for 14%

profile of v3, /device:TPU:0, one launch (start us, length us, event | category | flops | bytes accessed | tf_op | source)
XLA Modules:
  0.0 102.8 jit_solution(8004266303827355287)
XLA Ops:
  0.0 1.7 %broadcast_in_dim.6 = bf16[8,64,512]{2,1,0:T(8,128)(2,1)} broadcast(bf16[64,512]{1,0:T(8,128)(2,1)} %bitcast.29), dimensions={1,2} | broadcast | bytes 589824 | tf_op jit(solution)/shard_map/broadcast_in_dim | solution.py:469
  1.7 7.3 %all-to-all-start = ((bf16[8,64,512]{2,1,0:T(8,128)(2,1)}), bf16[8,64,512]{2,1,0:T(8,128)(2,1)S(1)}, u32[]{:S(2)}, u32[]{:S(2)}) async-start(bf16[8,64,512]{2,1,0:T(8,128)(2,1)} %broadcast_in_dim.6), calls=%async_computation | async-start | bytes 1048576 | tf_op jit(solution)/shard_map/all_to_all | solution.py:468
  11.6 3.6 %used_pages.1 = (bf16[2,128,256]{2,1,0:T(8,128)(2,1)S(1)}, bf16[2,128,256]{2,1,0:T(8,128)(2,1)}, bf16[2,128,256]{2,1,0:T(8,128)(2,1)}, bf16[2,128,256]{2,1,0:T(8,128)(2,1)}) custom-call(s32[4,32]{1,0:T(4,128)S(1)} %copy-done.9, s32[3]{0:T(128)S(1)} %pad_add_fusion.2.place, f32[16,16]{1,0:T(8,128)S(1)} %convert_element_type.11.scales, ...), custom_call_target="tpu_custom_call" | custom-call | tf_op jit(solution)/shard_map/used_pages/pallas_call | solution.py:85
  15.2 2.1 %collective-permute-start.6 = (bf16[2,128,256]{2,1,0:T(8,128)(2,1)}, bf16[2,128,256]{2,1,0:T(8,128)(2,1)}, u32[]{:S(2)}, u32[]{:S(2)}) collective-permute-start(bf16[2,128,256]{2,1,0:T(8,128)(2,1)} %get-tuple-element.34), channel_id=1, source_target_pairs={{0,2},{1,3},{2,0},{3,1},{4,6},{5,7},{6,4},{7,5},{8,10},{9,11},{10,... | collective-permute-start | bytes 393224 | tf_op jit(solution)/shard_map/ppermute | solution.py:478
  18.7 1.6 %copy-done.4 = bf16[512,2048]{1,0:T(8,128)(2,1)S(1)} copy-done((bf16[512,2048]{1,0:T(8,128)(2,1)S(1)}, bf16[512,2048]{1,0:T(8,128)(2,1)}, u32[]{:S(2)}) %copy-start.4) | copy-done | bytes 2097176
  21.9 6.1 %staged.1 = (bf16[64,512]{1,0:T(8,128)(2,1)S(1)}, f32[16,1,512]{2,1,0:T(1,128)S(1)}, bf16[512,2048]{1,0:T(8,128)(2,1)S(1)}, bf16[8192,512]{1,0:T(8,128)(2,1)S(1)}, bf16[512,8192]{1,0:T(8,128)(2,1)S(1)}) custom-call(bf16[64,512]{1,0:T(8,128)(2,1)S(1)} %bitcast.30, f32[16,1,512]{2,1,0:T(1,128)S(1)} %bitcast.33, bf16[512,2048]{1,0:T(8,128)(2,1)S(1)} %copy-done.4, ...), custom_call_target="tpu_custom_call" | custom-call | bytes 37945344 | tf_op jit(solution)/shard_map/staged/pallas_call | solution.py:54
  28.0 3.3 %copy-done = bf16[512,8192]{1,0:T(8,128)(2,1)} copy-done((bf16[512,8192]{1,0:T(8,128)(2,1)}, bf16[512,8192]{1,0:T(8,128)(2,1)S(1)}, u32[]{:S(2)}) %copy-start) | copy-done | bytes 8388632
  31.3 3.3 %copy-done.2 = bf16[8192,512]{1,0:T(8,128)(2,1)} copy-done((bf16[8192,512]{1,0:T(8,128)(2,1)}, bf16[8192,512]{1,0:T(8,128)(2,1)S(1)}, u32[]{:S(2)}) %copy-start.2) | copy-done | bytes 8388632
  34.7 1.8 %collective-permute-done.other_ref = bf16[8,64,512]{2,1,0:T(8,128)(2,1)S(1)} collective-permute-done((bf16[8,64,512]{2,1,0:T(8,128)(2,1)S(1)}, bf16[8,64,512]{2,1,0:T(8,128)(2,1)S(1)}, u32[]{:S(2)}, u32[]{:S(2)}) %collective-permute-start) | collective-permute-done | bytes 524320 | tf_op jit(solution)/shard_map/ppermute | solution.py:436
  37.9 4.6 %all-to-all-start.1 = ((f32[16,16,512]{2,1,0:T(8,128)}), f32[16,16,512]{2,1,0:T(8,128)S(1)}, u32[]{:S(2)}, u32[]{:S(2)}) async-start(f32[16,16,512]{2,1,0:T(8,128)} %bitcast.28), calls=%async_computation.1 | async-start | bytes 1048576 | tf_op jit(solution)/shard_map/all_to_all | solution.py:498
  43.5 3.4 %copy-done.3 = bf16[8192,512]{1,0:T(8,128)(2,1)S(1)} copy-done((bf16[8192,512]{1,0:T(8,128)(2,1)S(1)}, bf16[8192,512]{1,0:T(8,128)(2,1)}, u32[]{:S(2)}) %copy-start.3) | copy-done | bytes 8388632
  46.9 2.2 %queries.1 = bf16[4,16,512]{2,1,0:T(8,128)(2,1)S(1)} custom-call(s32[2]{0:T(128)S(1)} %pad_add_fusion.1.place, bf16[8,64,512]{2,1,0:T(8,128)(2,1)S(1)} %all-to-all-done.mine_ref, bf16[8,64,512]{2,1,0:T(8,128)(2,1)S(1)} %collective-permute-done.other_ref, f32[64,128]{1,0:T(8,128)S(1)} %get-tuple-element.29.scale_ref, ...), custom_call_target="tpu_custom_call" | custom-call | tf_op jit(solution)/shard_map/queries/pallas_call | solution.py:185
  49.8 3.4 %collective-permute-start.2 = (bf16[16,512]{1,0:T(8,128)(2,1)S(1)}, bf16[16,512]{1,0:T(8,128)(2,1)S(1)}, u32[]{:S(2)}, u32[]{:S(2)}) collective-permute-start(bf16[16,512]{1,0:T(8,128)(2,1)S(1)} %get-tuple-element.49), channel_id=1, source_target_pairs={{0,4},{1,8},{2,12},{3,0},{4,5},{5,9},{6,13},{7,1},{8,6},{9,10},{10... | collective-permute-start | bytes 49160 | tf_op jit(solution)/shard_map/ppermute | solution.py:521
  53.2 3.5 %collective-permute-start.3 = (bf16[16,512]{1,0:T(8,128)(2,1)S(1)}, bf16[16,512]{1,0:T(8,128)(2,1)S(1)}, u32[]{:S(2)}, u32[]{:S(2)}) collective-permute-start(bf16[16,512]{1,0:T(8,128)(2,1)S(1)} %get-tuple-element.48), channel_id=1, source_target_pairs={{0,8},{1,12},{2,0},{3,4},{4,9},{5,13},{6,1},{7,5},{8,10},{9,14},{1... | collective-permute-start | bytes 49160 | tf_op jit(solution)/shard_map/ppermute | solution.py:521
  56.6 2.3 %collective-permute-start.4 = (bf16[16,512]{1,0:T(8,128)(2,1)S(1)}, bf16[16,512]{1,0:T(8,128)(2,1)S(1)}, u32[]{:S(2)}, u32[]{:S(2)}) collective-permute-start(bf16[16,512]{1,0:T(8,128)(2,1)S(1)} %get-tuple-element.47), channel_id=1, source_target_pairs={{0,12},{1,0},{2,4},{3,8},{4,13},{5,1},{6,5},{7,9},{8,14},{9,2},{10... | collective-permute-start | bytes 49160 | tf_op jit(solution)/shard_map/ppermute | solution.py:521
  60.4 2.2 %attend.1 = (bf16[16,512]{1,0:T(8,128)(2,1)S(1)}, bf16[16,512]{1,0:T(8,128)(2,1)S(1)}, bf16[16,512]{1,0:T(8,128)(2,1)S(1)}, bf16[16,512]{1,0:T(8,128)(2,1)S(1)}) custom-call(s32[3]{0:T(128)S(1)} %pad_add_fusion.place, bf16[16,512]{1,0:T(8,128)(2,1)S(1)} %collective-permute-done.1.refs_0_, bf16[16,512]{1,0:T(8,128)(2,1)S(1)} %collective-permute-done.2.refs_1_, ...), custom_call_target="tpu_custom_call" | custom-call | tf_op jit(solution)/shard_map/attend/pallas_call | solution.py:268
  62.6 2.3 %collective-permute-start.10 = (bf16[16,512]{1,0:T(8,128)(2,1)S(1)}, bf16[16,512]{1,0:T(8,128)(2,1)S(1)}, u32[]{:S(2)}, u32[]{:S(2)}) collective-permute-start(bf16[16,512]{1,0:T(8,128)(2,1)S(1)} %get-tuple-element.38), channel_id=1, source_target_pairs={{8,0},{12,1},{0,2},{4,3},{9,4},{13,5},{1,6},{5,7},{10,8},{14,9},{2... | collective-permute-start | bytes 49160 | tf_op jit(solution)/shard_map/ppermute | solution.py:538
  65.5 6.3 %collective-permute-start.9 = (bf16[16,512]{1,0:T(8,128)(2,1)S(1)}, bf16[16,512]{1,0:T(8,128)(2,1)S(1)}, u32[]{:S(2)}, u32[]{:S(2)}) collective-permute-start(bf16[16,512]{1,0:T(8,128)(2,1)S(1)} %get-tuple-element.37), channel_id=1, source_target_pairs={{4,0},{8,1},{12,2},{0,3},{5,4},{9,5},{13,6},{1,7},{6,8},{10,9},{14... | collective-permute-start | bytes 49160 | tf_op jit(solution)/shard_map/ppermute | solution.py:538
  73.3 3.4 %copy-done.1 = bf16[512,8192]{1,0:T(8,128)(2,1)S(1)} copy-done((bf16[512,8192]{1,0:T(8,128)(2,1)S(1)}, bf16[512,8192]{1,0:T(8,128)(2,1)}, u32[]{:S(2)}) %copy-start.1) | copy-done | bytes 8388632
  81.1 5.7 %collective-permute-start.13 = (s16[1040,128]{1,0:T(8,128)(2,1)S(1)}, s16[1040,128]{1,0:T(8,128)(2,1)S(1)}, u32[]{:S(2)}, u32[]{:S(2)}) collective-permute-start(s16[1040,128]{1,0:T(8,128)(2,1)S(1)} %get-tuple-element.42), channel_id=1, source_target_pairs={{0,2},{2,0},{1,3},{3,1},{4,6},{6,4},{5,7},{7,5},{8,10},{10,8},{9,1... | collective-permute-start | bytes 798728 | tf_op jit(solution)/shard_map/ppermute | solution.py:436
  86.7 6.7 %collective-permute-done.13.refs_0_ = s16[1040,128]{1,0:T(8,128)(2,1)S(1)} collective-permute-done((s16[1040,128]{1,0:T(8,128)(2,1)S(1)}, s16[1040,128]{1,0:T(8,128)(2,1)S(1)}, u32[]{:S(2)}, u32[]{:S(2)}) %collective-permute-start.13) | collective-permute-done | bytes 266272 | tf_op jit(solution)/shard_map/ppermute | solution.py:436
  94.3 3.3 %collective-permute-start.16 = (s16[272,128]{1,0:T(8,128)(2,1)S(1)}, s16[272,128]{1,0:T(8,128)(2,1)S(1)}, u32[]{:S(2)}, u32[]{:S(2)}) collective-permute-start(s16[272,128]{1,0:T(8,128)(2,1)S(1)} %get-tuple-element.46), channel_id=1, source_target_pairs={{0,12},{4,0},{8,4},{12,8},{1,13},{5,1},{9,5},{13,9},{2,14},{6,2},{... | collective-permute-start | bytes 208904 | tf_op jit(solution)/shard_map/ppermute | solution.py:436
  97.5 3.1 %collective-permute-done.14.refs_0_ = s16[272,128]{1,0:T(8,128)(2,1)S(1)} collective-permute-done((s16[272,128]{1,0:T(8,128)(2,1)S(1)}, s16[272,128]{1,0:T(8,128)(2,1)S(1)}, u32[]{:S(2)}, u32[]{:S(2)}) %collective-permute-start.14) | collective-permute-done | bytes 69664 | tf_op jit(solution)/shard_map/ppermute | solution.py:436
  100.6 1.5 %collective-permute-done.15.refs_1_ = s16[272,128]{1,0:T(8,128)(2,1)S(1)} collective-permute-done((s16[272,128]{1,0:T(8,128)(2,1)S(1)}, s16[272,128]{1,0:T(8,128)(2,1)S(1)}, u32[]{:S(2)}, u32[]{:S(2)}) %collective-permute-start.15) | collective-permute-done | bytes 69664 | tf_op jit(solution)/shard_map/ppermute | solution.py:436
  (64 shorter events, 18.3 us)
Async XLA Ops:
  1.7 32.9 %all-to-all-start = ((bf16[8,64,512]{2,1,0:T(8,128)(2,1)}), bf16[8,64,512]{2,1,0:T(8,128)(2,1)S(1)}, u32[]{:S(2)}, u32[]{:S(2)}) async-start(bf16[8,64,512]{2,1,0:T(8,128)(2,1)} %broadcast_in_dim.6), calls=%async_computation | async-start | bytes 1048576 | tf_op jit(solution)/shard_map/all_to_all | solution.py:468
  15.2 37.9 %collective-permute-start.5 = (bf16[2,128,256]{2,1,0:T(8,128)(2,1)}, bf16[2,128,256]{2,1,0:T(8,128)(2,1)S(1)}, u32[]{:S(2)}, u32[]{:S(2)}) collective-permute-start(bf16[2,128,256]{2,1,0:T(8,128)(2,1)} %get-tuple-element.33), channel_id=1, source_target_pairs={{0,1},{1,2},{2,3},{3,0},{4,5},{5,6},{6,7},{7,4},{8,9},{9,10},{10,1... | collective-permute-start | bytes 393224 | tf_op jit(solution)/shard_map/ppermute | solution.py:478
  15.2 41.4 %collective-permute-start.6 = (bf16[2,128,256]{2,1,0:T(8,128)(2,1)}, bf16[2,128,256]{2,1,0:T(8,128)(2,1)}, u32[]{:S(2)}, u32[]{:S(2)}) collective-permute-start(bf16[2,128,256]{2,1,0:T(8,128)(2,1)} %get-tuple-element.34), channel_id=1, source_target_pairs={{0,2},{1,3},{2,0},{3,1},{4,6},{5,7},{6,4},{7,5},{8,10},{9,11},{10,... | collective-permute-start | bytes 393224 | tf_op jit(solution)/shard_map/ppermute | solution.py:478
  17.3 42.4 %collective-permute-start.7 = (bf16[2,128,256]{2,1,0:T(8,128)(2,1)}, bf16[2,128,256]{2,1,0:T(8,128)(2,1)}, u32[]{:S(2)}, u32[]{:S(2)}) collective-permute-start(bf16[2,128,256]{2,1,0:T(8,128)(2,1)} %get-tuple-element.35), channel_id=1, source_target_pairs={{0,3},{1,0},{2,1},{3,2},{4,7},{5,4},{6,5},{7,6},{8,11},{9,8},{10,9... | collective-permute-start | bytes 393224 | tf_op jit(solution)/shard_map/ppermute | solution.py:478
  21.9 12.6 %copy-start.10 = (s32[4]{0:T(128)S(1)}, s32[4]{0:T(128)}, u32[]{:S(2)}) copy-start(s32[4]{0:T(128)} %param.16) | copy-start | bytes 52
  28.0 3.3 %copy-start = (bf16[512,8192]{1,0:T(8,128)(2,1)}, bf16[512,8192]{1,0:T(8,128)(2,1)S(1)}, u32[]{:S(2)}) copy-start(bf16[512,8192]{1,0:T(8,128)(2,1)S(1)} %get-tuple-element.40.refs_4_) | copy-start | bytes 25165828
  31.3 3.3 %copy-start.2 = (bf16[8192,512]{1,0:T(8,128)(2,1)}, bf16[8192,512]{1,0:T(8,128)(2,1)S(1)}, u32[]{:S(2)}) copy-start(bf16[8192,512]{1,0:T(8,128)(2,1)S(1)} %get-tuple-element.30.weight_ref) | copy-start | bytes 25165828
  34.5 1.9 %collective-permute-start = (bf16[8,64,512]{2,1,0:T(8,128)(2,1)S(1)}, bf16[8,64,512]{2,1,0:T(8,128)(2,1)S(1)}, u32[]{:S(2)}, u32[]{:S(2)}) collective-permute-start(bf16[8,64,512]{2,1,0:T(8,128)(2,1)S(1)} %all-to-all-done.mine_ref), channel_id=1, source_target_pairs={{0,1},{1,0},{2,3},{3,2},{4,5},{5,4},{6,7},{7,6},{8,9},{9,8},{10,11... | collective-permute-start | bytes 1572872 | tf_op jit(solution)/shard_map/ppermute | solution.py:436
  37.9 22.5 %all-to-all-start.1 = ((f32[16,16,512]{2,1,0:T(8,128)}), f32[16,16,512]{2,1,0:T(8,128)S(1)}, u32[]{:S(2)}, u32[]{:S(2)}) async-start(f32[16,16,512]{2,1,0:T(8,128)} %bitcast.28), calls=%async_computation.1 | async-start | bytes 1048576 | tf_op jit(solution)/shard_map/all_to_all | solution.py:498
  43.5 3.4 %copy-start.3 = (bf16[8192,512]{1,0:T(8,128)(2,1)S(1)}, bf16[8192,512]{1,0:T(8,128)(2,1)}, u32[]{:S(2)}) copy-start(bf16[8192,512]{1,0:T(8,128)(2,1)} %copy-done.2) | copy-start | bytes 25165828
  49.1 10.5 %collective-permute-start.1 = (bf16[16,512]{1,0:T(8,128)(2,1)S(1)}, bf16[16,512]{1,0:T(8,128)(2,1)S(1)}, u32[]{:S(2)}, u32[]{:S(2)}) collective-permute-start(bf16[16,512]{1,0:T(8,128)(2,1)S(1)} %get-tuple-element.50), channel_id=1, source_target_pairs={{0,0},{1,4},{2,8},{3,12},{4,1},{5,5},{6,9},{7,13},{8,2},{9,6},{10,... | collective-permute-start | bytes 49160 | tf_op jit(solution)/shard_map/ppermute | solution.py:521
  49.8 9.9 %collective-permute-start.2 = (bf16[16,512]{1,0:T(8,128)(2,1)S(1)}, bf16[16,512]{1,0:T(8,128)(2,1)S(1)}, u32[]{:S(2)}, u32[]{:S(2)}) collective-permute-start(bf16[16,512]{1,0:T(8,128)(2,1)S(1)} %get-tuple-element.49), channel_id=1, source_target_pairs={{0,4},{1,8},{2,12},{3,0},{4,5},{5,9},{6,13},{7,1},{8,6},{9,10},{10... | collective-permute-start | bytes 49160 | tf_op jit(solution)/shard_map/ppermute | solution.py:521
  53.2 6.5 %collective-permute-start.3 = (bf16[16,512]{1,0:T(8,128)(2,1)S(1)}, bf16[16,512]{1,0:T(8,128)(2,1)S(1)}, u32[]{:S(2)}, u32[]{:S(2)}) collective-permute-start(bf16[16,512]{1,0:T(8,128)(2,1)S(1)} %get-tuple-element.48), channel_id=1, source_target_pairs={{0,8},{1,12},{2,0},{3,4},{4,9},{5,13},{6,1},{7,5},{8,10},{9,14},{1... | collective-permute-start | bytes 49160 | tf_op jit(solution)/shard_map/ppermute | solution.py:521
  56.6 3.8 %collective-permute-start.4 = (bf16[16,512]{1,0:T(8,128)(2,1)S(1)}, bf16[16,512]{1,0:T(8,128)(2,1)S(1)}, u32[]{:S(2)}, u32[]{:S(2)}) collective-permute-start(bf16[16,512]{1,0:T(8,128)(2,1)S(1)} %get-tuple-element.47), channel_id=1, source_target_pairs={{0,12},{1,0},{2,4},{3,8},{4,13},{5,1},{6,5},{7,9},{8,14},{9,2},{10... | collective-permute-start | bytes 49160 | tf_op jit(solution)/shard_map/ppermute | solution.py:521
  62.6 9.4 %collective-permute-start.10 = (bf16[16,512]{1,0:T(8,128)(2,1)S(1)}, bf16[16,512]{1,0:T(8,128)(2,1)S(1)}, u32[]{:S(2)}, u32[]{:S(2)}) collective-permute-start(bf16[16,512]{1,0:T(8,128)(2,1)S(1)} %get-tuple-element.38), channel_id=1, source_target_pairs={{8,0},{12,1},{0,2},{4,3},{9,4},{13,5},{1,6},{5,7},{10,8},{14,9},{2... | collective-permute-start | bytes 49160 | tf_op jit(solution)/shard_map/ppermute | solution.py:538
  64.9 7.1 %collective-permute-start.11 = (bf16[16,512]{1,0:T(8,128)(2,1)S(1)}, bf16[16,512]{1,0:T(8,128)(2,1)S(1)}, u32[]{:S(2)}, u32[]{:S(2)}) collective-permute-start(bf16[16,512]{1,0:T(8,128)(2,1)S(1)} %get-tuple-element.39), channel_id=1, source_target_pairs={{12,0},{0,1},{4,2},{8,3},{13,4},{1,5},{5,6},{9,7},{14,8},{2,9},{6,... | collective-permute-start | bytes 49160 | tf_op jit(solution)/shard_map/ppermute | solution.py:538
  64.9 7.1 %collective-permute-start.8 = (bf16[16,512]{1,0:T(8,128)(2,1)S(1)}, bf16[16,512]{1,0:T(8,128)(2,1)S(1)}, u32[]{:S(2)}, u32[]{:S(2)}) collective-permute-start(bf16[16,512]{1,0:T(8,128)(2,1)S(1)} %get-tuple-element.36), channel_id=1, source_target_pairs={{0,0},{4,1},{8,2},{12,3},{1,4},{5,5},{9,6},{13,7},{2,8},{6,9},{10,... | collective-permute-start | bytes 49160 | tf_op jit(solution)/shard_map/ppermute | solution.py:538
  65.5 7.8 %collective-permute-start.9 = (bf16[16,512]{1,0:T(8,128)(2,1)S(1)}, bf16[16,512]{1,0:T(8,128)(2,1)S(1)}, u32[]{:S(2)}, u32[]{:S(2)}) collective-permute-start(bf16[16,512]{1,0:T(8,128)(2,1)S(1)} %get-tuple-element.37), channel_id=1, source_target_pairs={{4,0},{8,1},{12,2},{0,3},{5,4},{9,5},{13,6},{1,7},{6,8},{10,9},{14... | collective-permute-start | bytes 49160 | tf_op jit(solution)/shard_map/ppermute | solution.py:538
  73.3 3.4 %copy-start.1 = (bf16[512,8192]{1,0:T(8,128)(2,1)S(1)}, bf16[512,8192]{1,0:T(8,128)(2,1)}, u32[]{:S(2)}) copy-start(bf16[512,8192]{1,0:T(8,128)(2,1)} %copy-done) | copy-start | bytes 25165828
  78.1 2.7 %collective-permute-start.12 = (f32[8,64,512]{2,1,0:T(8,128)S(1)}, f32[8,64,512]{2,1,0:T(8,128)S(1)}, u32[]{:S(2)}, u32[]{:S(2)}) collective-permute-start(f32[8,64,512]{2,1,0:T(8,128)S(1)} %outputs.3), channel_id=1, source_target_pairs={{0,1},{1,0},{2,3},{3,2},{4,5},{5,4},{6,7},{7,6},{8,9},{9,8},{10,11... | collective-permute-start | bytes 3145736 | tf_op jit(solution)/shard_map/ppermute | solution.py:436
  81.1 12.4 %collective-permute-start.13 = (s16[1040,128]{1,0:T(8,128)(2,1)S(1)}, s16[1040,128]{1,0:T(8,128)(2,1)S(1)}, u32[]{:S(2)}, u32[]{:S(2)}) collective-permute-start(s16[1040,128]{1,0:T(8,128)(2,1)S(1)} %get-tuple-element.42), channel_id=1, source_target_pairs={{0,2},{2,0},{1,3},{3,1},{4,6},{6,4},{5,7},{7,5},{8,10},{10,8},{9,1... | collective-permute-start | bytes 798728 | tf_op jit(solution)/shard_map/ppermute | solution.py:436
  93.6 6.9 %collective-permute-start.14 = (s16[272,128]{1,0:T(8,128)(2,1)S(1)}, s16[272,128]{1,0:T(8,128)(2,1)S(1)}, u32[]{:S(2)}, u32[]{:S(2)}) collective-permute-start(s16[272,128]{1,0:T(8,128)(2,1)S(1)} %get-tuple-element.44), channel_id=1, source_target_pairs={{0,4},{4,8},{8,12},{12,0},{1,5},{5,9},{9,13},{13,1},{2,6},{6,10},{... | collective-permute-start | bytes 208904 | tf_op jit(solution)/shard_map/ppermute | solution.py:436
  93.7 8.4 %collective-permute-start.15 = (s16[272,128]{1,0:T(8,128)(2,1)S(1)}, s16[272,128]{1,0:T(8,128)(2,1)S(1)}, u32[]{:S(2)}, u32[]{:S(2)}) collective-permute-start(s16[272,128]{1,0:T(8,128)(2,1)S(1)} %get-tuple-element.45), channel_id=1, source_target_pairs={{0,8},{4,12},{8,0},{12,4},{1,9},{5,13},{9,1},{13,5},{2,10},{6,14},... | collective-permute-start | bytes 208904 | tf_op jit(solution)/shard_map/ppermute | solution.py:436
  94.3 7.8 %collective-permute-start.16 = (s16[272,128]{1,0:T(8,128)(2,1)S(1)}, s16[272,128]{1,0:T(8,128)(2,1)S(1)}, u32[]{:S(2)}, u32[]{:S(2)}) collective-permute-start(s16[272,128]{1,0:T(8,128)(2,1)S(1)} %get-tuple-element.46), channel_id=1, source_target_pairs={{0,12},{4,0},{8,4},{12,8},{1,13},{5,1},{9,5},{13,9},{2,14},{6,2},{... | collective-permute-start | bytes 208904 | tf_op jit(solution)/shard_map/ppermute | solution.py:436
  (6 other events, 5.9 us)

commit v4 on v3

v4 whole, which is shorter than its diff:
```python
import jax
import jax.numpy as jnp
from jax import lax
from jax.experimental import pallas as pl
from jax.experimental.pallas import tpu as pltpu
from jax.sharding import Mesh
from jax.sharding import PartitionSpec as P

QUERY_HEADS = 64
KEY_VALUE_HEADS = 8
HEAD_SIZE = 128
GROUP_REQUESTS = 4
SAMPLES = 8
PAGE_TOKENS = 16
STEPS = 2
ROWS = STEPS * SAMPLES
PAIR = 2 * HEAD_SIZE
LANES = 128
TAIL = 16
DEVICES = ("req", "sub", "section")

theta_base = 500000.0
eps_norm = 1e-05
VMEM = 16 * 2**20


def params(**more):
    return pltpu.CompilerParams(vmem_limit_bytes=VMEM, **more)


def whole_spec(shape):
    return pl.BlockSpec(shape, lambda *_: (0,) * len(shape))


def turn(vectors, cosine, sine):
    return vectors * cosine + pltpu.roll(vectors, HEAD_SIZE // 2, vectors.ndim - 1) * sine


def stage_kernel(*refs):
    half = (len(refs) - 1) // 2
    copies = [
        pltpu.make_async_copy(refs[i], refs[half + i], refs[-1].at[i]) for i in range(half)
    ]
    for copy in copies:
        copy.start()
    for copy in copies:
        copy.wait()


def staged(*arrays):
    size = sum(array.size * array.dtype.itemsize for array in arrays)
    return pl.pallas_call(
        stage_kernel,
        in_specs=[pl.BlockSpec(memory_space=pltpu.HBM)] * len(arrays),
        out_specs=[pl.BlockSpec(memory_space=pltpu.VMEM)] * len(arrays),
        out_shape=[jax.ShapeDtypeStruct(array.shape, array.dtype) for array in arrays],
        scratch_shapes=[pltpu.SemaphoreType.DMA((len(arrays),))],
        compiler_params=pltpu.CompilerParams(vmem_limit_bytes=30 * 2**20),
        cost_estimate=pl.CostEstimate(flops=0, bytes_accessed=2 * size, transcendentals=0),
        name="staged",
    )(*arrays)


def pages_kernel(table, place, scales, page_ref, *out_refs):
    e = pl.program_id(0)
    subs = len(out_refs)
    targets = 2 * subs
    page = table[place[0], e * targets + place[1]] - place[2]
    for shift, out_ref in enumerate(out_refs):
        half = lax.rem(place[1] // 2 + shift, subs) // (subs // 2)
        for z in range(GROUP_REQUESTS):
            head = 2 * lax.rem(place[0] + z, GROUP_REQUESTS) + half
            for part in range(2):
                c = head * 2 + part
                columns = pl.ds(pl.multiple_of(c * HEAD_SIZE, HEAD_SIZE), HEAD_SIZE)
                block = page_ref[0, :, columns].astype(jnp.float32)
                out_ref[z, :, part * HEAD_SIZE : (part + 1) * HEAD_SIZE] = (
                    block * scales[page, c]
                ).astype(jnp.bfloat16)


def used_pages(pages, scales, table, place, subs):
    targets = 2 * subs
    entries = table.shape[1] // targets
    return pl.pallas_call(
        pages_kernel,
        grid_spec=pltpu.PrefetchScalarGridSpec(
            num_scalar_prefetch=3,
            grid=(entries,),
            in_specs=[
                pl.BlockSpec(
                    (1, PAGE_TOKENS, pages.shape[2]),
                    lambda e, table, place, scales: (
                        table[place[0], e * targets + place[1]] - place[2],
                        0,
                        0,
                    ),
                )
            ],
            out_specs=[
                pl.BlockSpec((GROUP_REQUESTS, PAGE_TOKENS, PAIR), lambda e, *_: (0, e, 0))
            ]
            * subs,
        ),
        out_shape=[
            jax.ShapeDtypeStruct((GROUP_REQUESTS, entries * PAGE_TOKENS, PAIR), jnp.bfloat16)
        ]
        * subs,
        compiler_params=params(),
        name="used_pages",
    )(table, place, scales.astype(jnp.float32), pages)


def regroup_kernel(*refs):
    ins, outs = refs[:-GROUP_REQUESTS], refs[-GROUP_REQUESTS:]
    for z, out_ref in enumerate(outs):
        for j, ref in enumerate(ins):
            out_ref[j] = ref[z]


def regroup(parts):
    shape = jax.ShapeDtypeStruct((len(parts),) + parts[0].shape[1:], parts[0].dtype)
    return pl.pallas_call(
        regroup_kernel,
        in_specs=[pl.BlockSpec(memory_space=pltpu.VMEM)] * len(parts),
        out_specs=[pl.BlockSpec(memory_space=pltpu.VMEM)] * GROUP_REQUESTS,
        out_shape=[shape] * GROUP_REQUESTS,
        compiler_params=params(),
        name="regroup",
    )(*parts)


def pack_kernel(*refs):
    for i, ref in enumerate(refs[:-1]):
        refs[-1][i] = ref[...]


def pack(parts):
    return pl.pallas_call(
        pack_kernel,
        in_specs=[pl.BlockSpec(memory_space=pltpu.VMEM)] * len(parts),
        out_specs=pl.BlockSpec(memory_space=pltpu.VMEM),
        out_shape=jax.ShapeDtypeStruct((len(parts),) + parts[0].shape, parts[0].dtype),
        compiler_params=params(),
        name="pack",
    )(*parts)


def blocks_of(place, refs):
    request, sub, core = place[0], place[1], place[2]
    subs = len(refs) // 2
    for i, ref in enumerate(refs):
        from_core = core if i < subs else 1 - core
        from_sub = lax.rem(sub - i % subs + subs, subs)
        for z in range(GROUP_REQUESTS):
            from_request = lax.rem(request - z + GROUP_REQUESTS, GROUP_REQUESTS)
            yield ref, z, (from_request * subs + from_sub) * 2 + from_core


def pairs_kernel(place, rows_ref, gain_ref, weight_ref, *refs):
    subs = (len(refs) - 1) // 3
    x_refs, scale_ref, kept_ref, out_refs = (
        refs[: 2 * subs],
        refs[2 * subs],
        refs[2 * subs + 1],
        refs[2 * subs + 2 :],
    )
    request, sub, core = place[0], place[1], place[2]
    rows, width = rows_ref.shape
    total = jnp.zeros((rows, LANES), jnp.float32)
    for ref in x_refs:
        for z in range(GROUP_REQUESTS):
            for piece in pieces_of(ref[z].astype(jnp.float32)):
                total += piece * piece
    mean = jnp.sum(total, axis=-1, keepdims=True) / (2 * subs * GROUP_REQUESTS * width)
    scale = lax.rsqrt(mean + eps_norm)
    scale_ref[...] = jnp.broadcast_to(scale, scale_ref.shape)
    device = (request * subs + sub) * 2 + core
    x = rows_ref[...].astype(jnp.float32)
    mine = (x * scale * gain_ref[device]).astype(jnp.bfloat16)
    for shift in range(subs):
        half = lax.rem(sub + shift, subs) // (subs // 2)
        pieces = []
        for z in range(GROUP_REQUESTS):
            head = 2 * lax.rem(request + z, GROUP_REQUESTS) + half
            columns = pl.ds(pl.multiple_of(head * PAIR, PAIR), PAIR)
            part = jnp.dot(mine, weight_ref[:, columns], preferred_element_type=jnp.float32)
            if shift == 0:
                kept_ref[z] = part
            pieces += pieces_of(part)
        if shift:
            encode(out_refs[shift - 1], pieces)


def scale_and_pairs(place, rows, gain, weight, gathered):
    subs = len(gathered) // 2
    count = rows.shape[0]
    sent = jax.ShapeDtypeStruct((2 * GROUP_REQUESTS * count + TAIL, LANES), jnp.int16)
    shapes = [
        jax.ShapeDtypeStruct((count, LANES), jnp.float32),
        jax.ShapeDtypeStruct((GROUP_REQUESTS, count, PAIR), jnp.float32),
    ] + [sent] * (subs - 1)
    return pl.pallas_call(
        pairs_kernel,
        in_specs=[pl.BlockSpec(memory_space=pltpu.SMEM)]
        + [pl.BlockSpec(memory_space=pltpu.VMEM)] * (3 + len(gathered)),
        out_specs=[pl.BlockSpec(memory_space=pltpu.VMEM)] * len(shapes),
        out_shape=shapes,
        compiler_params=params(),
        name="scale_and_pairs",
    )(place, rows, gain, weight, *gathered)


def query_kernel(place, scale_ref, gain_ref, weight_ref, cos_ref, sin_ref, *refs):
    out_ref = refs[-1]
    _, rows, width = refs[0].shape
    columns = weight_ref.shape[1]
    scale = scale_ref[:, :1]
    total = jnp.zeros((rows, columns), jnp.float32)
    for ref, z, block in blocks_of(place, refs[:-1]):
        x = ref[z].astype(jnp.float32)
        x = (x * scale * gain_ref[block]).astype(jnp.bfloat16)
        depth = pl.ds(pl.multiple_of(block * width, width), width)
        total += jnp.dot(x, weight_ref[depth, :], preferred_element_type=jnp.float32)
    for head in range(columns // HEAD_SIZE):
        part = slice(head * HEAD_SIZE, (head + 1) * HEAD_SIZE)
        turned = turn(total[:, part], cos_ref[...], sin_ref[...])
        for r in range(GROUP_REQUESTS):
            first, second = r * SAMPLES, (GROUP_REQUESTS + r) * SAMPLES
            out_ref[r, :, part] = jnp.concatenate(
                [turned[first : first + SAMPLES], turned[second : second + SAMPLES]], axis=0
            ).astype(jnp.bfloat16)


def queries(place, scale, gain, weight, cosine, sine, gathered):
    columns = weight.shape[1]
    return pl.pallas_call(
        query_kernel,
        in_specs=[pl.BlockSpec(memory_space=pltpu.SMEM)]
        + [pl.BlockSpec(memory_space=pltpu.VMEM)] * (5 + len(gathered)),
        out_specs=pl.BlockSpec(memory_space=pltpu.VMEM),
        out_shape=jax.ShapeDtypeStruct((GROUP_REQUESTS, ROWS, columns), jnp.bfloat16),
        compiler_params=params(),
        name="queries",
    )(place, scale, gain, weight, cosine, sine, *gathered)


def attend_kernel(place, lengths, q_ref, mine_ref, other_ref, cos_ref, sin_ref, *refs):
    caches, out_ref, key_ref, value_ref = refs[:-3], refs[-3], refs[-2], refs[-1]
    request, sub, core = place[0], place[1], place[2]
    subs, span, _ = caches[0].shape
    targets = 2 * subs
    tokens = targets * span
    quarter = q_ref.shape[2] // HEAD_SIZE
    pair = mine_ref[...] + other_ref[...]
    key_ref[...] = turn(pair[:, :HEAD_SIZE], cos_ref[...], sin_ref[...])
    value_ref[...] = pair[:, HEAD_SIZE:]
    column = lax.broadcasted_iota(jnp.int32, (1, tokens), 1)
    source, inside = column // span, column % span
    from_core = jnp.where(source < subs, core, 1 - core)
    from_sub = (sub - source % subs + subs) % subs
    entry = inside // PAGE_TOKENS * targets + from_sub * 2 + from_core
    position = entry * PAGE_TOKENS + inside % PAGE_TOKENS
    count = quarter * ROWS
    row = lax.broadcasted_iota(jnp.int32, (count, ROWS), 0) % ROWS
    other = lax.broadcasted_iota(jnp.int32, (count, ROWS), 1)
    own_visible = (row % SAMPLES == other % SAMPLES) & (other // SAMPLES <= row // SAMPLES)
    factor = HEAD_SIZE ** (-0.5)
    contract = (((1,), (1,)), ((), ()))
    for z in range(GROUP_REQUESTS):
        r = lax.rem(request - z + GROUP_REQUESTS, GROUP_REQUESTS)
        fresh = [
            pl.ds(pl.multiple_of((step * GROUP_REQUESTS + r) * SAMPLES, SAMPLES), SAMPLES)
            for step in range(STEPS)
        ]
        new_key = jnp.concatenate([key_ref[rows] for rows in fresh], axis=0)
        new_value = jnp.concatenate([value_ref[rows] for rows in fresh], axis=0)
        new_key, new_value = new_key.astype(jnp.bfloat16), new_value.astype(jnp.bfloat16)
        pair_of_caches = (caches[z], caches[GROUP_REQUESTS + z])
        keys = jnp.concatenate(
            [c[j, :, :HEAD_SIZE] for c in pair_of_caches for j in range(subs)], axis=0
        )
        values = jnp.concatenate(
            [c[j, :, HEAD_SIZE:] for c in pair_of_caches for j in range(subs)], axis=0
        )
        query = jnp.concatenate(
            [q_ref[r, :, h * HEAD_SIZE : (h + 1) * HEAD_SIZE] for h in range(quarter)], axis=0
        )
        scores = lax.dot_general(query, keys, contract, preferred_element_type=jnp.float32)
        scores = jnp.where(position < lengths[r], scores * factor, -jnp.inf)
        own = lax.dot_general(query, new_key, contract, preferred_element_type=jnp.float32)
        own = jnp.where(own_visible, own * factor, -jnp.inf)
        highest = jnp.maximum(
            jnp.max(scores, axis=-1, keepdims=True), jnp.max(own, axis=-1, keepdims=True)
        )
        scores = jnp.exp(scores - highest)
        own = jnp.exp(own - highest)
        total = jnp.sum(scores, axis=-1, keepdims=True) + jnp.sum(own, axis=-1, keepdims=True)
        mixed = jnp.dot(
            (scores / total).astype(jnp.bfloat16), values, preferred_element_type=jnp.float32
        ) + jnp.dot(
            (own / total).astype(jnp.bfloat16), new_value, preferred_element_type=jnp.float32
        )
        mixed = mixed.astype(jnp.bfloat16)
        for h in range(quarter):
            out_ref[r, :, h * HEAD_SIZE : (h + 1) * HEAD_SIZE] = mixed[
                h * ROWS : (h + 1) * ROWS
            ]


def attend(place, lengths, query, mine, other, cosine, sine, caches):
    return pl.pallas_call(
        attend_kernel,
        in_specs=[pl.BlockSpec(memory_space=pltpu.SMEM)] * 2
        + [pl.BlockSpec(memory_space=pltpu.VMEM)] * (5 + len(caches)),
        out_specs=pl.BlockSpec(memory_space=pltpu.VMEM),
        out_shape=jax.ShapeDtypeStruct(query.shape, jnp.bfloat16),
        scratch_shapes=[pltpu.VMEM(cosine.shape, jnp.float32)] * 2,
        compiler_params=params(),
        name="attend",
    )(place, lengths, query, mine, other, cosine, sine, *caches)


def output_kernel(place, x_ref, weight_ref, out_ref):
    blocks, rows, width = out_ref.shape
    x = x_ref[...].reshape(rows, -1)
    for i in range(blocks):
        columns = pl.ds(pl.multiple_of((2 * i + place[0]) * width, width), width)
        part = jnp.dot(x, weight_ref[:, columns], preferred_element_type=jnp.float32)
        for r in range(GROUP_REQUESTS):
            for step in range(STEPS):
                source = r * ROWS + step * SAMPLES
                target = (step * GROUP_REQUESTS + r) * SAMPLES
                out_ref[i, target : target + SAMPLES] = part[source : source + SAMPLES]


def outputs(place, mixed, weight, blocks):
    rows = GROUP_REQUESTS * ROWS
    width = weight.shape[1] // (2 * blocks)
    return pl.pallas_call(
        output_kernel,
        in_specs=[pl.BlockSpec(memory_space=pltpu.SMEM)]
        + [pl.BlockSpec(memory_space=pltpu.VMEM)] * 2,
        out_specs=pl.BlockSpec(memory_space=pltpu.VMEM),
        out_shape=jax.ShapeDtypeStruct((blocks, rows, width), jnp.float32),
        compiler_params=params(),
        name="outputs",
    )(place, mixed, weight)


def pieces_of(block):
    return [block[:, c : c + LANES] for c in range(0, block.shape[1], LANES)]


def encode(out_ref, pieces):
    rows = pieces[0].shape[0]
    peak = jnp.abs(pieces[0])
    for piece in pieces[1:]:
        peak = jnp.maximum(peak, jnp.abs(piece))
    peak = jnp.maximum(jnp.max(peak, axis=0, keepdims=True), 1e-30)
    exponent = jnp.floor(jnp.log2(peak)) - 14.0
    inverse = jnp.exp2(-exponent)
    for i, piece in enumerate(pieces):
        code = jnp.clip(jnp.floor(piece * inverse + 0.5), -32767.0, 32767.0)
        out_ref[i * rows : (i + 1) * rows] = code.astype(jnp.int32).astype(jnp.int16)
    out_ref[len(pieces) * rows :] = (
        jnp.broadcast_to(exponent, (TAIL, LANES)).astype(jnp.int32).astype(jnp.int16)
    )


def step_of(ref):
    tail = ref[ref.shape[0] - TAIL :].astype(jnp.int32).astype(jnp.float32)
    return jnp.exp2(tail[:1])


def decoded(ref, first, rows, step):
    return ref[pl.ds(first, rows)].astype(jnp.int32).astype(jnp.float32) * step


def fold_core_kernel(place, mine_ref, got_ref, kept_ref, *out_refs):
    subs = 1 + len(out_refs)
    for shift in range(subs):
        sub = lax.rem(place[0] + shift, subs)
        pieces = []
        for i in range(GROUP_REQUESTS):
            block = mine_ref[i * subs + sub] + got_ref[i * subs + sub]
            if shift == 0:
                kept_ref[i] = block
            pieces += pieces_of(block)
        if shift:
            encode(out_refs[shift - 1], pieces)


def fold_core(place, mine, got, subs):
    _, rows, width = mine.shape
    kept = jax.ShapeDtypeStruct((GROUP_REQUESTS, rows, width), jnp.float32)
    sent = jax.ShapeDtypeStruct(
        (GROUP_REQUESTS * width // LANES * rows + TAIL, LANES), jnp.int16
    )
    return pl.pallas_call(
        fold_core_kernel,
        in_specs=[pl.BlockSpec(memory_space=pltpu.SMEM)]
        + [pl.BlockSpec(memory_space=pltpu.VMEM)] * 2,
        out_specs=[pl.BlockSpec(memory_space=pltpu.VMEM)] * subs,
        out_shape=[kept] + [sent] * (subs - 1),
        compiler_params=params(),
        name="fold_core",
    )(place, mine, got)


def fold_sub_kernel(place, kept_ref, *refs):
    in_refs, total_ref, out_refs = (
        refs[:-GROUP_REQUESTS],
        refs[-GROUP_REQUESTS],
        refs[1 - GROUP_REQUESTS :],
    )
    _, rows, width = kept_ref.shape
    steps = [step_of(ref) for ref in in_refs]
    for shift in range(GROUP_REQUESTS):
        block = lax.rem(place[0] + shift, GROUP_REQUESTS)
        pieces = pieces_of(kept_ref[block])
        for c in range(len(pieces)):
            first = pl.multiple_of((block * len(pieces) + c) * rows, rows)
            for ref, step in zip(in_refs, steps):
                pieces[c] = pieces[c] + decoded(ref, first, rows, step)
        if shift:
            encode(out_refs[shift - 1], pieces)
        else:
            for c, piece in enumerate(pieces):
                total_ref[:, c * LANES : (c + 1) * LANES] = piece


def fold_sub(place, kept, parts):
    _, rows, width = kept.shape
    total = jax.ShapeDtypeStruct((rows, width), jnp.float32)
    sent = jax.ShapeDtypeStruct((width // LANES * rows + TAIL, LANES), jnp.int16)
    return pl.pallas_call(
        fold_sub_kernel,
        in_specs=[pl.BlockSpec(memory_space=pltpu.SMEM)]
        + [pl.BlockSpec(memory_space=pltpu.VMEM)] * (1 + len(parts)),
        out_specs=[pl.BlockSpec(memory_space=pltpu.VMEM)] * GROUP_REQUESTS,
        out_shape=[total] + [sent] * (GROUP_REQUESTS - 1),
        compiler_params=params(),
        name="fold_sub",
    )(place, kept, *parts)


def fold_pairs_kernel(total_ref, *refs):
    rows = total_ref.shape[0]
    steps = [step_of(ref) for ref in refs[:-1]]
    for c in range(total_ref.shape[1] // LANES):
        part = slice(c * LANES, (c + 1) * LANES)
        total = total_ref[:, part]
        for ref, step in zip(refs[:-1], steps):
            total = total + decoded(ref, c * rows, rows, step)
        refs[-1][:, part] = total


def fold_pairs(total, parts):
    return pl.pallas_call(
        fold_pairs_kernel,
        in_specs=[pl.BlockSpec(memory_space=pltpu.VMEM)] * (1 + len(parts)),
        out_specs=pl.BlockSpec(memory_space=pltpu.VMEM),
        out_shape=jax.ShapeDtypeStruct(total.shape, jnp.float32),
        compiler_params=params(),
        name="fold_pairs",
    )(total, *parts)


def finish_kernel(rows_ref, total_ref, *refs):
    rows = rows_ref.shape[0]
    steps = [step_of(ref) for ref in refs[:-1]]
    for c in range(rows_ref.shape[1] // LANES):
        part = slice(c * LANES, (c + 1) * LANES)
        total = total_ref[:, part]
        for ref, step in zip(refs[:-1], steps):
            total = total + decoded(ref, c * rows, rows, step)
        refs[-1][:, part] = (total + rows_ref[:, part].astype(jnp.float32)).astype(jnp.bfloat16)


def finish(rows, total, parts):
    return pl.pallas_call(
        finish_kernel,
        in_specs=[pl.BlockSpec(memory_space=pltpu.VMEM)] * (2 + len(parts)),
        out_specs=pl.BlockSpec(memory_space=pltpu.VMEM),
        out_shape=jax.ShapeDtypeStruct(rows.shape, jnp.bfloat16),
        compiler_params=params(),
        name="finish",
    )(rows, total, *parts)


def passed(array, axis, shift):
    size = lax.axis_size(axis)
    return lax.ppermute(array, axis, [(i, (i + shift) % size) for i in range(size)])


def scalars(*values):
    return jnp.stack([jnp.asarray(value, jnp.int32) for value in values])


def shards(
    hidden,
    norm_gain,
    w_query,
    key_value_weight,
    w_output,
    prompt_cache_pages,
    per_page_scales,
    lengths,
    block_table,
):
    devices = lax.axis_size(DEVICES)
    subs = lax.axis_size("sub")
    device = lax.axis_index(DEVICES)
    request = lax.axis_index("req")
    sub = lax.axis_index("sub")
    core = lax.axis_index("section")
    width = hidden.shape[2]
    place = scalars(request, sub, core)

    rows = hidden.reshape(GROUP_REQUESTS * ROWS, width)
    column = pack([rows] + [passed(rows, "req", s) for s in range(1, GROUP_REQUESTS)])
    gathered = [column] + [passed(column, "sub", s) for s in range(1, subs)]
    gathered = gathered + [passed(part, "section", 1) for part in gathered]

    where = scalars(request, sub * 2 + core, device * prompt_cache_pages.shape[0])
    parts = used_pages(prompt_cache_pages, per_page_scales, block_table, where, subs)
    parts = [parts[0]] + [passed(parts[s], "sub", s) for s in range(1, subs)]
    parts = regroup(parts)
    caches = [parts[0]] + [passed(parts[s], "req", s) for s in range(1, GROUP_REQUESTS)]
    caches = caches + [passed(part, "section", 1) for part in caches]

    half = HEAD_SIZE // 2
    freqs = jnp.exp(
        -jnp.log(theta_base) * jnp.arange(half, dtype=jnp.float32) * (2.0 / HEAD_SIZE)
    )
    positions = (lengths[None, :] + jnp.arange(STEPS)[:, None]).astype(jnp.float32)
    angles = positions[..., None] * freqs
    cosine, sine = jnp.cos(angles), jnp.sin(angles)
    cosine = jnp.repeat(jnp.concatenate([cosine, cosine], axis=-1)[:, :, None], SAMPLES, axis=2)
    sine = jnp.repeat(jnp.concatenate([-sine, sine], axis=-1)[:, :, None], SAMPLES, axis=2)
    cosine = cosine.reshape(-1, HEAD_SIZE)
    sine = sine.reshape(-1, HEAD_SIZE)

    rows, gain, key_value_weight, w_query = staged(
        rows, norm_gain.reshape(devices, 1, width), key_value_weight, w_query
    )
    (w_output,) = staged(w_output)
    scale, kept, *parts = scale_and_pairs(place, rows, gain, key_value_weight, gathered)
    parts = [passed(part, "sub", s + 1) for s, part in enumerate(parts)]
    total, *parts = fold_sub(scalars(0), kept, parts)
    parts = [passed(part, "req", s + 1) for s, part in enumerate(parts)]
    mine = fold_pairs(total, parts)
    other = passed(mine, "section", 1)

    query = queries(place, scale, gain, w_query, cosine, sine, gathered)
    mixed = attend(
        place, lengths.astype(jnp.int32), query, mine, other, cosine, sine, caches
    )

    away = outputs(scalars(1 - core), mixed, w_output, devices // 2)
    arrived = passed(away, "section", 1)
    kept = outputs(scalars(core), mixed, w_output, devices // 2)
    kept, *parts = fold_core(scalars(sub), kept, arrived, subs)
    parts = [passed(part, "sub", s + 1) for s, part in enumerate(parts)]
    total, *parts = fold_sub(scalars(request), kept, parts)
    parts = [passed(part, "req", s + 1) for s, part in enumerate(parts)]
    return finish(rows, total, parts).reshape(hidden.shape)


def solution(mesh):
    groups, tp, section = mesh.devices.shape
    finer = Mesh(
        mesh.devices.reshape(groups, GROUP_REQUESTS, tp // GROUP_REQUESTS, section),
        ("groups",) + DEVICES,
    )
    placed = (
        P(None, "groups", DEVICES),
        P(),
        P(None, DEVICES),
        P(DEVICES, None),
        P(DEVICES, None),
        P(("groups",) + DEVICES, None, None),
        P(("groups",) + DEVICES, None),
        P("groups"),
        P("groups", None),
    )
    return jax.shard_map(
        shards,
        mesh=finer,
        in_specs=placed,
        out_specs=P(None, "groups", DEVICES),
        check_vma=False,
    )
```

time: 104 us -> 85.5 us (0.82)
  starting transfers between devices: 44.1 us -> 25.2 us
  waiting for transfers between devices: 16.3 us -> 27.4 us
  Pallas kernels: 18.7 us -> 11.8 us
  local copies, waits for them, and re-layouts: 21.5 us -> 19.4 us
    ppermute x11 -> x0, starting transfers between devices: 22.6 us -> none  [the longest x4 9.8 us: shards(): got.append(lax.ppermute(block, DEVICES, there))]
    ppermute x6 -> x24, starting transfers between devices: 9.62 us -> 25.2 us  [passed(): lax.ppermute(array, axis, [(i, (i + shift) % size) for i in range(size)])]
    ppermute x6 -> x24, waiting for transfers between devices: 14.2 us -> 27.4 us  [passed(): lax.ppermute(array, axis, [(i, (i + shift) % size) for i in range(size)])]
    all_to_all x2 -> x0, starting transfers between devices: 11.9 us -> none  [the longest x1 7.28 us: shards(): lax.all_to_all(jnp.broadcast_to(rows[None], (chips,) + rows.shape), CHIPS...]
    pallas_call x1 -> x2, Pallas kernels: 6.05 us -> 1.4 us  [staged(): pl.pallas_call(stage_kernel, in_specs=[pl.BlockSpec(memory_space=pltpu.HB...]
    pallas_call x1, Pallas kernels: 3.62 us -> 1.52 us  [used_pages(): pl.pallas_call(pages_kernel, grid_spec=pltpu.PrefetchScalarGridSpec(num_s...]
    ppermute x11 -> x0, waiting for transfers between devices: 2.09 us -> none  [the longest x4 1.36 us: shards(): got.append(lax.ppermute(mixed[s], DEVICES, back))]
    broadcast_in_dim x1 -> x0, local copies, waits for them, and re-layouts: 1.66 us -> none  [shards(): jnp.broadcast_to(rows[None], (chips,) + rows.shape)]
  transfers between devices with their start and end apart: 19 -> 24, of which waited for: 7 -> 12; matrix products, arithmetic and copies ran while one was open for 3% -> 1% of each run, Pallas kernels for 14% -> 9%
where the time goes in v4:
time: 85.5 us; the launch traced here: 85 us
  waiting for transfers between devices  27.4 us (32%)
  starting transfers between devices  25.2 us (29%)
  local copies, waits for them, and re-layouts  19.4 us (23%)
  Pallas kernels  11.8 us (14%)
  other arithmetic  1.05 us (1%)
    ppermute x24, waiting for transfers between devices, passed(): lax.ppermute(array, axis, [(i, (i + shift) % size) for i in range(size)])  27.4 us
    ppermute x24, starting transfers between devices, passed(): lax.ppermute(array, axis, [(i, (i + shift) % size) for i in range(size)])  25.2 us
    unnamed x22, local copies, waits for them, and re-layouts  19.3 us
    pallas_call x1, Pallas kernels, queries(): pl.pallas_call(query_kernel, in_specs=[pl.BlockSpec(memory_space=pltpu.SM...  2.26 us
    pallas_call x1, Pallas kernels, attend(): pl.pallas_call(attend_kernel, in_specs=[pl.BlockSpec(memory_space=pltpu.S...  2.18 us
  transfers between devices with their start and end apart: 24, of which 12 were waited for; matrix products, arithmetic and copies ran while one was open for 1% of the time, Pallas kernels for 9%

profile of v4, /device:TPU:0, one launch (start us, length us, event | category | flops | bytes accessed | tf_op | source)
XLA Modules:
  0.0 85.0 jit_solution(3048750532355224073)
XLA Ops:
  0.0 3.0 %collective-permute-start = (bf16[64,512]{1,0:T(8,128)(2,1)}, bf16[64,512]{1,0:T(8,128)(2,1)S(1)}, u32[]{:S(2)}, u32[]{:S(2)}) collective-permute-start(bf16[64,512]{1,0:T(8,128)(2,1)} %bitcast.15), channel_id=1, source_target_pairs={{0,4},{4,8},{8,12},{12,0},{1,5},{5,9},{9,13},{13,1},{2,6},{6,10},{... | collective-permute-start | bytes 196616 | tf_op jit(solution)/shard_map/ppermute | solution.py:494
  3.0 2.6 %collective-permute-start.1 = (bf16[64,512]{1,0:T(8,128)(2,1)}, bf16[64,512]{1,0:T(8,128)(2,1)S(1)}, u32[]{:S(2)}, u32[]{:S(2)}) collective-permute-start(bf16[64,512]{1,0:T(8,128)(2,1)} %bitcast.16), channel_id=1, source_target_pairs={{0,8},{4,12},{8,0},{12,4},{1,9},{5,13},{9,1},{13,5},{2,10},{6,14},... | collective-permute-start | bytes 196616 | tf_op jit(solution)/shard_map/ppermute | solution.py:494
  7.8 2.5 %collective-permute-done.1.refs_2_ = bf16[64,512]{1,0:T(8,128)(2,1)S(1)} collective-permute-done((bf16[64,512]{1,0:T(8,128)(2,1)}, bf16[64,512]{1,0:T(8,128)(2,1)S(1)}, u32[]{:S(2)}, u32[]{:S(2)}) %collective-permute-start.1) | collective-permute-done | bytes 65568 | tf_op jit(solution)/shard_map/ppermute | solution.py:494
  11.4 1.6 %collective-permute-start.3 = (bf16[4,64,512]{2,1,0:T(8,128)(2,1)S(1)}, bf16[4,64,512]{2,1,0:T(8,128)(2,1)S(1)}, u32[]{:S(2)}, u32[]{:S(2)}) collective-permute-start(bf16[4,64,512]{2,1,0:T(8,128)(2,1)S(1)} %pack.1.refs_0_), channel_id=1, source_target_pairs={{0,2},{2,0},{1,3},{3,1},{4,6},{6,4},{5,7},{7,5},{8,10},{10,8},{9,1... | collective-permute-start | bytes 786440 | tf_op jit(solution)/shard_map/ppermute | solution.py:494
  17.8 2.3 %collective-permute-done.3.refs_1_ = bf16[4,64,512]{2,1,0:T(8,128)(2,1)S(1)} collective-permute-done((bf16[4,64,512]{2,1,0:T(8,128)(2,1)S(1)}, bf16[4,64,512]{2,1,0:T(8,128)(2,1)S(1)}, u32[]{:S(2)}, u32[]{:S(2)}) %collective-permute-start.3) | collective-permute-done | bytes 262176 | tf_op jit(solution)/shard_map/ppermute | solution.py:494
  20.0 3.4 %copy-done = bf16[8192,512]{1,0:T(8,128)(2,1)S(1)} copy-done((bf16[8192,512]{1,0:T(8,128)(2,1)S(1)}, bf16[8192,512]{1,0:T(8,128)(2,1)}, u32[]{:S(2)}) %copy-start) | copy-done | bytes 8388632
  23.4 1.6 %copy-done.4 = bf16[512,2048]{1,0:T(8,128)(2,1)S(1)} copy-done((bf16[512,2048]{1,0:T(8,128)(2,1)S(1)}, bf16[512,2048]{1,0:T(8,128)(2,1)}, u32[]{:S(2)}) %copy-start.4) | copy-done | bytes 2097176
  27.5 3.3 %copy-done.1 = bf16[8192,512]{1,0:T(8,128)(2,1)} copy-done((bf16[8192,512]{1,0:T(8,128)(2,1)}, bf16[8192,512]{1,0:T(8,128)(2,1)S(1)}, u32[]{:S(2)}) %copy-start.1) | copy-done | bytes 8388632
  30.8 1.6 %collective-permute-start.12 = (bf16[2,128,256]{2,1,0:T(8,128)(2,1)S(1)}, bf16[2,128,256]{2,1,0:T(8,128)(2,1)S(1)}, u32[]{:S(2)}, u32[]{:S(2)}) collective-permute-start(bf16[2,128,256]{2,1,0:T(8,128)(2,1)S(1)} %get-tuple-element.42), channel_id=1, source_target_pairs={{0,4},{4,8},{8,12},{12,0},{1,5},{5,9},{9,13},{13,1},{2,6},{6,10},{... | collective-permute-start | bytes 393224 | tf_op jit(solution)/shard_map/ppermute | solution.py:494
  32.7 2.1 %collective-permute-start.14 = (bf16[2,128,256]{2,1,0:T(8,128)(2,1)S(1)}, bf16[2,128,256]{2,1,0:T(8,128)(2,1)S(1)}, u32[]{:S(2)}, u32[]{:S(2)}) collective-permute-start(bf16[2,128,256]{2,1,0:T(8,128)(2,1)S(1)} %get-tuple-element.44), channel_id=1, source_target_pairs={{0,12},{4,0},{8,4},{12,8},{1,13},{5,1},{9,5},{13,9},{2,14},{6,2},{... | collective-permute-start | bytes 393224 | tf_op jit(solution)/shard_map/ppermute | solution.py:494
  36.2 1.8 %collective-permute-start.6 = (s16[528,128]{1,0:T(8,128)(2,1)S(1)}, s16[528,128]{1,0:T(8,128)(2,1)S(1)}, u32[]{:S(2)}, u32[]{:S(2)}) collective-permute-start(s16[528,128]{1,0:T(8,128)(2,1)S(1)} %get-tuple-element.34), channel_id=1, source_target_pairs={{0,2},{2,0},{1,3},{3,1},{4,6},{6,4},{5,7},{7,5},{8,10},{10,8},{9,1... | collective-permute-start | bytes 405512 | tf_op jit(solution)/shard_map/ppermute | solution.py:494
  38.0 3.7 %collective-permute-done.6.refs_0_ = s16[528,128]{1,0:T(8,128)(2,1)S(1)} collective-permute-done((s16[528,128]{1,0:T(8,128)(2,1)S(1)}, s16[528,128]{1,0:T(8,128)(2,1)S(1)}, u32[]{:S(2)}, u32[]{:S(2)}) %collective-permute-start.6) | collective-permute-done | bytes 135200 | tf_op jit(solution)/shard_map/ppermute | solution.py:494
  42.4 1.8 %collective-permute-start.8 = (s16[144,128]{1,0:T(8,128)(2,1)S(1)}, s16[144,128]{1,0:T(8,128)(2,1)S(1)}, u32[]{:S(2)}, u32[]{:S(2)}) collective-permute-start(s16[144,128]{1,0:T(8,128)(2,1)S(1)} %get-tuple-element.37), channel_id=1, source_target_pairs={{0,8},{4,12},{8,0},{12,4},{1,9},{5,13},{9,1},{13,5},{2,10},{6,14},... | collective-permute-start | bytes 110600 | tf_op jit(solution)/shard_map/ppermute | solution.py:494
  44.8 2.9 %collective-permute-done.7.refs_0_ = s16[144,128]{1,0:T(8,128)(2,1)S(1)} collective-permute-done((s16[144,128]{1,0:T(8,128)(2,1)S(1)}, s16[144,128]{1,0:T(8,128)(2,1)S(1)}, u32[]{:S(2)}, u32[]{:S(2)}) %collective-permute-start.7) | collective-permute-done | bytes 36896 | tf_op jit(solution)/shard_map/ppermute | solution.py:494
  47.8 1.7 %collective-permute-done.8.refs_1_ = s16[144,128]{1,0:T(8,128)(2,1)S(1)} collective-permute-done((s16[144,128]{1,0:T(8,128)(2,1)S(1)}, s16[144,128]{1,0:T(8,128)(2,1)S(1)}, u32[]{:S(2)}, u32[]{:S(2)}) %collective-permute-start.8) | collective-permute-done | bytes 36896 | tf_op jit(solution)/shard_map/ppermute | solution.py:494
  50.7 3.4 %copy-done.3 = bf16[512,8192]{1,0:T(8,128)(2,1)S(1)} copy-done((bf16[512,8192]{1,0:T(8,128)(2,1)S(1)}, bf16[512,8192]{1,0:T(8,128)(2,1)}, u32[]{:S(2)}) %copy-start.3) | copy-done | bytes 8388632
  54.9 3.4 %copy-done.2 = bf16[8192,512]{1,0:T(8,128)(2,1)S(1)} copy-done((bf16[8192,512]{1,0:T(8,128)(2,1)S(1)}, bf16[8192,512]{1,0:T(8,128)(2,1)}, u32[]{:S(2)}) %copy-start.2) | copy-done | bytes 8388632
  58.3 2.3 %queries.1.q_ref = bf16[4,16,512]{2,1,0:T(8,128)(2,1)S(1)} custom-call(s32[3]{0:T(128)S(1)} %pad_add_fusion.place, f32[64,128]{1,0:T(8,128)S(1)} %get-tuple-element.31.scale_ref, f32[16,1,512]{2,1,0:T(1,128)S(1)} %get-tuple-element.29.gain_ref, bf16[8192,512]{1,0:T(8,128)(2,1)S(1)} %copy-done.2, f32[64,128]{1,0:T(8,128)S(1)} %bitcast.11, ...), custom_call_target="tpu_custom_call" | custom-call | tf_op jit(solution)/shard_map/queries/pallas_call | solution.py:237
  60.6 2.2 %attend.1.x_ref = bf16[4,16,512]{2,1,0:T(8,128)(2,1)S(1)} custom-call(s32[3]{0:T(128)S(1)} %pad_add_fusion.place, s32[4]{0:T(128)S(1)} %copy-done.10, bf16[4,16,512]{2,1,0:T(8,128)(2,1)S(1)} %queries.1.q_ref, f32[64,256]{1,0:T(8,128)S(1)} %fold_pairs.1.mine_ref, f32[64,256]{1,0:T(8,128)S(1)} %collective-permute-done.10.other_ref, f32[64,128]{1,0:T(8,128)S(1)} %bitcast.12, ...), custom_call_target="tpu_custom_call" | custom-call | tf_op jit(solution)/shard_map/attend/pallas_call | solution.py:312
  66.7 1.8 %collective-permute-start.20 = (s16[1040,128]{1,0:T(8,128)(2,1)S(1)}, s16[1040,128]{1,0:T(8,128)(2,1)S(1)}, u32[]{:S(2)}, u32[]{:S(2)}) collective-permute-start(s16[1040,128]{1,0:T(8,128)(2,1)S(1)} %get-tuple-element.46), channel_id=1, source_target_pairs={{0,2},{2,0},{1,3},{3,1},{4,6},{6,4},{5,7},{7,5},{8,10},{10,8},{9,1... | collective-permute-start | bytes 798728 | tf_op jit(solution)/shard_map/ppermute | solution.py:494
  68.5 6.9 %collective-permute-done.20.refs_0_ = s16[1040,128]{1,0:T(8,128)(2,1)S(1)} collective-permute-done((s16[1040,128]{1,0:T(8,128)(2,1)S(1)}, s16[1040,128]{1,0:T(8,128)(2,1)S(1)}, u32[]{:S(2)}, u32[]{:S(2)}) %collective-permute-start.20) | collective-permute-done | bytes 266272 | tf_op jit(solution)/shard_map/ppermute | solution.py:494
  78.0 1.6 %collective-permute-start.23 = (s16[272,128]{1,0:T(8,128)(2,1)S(1)}, s16[272,128]{1,0:T(8,128)(2,1)S(1)}, u32[]{:S(2)}, u32[]{:S(2)}) collective-permute-start(s16[272,128]{1,0:T(8,128)(2,1)S(1)} %get-tuple-element.50), channel_id=1, source_target_pairs={{0,12},{4,0},{8,4},{12,8},{1,13},{5,1},{9,5},{13,9},{2,14},{6,2},{... | collective-permute-start | bytes 208904 | tf_op jit(solution)/shard_map/ppermute | solution.py:494
  79.6 3.2 %collective-permute-done.21.refs_0_ = s16[272,128]{1,0:T(8,128)(2,1)S(1)} collective-permute-done((s16[272,128]{1,0:T(8,128)(2,1)S(1)}, s16[272,128]{1,0:T(8,128)(2,1)S(1)}, u32[]{:S(2)}, u32[]{:S(2)}) %collective-permute-start.21) | collective-permute-done | bytes 69664 | tf_op jit(solution)/shard_map/ppermute | solution.py:494
  82.7 1.6 %collective-permute-done.22.refs_1_ = s16[272,128]{1,0:T(8,128)(2,1)S(1)} collective-permute-done((s16[272,128]{1,0:T(8,128)(2,1)S(1)}, s16[272,128]{1,0:T(8,128)(2,1)S(1)}, u32[]{:S(2)}, u32[]{:S(2)}) %collective-permute-start.22) | collective-permute-done | bytes 69664 | tf_op jit(solution)/shard_map/ppermute | solution.py:494
  (70 shorter events, 22.7 us)
Async XLA Ops:
  0.0 7.8 %collective-permute-start = (bf16[64,512]{1,0:T(8,128)(2,1)}, bf16[64,512]{1,0:T(8,128)(2,1)S(1)}, u32[]{:S(2)}, u32[]{:S(2)}) collective-permute-start(bf16[64,512]{1,0:T(8,128)(2,1)} %bitcast.15), channel_id=1, source_target_pairs={{0,4},{4,8},{8,12},{12,0},{1,5},{5,9},{9,13},{13,1},{2,6},{6,10},{... | collective-permute-start | bytes 196616 | tf_op jit(solution)/shard_map/ppermute | solution.py:494
  3.0 7.3 %collective-permute-start.1 = (bf16[64,512]{1,0:T(8,128)(2,1)}, bf16[64,512]{1,0:T(8,128)(2,1)S(1)}, u32[]{:S(2)}, u32[]{:S(2)}) collective-permute-start(bf16[64,512]{1,0:T(8,128)(2,1)} %bitcast.16), channel_id=1, source_target_pairs={{0,8},{4,12},{8,0},{12,4},{1,9},{5,13},{9,1},{13,5},{2,10},{6,14},... | collective-permute-start | bytes 196616 | tf_op jit(solution)/shard_map/ppermute | solution.py:494
  5.6 4.9 %collective-permute-start.2 = (bf16[64,512]{1,0:T(8,128)(2,1)}, bf16[64,512]{1,0:T(8,128)(2,1)S(1)}, u32[]{:S(2)}, u32[]{:S(2)}) collective-permute-start(bf16[64,512]{1,0:T(8,128)(2,1)} %bitcast.17), channel_id=1, source_target_pairs={{0,12},{4,0},{8,4},{12,8},{1,13},{5,1},{9,5},{13,9},{2,14},{6,2},{... | collective-permute-start | bytes 196616 | tf_op jit(solution)/shard_map/ppermute | solution.py:494
  11.4 8.6 %collective-permute-start.3 = (bf16[4,64,512]{2,1,0:T(8,128)(2,1)S(1)}, bf16[4,64,512]{2,1,0:T(8,128)(2,1)S(1)}, u32[]{:S(2)}, u32[]{:S(2)}) collective-permute-start(bf16[4,64,512]{2,1,0:T(8,128)(2,1)S(1)} %pack.1.refs_0_), channel_id=1, source_target_pairs={{0,2},{2,0},{1,3},{3,1},{4,6},{6,4},{5,7},{7,5},{8,10},{10,8},{9,1... | collective-permute-start | bytes 786440 | tf_op jit(solution)/shard_map/ppermute | solution.py:494
  17.2 13.6 %collective-permute-start.11 = (bf16[4,128,256]{2,1,0:T(8,128)(2,1)S(1)}, bf16[4,128,256]{2,1,0:T(8,128)(2,1)S(1)}, u32[]{:S(2)}, u32[]{:S(2)}) collective-permute-start(bf16[4,128,256]{2,1,0:T(8,128)(2,1)S(1)} %get-tuple-element.40), channel_id=1, source_target_pairs={{0,2},{2,0},{1,3},{3,1},{4,6},{6,4},{5,7},{7,5},{8,10},{10,8},{9,1... | collective-permute-start | bytes 786440 | tf_op jit(solution)/shard_map/ppermute | solution.py:494
  17.8 17.1 %collective-permute-start.4 = (bf16[4,64,512]{2,1,0:T(8,128)(2,1)S(1)}, bf16[4,64,512]{2,1,0:T(8,128)(2,1)S(1)}, u32[]{:S(2)}, u32[]{:S(2)}) collective-permute-start(bf16[4,64,512]{2,1,0:T(8,128)(2,1)S(1)} %pack.1.refs_0_), channel_id=1, source_target_pairs={{0,1},{1,0},{2,3},{3,2},{4,5},{5,4},{6,7},{7,6},{8,9},{9,8},{10,11... | collective-permute-start | bytes 786440 | tf_op jit(solution)/shard_map/ppermute | solution.py:494
  20.0 14.8 %collective-permute-start.5 = (bf16[4,64,512]{2,1,0:T(8,128)(2,1)S(1)}, bf16[4,64,512]{2,1,0:T(8,128)(2,1)S(1)}, u32[]{:S(2)}, u32[]{:S(2)}) collective-permute-start(bf16[4,64,512]{2,1,0:T(8,128)(2,1)S(1)} %collective-permute-done.3.refs_1_), channel_id=1, source_target_pairs={{0,1},{1,0},{2,3},{3,2},{4,5},{5,4},{6,7},{7,6},{8,9},{9,8},{10,11... | collective-permute-start | bytes 786440 | tf_op jit(solution)/shard_map/ppermute | solution.py:494
  30.8 13.3 %collective-permute-start.12 = (bf16[2,128,256]{2,1,0:T(8,128)(2,1)S(1)}, bf16[2,128,256]{2,1,0:T(8,128)(2,1)S(1)}, u32[]{:S(2)}, u32[]{:S(2)}) collective-permute-start(bf16[2,128,256]{2,1,0:T(8,128)(2,1)S(1)} %get-tuple-element.42), channel_id=1, source_target_pairs={{0,4},{4,8},{8,12},{12,0},{1,5},{5,9},{9,13},{13,1},{2,6},{6,10},{... | collective-permute-start | bytes 393224 | tf_op jit(solution)/shard_map/ppermute | solution.py:494
  32.4 11.9 %collective-permute-start.13 = (bf16[2,128,256]{2,1,0:T(8,128)(2,1)S(1)}, bf16[2,128,256]{2,1,0:T(8,128)(2,1)S(1)}, u32[]{:S(2)}, u32[]{:S(2)}) collective-permute-start(bf16[2,128,256]{2,1,0:T(8,128)(2,1)S(1)} %get-tuple-element.43), channel_id=1, source_target_pairs={{0,8},{4,12},{8,0},{12,4},{1,9},{5,13},{9,1},{13,5},{2,10},{6,14},... | collective-permute-start | bytes 393224 | tf_op jit(solution)/shard_map/ppermute | solution.py:494
  32.7 12.0 %collective-permute-start.14 = (bf16[2,128,256]{2,1,0:T(8,128)(2,1)S(1)}, bf16[2,128,256]{2,1,0:T(8,128)(2,1)S(1)}, u32[]{:S(2)}, u32[]{:S(2)}) collective-permute-start(bf16[2,128,256]{2,1,0:T(8,128)(2,1)S(1)} %get-tuple-element.44), channel_id=1, source_target_pairs={{0,12},{4,0},{8,4},{12,8},{1,13},{5,1},{9,5},{13,9},{2,14},{6,2},{... | collective-permute-start | bytes 393224 | tf_op jit(solution)/shard_map/ppermute | solution.py:494
  36.2 5.5 %collective-permute-start.6 = (s16[528,128]{1,0:T(8,128)(2,1)S(1)}, s16[528,128]{1,0:T(8,128)(2,1)S(1)}, u32[]{:S(2)}, u32[]{:S(2)}) collective-permute-start(s16[528,128]{1,0:T(8,128)(2,1)S(1)} %get-tuple-element.34), channel_id=1, source_target_pairs={{0,2},{2,0},{1,3},{3,1},{4,6},{6,4},{5,7},{7,5},{8,10},{10,8},{9,1... | collective-permute-start | bytes 405512 | tf_op jit(solution)/shard_map/ppermute | solution.py:494
  41.9 5.9 %collective-permute-start.7 = (s16[144,128]{1,0:T(8,128)(2,1)S(1)}, s16[144,128]{1,0:T(8,128)(2,1)S(1)}, u32[]{:S(2)}, u32[]{:S(2)}) collective-permute-start(s16[144,128]{1,0:T(8,128)(2,1)S(1)} %get-tuple-element.36), channel_id=1, source_target_pairs={{0,4},{4,8},{8,12},{12,0},{1,5},{5,9},{9,13},{13,1},{2,6},{6,10},{... | collective-permute-start | bytes 110600 | tf_op jit(solution)/shard_map/ppermute | solution.py:494
  42.4 7.1 %collective-permute-start.8 = (s16[144,128]{1,0:T(8,128)(2,1)S(1)}, s16[144,128]{1,0:T(8,128)(2,1)S(1)}, u32[]{:S(2)}, u32[]{:S(2)}) collective-permute-start(s16[144,128]{1,0:T(8,128)(2,1)S(1)} %get-tuple-element.37), channel_id=1, source_target_pairs={{0,8},{4,12},{8,0},{12,4},{1,9},{5,13},{9,1},{13,5},{2,10},{6,14},... | collective-permute-start | bytes 110600 | tf_op jit(solution)/shard_map/ppermute | solution.py:494
  44.2 16.4 %collective-permute-start.15 = (bf16[2,128,256]{2,1,0:T(8,128)(2,1)S(1)}, bf16[2,128,256]{2,1,0:T(8,128)(2,1)S(1)}, u32[]{:S(2)}, u32[]{:S(2)}) collective-permute-start(bf16[2,128,256]{2,1,0:T(8,128)(2,1)S(1)} %get-tuple-element.41.refs_0_), channel_id=1, source_target_pairs={{0,1},{1,0},{2,3},{3,2},{4,5},{5,4},{6,7},{7,6},{8,9},{9,8},{10,11... | collective-permute-start | bytes 393224 | tf_op jit(solution)/shard_map/ppermute | solution.py:494
  44.3 16.2 %collective-permute-start.16 = (bf16[2,128,256]{2,1,0:T(8,128)(2,1)S(1)}, bf16[2,128,256]{2,1,0:T(8,128)(2,1)S(1)}, u32[]{:S(2)}, u32[]{:S(2)}) collective-permute-start(bf16[2,128,256]{2,1,0:T(8,128)(2,1)S(1)} %collective-permute-done.12.refs_1_), channel_id=1, source_target_pairs={{0,1},{1,0},{2,3},{3,2},{4,5},{5,4},{6,7},{7,6},{8,9},{9,8},{10,11... | collective-permute-start | bytes 393224 | tf_op jit(solution)/shard_map/ppermute | solution.py:494
  44.7 15.8 %collective-permute-start.17 = (bf16[2,128,256]{2,1,0:T(8,128)(2,1)S(1)}, bf16[2,128,256]{2,1,0:T(8,128)(2,1)S(1)}, u32[]{:S(2)}, u32[]{:S(2)}) collective-permute-start(bf16[2,128,256]{2,1,0:T(8,128)(2,1)S(1)} %collective-permute-done.13.refs_2_), channel_id=1, source_target_pairs={{0,1},{1,0},{2,3},{3,2},{4,5},{5,4},{6,7},{7,6},{8,9},{9,8},{10,11... | collective-permute-start | bytes 393224 | tf_op jit(solution)/shard_map/ppermute | solution.py:494
  47.8 12.8 %collective-permute-start.18 = (bf16[2,128,256]{2,1,0:T(8,128)(2,1)S(1)}, bf16[2,128,256]{2,1,0:T(8,128)(2,1)S(1)}, u32[]{:S(2)}, u32[]{:S(2)}) collective-permute-start(bf16[2,128,256]{2,1,0:T(8,128)(2,1)S(1)} %collective-permute-done.14.refs_3_), channel_id=1, source_target_pairs={{0,1},{1,0},{2,3},{3,2},{4,5},{5,4},{6,7},{7,6},{8,9},{9,8},{10,11... | collective-permute-start | bytes 393224 | tf_op jit(solution)/shard_map/ppermute | solution.py:494
  49.4 5.2 %collective-permute-start.9 = (s16[144,128]{1,0:T(8,128)(2,1)S(1)}, s16[144,128]{1,0:T(8,128)(2,1)S(1)}, u32[]{:S(2)}, u32[]{:S(2)}) collective-permute-start(s16[144,128]{1,0:T(8,128)(2,1)S(1)} %get-tuple-element.38), channel_id=1, source_target_pairs={{0,12},{4,0},{8,4},{12,8},{1,13},{5,1},{9,5},{13,9},{2,14},{6,2},{... | collective-permute-start | bytes 110600 | tf_op jit(solution)/shard_map/ppermute | solution.py:494
  54.7 5.9 %collective-permute-start.10 = (f32[64,256]{1,0:T(8,128)S(1)}, f32[64,256]{1,0:T(8,128)S(1)}, u32[]{:S(2)}, u32[]{:S(2)}) collective-permute-start(f32[64,256]{1,0:T(8,128)S(1)} %fold_pairs.1.mine_ref), channel_id=1, source_target_pairs={{0,1},{1,0},{2,3},{3,2},{4,5},{5,4},{6,7},{7,6},{8,9},{9,8},{10,11... | collective-permute-start | bytes 196616 | tf_op jit(solution)/shard_map/ppermute | solution.py:494
  63.6 2.8 %collective-permute-start.19 = (f32[8,64,512]{2,1,0:T(8,128)S(1)}, f32[8,64,512]{2,1,0:T(8,128)S(1)}, u32[]{:S(2)}, u32[]{:S(2)}) collective-permute-start(f32[8,64,512]{2,1,0:T(8,128)S(1)} %outputs.3), channel_id=1, source_target_pairs={{0,1},{1,0},{2,3},{3,2},{4,5},{5,4},{6,7},{7,6},{8,9},{9,8},{10,11... | collective-permute-start | bytes 3145736 | tf_op jit(solution)/shard_map/ppermute | solution.py:494
  66.7 8.7 %collective-permute-start.20 = (s16[1040,128]{1,0:T(8,128)(2,1)S(1)}, s16[1040,128]{1,0:T(8,128)(2,1)S(1)}, u32[]{:S(2)}, u32[]{:S(2)}) collective-permute-start(s16[1040,128]{1,0:T(8,128)(2,1)S(1)} %get-tuple-element.46), channel_id=1, source_target_pairs={{0,2},{2,0},{1,3},{3,1},{4,6},{6,4},{5,7},{7,5},{8,10},{10,8},{9,1... | collective-permute-start | bytes 798728 | tf_op jit(solution)/shard_map/ppermute | solution.py:494
  75.7 7.1 %collective-permute-start.21 = (s16[272,128]{1,0:T(8,128)(2,1)S(1)}, s16[272,128]{1,0:T(8,128)(2,1)S(1)}, u32[]{:S(2)}, u32[]{:S(2)}) collective-permute-start(s16[272,128]{1,0:T(8,128)(2,1)S(1)} %get-tuple-element.48), channel_id=1, source_target_pairs={{0,4},{4,8},{8,12},{12,0},{1,5},{5,9},{9,13},{13,1},{2,6},{6,10},{... | collective-permute-start | bytes 208904 | tf_op jit(solution)/shard_map/ppermute | solution.py:494
  76.6 7.7 %collective-permute-start.22 = (s16[272,128]{1,0:T(8,128)(2,1)S(1)}, s16[272,128]{1,0:T(8,128)(2,1)S(1)}, u32[]{:S(2)}, u32[]{:S(2)}) collective-permute-start(s16[272,128]{1,0:T(8,128)(2,1)S(1)} %get-tuple-element.49), channel_id=1, source_target_pairs={{0,8},{4,12},{8,0},{12,4},{1,9},{5,13},{9,1},{13,5},{2,10},{6,14},... | collective-permute-start | bytes 208904 | tf_op jit(solution)/shard_map/ppermute | solution.py:494
  78.0 6.4 %collective-permute-start.23 = (s16[272,128]{1,0:T(8,128)(2,1)S(1)}, s16[272,128]{1,0:T(8,128)(2,1)S(1)}, u32[]{:S(2)}, u32[]{:S(2)}) collective-permute-start(s16[272,128]{1,0:T(8,128)(2,1)S(1)} %get-tuple-element.50), channel_id=1, source_target_pairs={{0,12},{4,0},{8,4},{12,8},{1,13},{5,1},{9,5},{13,9},{2,14},{6,2},{... | collective-permute-start | bytes 208904 | tf_op jit(solution)/shard_map/ppermute | solution.py:494
  (11 other events, 57.4 us)

commit v5 on v4

--- a/solution.py
+++ b/solution.py
@@ -1,3 +1,5 @@
+import functools
+
 import jax
 import jax.numpy as jnp
 from jax import lax
@@ -16,49 +18,54 @@
 ROWS = STEPS * SAMPLES
 PAIR = 2 * HEAD_SIZE
 LANES = 128
+HALVES = ((0, 3), (1, 2))
 TAIL = 16
 DEVICES = ("req", "sub", "section")
 
 theta_base = 500000.0
 eps_norm = 1e-05
 VMEM = 16 * 2**20
+LARGE_VMEM = 51 * 2**20
 
 
 def params(**more):
     return pltpu.CompilerParams(vmem_limit_bytes=VMEM, **more)
 
 
-def whole_spec(shape):
-    return pl.BlockSpec(shape, lambda *_: (0,) * len(shape))
+def cost(*groups, flops=0):
+    size = sum(array.size * array.dtype.itemsize for arrays in groups for array in arrays)
+    return pl.CostEstimate(flops=flops, bytes_accessed=size, transcendentals=0)
+
+
+def unread(arrays):
+    return [pl.BlockSpec(memory_space=pl.ANY)] * len(arrays)
 
 
 def turn(vectors, cosine, sine):
     return vectors * cosine + pltpu.roll(vectors, HEAD_SIZE // 2, vectors.ndim - 1) * sine
 
 
-def stage_kernel(*refs):
-    half = (len(refs) - 1) // 2
-    copies = [
-        pltpu.make_async_copy(refs[i], refs[half + i], refs[-1].at[i]) for i in range(half)
-    ]
+def stage_kernel(count, *refs):
+    ins, outs, sems = refs[:count], refs[-1 - count : -1], refs[-1]
+    copies = [pltpu.make_async_copy(ins[i], outs[i], sems.at[i]) for i in range(count)]
     for copy in copies:
         copy.start()
     for copy in copies:
         copy.wait()
 
 
-def staged(*arrays):
-    size = sum(array.size * array.dtype.itemsize for array in arrays)
-    return pl.pallas_call(
-        stage_kernel,
-        in_specs=[pl.BlockSpec(memory_space=pltpu.HBM)] * len(arrays),
-        out_specs=[pl.BlockSpec(memory_space=pltpu.VMEM)] * len(arrays),
+def staged(arrays, after=()):
+    count = len(arrays)
+    return pl.pallas_call(
+        functools.partial(stage_kernel, count),
+        in_specs=[pl.BlockSpec(memory_space=pltpu.HBM)] * count + unread(after),
+        out_specs=[pl.BlockSpec(memory_space=pltpu.VMEM)] * count,
         out_shape=[jax.ShapeDtypeStruct(array.shape, array.dtype) for array in arrays],
-        scratch_shapes=[pltpu.SemaphoreType.DMA((len(arrays),))],
-        compiler_params=pltpu.CompilerParams(vmem_limit_bytes=30 * 2**20),
-        cost_estimate=pl.CostEstimate(flops=0, bytes_accessed=2 * size, transcendentals=0),
+        scratch_shapes=[pltpu.SemaphoreType.DMA((count,))],
+        compiler_params=params(),
+        cost_estimate=cost(arrays, arrays),
         name="staged",
-    )(*arrays)
+    )(*arrays, *after)
 
 
 def pages_kernel(table, place, scales, page_ref, *out_refs):
@@ -107,6 +114,9 @@
         ]
         * subs,
         compiler_params=params(),
+        cost_estimate=pl.CostEstimate(
+            flops=0, bytes_accessed=4 * entries * PAGE_TOKENS * pages.shape[2], transcendentals=0
+        ),
         name="used_pages",
     )(table, place, scales.astype(jnp.float32), pages)
 
@@ -126,6 +136,7 @@
         out_specs=[pl.BlockSpec(memory_space=pltpu.VMEM)] * GROUP_REQUESTS,
         out_shape=[shape] * GROUP_REQUESTS,
         compiler_params=params(),
+        cost_estimate=cost(parts, parts),
         name="regroup",
     )(*parts)
 
@@ -142,6 +153,7 @@
         out_specs=pl.BlockSpec(memory_space=pltpu.VMEM),
         out_shape=jax.ShapeDtypeStruct((len(parts),) + parts[0].shape, parts[0].dtype),
         compiler_params=params(),
+        cost_estimate=cost(parts, parts),
         name="pack",
     )(*parts)
 
@@ -157,7 +169,7 @@
             yield ref, z, (from_request * subs + from_sub) * 2 + from_core
 
 
-def pairs_kernel(place, rows_ref, gain_ref, weight_ref, *refs):
+def pairs_kernel(place, gain_ref, weight_ref, *refs):
     subs = (len(refs) - 1) // 3
     x_refs, scale_ref, kept_ref, out_refs = (
         refs[: 2 * subs],
@@ -166,7 +178,7 @@
         refs[2 * subs + 2 :],
     )
     request, sub, core = place[0], place[1], place[2]
-    rows, width = rows_ref.shape
+    _, rows, width = x_refs[0].shape
     total = jnp.zeros((rows, LANES), jnp.float32)
     for ref in x_refs:
         for z in range(GROUP_REQUESTS):
@@ -176,7 +188,7 @@
     scale = lax.rsqrt(mean + eps_norm)
     scale_ref[...] = jnp.broadcast_to(scale, scale_ref.shape)
     device = (request * subs + sub) * 2 + core
-    x = rows_ref[...].astype(jnp.float32)
+    x = x_refs[0][0].astype(jnp.float32)
     mine = (x * scale * gain_ref[device]).astype(jnp.bfloat16)
     for shift in range(subs):
         half = lax.rem(sub + shift, subs) // (subs // 2)
@@ -192,9 +204,9 @@
             encode(out_refs[shift - 1], pieces)
 
 
-def scale_and_pairs(place, rows, gain, weight, gathered):
+def scale_and_pairs(place, gain, weight, gathered):
     subs = len(gathered) // 2
-    count = rows.shape[0]
+    count = gathered[0].shape[1]
     sent = jax.ShapeDtypeStruct((2 * GROUP_REQUESTS * count + TAIL, LANES), jnp.int16)
     shapes = [
         jax.ShapeDtypeStruct((count, LANES), jnp.float32),
@@ -203,25 +215,33 @@
     return pl.pallas_call(
         pairs_kernel,
         in_specs=[pl.BlockSpec(memory_space=pltpu.SMEM)]
-        + [pl.BlockSpec(memory_space=pltpu.VMEM)] * (3 + len(gathered)),
+        + [pl.BlockSpec(memory_space=pltpu.VMEM)] * (2 + len(gathered)),
         out_specs=[pl.BlockSpec(memory_space=pltpu.VMEM)] * len(shapes),
         out_shape=shapes,
         compiler_params=params(),
+        cost_estimate=cost(gathered, [weight], flops=2 * count * weight.size),
         name="scale_and_pairs",
-    )(place, rows, gain, weight, *gathered)
+    )(place, gain, weight, *gathered)
 
 
 def query_kernel(place, scale_ref, gain_ref, weight_ref, cos_ref, sin_ref, *refs):
-    out_ref = refs[-1]
-    _, rows, width = refs[0].shape
+    x_refs, out_ref, held, sems = refs[:-3], refs[-3], refs[-2], refs[-1]
+    _, rows, width = x_refs[0].shape
     columns = weight_ref.shape[1]
+    blocks = list(blocks_of(place, x_refs))
+    copies = []
+    for i, (_, _, block) in enumerate(blocks):
+        depth = pl.ds(pl.multiple_of(block * width, width), width)
+        copies.append(pltpu.make_async_copy(weight_ref.at[depth], held.at[i], sems.at[i]))
+    for copy in copies:
+        copy.start()
     scale = scale_ref[:, :1]
     total = jnp.zeros((rows, columns), jnp.float32)
-    for ref, z, block in blocks_of(place, refs[:-1]):
+    for i, (ref, z, block) in enumerate(blocks):
         x = ref[z].astype(jnp.float32)
         x = (x * scale * gain_ref[block]).astype(jnp.bfloat16)
-        depth = pl.ds(pl.multiple_of(block * width, width), width)
-        total += jnp.dot(x, weight_ref[depth, :], preferred_element_type=jnp.float32)
+        copies[i].wait()
+        total += jnp.dot(x, held[i], preferred_element_type=jnp.float32)
     for head in range(columns // HEAD_SIZE):
         part = slice(head * HEAD_SIZE, (head + 1) * HEAD_SIZE)
         turned = turn(total[:, part], cos_ref[...], sin_ref[...])
@@ -234,13 +254,22 @@
 
 def queries(place, scale, gain, weight, cosine, sine, gathered):
     columns = weight.shape[1]
+    _, rows, width = gathered[0].shape
+    blocks = weight.shape[0] // width
     return pl.pallas_call(
         query_kernel,
         in_specs=[pl.BlockSpec(memory_space=pltpu.SMEM)]
-        + [pl.BlockSpec(memory_space=pltpu.VMEM)] * (5 + len(gathered)),
+        + [pl.BlockSpec(memory_space=pltpu.VMEM)] * 2
+        + [pl.BlockSpec(memory_space=pltpu.HBM)]
+        + [pl.BlockSpec(memory_space=pltpu.VMEM)] * (2 + len(gathered)),
         out_specs=pl.BlockSpec(memory_space=pltpu.VMEM),
         out_shape=jax.ShapeDtypeStruct((GROUP_REQUESTS, ROWS, columns), jnp.bfloat16),
-        compiler_params=params(),
+        scratch_shapes=[
+            pltpu.VMEM((blocks, width, columns), jnp.bfloat16),
+            pltpu.SemaphoreType.DMA((blocks,)),
+        ],
+        compiler_params=pltpu.CompilerParams(vmem_limit_bytes=LARGE_VMEM),
+        cost_estimate=cost([weight], flops=2 * rows * weight.size),
         name="queries",
     )(place, scale, gain, weight, cosine, sine, *gathered)
 
@@ -317,6 +346,7 @@
         out_shape=jax.ShapeDtypeStruct(query.shape, jnp.bfloat16),
         scratch_shapes=[pltpu.VMEM(cosine.shape, jnp.float32)] * 2,
         compiler_params=params(),
+        cost_estimate=cost(caches, caches, caches, flops=2**28),
         name="attend",
     )(place, lengths, query, mine, other, cosine, sine, *caches)
 
@@ -344,6 +374,7 @@
         out_specs=pl.BlockSpec(memory_space=pltpu.VMEM),
         out_shape=jax.ShapeDtypeStruct((blocks, rows, width), jnp.float32),
         compiler_params=params(),
+        cost_estimate=cost([weight], flops=rows * weight.size),
         name="outputs",
     )(place, mixed, weight)
 
@@ -378,74 +409,94 @@
 
 
 def fold_core_kernel(place, mine_ref, got_ref, kept_ref, *out_refs):
-    subs = 1 + len(out_refs)
+    subs = 1 + len(out_refs) // 2
     for shift in range(subs):
-        sub = lax.rem(place[0] + shift, subs)
-        pieces = []
-        for i in range(GROUP_REQUESTS):
-            block = mine_ref[i * subs + sub] + got_ref[i * subs + sub]
-            if shift == 0:
-                kept_ref[i] = block
-            pieces += pieces_of(block)
-        if shift:
-            encode(out_refs[shift - 1], pieces)
+        sub = lax.rem(place[1] + shift, subs)
+        for half in range(2):
+            pieces = []
+            for z in HALVES[half]:
+                block = lax.rem(place[0] + z, GROUP_REQUESTS) * subs + sub
+                block = mine_ref[block] + got_ref[block]
+                if shift == 0:
+                    kept_ref[z] = block
+                pieces += pieces_of(block)
+            if shift:
+                encode(out_refs[(shift - 1) * 2 + half], pieces)
 
 
 def fold_core(place, mine, got, subs):
     _, rows, width = mine.shape
     kept = jax.ShapeDtypeStruct((GROUP_REQUESTS, rows, width), jnp.float32)
-    sent = jax.ShapeDtypeStruct(
-        (GROUP_REQUESTS * width // LANES * rows + TAIL, LANES), jnp.int16
-    )
+    sent = jax.ShapeDtypeStruct((2 * width // LANES * rows + TAIL, LANES), jnp.int16)
     return pl.pallas_call(
         fold_core_kernel,
         in_specs=[pl.BlockSpec(memory_space=pltpu.SMEM)]
         + [pl.BlockSpec(memory_space=pltpu.VMEM)] * 2,
-        out_specs=[pl.BlockSpec(memory_space=pltpu.VMEM)] * subs,
-        out_shape=[kept] + [sent] * (subs - 1),
-        compiler_params=params(),
+        out_specs=[pl.BlockSpec(memory_space=pltpu.VMEM)] * (2 * subs - 1),
+        out_shape=[kept] + [sent] * (2 * subs - 2),
+        compiler_params=params(),
+        cost_estimate=cost([mine, got]),
         name="fold_core",
     )(place, mine, got)
 
 
-def fold_sub_kernel(place, kept_ref, *refs):
-    in_refs, total_ref, out_refs = (
-        refs[:-GROUP_REQUESTS],
-        refs[-GROUP_REQUESTS],
-        refs[1 - GROUP_REQUESTS :],
-    )
+def fold_sub_kernel(order, count, kept_ref, *refs):
+    in_refs, out_refs = refs[:count], refs[-len(order) :]
     _, rows, width = kept_ref.shape
     steps = [step_of(ref) for ref in in_refs]
-    for shift in range(GROUP_REQUESTS):
-        block = lax.rem(place[0] + shift, GROUP_REQUESTS)
-        pieces = pieces_of(kept_ref[block])
+    for i, (z, out_ref) in enumerate(zip(order, out_refs)):
+        pieces = pieces_of(kept_ref[z])
         for c in range(len(pieces)):
-            first = pl.multiple_of((block * len(pieces) + c) * rows, rows)
             for ref, step in zip(in_refs, steps):
+                first = (i * len(pieces) + c) * rows
                 pieces[c] = pieces[c] + decoded(ref, first, rows, step)
-        if shift:
-            encode(out_refs[shift - 1], pieces)
+        if z:
+            encode(out_ref, pieces)
         else:
             for c, piece in enumerate(pieces):
-                total_ref[:, c * LANES : (c + 1) * LANES] = piece
-
-
-def fold_sub(place, kept, parts):
+                out_ref[:, c * LANES : (c + 1) * LANES] = piece
+
+
+def fold_sub(order, kept, parts, after=()):
     _, rows, width = kept.shape
     total = jax.ShapeDtypeStruct((rows, width), jnp.float32)
     sent = jax.ShapeDtypeStruct((width // LANES * rows + TAIL, LANES), jnp.int16)
     return pl.pallas_call(
-        fold_sub_kernel,
-        in_specs=[pl.BlockSpec(memory_space=pltpu.SMEM)]
-        + [pl.BlockSpec(memory_space=pltpu.VMEM)] * (1 + len(parts)),
-        out_specs=[pl.BlockSpec(memory_space=pltpu.VMEM)] * GROUP_REQUESTS,
-        out_shape=[total] + [sent] * (GROUP_REQUESTS - 1),
-        compiler_params=params(),
+        functools.partial(fold_sub_kernel, order, len(parts)),
+        in_specs=[pl.BlockSpec(memory_space=pltpu.VMEM)] * (1 + len(parts)) + unread(after),
+        out_specs=[pl.BlockSpec(memory_space=pltpu.VMEM)] * len(order),
+        out_shape=[sent if z else total for z in order],
+        compiler_params=params(),
+        cost_estimate=cost([kept], parts),
         name="fold_sub",
-    )(place, kept, *parts)
-
-
-def fold_pairs_kernel(total_ref, *refs):
+    )(kept, *parts, *after)
+
+
+def fold_pairs_kernel(count, total_ref, *refs):
+    rows = total_ref.shape[0]
+    refs, out_ref = refs[:count], refs[-1]
+    steps = [step_of(ref) for ref in refs]
+    for c in range(total_ref.shape[1] // LANES):
+        part = slice(c * LANES, (c + 1) * LANES)
+        total = total_ref[:, part]
+        for ref, step in zip(refs, steps):
+            total = total + decoded(ref, c * rows, rows, step)
+        out_ref[:, part] = total
+
+
+def fold_pairs(total, parts, after=()):
+    return pl.pallas_call(
+        functools.partial(fold_pairs_kernel, len(parts)),
+        in_specs=[pl.BlockSpec(memory_space=pltpu.VMEM)] * (1 + len(parts)) + unread(after),
+        out_specs=pl.BlockSpec(memory_space=pltpu.VMEM),
+        out_shape=jax.ShapeDtypeStruct(total.shape, jnp.float32),
+        compiler_params=params(),
+        cost_estimate=cost([total], parts),
+        name="fold_pairs",
+    )(total, *parts, *after)
+
+
+def finish_kernel(rows_ref, total_ref, *refs):
     rows = total_ref.shape[0]
     steps = [step_of(ref) for ref in refs[:-1]]
     for c in range(total_ref.shape[1] // LANES):
@@ -453,29 +504,9 @@
         total = total_ref[:, part]
         for ref, step in zip(refs[:-1], steps):
             total = total + decoded(ref, c * rows, rows, step)
-        refs[-1][:, part] = total
-
-
-def fold_pairs(total, parts):
-    return pl.pallas_call(
-        fold_pairs_kernel,
-        in_specs=[pl.BlockSpec(memory_space=pltpu.VMEM)] * (1 + len(parts)),
-        out_specs=pl.BlockSpec(memory_space=pltpu.VMEM),
-        out_shape=jax.ShapeDtypeStruct(total.shape, jnp.float32),
-        compiler_params=params(),
-        name="fold_pairs",
-    )(total, *parts)
-
-
-def finish_kernel(rows_ref, total_ref, *refs):
-    rows = rows_ref.shape[0]
-    steps = [step_of(ref) for ref in refs[:-1]]
-    for c in range(rows_ref.shape[1] // LANES):
-        part = slice(c * LANES, (c + 1) * LANES)
-        total = total_ref[:, part]
-        for ref, step in zip(refs[:-1], steps):
-            total = total + decoded(ref, c * rows, rows, step)
-        refs[-1][:, part] = (total + rows_ref[:, part].astype(jnp.float32)).astype(jnp.bfloat16)
+        refs[-1][:, part] = (total + rows_ref[0, :, part].astype(jnp.float32)).astype(
+            jnp.bfloat16
+        )
 
 
 def finish(rows, total, parts):
@@ -483,8 +514,9 @@
         finish_kernel,
         in_specs=[pl.BlockSpec(memory_space=pltpu.VMEM)] * (2 + len(parts)),
         out_specs=pl.BlockSpec(memory_space=pltpu.VMEM),
-        out_shape=jax.ShapeDtypeStruct(rows.shape, jnp.bfloat16),
-        compiler_params=params(),
+        out_shape=jax.ShapeDtypeStruct(total.shape, jnp.bfloat16),
+        compiler_params=params(),
+        cost_estimate=cost([total], parts),
         name="finish",
     )(rows, total, *parts)
 
@@ -519,8 +551,10 @@
     place = scalars(request, sub, core)
 
     rows = hidden.reshape(GROUP_REQUESTS * ROWS, width)
-    column = pack([rows] + [passed(rows, "req", s) for s in range(1, GROUP_REQUESTS)])
-    gathered = [column] + [passed(column, "sub", s) for s in range(1, subs)]
+    column = [rows] + [passed(rows, "req", s) for s in range(1, GROUP_REQUESTS)]
+    gathered = [pack(column)]
+    for s in range(1, subs):
+        gathered.append(pack([passed(part, "sub", s) for part in column]))
     gathered = gathered + [passed(part, "section", 1) for part in gathered]
 
     where = scalars(request, sub * 2 + core, device * prompt_cache_pages.shape[0])
@@ -542,18 +576,16 @@
     cosine = cosine.reshape(-1, HEAD_SIZE)
     sine = sine.reshape(-1, HEAD_SIZE)
 
-    rows, gain, key_value_weight, w_query = staged(
-        rows, norm_gain.reshape(devices, 1, width), key_value_weight, w_query
-    )
-    (w_output,) = staged(w_output)
-    scale, kept, *parts = scale_and_pairs(place, rows, gain, key_value_weight, gathered)
+    gain, key_value_weight = staged([norm_gain.reshape(devices, 1, width), key_value_weight])
+    scale, kept, *parts = scale_and_pairs(place, gain, key_value_weight, gathered)
     parts = [passed(part, "sub", s + 1) for s, part in enumerate(parts)]
-    total, *parts = fold_sub(scalars(0), kept, parts)
+    query = queries(place, scale, gain, w_query, cosine, sine, gathered)
+    total, *parts = fold_sub((0, 1, 2, 3), kept, parts, after=[query])
     parts = [passed(part, "req", s + 1) for s, part in enumerate(parts)]
-    mine = fold_pairs(total, parts)
+    (w_output,) = staged([w_output], after=[query])
+    mine = fold_pairs(total, parts, after=[w_output])
     other = passed(mine, "section", 1)
 
-    query = queries(place, scale, gain, w_query, cosine, sine, gathered)
     mixed = attend(
         place, lengths.astype(jnp.int32), query, mine, other, cosine, sine, caches
     )
@@ -561,11 +593,13 @@
     away = outputs(scalars(1 - core), mixed, w_output, devices // 2)
     arrived = passed(away, "section", 1)
     kept = outputs(scalars(core), mixed, w_output, devices // 2)
-    kept, *parts = fold_core(scalars(sub), kept, arrived, subs)
-    parts = [passed(part, "sub", s + 1) for s, part in enumerate(parts)]
-    total, *parts = fold_sub(scalars(request), kept, parts)
-    parts = [passed(part, "req", s + 1) for s, part in enumerate(parts)]
-    return finish(rows, total, parts).reshape(hidden.shape)
+    kept, *parts = fold_core(place, kept, arrived, subs)
+    parts = [passed(part, "sub", i // 2 + 1) for i, part in enumerate(parts)]
+    last = {}
+    for half, order in enumerate(HALVES):
+        last.update(zip(order, fold_sub(order, kept, parts[half::2])))
+    parts = [passed(last[s], "req", s) for s in range(1, GROUP_REQUESTS)]
+    return finish(gathered[0], last[0], parts).reshape(hidden.shape)
 
 
 def solution(mesh):

time: 85.5 us -> 81 us (0.947)
  local copies, waits for them, and re-layouts: 19.4 us -> 11.8 us
  starting transfers between devices: 25.2 us -> 31.6 us
  waiting for transfers between devices: 27.4 us -> 21.1 us
  Pallas kernels: 11.8 us -> 14.1 us
    unnamed x22 -> x20, local copies, waits for them, and re-layouts: 19.3 us -> 11.8 us
    ppermute x24 -> x28, starting transfers between devices: 25.2 us -> 31.6 us  [passed(): lax.ppermute(array, axis, [(i, (i + shift) % size) for i in range(size)])]
    ppermute x24 -> x28, waiting for transfers between devices: 27.4 us -> 21.1 us  [passed(): lax.ppermute(array, axis, [(i, (i + shift) % size) for i in range(size)])]
    pallas_call x1, Pallas kernels: 2.26 us -> 4.64 us  [queries(): pl.pallas_call(query_kernel, in_specs=[pl.BlockSpec(memory_space=pltpu.SM...]
    pallas_call x5 -> x6, Pallas kernels: 1.74 us -> 1.1 us  [the longest x2 0.74 us: staged(): pl.pallas_call(functools.partial(stage_kernel, count), in_specs=[pl.Block...]
  transfers between devices with their start and end apart: 24 -> 28, of which waited for: 12 -> 10; matrix products, arithmetic and copies ran while one was open for 1% -> 2% of each run, Pallas kernels for 9% -> 12%
where the time goes in v5:
time: 81 us; the launch traced here: 80.6 us
  starting transfers between devices  31.6 us (39%)
  waiting for transfers between devices  21.1 us (26%)
  Pallas kernels  14.1 us (17%)
  local copies, waits for them, and re-layouts  11.8 us (15%)
  other arithmetic  1.71 us (2%)
    ppermute x28, starting transfers between devices, passed(): lax.ppermute(array, axis, [(i, (i + shift) % size) for i in range(size)])  31.6 us
    ppermute x28, waiting for transfers between devices, passed(): lax.ppermute(array, axis, [(i, (i + shift) % size) for i in range(size)])  21.1 us
    unnamed x20, local copies, waits for them, and re-layouts  11.8 us
    pallas_call x1, Pallas kernels, queries(): pl.pallas_call(query_kernel, in_specs=[pl.BlockSpec(memory_space=pltpu.SM...  4.64 us
    pallas_call x1, Pallas kernels, attend(): pl.pallas_call(attend_kernel, in_specs=[pl.BlockSpec(memory_space=pltpu.S...  2.18 us
    pallas_call x2, Pallas kernels, outputs(): pl.pallas_call(output_kernel, in_specs=[pl.BlockSpec(memory_space=pltpu.S...  1.71 us
  transfers between devices with their start and end apart: 28, of which 10 were waited for; matrix products, arithmetic and copies ran while one was open for 2% of the time, Pallas kernels for 12%

profile of v5, /device:TPU:0, one launch (start us, length us, event | category | flops | bytes accessed | tf_op | source)
XLA Modules:
  0.0 80.6 jit_solution(12871173289962741966)
XLA Ops:
  0.0 3.0 %collective-permute-start.3 = (bf16[64,512]{1,0:T(8,128)(2,1)}, bf16[64,512]{1,0:T(8,128)(2,1)S(1)}, u32[]{:S(2)}, u32[]{:S(2)}) collective-permute-start(bf16[64,512]{1,0:T(8,128)(2,1)} %bitcast.17), channel_id=1, source_target_pairs={{0,2},{2,0},{1,3},{3,1},{4,6},{6,4},{5,7},{7,5},{8,10},{10,8},{9,1... | collective-permute-start | bytes 196616 | tf_op jit(solution)/shard_map/ppermute | solution.py:526
  3.0 3.6 %collective-permute-start.2 = (bf16[64,512]{1,0:T(8,128)(2,1)}, bf16[64,512]{1,0:T(8,128)(2,1)S(1)}, u32[]{:S(2)}, u32[]{:S(2)}) collective-permute-start(bf16[64,512]{1,0:T(8,128)(2,1)} %bitcast.18), channel_id=1, source_target_pairs={{0,12},{4,0},{8,4},{12,8},{1,13},{5,1},{9,5},{13,9},{2,14},{6,2},{... | collective-permute-start | bytes 196616 | tf_op jit(solution)/shard_map/ppermute | solution.py:526
  8.4 1.2 %copy-done.3 = bf16[16,16,2048]{2,1,0:T(8,128)(2,1)S(1)} copy-done((bf16[16,16,2048]{2,1,0:T(8,128)(2,1)S(1)}, bf16[16,16,2048]{2,1,0:T(8,128)(2,1)}, u32[]{:S(2)}) %copy-start.3) | copy-done | bytes 1048600
  10.3 1.5 %used_pages.1 = (bf16[4,128,256]{2,1,0:T(8,128)(2,1)S(1)}, bf16[4,128,256]{2,1,0:T(8,128)(2,1)S(1)}) custom-call(s32[4,32]{1,0:T(4,128)S(1)} %copy-done.6, s32[3]{0:T(128)S(1)} %pad_add_fusion.1.place, f32[16,16]{1,0:T(8,128)S(1)} %convert_element_type.11.scales, bf16[16,16,2048]{2,1,0:T(8,128)(2,1)S(1)} %copy-done.3), custom_call_target="tpu_custom_call" | custom-call | bytes 1048576 | tf_op jit(solution)/shard_map/used_pages/pallas_call | solution.py:92
  13.0 1.5 %collective-permute-start.6 = (bf16[64,512]{1,0:T(8,128)(2,1)S(1)}, bf16[64,512]{1,0:T(8,128)(2,1)S(1)}, u32[]{:S(2)}, u32[]{:S(2)}) collective-permute-start(bf16[64,512]{1,0:T(8,128)(2,1)S(1)} %collective-permute-done.2.refs_3_), channel_id=1, source_target_pairs={{0,2},{2,0},{1,3},{3,1},{4,6},{6,4},{5,7},{7,5},{8,10},{10,8},{9,1... | collective-permute-start | bytes 196616 | tf_op jit(solution)/shard_map/ppermute | solution.py:526
  15.1 1.5 %collective-permute-start.4 = (bf16[64,512]{1,0:T(8,128)(2,1)S(1)}, bf16[64,512]{1,0:T(8,128)(2,1)S(1)}, u32[]{:S(2)}, u32[]{:S(2)}) collective-permute-start(bf16[64,512]{1,0:T(8,128)(2,1)S(1)} %collective-permute-done.refs_1_), channel_id=1, source_target_pairs={{0,2},{2,0},{1,3},{3,1},{4,6},{6,4},{5,7},{7,5},{8,10},{10,8},{9,1... | collective-permute-start | bytes 196616 | tf_op jit(solution)/shard_map/ppermute | solution.py:526
  17.6 4.0 %collective-permute-done.6.refs_3_ = bf16[64,512]{1,0:T(8,128)(2,1)S(1)} collective-permute-done((bf16[64,512]{1,0:T(8,128)(2,1)S(1)}, bf16[64,512]{1,0:T(8,128)(2,1)S(1)}, u32[]{:S(2)}, u32[]{:S(2)}) %collective-permute-start.6) | collective-permute-done | bytes 65568 | tf_op jit(solution)/shard_map/ppermute | solution.py:526
  23.2 1.6 %copy-done.2 = bf16[512,2048]{1,0:T(8,128)(2,1)S(1)} copy-done((bf16[512,2048]{1,0:T(8,128)(2,1)S(1)}, bf16[512,2048]{1,0:T(8,128)(2,1)}, u32[]{:S(2)}) %copy-start.2) | copy-done | bytes 2097176
  25.9 2.5 %collective-permute-start.15 = (bf16[2,128,256]{2,1,0:T(8,128)(2,1)S(1)}, bf16[2,128,256]{2,1,0:T(8,128)(2,1)S(1)}, u32[]{:S(2)}, u32[]{:S(2)}) collective-permute-start(bf16[2,128,256]{2,1,0:T(8,128)(2,1)S(1)} %get-tuple-element.39), channel_id=1, source_target_pairs={{0,4},{4,8},{8,12},{12,0},{1,5},{5,9},{9,13},{13,1},{2,6},{6,10},{... | collective-permute-start | bytes 393224 | tf_op jit(solution)/shard_map/ppermute | solution.py:526
  29.6 1.5 %collective-permute-start.17 = (bf16[2,128,256]{2,1,0:T(8,128)(2,1)S(1)}, bf16[2,128,256]{2,1,0:T(8,128)(2,1)S(1)}, u32[]{:S(2)}, u32[]{:S(2)}) collective-permute-start(bf16[2,128,256]{2,1,0:T(8,128)(2,1)S(1)} %get-tuple-element.41), channel_id=1, source_target_pairs={{0,12},{4,0},{8,4},{12,8},{1,13},{5,1},{9,5},{13,9},{2,14},{6,2},{... | collective-permute-start | bytes 393224 | tf_op jit(solution)/shard_map/ppermute | solution.py:526
  31.1 1.4 %scale_and_pairs.1 = (f32[64,128]{1,0:T(8,128)S(1)}, f32[4,64,256]{2,1,0:T(8,128)S(1)}, s16[528,128]{1,0:T(8,128)(2,1)S(1)}) custom-call(s32[3]{0:T(128)S(1)} %pad_add_fusion.place, f32[16,1,512]{2,1,0:T(1,128)S(1)} %get-tuple-element.27.gain_ref, bf16[512,2048]{1,0:T(8,128)(2,1)S(1)} %get-tuple-element.28.weight_ref, ...), custom_call_target="tpu_custom_call" | custom-call | flops 134217728 | bytes 3145728 | tf_op jit(solution)/shard_map/scale_and_pairs/pallas_call | solution.py:215
  33.1 4.6 %queries.1.refs_1_.q_ref = bf16[4,16,512]{2,1,0:T(8,128)(2,1)S(1)} custom-call(s32[3]{0:T(128)S(1)} %pad_add_fusion.place, f32[64,128]{1,0:T(8,128)S(1)} %get-tuple-element.29.scale_ref, f32[16,1,512]{2,1,0:T(1,128)S(1)} %get-tuple-element.27.gain_ref, bf16[8192,512]{1,0:T(8,128)(2,1)} %weight_ref.1, f32[64,128]{1,0:T(8,128)S(1)} %bitcast.13, ...), custom_call_target="tpu_custom_call" | custom-call | flops 536870912 | bytes 8388608 | tf_op jit(solution)/shard_map/queries/pallas_call | solution.py:259
  38.5 1.7 %collective-permute-start.11 = (s16[144,128]{1,0:T(8,128)(2,1)S(1)}, s16[144,128]{1,0:T(8,128)(2,1)S(1)}, u32[]{:S(2)}, u32[]{:S(2)}) collective-permute-start(s16[144,128]{1,0:T(8,128)(2,1)S(1)} %get-tuple-element.34), channel_id=1, source_target_pairs={{0,8},{4,12},{8,0},{12,4},{1,9},{5,13},{9,1},{13,5},{2,10},{6,14},... | collective-permute-start | bytes 110600 | tf_op jit(solution)/shard_map/ppermute | solution.py:526
  40.8 3.0 %collective-permute-done.10.refs_0_ = s16[144,128]{1,0:T(8,128)(2,1)S(1)} collective-permute-done((s16[144,128]{1,0:T(8,128)(2,1)S(1)}, s16[144,128]{1,0:T(8,128)(2,1)S(1)}, u32[]{:S(2)}, u32[]{:S(2)}) %collective-permute-start.10) | collective-permute-done | bytes 36896 | tf_op jit(solution)/shard_map/ppermute | solution.py:526
  44.4 2.2 %collective-permute-start.12 = (s16[144,128]{1,0:T(8,128)(2,1)S(1)}, s16[144,128]{1,0:T(8,128)(2,1)S(1)}, u32[]{:S(2)}, u32[]{:S(2)}) collective-permute-start(s16[144,128]{1,0:T(8,128)(2,1)S(1)} %get-tuple-element.35), channel_id=1, source_target_pairs={{0,12},{4,0},{8,4},{12,8},{1,13},{5,1},{9,5},{13,9},{2,14},{6,2},{... | collective-permute-start | bytes 110600 | tf_op jit(solution)/shard_map/ppermute | solution.py:526
  48.4 3.3 %copy-done = bf16[512,8192]{1,0:T(8,128)(2,1)} copy-done((bf16[512,8192]{1,0:T(8,128)(2,1)}, bf16[512,8192]{1,0:T(8,128)(2,1)S(1)}, u32[]{:S(2)}) %copy-start) | copy-done | bytes 8388632
  53.0 2.2 %attend.1.x_ref = bf16[4,16,512]{2,1,0:T(8,128)(2,1)S(1)} custom-call(s32[3]{0:T(128)S(1)} %pad_add_fusion.place, s32[4]{0:T(128)S(1)} %copy-done.7, bf16[4,16,512]{2,1,0:T(8,128)(2,1)S(1)} %queries.1.refs_1_.q_ref, f32[64,256]{1,0:T(8,128)S(1)} %fold_pairs.1.mine_ref, f32[64,256]{1,0:T(8,128)S(1)} %collective-permute-done.13.other_ref, ...), custom_call_target="tpu_custom_call" | custom-call | flops 268435456 | bytes 3145728 | tf_op jit(solution)/shard_map/attend/pallas_call | solution.py:341
  55.2 3.4 %copy-done.1 = bf16[512,8192]{1,0:T(8,128)(2,1)S(1)} copy-done((bf16[512,8192]{1,0:T(8,128)(2,1)S(1)}, bf16[512,8192]{1,0:T(8,128)(2,1)}, u32[]{:S(2)}) %copy-start.1) | copy-done | bytes 8388632
  60.5 1.6 %collective-permute-done.22.got_ref = f32[8,64,512]{2,1,0:T(8,128)S(1)} collective-permute-done((f32[8,64,512]{2,1,0:T(8,128)S(1)}, f32[8,64,512]{2,1,0:T(8,128)S(1)}, u32[]{:S(2)}, u32[]{:S(2)}) %collective-permute-start.22) | collective-permute-done | bytes 1048608 | tf_op jit(solution)/shard_map/ppermute | solution.py:526
  62.9 1.5 %collective-permute-start.23 = (s16[528,128]{1,0:T(8,128)(2,1)S(1)}, s16[528,128]{1,0:T(8,128)(2,1)S(1)}, u32[]{:S(2)}, u32[]{:S(2)}) collective-permute-start(s16[528,128]{1,0:T(8,128)(2,1)S(1)} %get-tuple-element.43), channel_id=1, source_target_pairs={{0,2},{2,0},{1,3},{3,1},{4,6},{6,4},{5,7},{7,5},{8,10},{10,8},{9,1... | collective-permute-start | bytes 405512 | tf_op jit(solution)/shard_map/ppermute | solution.py:526
  65.0 4.4 %collective-permute-done.23.refs_0_ = s16[528,128]{1,0:T(8,128)(2,1)S(1)} collective-permute-done((s16[528,128]{1,0:T(8,128)(2,1)S(1)}, s16[528,128]{1,0:T(8,128)(2,1)S(1)}, u32[]{:S(2)}, u32[]{:S(2)}) %collective-permute-start.23) | collective-permute-done | bytes 135200 | tf_op jit(solution)/shard_map/ppermute | solution.py:526
  69.5 4.0 %collective-permute-start.27 = (s16[272,128]{1,0:T(8,128)(2,1)S(1)}, s16[272,128]{1,0:T(8,128)(2,1)S(1)}, u32[]{:S(2)}, u32[]{:S(2)}) collective-permute-start(s16[272,128]{1,0:T(8,128)(2,1)S(1)} %get-tuple-element.48), channel_id=1, source_target_pairs={{0,12},{4,0},{8,4},{12,8},{1,13},{5,1},{9,5},{13,9},{2,14},{6,2},{... | collective-permute-start | bytes 208904 | tf_op jit(solution)/shard_map/ppermute | solution.py:526
  73.8 2.5 %collective-permute-start.26 = (s16[272,128]{1,0:T(8,128)(2,1)S(1)}, s16[272,128]{1,0:T(8,128)(2,1)S(1)}, u32[]{:S(2)}, u32[]{:S(2)}) collective-permute-start(s16[272,128]{1,0:T(8,128)(2,1)S(1)} %get-tuple-element.47), channel_id=1, source_target_pairs={{0,8},{4,12},{8,0},{12,4},{1,9},{5,13},{9,1},{13,5},{2,10},{6,14},... | collective-permute-start | bytes 208904 | tf_op jit(solution)/shard_map/ppermute | solution.py:526
  76.3 3.6 %collective-permute-done.25.refs_0_ = s16[272,128]{1,0:T(8,128)(2,1)S(1)} collective-permute-done((s16[272,128]{1,0:T(8,128)(2,1)S(1)}, s16[272,128]{1,0:T(8,128)(2,1)S(1)}, u32[]{:S(2)}, u32[]{:S(2)}) %collective-permute-start.25) | collective-permute-done | bytes 69664 | tf_op jit(solution)/shard_map/ppermute | solution.py:526
  (79 shorter events, 19.0 us)
Async XLA Ops:
  0.0 17.5 %collective-permute-start.3 = (bf16[64,512]{1,0:T(8,128)(2,1)}, bf16[64,512]{1,0:T(8,128)(2,1)S(1)}, u32[]{:S(2)}, u32[]{:S(2)}) collective-permute-start(bf16[64,512]{1,0:T(8,128)(2,1)} %bitcast.17), channel_id=1, source_target_pairs={{0,2},{2,0},{1,3},{3,1},{4,6},{6,4},{5,7},{7,5},{8,10},{10,8},{9,1... | collective-permute-start | bytes 196616 | tf_op jit(solution)/shard_map/ppermute | solution.py:526
  3.0 10.1 %collective-permute-start.2 = (bf16[64,512]{1,0:T(8,128)(2,1)}, bf16[64,512]{1,0:T(8,128)(2,1)S(1)}, u32[]{:S(2)}, u32[]{:S(2)}) collective-permute-start(bf16[64,512]{1,0:T(8,128)(2,1)} %bitcast.18), channel_id=1, source_target_pairs={{0,12},{4,0},{8,4},{12,8},{1,13},{5,1},{9,5},{13,9},{2,14},{6,2},{... | collective-permute-start | bytes 196616 | tf_op jit(solution)/shard_map/ppermute | solution.py:526
  6.6 8.0 %collective-permute-start.1 = (bf16[64,512]{1,0:T(8,128)(2,1)}, bf16[64,512]{1,0:T(8,128)(2,1)S(1)}, u32[]{:S(2)}, u32[]{:S(2)}) collective-permute-start(bf16[64,512]{1,0:T(8,128)(2,1)} %bitcast.19), channel_id=1, source_target_pairs={{0,8},{4,12},{8,0},{12,4},{1,9},{5,13},{9,1},{13,5},{2,10},{6,14},... | collective-permute-start | bytes 196616 | tf_op jit(solution)/shard_map/ppermute | solution.py:526
  6.6 8.5 %collective-permute-start = (bf16[64,512]{1,0:T(8,128)(2,1)}, bf16[64,512]{1,0:T(8,128)(2,1)S(1)}, u32[]{:S(2)}, u32[]{:S(2)}) collective-permute-start(bf16[64,512]{1,0:T(8,128)(2,1)} %bitcast.20), channel_id=1, source_target_pairs={{0,4},{4,8},{8,12},{12,0},{1,5},{5,9},{9,13},{13,1},{2,6},{6,10},{... | collective-permute-start | bytes 196616 | tf_op jit(solution)/shard_map/ppermute | solution.py:526
  11.8 14.0 %collective-permute-start.14 = (bf16[4,128,256]{2,1,0:T(8,128)(2,1)S(1)}, bf16[4,128,256]{2,1,0:T(8,128)(2,1)S(1)}, u32[]{:S(2)}, u32[]{:S(2)}) collective-permute-start(bf16[4,128,256]{2,1,0:T(8,128)(2,1)S(1)} %get-tuple-element.37), channel_id=1, source_target_pairs={{0,2},{2,0},{1,3},{3,1},{4,6},{6,4},{5,7},{7,5},{8,10},{10,8},{9,1... | collective-permute-start | bytes 786440 | tf_op jit(solution)/shard_map/ppermute | solution.py:526
  13.0 8.6 %collective-permute-start.6 = (bf16[64,512]{1,0:T(8,128)(2,1)S(1)}, bf16[64,512]{1,0:T(8,128)(2,1)S(1)}, u32[]{:S(2)}, u32[]{:S(2)}) collective-permute-start(bf16[64,512]{1,0:T(8,128)(2,1)S(1)} %collective-permute-done.2.refs_3_), channel_id=1, source_target_pairs={{0,2},{2,0},{1,3},{3,1},{4,6},{6,4},{5,7},{7,5},{8,10},{10,8},{9,1... | collective-permute-start | bytes 196616 | tf_op jit(solution)/shard_map/ppermute | solution.py:526
  14.5 7.7 %collective-permute-start.5 = (bf16[64,512]{1,0:T(8,128)(2,1)S(1)}, bf16[64,512]{1,0:T(8,128)(2,1)S(1)}, u32[]{:S(2)}, u32[]{:S(2)}) collective-permute-start(bf16[64,512]{1,0:T(8,128)(2,1)S(1)} %collective-permute-done.1.refs_2_), channel_id=1, source_target_pairs={{0,2},{2,0},{1,3},{3,1},{4,6},{6,4},{5,7},{7,5},{8,10},{10,8},{9,1... | collective-permute-start | bytes 196616 | tf_op jit(solution)/shard_map/ppermute | solution.py:526
  15.1 7.9 %collective-permute-start.4 = (bf16[64,512]{1,0:T(8,128)(2,1)S(1)}, bf16[64,512]{1,0:T(8,128)(2,1)S(1)}, u32[]{:S(2)}, u32[]{:S(2)}) collective-permute-start(bf16[64,512]{1,0:T(8,128)(2,1)S(1)} %collective-permute-done.refs_1_), channel_id=1, source_target_pairs={{0,2},{2,0},{1,3},{3,1},{4,6},{6,4},{5,7},{7,5},{8,10},{10,8},{9,1... | collective-permute-start | bytes 196616 | tf_op jit(solution)/shard_map/ppermute | solution.py:526
  17.5 13.6 %collective-permute-start.7 = (bf16[4,64,512]{2,1,0:T(8,128)(2,1)S(1)}, bf16[4,64,512]{2,1,0:T(8,128)(2,1)S(1)}, u32[]{:S(2)}, u32[]{:S(2)}) collective-permute-start(bf16[4,64,512]{2,1,0:T(8,128)(2,1)S(1)} %pack.2.refs_0_.rows_ref), channel_id=1, source_target_pairs={{0,1},{1,0},{2,3},{3,2},{4,5},{5,4},{6,7},{7,6},{8,9},{9,8},{10,11... | collective-permute-start | bytes 786440 | tf_op jit(solution)/shard_map/ppermute | solution.py:526
  23.0 8.0 %collective-permute-start.8 = (bf16[4,64,512]{2,1,0:T(8,128)(2,1)S(1)}, bf16[4,64,512]{2,1,0:T(8,128)(2,1)S(1)}, u32[]{:S(2)}, u32[]{:S(2)}) collective-permute-start(bf16[4,64,512]{2,1,0:T(8,128)(2,1)S(1)} %pack.3.refs_1_), channel_id=1, source_target_pairs={{0,1},{1,0},{2,3},{3,2},{4,5},{5,4},{6,7},{7,6},{8,9},{9,8},{10,11... | collective-permute-start | bytes 786440 | tf_op jit(solution)/shard_map/ppermute | solution.py:526
  25.9 14.4 %collective-permute-start.15 = (bf16[2,128,256]{2,1,0:T(8,128)(2,1)S(1)}, bf16[2,128,256]{2,1,0:T(8,128)(2,1)S(1)}, u32[]{:S(2)}, u32[]{:S(2)}) collective-permute-start(bf16[2,128,256]{2,1,0:T(8,128)(2,1)S(1)} %get-tuple-element.39), channel_id=1, source_target_pairs={{0,4},{4,8},{8,12},{12,0},{1,5},{5,9},{9,13},{13,1},{2,6},{6,10},{... | collective-permute-start | bytes 393224 | tf_op jit(solution)/shard_map/ppermute | solution.py:526
  28.4 11.8 %collective-permute-start.16 = (bf16[2,128,256]{2,1,0:T(8,128)(2,1)S(1)}, bf16[2,128,256]{2,1,0:T(8,128)(2,1)S(1)}, u32[]{:S(2)}, u32[]{:S(2)}) collective-permute-start(bf16[2,128,256]{2,1,0:T(8,128)(2,1)S(1)} %get-tuple-element.40), channel_id=1, source_target_pairs={{0,8},{4,12},{8,0},{12,4},{1,9},{5,13},{9,1},{13,5},{2,10},{6,14},... | collective-permute-start | bytes 393224 | tf_op jit(solution)/shard_map/ppermute | solution.py:526
  29.6 11.2 %collective-permute-start.17 = (bf16[2,128,256]{2,1,0:T(8,128)(2,1)S(1)}, bf16[2,128,256]{2,1,0:T(8,128)(2,1)S(1)}, u32[]{:S(2)}, u32[]{:S(2)}) collective-permute-start(bf16[2,128,256]{2,1,0:T(8,128)(2,1)S(1)} %get-tuple-element.41), channel_id=1, source_target_pairs={{0,12},{4,0},{8,4},{12,8},{1,13},{5,1},{9,5},{13,9},{2,14},{6,2},{... | collective-permute-start | bytes 393224 | tf_op jit(solution)/shard_map/ppermute | solution.py:526
  37.9 5.9 %collective-permute-start.10 = (s16[144,128]{1,0:T(8,128)(2,1)S(1)}, s16[144,128]{1,0:T(8,128)(2,1)S(1)}, u32[]{:S(2)}, u32[]{:S(2)}) collective-permute-start(s16[144,128]{1,0:T(8,128)(2,1)S(1)} %get-tuple-element.33), channel_id=1, source_target_pairs={{0,4},{4,8},{8,12},{12,0},{1,5},{5,9},{9,13},{13,1},{2,6},{6,10},{... | collective-permute-start | bytes 110600 | tf_op jit(solution)/shard_map/ppermute | solution.py:526
  38.5 5.9 %collective-permute-start.11 = (s16[144,128]{1,0:T(8,128)(2,1)S(1)}, s16[144,128]{1,0:T(8,128)(2,1)S(1)}, u32[]{:S(2)}, u32[]{:S(2)}) collective-permute-start(s16[144,128]{1,0:T(8,128)(2,1)S(1)} %get-tuple-element.34), channel_id=1, source_target_pairs={{0,8},{4,12},{8,0},{12,4},{1,9},{5,13},{9,1},{13,5},{2,10},{6,14},... | collective-permute-start | bytes 110600 | tf_op jit(solution)/shard_map/ppermute | solution.py:526
  40.2 11.5 %collective-permute-start.18 = (bf16[2,128,256]{2,1,0:T(8,128)(2,1)S(1)}, bf16[2,128,256]{2,1,0:T(8,128)(2,1)S(1)}, u32[]{:S(2)}, u32[]{:S(2)}) collective-permute-start(bf16[2,128,256]{2,1,0:T(8,128)(2,1)S(1)} %get-tuple-element.38.refs_0_), channel_id=1, source_target_pairs={{0,1},{1,0},{2,3},{3,2},{4,5},{5,4},{6,7},{7,6},{8,9},{9,8},{10,11... | collective-permute-start | bytes 393224 | tf_op jit(solution)/shard_map/ppermute | solution.py:526
  40.3 11.5 %collective-permute-start.19 = (bf16[2,128,256]{2,1,0:T(8,128)(2,1)S(1)}, bf16[2,128,256]{2,1,0:T(8,128)(2,1)S(1)}, u32[]{:S(2)}, u32[]{:S(2)}) collective-permute-start(bf16[2,128,256]{2,1,0:T(8,128)(2,1)S(1)} %collective-permute-done.15.refs_1_), channel_id=1, source_target_pairs={{0,1},{1,0},{2,3},{3,2},{4,5},{5,4},{6,7},{7,6},{8,9},{9,8},{10,11... | collective-permute-start | bytes 393224 | tf_op jit(solution)/shard_map/ppermute | solution.py:526
  40.8 11.0 %collective-permute-start.20 = (bf16[2,128,256]{2,1,0:T(8,128)(2,1)S(1)}, bf16[2,128,256]{2,1,0:T(8,128)(2,1)S(1)}, u32[]{:S(2)}, u32[]{:S(2)}) collective-permute-start(bf16[2,128,256]{2,1,0:T(8,128)(2,1)S(1)} %collective-permute-done.16.refs_2_), channel_id=1, source_target_pairs={{0,1},{1,0},{2,3},{3,2},{4,5},{5,4},{6,7},{7,6},{8,9},{9,8},{10,11... | collective-permute-start | bytes 393224 | tf_op jit(solution)/shard_map/ppermute | solution.py:526
  43.8 7.9 %collective-permute-start.21 = (bf16[2,128,256]{2,1,0:T(8,128)(2,1)S(1)}, bf16[2,128,256]{2,1,0:T(8,128)(2,1)S(1)}, u32[]{:S(2)}, u32[]{:S(2)}) collective-permute-start(bf16[2,128,256]{2,1,0:T(8,128)(2,1)S(1)} %collective-permute-done.17.refs_3_), channel_id=1, source_target_pairs={{0,1},{1,0},{2,3},{3,2},{4,5},{5,4},{6,7},{7,6},{8,9},{9,8},{10,11... | collective-permute-start | bytes 393224 | tf_op jit(solution)/shard_map/ppermute | solution.py:526
  62.9 6.5 %collective-permute-start.23 = (s16[528,128]{1,0:T(8,128)(2,1)S(1)}, s16[528,128]{1,0:T(8,128)(2,1)S(1)}, u32[]{:S(2)}, u32[]{:S(2)}) collective-permute-start(s16[528,128]{1,0:T(8,128)(2,1)S(1)} %get-tuple-element.43), channel_id=1, source_target_pairs={{0,2},{2,0},{1,3},{3,1},{4,6},{6,4},{5,7},{7,5},{8,10},{10,8},{9,1... | collective-permute-start | bytes 405512 | tf_op jit(solution)/shard_map/ppermute | solution.py:526
  64.4 9.2 %collective-permute-start.24 = (s16[528,128]{1,0:T(8,128)(2,1)S(1)}, s16[528,128]{1,0:T(8,128)(2,1)S(1)}, u32[]{:S(2)}, u32[]{:S(2)}) collective-permute-start(s16[528,128]{1,0:T(8,128)(2,1)S(1)} %get-tuple-element.45), channel_id=1, source_target_pairs={{0,2},{2,0},{1,3},{3,1},{4,6},{6,4},{5,7},{7,5},{8,10},{10,8},{9,1... | collective-permute-start | bytes 405512 | tf_op jit(solution)/shard_map/ppermute | solution.py:526
  69.5 6.8 %collective-permute-start.27 = (s16[272,128]{1,0:T(8,128)(2,1)S(1)}, s16[272,128]{1,0:T(8,128)(2,1)S(1)}, u32[]{:S(2)}, u32[]{:S(2)}) collective-permute-start(s16[272,128]{1,0:T(8,128)(2,1)S(1)} %get-tuple-element.48), channel_id=1, source_target_pairs={{0,12},{4,0},{8,4},{12,8},{1,13},{5,1},{9,5},{13,9},{2,14},{6,2},{... | collective-permute-start | bytes 208904 | tf_op jit(solution)/shard_map/ppermute | solution.py:526
  73.7 6.2 %collective-permute-start.25 = (s16[272,128]{1,0:T(8,128)(2,1)S(1)}, s16[272,128]{1,0:T(8,128)(2,1)S(1)}, u32[]{:S(2)}, u32[]{:S(2)}) collective-permute-start(s16[272,128]{1,0:T(8,128)(2,1)S(1)} %get-tuple-element.46), channel_id=1, source_target_pairs={{0,4},{4,8},{8,12},{12,0},{1,5},{5,9},{9,13},{13,1},{2,6},{6,10},{... | collective-permute-start | bytes 208904 | tf_op jit(solution)/shard_map/ppermute | solution.py:526
  73.8 6.1 %collective-permute-start.26 = (s16[272,128]{1,0:T(8,128)(2,1)S(1)}, s16[272,128]{1,0:T(8,128)(2,1)S(1)}, u32[]{:S(2)}, u32[]{:S(2)}) collective-permute-start(s16[272,128]{1,0:T(8,128)(2,1)S(1)} %get-tuple-element.47), channel_id=1, source_target_pairs={{0,8},{4,12},{8,0},{12,4},{1,9},{5,13},{9,1},{13,5},{2,10},{6,14},... | collective-permute-start | bytes 208904 | tf_op jit(solution)/shard_map/ppermute | solution.py:526
  (14 other events, 73.5 us)

commit v6 on v5

--- a/solution.py
+++ b/solution.py
@@ -46,21 +46,23 @@
 
 
 def stage_kernel(count, *refs):
-    ins, outs, sems = refs[:count], refs[-1 - count : -1], refs[-1]
+    ins, outs, sems = refs[:count], refs[-2 - count : -1], refs[-1]
     copies = [pltpu.make_async_copy(ins[i], outs[i], sems.at[i]) for i in range(count)]
     for copy in copies:
         copy.start()
+    outs[-1][...] = jnp.zeros_like(outs[-1])
     for copy in copies:
         copy.wait()
 
 
 def staged(arrays, after=()):
     count = len(arrays)
+    token = jax.ShapeDtypeStruct((8, LANES), jnp.float32)
     return pl.pallas_call(
         functools.partial(stage_kernel, count),
         in_specs=[pl.BlockSpec(memory_space=pltpu.HBM)] * count + unread(after),
-        out_specs=[pl.BlockSpec(memory_space=pltpu.VMEM)] * count,
-        out_shape=[jax.ShapeDtypeStruct(array.shape, array.dtype) for array in arrays],
+        out_specs=[pl.BlockSpec(memory_space=pltpu.VMEM)] * (count + 1),
+        out_shape=[jax.ShapeDtypeStruct(array.shape, array.dtype) for array in arrays] + [token],
         scratch_shapes=[pltpu.SemaphoreType.DMA((count,))],
         compiler_params=params(),
         cost_estimate=cost(arrays, arrays),
@@ -68,20 +70,37 @@
     )(*arrays, *after)
 
 
+def gate_kernel(*refs):
+    pass
+
+
+def gate(arrays, after):
+    count = len(arrays)
+    return pl.pallas_call(
+        gate_kernel,
+        in_specs=[pl.BlockSpec(memory_space=pl.ANY)] * count + unread(after),
+        out_specs=[pl.BlockSpec(memory_space=pl.ANY)] * count,
+        out_shape=[jax.ShapeDtypeStruct(array.shape, array.dtype) for array in arrays],
+        input_output_aliases={i: i for i in range(count)},
+        compiler_params=params(),
+        name="gate",
+    )(*arrays, *after)
+
+
 def pages_kernel(table, place, scales, page_ref, *out_refs):
     e = pl.program_id(0)
-    subs = len(out_refs)
+    subs = out_refs[0].shape[0]
     targets = 2 * subs
     page = table[place[0], e * targets + place[1]] - place[2]
-    for shift, out_ref in enumerate(out_refs):
-        half = lax.rem(place[1] // 2 + shift, subs) // (subs // 2)
-        for z in range(GROUP_REQUESTS):
-            head = 2 * lax.rem(place[0] + z, GROUP_REQUESTS) + half
+    for z, out_ref in enumerate(out_refs):
+        for j in range(subs):
+            half = (place[1] // 2 ^ j) // (subs // 2)
+            head = 2 * (place[0] ^ z) + half
             for part in range(2):
                 c = head * 2 + part
                 columns = pl.ds(pl.multiple_of(c * HEAD_SIZE, HEAD_SIZE), HEAD_SIZE)
                 block = page_ref[0, :, columns].astype(jnp.float32)
-                out_ref[z, :, part * HEAD_SIZE : (part + 1) * HEAD_SIZE] = (
+                out_ref[j, :, part * HEAD_SIZE : (part + 1) * HEAD_SIZE] = (
                     block * scales[page, c]
                 ).astype(jnp.bfloat16)
 
@@ -89,6 +108,7 @@
 def used_pages(pages, scales, table, place, subs):
     targets = 2 * subs
     entries = table.shape[1] // targets
+    shape = jax.ShapeDtypeStruct((subs, entries * PAGE_TOKENS, PAIR), jnp.bfloat16)
     return pl.pallas_call(
         pages_kernel,
         grid_spec=pltpu.PrefetchScalarGridSpec(
@@ -104,15 +124,10 @@
                     ),
                 )
             ],
-            out_specs=[
-                pl.BlockSpec((GROUP_REQUESTS, PAGE_TOKENS, PAIR), lambda e, *_: (0, e, 0))
-            ]
-            * subs,
+            out_specs=[pl.BlockSpec((subs, PAGE_TOKENS, PAIR), lambda e, *_: (0, e, 0))]
+            * GROUP_REQUESTS,
         ),
-        out_shape=[
-            jax.ShapeDtypeStruct((GROUP_REQUESTS, entries * PAGE_TOKENS, PAIR), jnp.bfloat16)
-        ]
-        * subs,
+        out_shape=[shape] * GROUP_REQUESTS,
         compiler_params=params(),
         cost_estimate=pl.CostEstimate(
             flops=0, bytes_accessed=4 * entries * PAGE_TOKENS * pages.shape[2], transcendentals=0
@@ -122,28 +137,29 @@
 
 
 def regroup_kernel(*refs):
-    ins, outs = refs[:-GROUP_REQUESTS], refs[-GROUP_REQUESTS:]
-    for z, out_ref in enumerate(outs):
-        for j, ref in enumerate(ins):
-            out_ref[j] = ref[z]
-
-
-def regroup(parts):
+    ins, outs = refs[:GROUP_REQUESTS], refs[-refs[0].shape[0] :]
+    for j, out_ref in enumerate(outs):
+        for z, ref in enumerate(ins):
+            out_ref[z] = ref[j]
+
+
+def regroup(parts, after=()):
+    subs = parts[0].shape[0]
     shape = jax.ShapeDtypeStruct((len(parts),) + parts[0].shape[1:], parts[0].dtype)
     return pl.pallas_call(
         regroup_kernel,
-        in_specs=[pl.BlockSpec(memory_space=pltpu.VMEM)] * len(parts),
-        out_specs=[pl.BlockSpec(memory_space=pltpu.VMEM)] * GROUP_REQUESTS,
-        out_shape=[shape] * GROUP_REQUESTS,
+        in_specs=[pl.BlockSpec(memory_space=pltpu.VMEM)] * len(parts) + unread(after),
+        out_specs=[pl.BlockSpec(memory_space=pltpu.VMEM)] * subs,
+        out_shape=[shape] * subs,
         compiler_params=params(),
         cost_estimate=cost(parts, parts),
         name="regroup",
-    )(*parts)
+    )(*parts, *after)
 
 
 def pack_kernel(*refs):
-    for i, ref in enumerate(refs[:-1]):
-        refs[-1][i] = ref[...]
+    for i in range(refs[-1].shape[0]):
+        refs[-1][i] = refs[i][...]
 
 
 def pack(parts):
@@ -163,10 +179,8 @@
     subs = len(refs) // 2
     for i, ref in enumerate(refs):
         from_core = core if i < subs else 1 - core
-        from_sub = lax.rem(sub - i % subs + subs, subs)
         for z in range(GROUP_REQUESTS):
-            from_request = lax.rem(request - z + GROUP_REQUESTS, GROUP_REQUESTS)
-            yield ref, z, (from_request * subs + from_sub) * 2 + from_core
+            yield ref, z, ((request ^ z) * subs + (sub ^ i % subs)) * 2 + from_core
 
 
 def pairs_kernel(place, gain_ref, weight_ref, *refs):
@@ -191,10 +205,10 @@
     x = x_refs[0][0].astype(jnp.float32)
     mine = (x * scale * gain_ref[device]).astype(jnp.bfloat16)
     for shift in range(subs):
-        half = lax.rem(sub + shift, subs) // (subs // 2)
+        half = (sub ^ shift) // (subs // 2)
         pieces = []
         for z in range(GROUP_REQUESTS):
-            head = 2 * lax.rem(request + z, GROUP_REQUESTS) + half
+            head = 2 * (request ^ z) + half
             columns = pl.ds(pl.multiple_of(head * PAIR, PAIR), PAIR)
             part = jnp.dot(mine, weight_ref[:, columns], preferred_element_type=jnp.float32)
             if shift == 0:
@@ -277,7 +291,7 @@
 def attend_kernel(place, lengths, q_ref, mine_ref, other_ref, cos_ref, sin_ref, *refs):
     caches, out_ref, key_ref, value_ref = refs[:-3], refs[-3], refs[-2], refs[-1]
     request, sub, core = place[0], place[1], place[2]
-    subs, span, _ = caches[0].shape
+    subs, span = len(caches) // 2, caches[0].shape[1]
     targets = 2 * subs
     tokens = targets * span
     quarter = q_ref.shape[2] // HEAD_SIZE
@@ -287,7 +301,7 @@
     column = lax.broadcasted_iota(jnp.int32, (1, tokens), 1)
     source, inside = column // span, column % span
     from_core = jnp.where(source < subs, core, 1 - core)
-    from_sub = (sub - source % subs + subs) % subs
+    from_sub = sub ^ source % subs
     entry = inside // PAGE_TOKENS * targets + from_sub * 2 + from_core
     position = entry * PAGE_TOKENS + inside % PAGE_TOKENS
     count = quarter * ROWS
@@ -297,7 +311,7 @@
     factor = HEAD_SIZE ** (-0.5)
     contract = (((1,), (1,)), ((), ()))
     for z in range(GROUP_REQUESTS):
-        r = lax.rem(request - z + GROUP_REQUESTS, GROUP_REQUESTS)
+        r = request ^ z
         fresh = [
             pl.ds(pl.multiple_of((step * GROUP_REQUESTS + r) * SAMPLES, SAMPLES), SAMPLES)
             for step in range(STEPS)
@@ -305,13 +319,8 @@
         new_key = jnp.concatenate([key_ref[rows] for rows in fresh], axis=0)
         new_value = jnp.concatenate([value_ref[rows] for rows in fresh], axis=0)
         new_key, new_value = new_key.astype(jnp.bfloat16), new_value.astype(jnp.bfloat16)
-        pair_of_caches = (caches[z], caches[GROUP_REQUESTS + z])
-        keys = jnp.concatenate(
-            [c[j, :, :HEAD_SIZE] for c in pair_of_caches for j in range(subs)], axis=0
-        )
-        values = jnp.concatenate(
-            [c[j, :, HEAD_SIZE:] for c in pair_of_caches for j in range(subs)], axis=0
-        )
+        keys = jnp.concatenate([ref[z, :, :HEAD_SIZE] for ref in caches], axis=0)
+        values = jnp.concatenate([ref[z, :, HEAD_SIZE:] for ref in caches], axis=0)
         query = jnp.concatenate(
             [q_ref[r, :, h * HEAD_SIZE : (h + 1) * HEAD_SIZE] for h in range(quarter)], axis=0
         )
@@ -411,11 +420,11 @@
 def fold_core_kernel(place, mine_ref, got_ref, kept_ref, *out_refs):
     subs = 1 + len(out_refs) // 2
     for shift in range(subs):
-        sub = lax.rem(place[1] + shift, subs)
+        sub = place[1] ^ shift
         for half in range(2):
             pieces = []
             for z in HALVES[half]:
-                block = lax.rem(place[0] + z, GROUP_REQUESTS) * subs + sub
+                block = (place[0] ^ z) * subs + sub
                 block = mine_ref[block] + got_ref[block]
                 if shift == 0:
                     kept_ref[z] = block
@@ -522,8 +531,7 @@
 
 
 def passed(array, axis, shift):
-    size = lax.axis_size(axis)
-    return lax.ppermute(array, axis, [(i, (i + shift) % size) for i in range(size)])
+    return lax.ppermute(array, axis, [(i, i ^ shift) for i in range(lax.axis_size(axis))])
 
 
 def scalars(*values):
@@ -552,17 +560,16 @@
 
     rows = hidden.reshape(GROUP_REQUESTS * ROWS, width)
     column = [rows] + [passed(rows, "req", s) for s in range(1, GROUP_REQUESTS)]
-    gathered = [pack(column)]
-    for s in range(1, subs):
-        gathered.append(pack([passed(part, "sub", s) for part in column]))
+    where = scalars(request, sub * 2 + core, device * prompt_cache_pages.shape[0])
+    pages = list(used_pages(prompt_cache_pages, per_page_scales, block_table, where, subs))
+    column = pack(column)
+    gathered = [passed(column, "sub", s) for s in range(1, subs)]
+    pages[1:] = [passed(pages[s], "req", s) for s in range(1, GROUP_REQUESTS)]
+    gain, key_value_weight, ready = staged(
+        [norm_gain.reshape(devices, 1, width), key_value_weight], after=[column]
+    )
+    gathered = [column] + list(gate(gathered, after=[ready]))
     gathered = gathered + [passed(part, "section", 1) for part in gathered]
-
-    where = scalars(request, sub * 2 + core, device * prompt_cache_pages.shape[0])
-    parts = used_pages(prompt_cache_pages, per_page_scales, block_table, where, subs)
-    parts = [parts[0]] + [passed(parts[s], "sub", s) for s in range(1, subs)]
-    parts = regroup(parts)
-    caches = [parts[0]] + [passed(parts[s], "req", s) for s in range(1, GROUP_REQUESTS)]
-    caches = caches + [passed(part, "section", 1) for part in caches]
 
     half = HEAD_SIZE // 2
     freqs = jnp.exp(
@@ -576,14 +583,17 @@
     cosine = cosine.reshape(-1, HEAD_SIZE)
     sine = sine.reshape(-1, HEAD_SIZE)
 
-    gain, key_value_weight = staged([norm_gain.reshape(devices, 1, width), key_value_weight])
     scale, kept, *parts = scale_and_pairs(place, gain, key_value_weight, gathered)
     parts = [passed(part, "sub", s + 1) for s, part in enumerate(parts)]
     query = queries(place, scale, gain, w_query, cosine, sine, gathered)
     total, *parts = fold_sub((0, 1, 2, 3), kept, parts, after=[query])
     parts = [passed(part, "req", s + 1) for s, part in enumerate(parts)]
-    (w_output,) = staged([w_output], after=[query])
-    mine = fold_pairs(total, parts, after=[w_output])
+    pages = regroup(pages, after=[total])
+    caches = [passed(pages[s], "sub", s) for s in range(1, subs)]
+    w_output, ready = staged([w_output], after=[query])
+    mine = fold_pairs(total, parts, after=[ready])
+    caches = list(pages[:1]) + list(gate(caches, after=[mine]))
+    caches = caches + [passed(part, "section", 1) for part in caches]
     other = passed(mine, "section", 1)
 
     mixed = attend(

time: 81 us -> 69.6 us (0.86)
  waiting for transfers between devices: 21.1 us -> 14.9 us
  starting transfers between devices: 31.6 us -> 26.6 us
    ppermute x28 -> x23, waiting for transfers between devices: 21.1 us -> 14.9 us  [passed(): lax.ppermute(array, axis, [(i, i ^ shift) for i in range(lax.axis_size(ax...]
    ppermute x28 -> x23, starting transfers between devices: 31.6 us -> 26.6 us  [passed(): lax.ppermute(array, axis, [(i, i ^ shift) for i in range(lax.axis_size(ax...]
  transfers between devices with their start and end apart: 28 -> 23, of which waited for: 10 -> 9; matrix products, arithmetic and copies ran while one was open for 2% -> 2% of each run, Pallas kernels for 12% -> 14%
where the time goes in v6:
time: 69.6 us; the launch traced here: 69.2 us
  starting transfers between devices  26.6 us (38%)
  waiting for transfers between devices  14.9 us (21%)
  Pallas kernels  14.1 us (20%)
  local copies, waits for them, and re-layouts  11.8 us (17%)
  other arithmetic  1.71 us (2%)
    ppermute x23, starting transfers between devices, passed(): lax.ppermute(array, axis, [(i, i ^ shift) for i in range(lax.axis_size(ax...  26.6 us
    ppermute x23, waiting for transfers between devices, passed(): lax.ppermute(array, axis, [(i, i ^ shift) for i in range(lax.axis_size(ax...  14.9 us
    unnamed x20, local copies, waits for them, and re-layouts  11.7 us
    pallas_call x1, Pallas kernels, queries(): pl.pallas_call(query_kernel, in_specs=[pl.BlockSpec(memory_space=pltpu.SM...  4.63 us
    pallas_call x1, Pallas kernels, attend(): pl.pallas_call(attend_kernel, in_specs=[pl.BlockSpec(memory_space=pltpu.S...  2.18 us
    pallas_call x2, Pallas kernels, outputs(): pl.pallas_call(output_kernel, in_specs=[pl.BlockSpec(memory_space=pltpu.S...  1.71 us
    pallas_call x1, Pallas kernels, used_pages(): pl.pallas_call(pages_kernel, grid_spec=pltpu.PrefetchScalarGridSpec(num_s...  1.51 us
  transfers between devices with their start and end apart: 23, of which 9 were waited for; matrix products, arithmetic and copies ran while one was open for 2% of the time, Pallas kernels for 14%

profile of v6, /device:TPU:0, one launch (start us, length us, event | category | flops | bytes accessed | tf_op | source)
XLA Modules:
  0.0 69.2 jit_solution(11790235493201412874)
XLA Ops:
  0.0 5.0 %collective-permute-start.2 = (bf16[64,512]{1,0:T(8,128)(2,1)}, bf16[64,512]{1,0:T(8,128)(2,1)S(1)}, u32[]{:S(2)}, u32[]{:S(2)}) collective-permute-start(bf16[64,512]{1,0:T(8,128)(2,1)} %bitcast.17), channel_id=1, source_target_pairs={{0,12},{4,8},{8,4},{12,0},{1,13},{5,9},{9,5},{13,1},{2,14},{6,10},... | collective-permute-start | bytes 196616 | tf_op jit(solution)/shard_map/ppermute | solution.py:534
  6.4 1.2 %copy-done.3 = bf16[16,16,2048]{2,1,0:T(8,128)(2,1)S(1)} copy-done((bf16[16,16,2048]{2,1,0:T(8,128)(2,1)S(1)}, bf16[16,16,2048]{2,1,0:T(8,128)(2,1)}, u32[]{:S(2)}) %copy-start.3) | copy-done | bytes 1048600
  8.3 1.5 %used_pages.1 = (bf16[2,128,256]{2,1,0:T(8,128)(2,1)S(1)}, bf16[2,128,256]{2,1,0:T(8,128)(2,1)S(1)}, bf16[2,128,256]{2,1,0:T(8,128)(2,1)S(1)}, bf16[2,128,256]{2,1,0:T(8,128)(2,1)S(1)}) custom-call(s32[4,32]{1,0:T(4,128)S(1)} %copy-done.6, s32[3]{0:T(128)S(1)} %pad_add_fusion.1.place, f32[16,16]{1,0:T(8,128)S(1)} %convert_element_type.11.scales, ...), custom_call_target="tpu_custom_call" | custom-call | bytes 1048576 | tf_op jit(solution)/shard_map/used_pages/pallas_call | solution.py:112
  9.8 1.5 %collective-permute-start.11 = (bf16[2,128,256]{2,1,0:T(8,128)(2,1)S(1)}, bf16[2,128,256]{2,1,0:T(8,128)(2,1)S(1)}, u32[]{:S(2)}, u32[]{:S(2)}) collective-permute-start(bf16[2,128,256]{2,1,0:T(8,128)(2,1)S(1)} %get-tuple-element.42), channel_id=1, source_target_pairs={{0,4},{4,0},{8,12},{12,8},{1,5},{5,1},{9,13},{13,9},{2,6},{6,2},{1... | collective-permute-start | bytes 393224 | tf_op jit(solution)/shard_map/ppermute | solution.py:534
  11.3 2.9 %collective-permute-start.12 = (bf16[2,128,256]{2,1,0:T(8,128)(2,1)S(1)}, bf16[2,128,256]{2,1,0:T(8,128)(2,1)S(1)}, u32[]{:S(2)}, u32[]{:S(2)}) collective-permute-start(bf16[2,128,256]{2,1,0:T(8,128)(2,1)S(1)} %get-tuple-element.43), channel_id=1, source_target_pairs={{0,8},{4,12},{8,0},{12,4},{1,9},{5,13},{9,1},{13,5},{2,10},{6,14},... | collective-permute-start | bytes 393224 | tf_op jit(solution)/shard_map/ppermute | solution.py:534
  15.1 1.8 %collective-permute-start.3 = (bf16[4,64,512]{2,1,0:T(8,128)(2,1)S(1)}, bf16[4,64,512]{2,1,0:T(8,128)(2,1)S(1)}, u32[]{:S(2)}, u32[]{:S(2)}) collective-permute-start(bf16[4,64,512]{2,1,0:T(8,128)(2,1)S(1)} %pack.1.refs_2_.refs_0_.rows_ref), channel_id=1, source_target_pairs={{0,2},{2,0},{1,3},{3,1},{4,6},{6,4},{5,7},{7,5},{8,10},{10,8},{9,1... | collective-permute-start | bytes 786440 | tf_op jit(solution)/shard_map/ppermute | solution.py:534
  17.6 1.6 %copy-done.2 = bf16[512,2048]{1,0:T(8,128)(2,1)S(1)} copy-done((bf16[512,2048]{1,0:T(8,128)(2,1)S(1)}, bf16[512,2048]{1,0:T(8,128)(2,1)}, u32[]{:S(2)}) %copy-start.2) | copy-done | bytes 2097176
  20.2 1.7 %collective-permute-done.3.refs_0_ = bf16[4,64,512]{2,1,0:T(8,128)(2,1)S(1)} collective-permute-done((bf16[4,64,512]{2,1,0:T(8,128)(2,1)S(1)}, bf16[4,64,512]{2,1,0:T(8,128)(2,1)S(1)}, u32[]{:S(2)}, u32[]{:S(2)}) %collective-permute-start.3) | collective-permute-done | bytes 262176 | tf_op jit(solution)/shard_map/ppermute | solution.py:534
  22.1 1.3 %collective-permute-done.5.refs_3_ = bf16[4,64,512]{2,1,0:T(8,128)(2,1)S(1)} collective-permute-done((bf16[4,64,512]{2,1,0:T(8,128)(2,1)S(1)}, bf16[4,64,512]{2,1,0:T(8,128)(2,1)S(1)}, u32[]{:S(2)}, u32[]{:S(2)}) %collective-permute-start.5) | collective-permute-done | bytes 262176 | tf_op jit(solution)/shard_map/ppermute | solution.py:534
  23.4 1.4 %scale_and_pairs.1 = (f32[64,128]{1,0:T(8,128)S(1)}, f32[4,64,256]{2,1,0:T(8,128)S(1)}, s16[528,128]{1,0:T(8,128)(2,1)S(1)}) custom-call(s32[3]{0:T(128)S(1)} %pad_add_fusion.place, f32[16,1,512]{2,1,0:T(1,128)S(1)} %get-tuple-element.30.gain_ref, bf16[512,2048]{1,0:T(8,128)(2,1)S(1)} %get-tuple-element.31.weight_ref, ...), custom_call_target="tpu_custom_call" | custom-call | flops 134217728 | bytes 3145728 | tf_op jit(solution)/shard_map/scale_and_pairs/pallas_call | solution.py:229
  24.8 1.6 %collective-permute-start.6 = (s16[528,128]{1,0:T(8,128)(2,1)S(1)}, s16[528,128]{1,0:T(8,128)(2,1)S(1)}, u32[]{:S(2)}, u32[]{:S(2)}) collective-permute-start(s16[528,128]{1,0:T(8,128)(2,1)S(1)} %get-tuple-element.35), channel_id=1, source_target_pairs={{0,2},{2,0},{1,3},{3,1},{4,6},{6,4},{5,7},{7,5},{8,10},{10,8},{9,1... | collective-permute-start | bytes 405512 | tf_op jit(solution)/shard_map/ppermute | solution.py:534
  26.5 4.6 %queries.1.refs_1_.q_ref = bf16[4,16,512]{2,1,0:T(8,128)(2,1)S(1)} custom-call(s32[3]{0:T(128)S(1)} %pad_add_fusion.place, f32[64,128]{1,0:T(8,128)S(1)} %get-tuple-element.33.scale_ref, f32[16,1,512]{2,1,0:T(1,128)S(1)} %get-tuple-element.30.gain_ref, bf16[8192,512]{1,0:T(8,128)(2,1)} %weight_ref.1, f32[64,128]{1,0:T(8,128)S(1)} %bitcast.13, ...), custom_call_target="tpu_custom_call" | custom-call | flops 536870912 | bytes 8388608 | tf_op jit(solution)/shard_map/queries/pallas_call | solution.py:273
  32.8 3.5 %collective-permute-start.8 = (s16[144,128]{1,0:T(8,128)(2,1)S(1)}, s16[144,128]{1,0:T(8,128)(2,1)S(1)}, u32[]{:S(2)}, u32[]{:S(2)}) collective-permute-start(s16[144,128]{1,0:T(8,128)(2,1)S(1)} %get-tuple-element.38), channel_id=1, source_target_pairs={{0,8},{4,12},{8,0},{12,4},{1,9},{5,13},{9,1},{13,5},{2,10},{6,14},... | collective-permute-start | bytes 110600 | tf_op jit(solution)/shard_map/ppermute | solution.py:534
  37.2 3.3 %copy-done = bf16[512,8192]{1,0:T(8,128)(2,1)} copy-done((bf16[512,8192]{1,0:T(8,128)(2,1)}, bf16[512,8192]{1,0:T(8,128)(2,1)S(1)}, u32[]{:S(2)}) %copy-start) | copy-done | bytes 8388632
  40.5 1.6 %collective-permute-done.9.refs_2_ = s16[144,128]{1,0:T(8,128)(2,1)S(1)} collective-permute-done((s16[144,128]{1,0:T(8,128)(2,1)S(1)}, s16[144,128]{1,0:T(8,128)(2,1)S(1)}, u32[]{:S(2)}, u32[]{:S(2)}) %collective-permute-start.9) | collective-permute-done | bytes 36896 | tf_op jit(solution)/shard_map/ppermute | solution.py:534
  43.9 2.2 %attend.1.x_ref = bf16[4,16,512]{2,1,0:T(8,128)(2,1)S(1)} custom-call(s32[3]{0:T(128)S(1)} %pad_add_fusion.place, s32[4]{0:T(128)S(1)} %copy-done.7, bf16[4,16,512]{2,1,0:T(8,128)(2,1)S(1)} %queries.1.refs_1_.q_ref, f32[64,256]{1,0:T(8,128)S(1)} %fold_pairs.1.refs_1_.mine_ref, f32[64,256]{1,0:T(8,128)S(1)} %collective-permute-done.10.other_ref, ...), custom_call_target="tpu_custom_call" | custom-call | flops 268435456 | bytes 3145728 | tf_op jit(solution)/shard_map/attend/pallas_call | solution.py:350
  46.1 3.4 %copy-done.1 = bf16[512,8192]{1,0:T(8,128)(2,1)S(1)} copy-done((bf16[512,8192]{1,0:T(8,128)(2,1)S(1)}, bf16[512,8192]{1,0:T(8,128)(2,1)}, u32[]{:S(2)}) %copy-start.1) | copy-done | bytes 8388632
  51.4 1.7 %collective-permute-done.17.got_ref = f32[8,64,512]{2,1,0:T(8,128)S(1)} collective-permute-done((f32[8,64,512]{2,1,0:T(8,128)S(1)}, f32[8,64,512]{2,1,0:T(8,128)S(1)}, u32[]{:S(2)}, u32[]{:S(2)}) %collective-permute-start.17) | collective-permute-done | bytes 1048608 | tf_op jit(solution)/shard_map/ppermute | solution.py:534
  53.8 1.2 %collective-permute-start.18 = (s16[528,128]{1,0:T(8,128)(2,1)S(1)}, s16[528,128]{1,0:T(8,128)(2,1)S(1)}, u32[]{:S(2)}, u32[]{:S(2)}) collective-permute-start(s16[528,128]{1,0:T(8,128)(2,1)S(1)} %get-tuple-element.49), channel_id=1, source_target_pairs={{0,2},{2,0},{1,3},{3,1},{4,6},{6,4},{5,7},{7,5},{8,10},{10,8},{9,1... | collective-permute-start | bytes 405512 | tf_op jit(solution)/shard_map/ppermute | solution.py:534
  55.9 4.4 %collective-permute-done.18.refs_0_ = s16[528,128]{1,0:T(8,128)(2,1)S(1)} collective-permute-done((s16[528,128]{1,0:T(8,128)(2,1)S(1)}, s16[528,128]{1,0:T(8,128)(2,1)S(1)}, u32[]{:S(2)}, u32[]{:S(2)}) %collective-permute-start.18) | collective-permute-done | bytes 135200 | tf_op jit(solution)/shard_map/ppermute | solution.py:534
  60.4 2.2 %collective-permute-start.22 = (s16[272,128]{1,0:T(8,128)(2,1)S(1)}, s16[272,128]{1,0:T(8,128)(2,1)S(1)}, u32[]{:S(2)}, u32[]{:S(2)}) collective-permute-start(s16[272,128]{1,0:T(8,128)(2,1)S(1)} %get-tuple-element.54), channel_id=1, source_target_pairs={{0,12},{4,8},{8,4},{12,0},{1,13},{5,9},{9,5},{13,1},{2,14},{6,10},... | collective-permute-start | bytes 208904 | tf_op jit(solution)/shard_map/ppermute | solution.py:534
  62.9 2.6 %collective-permute-start.21 = (s16[272,128]{1,0:T(8,128)(2,1)S(1)}, s16[272,128]{1,0:T(8,128)(2,1)S(1)}, u32[]{:S(2)}, u32[]{:S(2)}) collective-permute-start(s16[272,128]{1,0:T(8,128)(2,1)S(1)} %get-tuple-element.53), channel_id=1, source_target_pairs={{0,8},{4,12},{8,0},{12,4},{1,9},{5,13},{9,1},{13,5},{2,10},{6,14},... | collective-permute-start | bytes 208904 | tf_op jit(solution)/shard_map/ppermute | solution.py:534
  65.5 1.4 %collective-permute-done.22.refs_2_ = s16[272,128]{1,0:T(8,128)(2,1)S(1)} collective-permute-done((s16[272,128]{1,0:T(8,128)(2,1)S(1)}, s16[272,128]{1,0:T(8,128)(2,1)S(1)}, u32[]{:S(2)}, u32[]{:S(2)}) %collective-permute-start.22) | collective-permute-done | bytes 69664 | tf_op jit(solution)/shard_map/ppermute | solution.py:534
  66.9 1.1 %collective-permute-done.20.refs_0_ = s16[272,128]{1,0:T(8,128)(2,1)S(1)} collective-permute-done((s16[272,128]{1,0:T(8,128)(2,1)S(1)}, s16[272,128]{1,0:T(8,128)(2,1)S(1)}, u32[]{:S(2)}, u32[]{:S(2)}) %collective-permute-start.20) | collective-permute-done | bytes 69664 | tf_op jit(solution)/shard_map/ppermute | solution.py:534
  (70 shorter events, 14.1 us)
Async XLA Ops:
  0.0 14.3 %collective-permute-start.2 = (bf16[64,512]{1,0:T(8,128)(2,1)}, bf16[64,512]{1,0:T(8,128)(2,1)S(1)}, u32[]{:S(2)}, u32[]{:S(2)}) collective-permute-start(bf16[64,512]{1,0:T(8,128)(2,1)} %bitcast.17), channel_id=1, source_target_pairs={{0,12},{4,8},{8,4},{12,0},{1,13},{5,9},{9,5},{13,1},{2,14},{6,10},... | collective-permute-start | bytes 196616 | tf_op jit(solution)/shard_map/ppermute | solution.py:534
  5.0 9.2 %collective-permute-start.1 = (bf16[64,512]{1,0:T(8,128)(2,1)}, bf16[64,512]{1,0:T(8,128)(2,1)S(1)}, u32[]{:S(2)}, u32[]{:S(2)}) collective-permute-start(bf16[64,512]{1,0:T(8,128)(2,1)} %bitcast.18), channel_id=1, source_target_pairs={{0,8},{4,12},{8,0},{12,4},{1,9},{5,13},{9,1},{13,5},{2,10},{6,14},... | collective-permute-start | bytes 196616 | tf_op jit(solution)/shard_map/ppermute | solution.py:534
  5.1 9.2 %collective-permute-start = (bf16[64,512]{1,0:T(8,128)(2,1)}, bf16[64,512]{1,0:T(8,128)(2,1)S(1)}, u32[]{:S(2)}, u32[]{:S(2)}) collective-permute-start(bf16[64,512]{1,0:T(8,128)(2,1)} %bitcast.19), channel_id=1, source_target_pairs={{0,4},{4,0},{8,12},{12,8},{1,5},{5,1},{9,13},{13,9},{2,6},{6,2},{1... | collective-permute-start | bytes 196616 | tf_op jit(solution)/shard_map/ppermute | solution.py:534
  9.8 21.4 %collective-permute-start.11 = (bf16[2,128,256]{2,1,0:T(8,128)(2,1)S(1)}, bf16[2,128,256]{2,1,0:T(8,128)(2,1)S(1)}, u32[]{:S(2)}, u32[]{:S(2)}) collective-permute-start(bf16[2,128,256]{2,1,0:T(8,128)(2,1)S(1)} %get-tuple-element.42), channel_id=1, source_target_pairs={{0,4},{4,0},{8,12},{12,8},{1,5},{5,1},{9,13},{13,9},{2,6},{6,2},{1... | collective-permute-start | bytes 393224 | tf_op jit(solution)/shard_map/ppermute | solution.py:534
  11.3 19.9 %collective-permute-start.12 = (bf16[2,128,256]{2,1,0:T(8,128)(2,1)S(1)}, bf16[2,128,256]{2,1,0:T(8,128)(2,1)S(1)}, u32[]{:S(2)}, u32[]{:S(2)}) collective-permute-start(bf16[2,128,256]{2,1,0:T(8,128)(2,1)S(1)} %get-tuple-element.43), channel_id=1, source_target_pairs={{0,8},{4,12},{8,0},{12,4},{1,9},{5,13},{9,1},{13,5},{2,10},{6,14},... | collective-permute-start | bytes 393224 | tf_op jit(solution)/shard_map/ppermute | solution.py:534
  14.3 17.0 %collective-permute-start.13 = (bf16[2,128,256]{2,1,0:T(8,128)(2,1)S(1)}, bf16[2,128,256]{2,1,0:T(8,128)(2,1)S(1)}, u32[]{:S(2)}, u32[]{:S(2)}) collective-permute-start(bf16[2,128,256]{2,1,0:T(8,128)(2,1)S(1)} %get-tuple-element.44), channel_id=1, source_target_pairs={{0,12},{4,8},{8,4},{12,0},{1,13},{5,9},{9,5},{13,1},{2,14},{6,10},... | collective-permute-start | bytes 393224 | tf_op jit(solution)/shard_map/ppermute | solution.py:534
  15.1 6.7 %collective-permute-start.3 = (bf16[4,64,512]{2,1,0:T(8,128)(2,1)S(1)}, bf16[4,64,512]{2,1,0:T(8,128)(2,1)S(1)}, u32[]{:S(2)}, u32[]{:S(2)}) collective-permute-start(bf16[4,64,512]{2,1,0:T(8,128)(2,1)S(1)} %pack.1.refs_2_.refs_0_.rows_ref), channel_id=1, source_target_pairs={{0,2},{2,0},{1,3},{3,1},{4,6},{6,4},{5,7},{7,5},{8,10},{10,8},{9,1... | collective-permute-start | bytes 786440 | tf_op jit(solution)/shard_map/ppermute | solution.py:534
  17.6 4.4 %collective-permute-start.4 = (bf16[4,64,512]{2,1,0:T(8,128)(2,1)S(1)}, bf16[4,64,512]{2,1,0:T(8,128)(2,1)S(1)}, u32[]{:S(2)}, u32[]{:S(2)}) collective-permute-start(bf16[4,64,512]{2,1,0:T(8,128)(2,1)S(1)} %pack.1.refs_2_.refs_0_.rows_ref), channel_id=1, source_target_pairs={{0,1},{1,0},{2,3},{3,2},{4,5},{5,4},{6,7},{7,6},{8,9},{9,8},{10,11... | collective-permute-start | bytes 786440 | tf_op jit(solution)/shard_map/ppermute | solution.py:534
  21.9 1.5 %collective-permute-start.5 = (bf16[4,64,512]{2,1,0:T(8,128)(2,1)S(1)}, bf16[4,64,512]{2,1,0:T(8,128)(2,1)S(1)}, u32[]{:S(2)}, u32[]{:S(2)}) collective-permute-start(bf16[4,64,512]{2,1,0:T(8,128)(2,1)S(1)} %gate.2.refs_1_), channel_id=1, source_target_pairs={{0,1},{1,0},{2,3},{3,2},{4,5},{5,4},{6,7},{7,6},{8,9},{9,8},{10,11... | collective-permute-start | bytes 786440 | tf_op jit(solution)/shard_map/ppermute | solution.py:534
  24.8 6.3 %collective-permute-start.6 = (s16[528,128]{1,0:T(8,128)(2,1)S(1)}, s16[528,128]{1,0:T(8,128)(2,1)S(1)}, u32[]{:S(2)}, u32[]{:S(2)}) collective-permute-start(s16[528,128]{1,0:T(8,128)(2,1)S(1)} %get-tuple-element.35), channel_id=1, source_target_pairs={{0,2},{2,0},{1,3},{3,1},{4,6},{6,4},{5,7},{7,5},{8,10},{10,8},{9,1... | collective-permute-start | bytes 405512 | tf_op jit(solution)/shard_map/ppermute | solution.py:534
  26.5 17.4 %copy-start.7 = (s32[4]{0:T(128)S(1)}, s32[4]{0:T(128)}, u32[]{:S(2)}) copy-start(s32[4]{0:T(128)} %lengths.1) | copy-start | bytes 52
  31.3 10.8 %collective-permute-start.14 = (bf16[4,128,256]{2,1,0:T(8,128)(2,1)S(1)}, bf16[4,128,256]{2,1,0:T(8,128)(2,1)S(1)}, u32[]{:S(2)}, u32[]{:S(2)}) collective-permute-start(bf16[4,128,256]{2,1,0:T(8,128)(2,1)S(1)} %get-tuple-element.46), channel_id=1, source_target_pairs={{0,2},{2,0},{1,3},{3,1},{4,6},{6,4},{5,7},{7,5},{8,10},{10,8},{9,1... | collective-permute-start | bytes 786440 | tf_op jit(solution)/shard_map/ppermute | solution.py:534
  32.2 8.3 %collective-permute-start.7 = (s16[144,128]{1,0:T(8,128)(2,1)S(1)}, s16[144,128]{1,0:T(8,128)(2,1)S(1)}, u32[]{:S(2)}, u32[]{:S(2)}) collective-permute-start(s16[144,128]{1,0:T(8,128)(2,1)S(1)} %get-tuple-element.37), channel_id=1, source_target_pairs={{0,4},{4,0},{8,12},{12,8},{1,5},{5,1},{9,13},{13,9},{2,6},{6,2},{1... | collective-permute-start | bytes 110600 | tf_op jit(solution)/shard_map/ppermute | solution.py:534
  32.8 7.7 %collective-permute-start.8 = (s16[144,128]{1,0:T(8,128)(2,1)S(1)}, s16[144,128]{1,0:T(8,128)(2,1)S(1)}, u32[]{:S(2)}, u32[]{:S(2)}) collective-permute-start(s16[144,128]{1,0:T(8,128)(2,1)S(1)} %get-tuple-element.38), channel_id=1, source_target_pairs={{0,8},{4,12},{8,0},{12,4},{1,9},{5,13},{9,1},{13,5},{2,10},{6,14},... | collective-permute-start | bytes 110600 | tf_op jit(solution)/shard_map/ppermute | solution.py:534
  36.3 5.8 %collective-permute-start.9 = (s16[144,128]{1,0:T(8,128)(2,1)S(1)}, s16[144,128]{1,0:T(8,128)(2,1)S(1)}, u32[]{:S(2)}, u32[]{:S(2)}) collective-permute-start(s16[144,128]{1,0:T(8,128)(2,1)S(1)} %get-tuple-element.39), channel_id=1, source_target_pairs={{0,12},{4,8},{8,4},{12,0},{1,13},{5,9},{9,5},{13,1},{2,14},{6,10},... | collective-permute-start | bytes 110600 | tf_op jit(solution)/shard_map/ppermute | solution.py:534
  40.5 3.4 %collective-permute-start.15 = (bf16[4,128,256]{2,1,0:T(8,128)(2,1)S(1)}, bf16[4,128,256]{2,1,0:T(8,128)(2,1)S(1)}, u32[]{:S(2)}, u32[]{:S(2)}) collective-permute-start(bf16[4,128,256]{2,1,0:T(8,128)(2,1)S(1)} %get-tuple-element.45.refs_0_), channel_id=1, source_target_pairs={{0,1},{1,0},{2,3},{3,2},{4,5},{5,4},{6,7},{7,6},{8,9},{9,8},{10,11... | collective-permute-start | bytes 786440 | tf_op jit(solution)/shard_map/ppermute | solution.py:534
  42.2 1.7 %collective-permute-start.16 = (bf16[4,128,256]{2,1,0:T(8,128)(2,1)S(1)}, bf16[4,128,256]{2,1,0:T(8,128)(2,1)S(1)}, u32[]{:S(2)}, u32[]{:S(2)}) collective-permute-start(bf16[4,128,256]{2,1,0:T(8,128)(2,1)S(1)} %gate.3.refs_1_), channel_id=1, source_target_pairs={{0,1},{1,0},{2,3},{3,2},{4,5},{5,4},{6,7},{7,6},{8,9},{9,8},{10,11... | collective-permute-start | bytes 786440 | tf_op jit(solution)/shard_map/ppermute | solution.py:534
  42.2 1.6 %collective-permute-start.10 = (f32[64,256]{1,0:T(8,128)S(1)}, f32[64,256]{1,0:T(8,128)S(1)}, u32[]{:S(2)}, u32[]{:S(2)}) collective-permute-start(f32[64,256]{1,0:T(8,128)S(1)} %fold_pairs.1.refs_1_.mine_ref), channel_id=1, source_target_pairs={{0,1},{1,0},{2,3},{3,2},{4,5},{5,4},{6,7},{7,6},{8,9},{9,8},{10,11... | collective-permute-start | bytes 196616 | tf_op jit(solution)/shard_map/ppermute | solution.py:534
  50.3 2.7 %collective-permute-start.17 = (f32[8,64,512]{2,1,0:T(8,128)S(1)}, f32[8,64,512]{2,1,0:T(8,128)S(1)}, u32[]{:S(2)}, u32[]{:S(2)}) collective-permute-start(f32[8,64,512]{2,1,0:T(8,128)S(1)} %outputs.3), channel_id=1, source_target_pairs={{0,1},{1,0},{2,3},{3,2},{4,5},{5,4},{6,7},{7,6},{8,9},{9,8},{10,11... | collective-permute-start | bytes 3145736 | tf_op jit(solution)/shard_map/ppermute | solution.py:534
  53.8 6.5 %collective-permute-start.18 = (s16[528,128]{1,0:T(8,128)(2,1)S(1)}, s16[528,128]{1,0:T(8,128)(2,1)S(1)}, u32[]{:S(2)}, u32[]{:S(2)}) collective-permute-start(s16[528,128]{1,0:T(8,128)(2,1)S(1)} %get-tuple-element.49), channel_id=1, source_target_pairs={{0,2},{2,0},{1,3},{3,1},{4,6},{6,4},{5,7},{7,5},{8,10},{10,8},{9,1... | collective-permute-start | bytes 405512 | tf_op jit(solution)/shard_map/ppermute | solution.py:534
  55.1 7.6 %collective-permute-start.19 = (s16[528,128]{1,0:T(8,128)(2,1)S(1)}, s16[528,128]{1,0:T(8,128)(2,1)S(1)}, u32[]{:S(2)}, u32[]{:S(2)}) collective-permute-start(s16[528,128]{1,0:T(8,128)(2,1)S(1)} %get-tuple-element.51), channel_id=1, source_target_pairs={{0,2},{2,0},{1,3},{3,1},{4,6},{6,4},{5,7},{7,5},{8,10},{10,8},{9,1... | collective-permute-start | bytes 405512 | tf_op jit(solution)/shard_map/ppermute | solution.py:534
  60.4 6.5 %collective-permute-start.22 = (s16[272,128]{1,0:T(8,128)(2,1)S(1)}, s16[272,128]{1,0:T(8,128)(2,1)S(1)}, u32[]{:S(2)}, u32[]{:S(2)}) collective-permute-start(s16[272,128]{1,0:T(8,128)(2,1)S(1)} %get-tuple-element.54), channel_id=1, source_target_pairs={{0,12},{4,8},{8,4},{12,0},{1,13},{5,9},{9,5},{13,1},{2,14},{6,10},... | collective-permute-start | bytes 208904 | tf_op jit(solution)/shard_map/ppermute | solution.py:534
  62.8 5.3 %collective-permute-start.20 = (s16[272,128]{1,0:T(8,128)(2,1)S(1)}, s16[272,128]{1,0:T(8,128)(2,1)S(1)}, u32[]{:S(2)}, u32[]{:S(2)}) collective-permute-start(s16[272,128]{1,0:T(8,128)(2,1)S(1)} %get-tuple-element.52), channel_id=1, source_target_pairs={{0,4},{4,0},{8,12},{12,8},{1,5},{5,1},{9,13},{13,9},{2,6},{6,2},{1... | collective-permute-start | bytes 208904 | tf_op jit(solution)/shard_map/ppermute | solution.py:534
  62.9 5.6 %collective-permute-start.21 = (s16[272,128]{1,0:T(8,128)(2,1)S(1)}, s16[272,128]{1,0:T(8,128)(2,1)S(1)}, u32[]{:S(2)}, u32[]{:S(2)}) collective-permute-start(s16[272,128]{1,0:T(8,128)(2,1)S(1)} %get-tuple-element.53), channel_id=1, source_target_pairs={{0,8},{4,12},{8,0},{12,4},{1,9},{5,13},{9,1},{13,5},{2,10},{6,14},... | collective-permute-start | bytes 208904 | tf_op jit(solution)/shard_map/ppermute | solution.py:534
  (9 other events, 38.6 us)

commit v7 on v6

--- a/solution.py
+++ b/solution.py
@@ -87,8 +87,9 @@
     )(*arrays, *after)
 
 
-def pages_kernel(table, place, scales, page_ref, *out_refs):
+def pages_kernel(table, place, scales, page_ref, rows_ref, rows_out_ref, *out_refs):
     e = pl.program_id(0)
+    rows_out_ref[...] = rows_ref[...]
     subs = out_refs[0].shape[0]
     targets = 2 * subs
     page = table[place[0], e * targets + place[1]] - place[2]
@@ -105,7 +106,7 @@
                 ).astype(jnp.bfloat16)
 
 
-def used_pages(pages, scales, table, place, subs):
+def used_pages(pages, scales, table, place, subs, rows):
     targets = 2 * subs
     entries = table.shape[1] // targets
     shape = jax.ShapeDtypeStruct((subs, entries * PAGE_TOKENS, PAIR), jnp.bfloat16)
@@ -122,18 +123,20 @@
                         0,
                         0,
                     ),
-                )
+                ),
+                pl.BlockSpec(rows.shape, lambda e, *_: (0, 0)),
             ],
-            out_specs=[pl.BlockSpec((subs, PAGE_TOKENS, PAIR), lambda e, *_: (0, e, 0))]
+            out_specs=[pl.BlockSpec(rows.shape, lambda e, *_: (0, 0))]
+            + [pl.BlockSpec((subs, PAGE_TOKENS, PAIR), lambda e, *_: (0, e, 0))]
             * GROUP_REQUESTS,
         ),
-        out_shape=[shape] * GROUP_REQUESTS,
+        out_shape=[jax.ShapeDtypeStruct(rows.shape, rows.dtype)] + [shape] * GROUP_REQUESTS,
         compiler_params=params(),
         cost_estimate=pl.CostEstimate(
             flops=0, bytes_accessed=4 * entries * PAGE_TOKENS * pages.shape[2], transcendentals=0
         ),
         name="used_pages",
-    )(table, place, scales.astype(jnp.float32), pages)
+    )(table, place, scales.astype(jnp.float32), pages, rows)
 
 
 def regroup_kernel(*refs):
@@ -360,11 +363,15 @@
     )(place, lengths, query, mine, other, cosine, sine, *caches)
 
 
-def output_kernel(place, x_ref, weight_ref, out_ref):
+def output_kernel(away, subs, shifts, place, x_ref, weight_ref, *refs):
+    out_ref = refs[-1]
     blocks, rows, width = out_ref.shape
+    core = 1 - place[2] if away else place[2]
     x = x_ref[...].reshape(rows, -1)
     for i in range(blocks):
-        columns = pl.ds(pl.multiple_of((2 * i + place[0]) * width, width), width)
+        z, shift = i % GROUP_REQUESTS, shifts[i // GROUP_REQUESTS]
+        block = ((place[0] ^ z) * subs + (place[1] ^ shift)) * 2 + core
+        columns = pl.ds(pl.multiple_of(block * width, width), width)
         part = jnp.dot(x, weight_ref[:, columns], preferred_element_type=jnp.float32)
         for r in range(GROUP_REQUESTS):
             for step in range(STEPS):
@@ -373,19 +380,21 @@
                 out_ref[i, target : target + SAMPLES] = part[source : source + SAMPLES]
 
 
-def outputs(place, mixed, weight, blocks):
+def outputs(place, mixed, weight, away, subs, shifts, after=()):
     rows = GROUP_REQUESTS * ROWS
-    width = weight.shape[1] // (2 * blocks)
-    return pl.pallas_call(
-        output_kernel,
+    width = weight.shape[1] // (2 * GROUP_REQUESTS * subs)
+    blocks = GROUP_REQUESTS * len(shifts)
+    return pl.pallas_call(
+        functools.partial(output_kernel, away, subs, shifts),
         in_specs=[pl.BlockSpec(memory_space=pltpu.SMEM)]
-        + [pl.BlockSpec(memory_space=pltpu.VMEM)] * 2,
+        + [pl.BlockSpec(memory_space=pltpu.VMEM)] * 2
+        + unread(after),
         out_specs=pl.BlockSpec(memory_space=pltpu.VMEM),
         out_shape=jax.ShapeDtypeStruct((blocks, rows, width), jnp.float32),
         compiler_params=params(),
-        cost_estimate=cost([weight], flops=rows * weight.size),
+        cost_estimate=cost([mixed], flops=2 * rows * mixed.shape[2] * blocks * width),
         name="outputs",
-    )(place, mixed, weight)
+    )(place, mixed, weight, *after)
 
 
 def pieces_of(block):
@@ -417,44 +426,39 @@
     return ref[pl.ds(first, rows)].astype(jnp.int32).astype(jnp.float32) * step
 
 
-def fold_core_kernel(place, mine_ref, got_ref, kept_ref, *out_refs):
-    subs = 1 + len(out_refs) // 2
-    for shift in range(subs):
-        sub = place[1] ^ shift
-        for half in range(2):
-            pieces = []
-            for z in HALVES[half]:
-                block = (place[0] ^ z) * subs + sub
-                block = mine_ref[block] + got_ref[block]
-                if shift == 0:
-                    kept_ref[z] = block
-                pieces += pieces_of(block)
-            if shift:
-                encode(out_refs[(shift - 1) * 2 + half], pieces)
-
-
-def fold_core(place, mine, got, subs):
-    _, rows, width = mine.shape
-    kept = jax.ShapeDtypeStruct((GROUP_REQUESTS, rows, width), jnp.float32)
+def fold_core_kernel(mine_ref, got_ref, *out_refs):
+    for i, out_ref in enumerate(out_refs):
+        pieces = []
+        for z in HALVES[i % 2]:
+            block = i // 2 * GROUP_REQUESTS + z
+            pieces += pieces_of(mine_ref[block] + got_ref[block])
+        encode(out_ref, pieces)
+
+
+def fold_core(mine, got):
+    blocks, rows, width = mine.shape
+    count = 2 * (blocks // GROUP_REQUESTS)
     sent = jax.ShapeDtypeStruct((2 * width // LANES * rows + TAIL, LANES), jnp.int16)
     return pl.pallas_call(
         fold_core_kernel,
-        in_specs=[pl.BlockSpec(memory_space=pltpu.SMEM)]
-        + [pl.BlockSpec(memory_space=pltpu.VMEM)] * 2,
-        out_specs=[pl.BlockSpec(memory_space=pltpu.VMEM)] * (2 * subs - 1),
-        out_shape=[kept] + [sent] * (2 * subs - 2),
+        in_specs=[pl.BlockSpec(memory_space=pltpu.VMEM)] * 2,
+        out_specs=[pl.BlockSpec(memory_space=pltpu.VMEM)] * count,
+        out_shape=[sent] * count,
         compiler_params=params(),
         cost_estimate=cost([mine, got]),
         name="fold_core",
-    )(place, mine, got)
-
-
-def fold_sub_kernel(order, count, kept_ref, *refs):
-    in_refs, out_refs = refs[:count], refs[-len(order) :]
-    _, rows, width = kept_ref.shape
+    )(mine, got)
+
+
+def fold_sub_kernel(order, count, own, *refs):
+    own_refs, in_refs, out_refs = refs[:own], refs[own : own + count], refs[-len(order) :]
+    _, rows, width = own_refs[0].shape
     steps = [step_of(ref) for ref in in_refs]
     for i, (z, out_ref) in enumerate(zip(order, out_refs)):
-        pieces = pieces_of(kept_ref[z])
+        block = own_refs[0][z]
+        for ref in own_refs[1:]:
+            block = block + ref[z]
+        pieces = pieces_of(block)
         for c in range(len(pieces)):
             for ref, step in zip(in_refs, steps):
                 first = (i * len(pieces) + c) * rows
@@ -466,19 +470,20 @@
                 out_ref[:, c * LANES : (c + 1) * LANES] = piece
 
 
-def fold_sub(order, kept, parts, after=()):
-    _, rows, width = kept.shape
+def fold_sub(order, own, parts, after=()):
+    _, rows, width = own[0].shape
     total = jax.ShapeDtypeStruct((rows, width), jnp.float32)
     sent = jax.ShapeDtypeStruct((width // LANES * rows + TAIL, LANES), jnp.int16)
     return pl.pallas_call(
-        functools.partial(fold_sub_kernel, order, len(parts)),
-        in_specs=[pl.BlockSpec(memory_space=pltpu.VMEM)] * (1 + len(parts)) + unread(after),
+        functools.partial(fold_sub_kernel, order, len(parts), len(own)),
+        in_specs=[pl.BlockSpec(memory_space=pltpu.VMEM)] * (len(own) + len(parts))
+        + unread(after),
         out_specs=[pl.BlockSpec(memory_space=pltpu.VMEM)] * len(order),
         out_shape=[sent if z else total for z in order],
         compiler_params=params(),
-        cost_estimate=cost([kept], parts),
+        cost_estimate=cost(own, parts),
         name="fold_sub",
-    )(kept, *parts, *after)
+    )(*own, *parts, *after)
 
 
 def fold_pairs_kernel(count, total_ref, *refs):
@@ -559,10 +564,12 @@
     place = scalars(request, sub, core)
 
     rows = hidden.reshape(GROUP_REQUESTS * ROWS, width)
-    column = [rows] + [passed(rows, "req", s) for s in range(1, GROUP_REQUESTS)]
+    column = [passed(rows, "req", s) for s in range(1, GROUP_REQUESTS)]
     where = scalars(request, sub * 2 + core, device * prompt_cache_pages.shape[0])
-    pages = list(used_pages(prompt_cache_pages, per_page_scales, block_table, where, subs))
-    column = pack(column)
+    rows, *pages = used_pages(
+        prompt_cache_pages, per_page_scales, block_table, where, subs, rows
+    )
+    column = pack([rows] + column)
     gathered = [passed(column, "sub", s) for s in range(1, subs)]
     pages[1:] = [passed(pages[s], "req", s) for s in range(1, GROUP_REQUESTS)]
     gain, key_value_weight, ready = staged(
@@ -586,7 +593,7 @@
     scale, kept, *parts = scale_and_pairs(place, gain, key_value_weight, gathered)
     parts = [passed(part, "sub", s + 1) for s, part in enumerate(parts)]
     query = queries(place, scale, gain, w_query, cosine, sine, gathered)
-    total, *parts = fold_sub((0, 1, 2, 3), kept, parts, after=[query])
+    total, *parts = fold_sub((0, 1, 2, 3), [kept], parts, after=[query])
     parts = [passed(part, "req", s + 1) for s, part in enumerate(parts)]
     pages = regroup(pages, after=[total])
     caches = [passed(pages[s], "sub", s) for s in range(1, subs)]
@@ -600,14 +607,18 @@
         place, lengths.astype(jnp.int32), query, mine, other, cosine, sine, caches
     )
 
-    away = outputs(scalars(1 - core), mixed, w_output, devices // 2)
-    arrived = passed(away, "section", 1)
-    kept = outputs(scalars(core), mixed, w_output, devices // 2)
-    kept, *parts = fold_core(place, kept, arrived, subs)
+    others = tuple(range(1, subs))
+    first = outputs(place, mixed, w_output, True, subs, others)
+    got_first = passed(first, "section", 1)
+    second = outputs(place, mixed, w_output, True, subs, (0,), after=[first])
+    got_second = passed(second, "section", 1)
+    kept = outputs(place, mixed, w_output, False, subs, others, after=[second])
+    parts = fold_core(kept, got_first)
+    kept = outputs(place, mixed, w_output, False, subs, (0,), after=parts[:1])
     parts = [passed(part, "sub", i // 2 + 1) for i, part in enumerate(parts)]
     last = {}
     for half, order in enumerate(HALVES):
-        last.update(zip(order, fold_sub(order, kept, parts[half::2])))
+        last.update(zip(order, fold_sub(order, [kept, got_second], parts[half::2])))
     parts = [passed(last[s], "req", s) for s in range(1, GROUP_REQUESTS)]
     return finish(gathered[0], last[0], parts).reshape(hidden.shape)
 

time: 69.6 us -> 66.1 us (0.950)
  local copies, waits for them, and re-layouts: 11.8 us -> 5.12 us
  Pallas kernels: 14.1 us -> 16 us
  waiting for transfers between devices: 14.9 us -> 16.5 us
    unnamed x20 -> x16, local copies, waits for them, and re-layouts: 11.7 us -> 5.11 us
    pallas_call x5 -> x7, Pallas kernels: 2.04 us -> 4.49 us  [the longest x4 4.13 us: outputs(): pl.pallas_call(functools.partial(output_kernel, away, subs, shifts), in_s...]
    ppermute x23 -> x24, waiting for transfers between devices: 14.9 us -> 16.5 us  [passed(): lax.ppermute(array, axis, [(i, i ^ shift) for i in range(lax.axis_size(ax...]
    ppermute x23 -> x24, starting transfers between devices: 26.6 us -> 26.1 us  [passed(): lax.ppermute(array, axis, [(i, i ^ shift) for i in range(lax.axis_size(ax...]
  transfers between devices with their start and end apart: 23 -> 24, of which waited for: 9 -> 9; matrix products, arithmetic and copies ran while one was open for 2% -> 3% of each run, Pallas kernels for 14% -> 18%
where the time goes in v7:
time: 66.1 us; the launch traced here: 65.7 us
  starting transfers between devices  26.1 us (39%)
  waiting for transfers between devices  16.5 us (25%)
  Pallas kernels  16 us (24%)
  local copies, waits for them, and re-layouts  5.12 us (8%)
  other arithmetic  1.71 us (3%)
    ppermute x24, starting transfers between devices, passed(): lax.ppermute(array, axis, [(i, i ^ shift) for i in range(lax.axis_size(ax...  26.1 us
    ppermute x24, waiting for transfers between devices, passed(): lax.ppermute(array, axis, [(i, i ^ shift) for i in range(lax.axis_size(ax...  16.5 us
    unnamed x16, local copies, waits for them, and re-layouts  5.11 us
    pallas_call x1, Pallas kernels, queries(): pl.pallas_call(query_kernel, in_specs=[pl.BlockSpec(memory_space=pltpu.SM...  4.63 us
    pallas_call x4, Pallas kernels, outputs(): pl.pallas_call(functools.partial(output_kernel, away, subs, shifts), in_s...  4.13 us
    pallas_call x1, Pallas kernels, attend(): pl.pallas_call(attend_kernel, in_specs=[pl.BlockSpec(memory_space=pltpu.S...  2.18 us
    pallas_call x1, Pallas kernels, used_pages(): pl.pallas_call(pages_kernel, grid_spec=pltpu.PrefetchScalarGridSpec(num_s...  1.51 us
    pallas_call x1, Pallas kernels, scale_and_pairs(): pl.pallas_call(pairs_kernel, in_specs=[pl.BlockSpec(memory_space=pltpu.SM...  1.37 us
  transfers between devices with their start and end apart: 24, of which 9 were waited for; matrix products, arithmetic and copies ran while one was open for 3% of the time, Pallas kernels for 18%

profile of v7, /device:TPU:0, one launch (start us, length us, event | category | flops | bytes accessed | tf_op | source)
XLA Modules:
  0.0 65.7 jit_solution(13854586766503480811)
XLA Ops:
  0.0 5.0 %collective-permute-start.2 = (bf16[64,512]{1,0:T(8,128)(2,1)}, bf16[64,512]{1,0:T(8,128)(2,1)S(1)}, u32[]{:S(2)}, u32[]{:S(2)}) collective-permute-start(bf16[64,512]{1,0:T(8,128)(2,1)} %bitcast.16), channel_id=1, source_target_pairs={{0,12},{4,8},{8,4},{12,0},{1,13},{5,9},{9,5},{13,1},{2,14},{6,10},... | collective-permute-start | bytes 196616 | tf_op jit(solution)/shard_map/ppermute | solution.py:539
  6.4 1.2 %copy-done.1 = bf16[16,16,2048]{2,1,0:T(8,128)(2,1)S(1)} copy-done((bf16[16,16,2048]{2,1,0:T(8,128)(2,1)S(1)}, bf16[16,16,2048]{2,1,0:T(8,128)(2,1)}, u32[]{:S(2)}) %copy-start.1) | copy-done | bytes 1048600
  9.1 1.5 %used_pages.1 = (bf16[64,512]{1,0:T(8,128)(2,1)S(1)}, bf16[2,128,256]{2,1,0:T(8,128)(2,1)S(1)}, bf16[2,128,256]{2,1,0:T(8,128)(2,1)S(1)}, bf16[2,128,256]{2,1,0:T(8,128)(2,1)S(1)}, bf16[2,128,256]{2,1,0:T(8,128)(2,1)S(1)}) custom-call(s32[4,32]{1,0:T(4,128)S(1)} %copy-done.4, s32[3]{0:T(128)S(1)} %pad_add_fusion.place, ...), custom_call_target="tpu_custom_call" | custom-call | bytes 1048576 | tf_op jit(solution)/shard_map/used_pages/pallas_call | solution.py:113
  10.7 1.5 %collective-permute-start.11 = (bf16[2,128,256]{2,1,0:T(8,128)(2,1)S(1)}, bf16[2,128,256]{2,1,0:T(8,128)(2,1)S(1)}, u32[]{:S(2)}, u32[]{:S(2)}) collective-permute-start(bf16[2,128,256]{2,1,0:T(8,128)(2,1)S(1)} %get-tuple-element.43), channel_id=1, source_target_pairs={{0,4},{4,0},{8,12},{12,8},{1,5},{5,1},{9,13},{13,9},{2,6},{6,2},{1... | collective-permute-start | bytes 393224 | tf_op jit(solution)/shard_map/ppermute | solution.py:539
  12.2 2.9 %collective-permute-start.12 = (bf16[2,128,256]{2,1,0:T(8,128)(2,1)S(1)}, bf16[2,128,256]{2,1,0:T(8,128)(2,1)S(1)}, u32[]{:S(2)}, u32[]{:S(2)}) collective-permute-start(bf16[2,128,256]{2,1,0:T(8,128)(2,1)S(1)} %get-tuple-element.44), channel_id=1, source_target_pairs={{0,8},{4,12},{8,0},{12,4},{1,9},{5,13},{9,1},{13,5},{2,10},{6,14},... | collective-permute-start | bytes 393224 | tf_op jit(solution)/shard_map/ppermute | solution.py:539
  15.2 1.8 %collective-permute-start.3 = (bf16[4,64,512]{2,1,0:T(8,128)(2,1)S(1)}, bf16[4,64,512]{2,1,0:T(8,128)(2,1)S(1)}, u32[]{:S(2)}, u32[]{:S(2)}) collective-permute-start(bf16[4,64,512]{2,1,0:T(8,128)(2,1)S(1)} %pack.1.refs_2_.refs_0_.rows_ref), channel_id=1, source_target_pairs={{0,2},{2,0},{1,3},{3,1},{4,6},{6,4},{5,7},{7,5},{8,10},{10,8},{9,1... | collective-permute-start | bytes 786440 | tf_op jit(solution)/shard_map/ppermute | solution.py:539
  17.6 1.6 %copy-done = bf16[512,2048]{1,0:T(8,128)(2,1)S(1)} copy-done((bf16[512,2048]{1,0:T(8,128)(2,1)S(1)}, bf16[512,2048]{1,0:T(8,128)(2,1)}, u32[]{:S(2)}) %copy-start) | copy-done | bytes 2097176
  20.2 1.7 %collective-permute-done.3.refs_0_ = bf16[4,64,512]{2,1,0:T(8,128)(2,1)S(1)} collective-permute-done((bf16[4,64,512]{2,1,0:T(8,128)(2,1)S(1)}, bf16[4,64,512]{2,1,0:T(8,128)(2,1)S(1)}, u32[]{:S(2)}, u32[]{:S(2)}) %collective-permute-start.3) | collective-permute-done | bytes 262176 | tf_op jit(solution)/shard_map/ppermute | solution.py:539
  22.1 1.3 %collective-permute-done.5.refs_3_ = bf16[4,64,512]{2,1,0:T(8,128)(2,1)S(1)} collective-permute-done((bf16[4,64,512]{2,1,0:T(8,128)(2,1)S(1)}, bf16[4,64,512]{2,1,0:T(8,128)(2,1)S(1)}, u32[]{:S(2)}, u32[]{:S(2)}) %collective-permute-start.5) | collective-permute-done | bytes 262176 | tf_op jit(solution)/shard_map/ppermute | solution.py:539
  23.4 1.4 %scale_and_pairs.1 = (f32[64,128]{1,0:T(8,128)S(1)}, f32[4,64,256]{2,1,0:T(8,128)S(1)}, s16[528,128]{1,0:T(8,128)(2,1)S(1)}) custom-call(s32[3]{0:T(128)S(1)} %pad_add_fusion.1.place, f32[16,1,512]{2,1,0:T(1,128)S(1)} %get-tuple-element.31.gain_ref, bf16[512,2048]{1,0:T(8,128)(2,1)S(1)} %get-tuple-element.32.weight_ref, ...), custom_call_target="tpu_custom_call" | custom-call | flops 134217728 | bytes 3145728 | tf_op jit(solution)/shard_map/scale_and_pairs/pallas_call | solution.py:232
  24.8 1.6 %collective-permute-start.6 = (s16[528,128]{1,0:T(8,128)(2,1)S(1)}, s16[528,128]{1,0:T(8,128)(2,1)S(1)}, u32[]{:S(2)}, u32[]{:S(2)}) collective-permute-start(s16[528,128]{1,0:T(8,128)(2,1)S(1)} %get-tuple-element.36), channel_id=1, source_target_pairs={{0,2},{2,0},{1,3},{3,1},{4,6},{6,4},{5,7},{7,5},{8,10},{10,8},{9,1... | collective-permute-start | bytes 405512 | tf_op jit(solution)/shard_map/ppermute | solution.py:539
  26.5 4.6 %queries.1.refs_2_.refs_1_.q_ref = bf16[4,16,512]{2,1,0:T(8,128)(2,1)S(1)} custom-call(s32[3]{0:T(128)S(1)} %pad_add_fusion.1.place, f32[64,128]{1,0:T(8,128)S(1)} %get-tuple-element.34.scale_ref, f32[16,1,512]{2,1,0:T(1,128)S(1)} %get-tuple-element.31.gain_ref, bf16[8192,512]{1,0:T(8,128)(2,1)} %weight_ref.1, f32[64,128]{1,0:T(8,128)S(1)} %bitcast.12, ...), custom_call_target="tpu_custom_call" | custom-call | flops 536870912 | bytes 8388608 | tf_op jit(solution)/shard_map/queries/pallas_call | solution.py:276
  32.8 3.5 %collective-permute-start.8 = (s16[144,128]{1,0:T(8,128)(2,1)S(1)}, s16[144,128]{1,0:T(8,128)(2,1)S(1)}, u32[]{:S(2)}, u32[]{:S(2)}) collective-permute-start(s16[144,128]{1,0:T(8,128)(2,1)S(1)} %get-tuple-element.39), channel_id=1, source_target_pairs={{0,8},{4,12},{8,0},{12,4},{1,9},{5,13},{9,1},{13,5},{2,10},{6,14},... | collective-permute-start | bytes 110600 | tf_op jit(solution)/shard_map/ppermute | solution.py:539
  37.3 1.4 %collective-permute-done.8.refs_1_ = s16[144,128]{1,0:T(8,128)(2,1)S(1)} collective-permute-done((s16[144,128]{1,0:T(8,128)(2,1)S(1)}, s16[144,128]{1,0:T(8,128)(2,1)S(1)}, u32[]{:S(2)}, u32[]{:S(2)}) %collective-permute-start.8) | collective-permute-done | bytes 36896 | tf_op jit(solution)/shard_map/ppermute | solution.py:539
  38.7 3.4 %collective-permute-done.9.refs_2_ = s16[144,128]{1,0:T(8,128)(2,1)S(1)} collective-permute-done((s16[144,128]{1,0:T(8,128)(2,1)S(1)}, s16[144,128]{1,0:T(8,128)(2,1)S(1)}, u32[]{:S(2)}, u32[]{:S(2)}) %collective-permute-start.9) | collective-permute-done | bytes 36896 | tf_op jit(solution)/shard_map/ppermute | solution.py:539
  42.7 1.1 %collective-permute-done.10.other_ref = f32[64,256]{1,0:T(8,128)S(1)} collective-permute-done((f32[64,256]{1,0:T(8,128)S(1)}, f32[64,256]{1,0:T(8,128)S(1)}, u32[]{:S(2)}, u32[]{:S(2)}) %collective-permute-start.10) | collective-permute-done | bytes 65568 | tf_op jit(solution)/shard_map/ppermute | solution.py:539
  43.9 2.2 %attend.1.x_ref = bf16[4,16,512]{2,1,0:T(8,128)(2,1)S(1)} custom-call(s32[3]{0:T(128)S(1)} %pad_add_fusion.1.place, s32[4]{0:T(128)S(1)} %copy-done.5, bf16[4,16,512]{2,1,0:T(8,128)(2,1)S(1)} %queries.1.refs_2_.refs_1_.q_ref, f32[64,256]{1,0:T(8,128)S(1)} %fold_pairs.1.refs_1_.mine_ref, f32[64,256]{1,0:T(8,128)S(1)} %collective-permute-done.10.other_ref, ...), custom_call_target="tpu_custom_call" | custom-call | flops 268435456 | bytes 3145728 | tf_op jit(solution)/shard_map/attend/pallas_call | solution.py:353
  46.1 1.0 %outputs.4.refs_0_ = f32[4,64,512]{2,1,0:T(8,128)S(1)} custom-call(s32[3]{0:T(128)S(1)} %pad_add_fusion.1.place, bf16[4,16,512]{2,1,0:T(8,128)(2,1)S(1)} %attend.1.x_ref, bf16[512,8192]{1,0:T(8,128)(2,1)S(1)} %get-tuple-element.48.weight_ref), custom_call_target="tpu_custom_call" | custom-call | flops 134217728 | bytes 65536 | tf_op jit(solution)/shard_map/outputs/pallas_call | solution.py:387
  50.1 1.2 %collective-permute-start.20 = (s16[528,128]{1,0:T(8,128)(2,1)S(1)}, s16[528,128]{1,0:T(8,128)(2,1)S(1)}, u32[]{:S(2)}, u32[]{:S(2)}) collective-permute-start(s16[528,128]{1,0:T(8,128)(2,1)S(1)} %get-tuple-element.51), channel_id=1, source_target_pairs={{0,2},{2,0},{1,3},{3,1},{4,6},{6,4},{5,7},{7,5},{8,10},{10,8},{9,1... | collective-permute-start | bytes 405512 | tf_op jit(solution)/shard_map/ppermute | solution.py:539
  52.1 1.0 %outputs.7.refs_0_ = f32[4,64,512]{2,1,0:T(8,128)S(1)} custom-call(s32[3]{0:T(128)S(1)} %pad_add_fusion.1.place, bf16[4,16,512]{2,1,0:T(8,128)(2,1)S(1)} %attend.1.x_ref, bf16[512,8192]{1,0:T(8,128)(2,1)S(1)} %get-tuple-element.48.weight_ref, s16[528,128]{1,0:T(8,128)(2,1)S(1)} %get-tuple-element.49.refs_0_), custom_call_target="tpu_custom_call" | custom-call | flops 134217728 | bytes 65536 | tf_op jit(solution)/shard_map/outputs/pallas_call | solution.py:387
  53.2 3.4 %collective-permute-done.20.refs_2_ = s16[528,128]{1,0:T(8,128)(2,1)S(1)} collective-permute-done((s16[528,128]{1,0:T(8,128)(2,1)S(1)}, s16[528,128]{1,0:T(8,128)(2,1)S(1)}, u32[]{:S(2)}, u32[]{:S(2)}) %collective-permute-start.20) | collective-permute-done | bytes 135200 | tf_op jit(solution)/shard_map/ppermute | solution.py:539
  56.8 1.3 %collective-permute-start.22 = (s16[272,128]{1,0:T(8,128)(2,1)S(1)}, s16[272,128]{1,0:T(8,128)(2,1)S(1)}, u32[]{:S(2)}, u32[]{:S(2)}) collective-permute-start(s16[272,128]{1,0:T(8,128)(2,1)S(1)} %get-tuple-element.53), channel_id=1, source_target_pairs={{0,8},{4,12},{8,0},{12,4},{1,9},{5,13},{9,1},{13,5},{2,10},{6,14},... | collective-permute-start | bytes 208904 | tf_op jit(solution)/shard_map/ppermute | solution.py:539
  58.8 2.6 %collective-permute-start.23 = (s16[272,128]{1,0:T(8,128)(2,1)S(1)}, s16[272,128]{1,0:T(8,128)(2,1)S(1)}, u32[]{:S(2)}, u32[]{:S(2)}) collective-permute-start(s16[272,128]{1,0:T(8,128)(2,1)S(1)} %get-tuple-element.54), channel_id=1, source_target_pairs={{0,12},{4,8},{8,4},{12,0},{1,13},{5,9},{9,5},{13,1},{2,14},{6,10},... | collective-permute-start | bytes 208904 | tf_op jit(solution)/shard_map/ppermute | solution.py:539
  62.0 3.0 %collective-permute-done.23.refs_2_ = s16[272,128]{1,0:T(8,128)(2,1)S(1)} collective-permute-done((s16[272,128]{1,0:T(8,128)(2,1)S(1)}, s16[272,128]{1,0:T(8,128)(2,1)S(1)}, u32[]{:S(2)}, u32[]{:S(2)}) %collective-permute-start.23) | collective-permute-done | bytes 69664 | tf_op jit(solution)/shard_map/ppermute | solution.py:539
  (70 shorter events, 14.0 us)
Async XLA Ops:
  0.0 15.1 %collective-permute-start.2 = (bf16[64,512]{1,0:T(8,128)(2,1)}, bf16[64,512]{1,0:T(8,128)(2,1)S(1)}, u32[]{:S(2)}, u32[]{:S(2)}) collective-permute-start(bf16[64,512]{1,0:T(8,128)(2,1)} %bitcast.16), channel_id=1, source_target_pairs={{0,12},{4,8},{8,4},{12,0},{1,13},{5,9},{9,5},{13,1},{2,14},{6,10},... | collective-permute-start | bytes 196616 | tf_op jit(solution)/shard_map/ppermute | solution.py:539
  5.0 10.1 %collective-permute-start.1 = (bf16[64,512]{1,0:T(8,128)(2,1)}, bf16[64,512]{1,0:T(8,128)(2,1)S(1)}, u32[]{:S(2)}, u32[]{:S(2)}) collective-permute-start(bf16[64,512]{1,0:T(8,128)(2,1)} %bitcast.17), channel_id=1, source_target_pairs={{0,8},{4,12},{8,0},{12,4},{1,9},{5,13},{9,1},{13,5},{2,10},{6,14},... | collective-permute-start | bytes 196616 | tf_op jit(solution)/shard_map/ppermute | solution.py:539
  5.1 10.1 %collective-permute-start = (bf16[64,512]{1,0:T(8,128)(2,1)}, bf16[64,512]{1,0:T(8,128)(2,1)S(1)}, u32[]{:S(2)}, u32[]{:S(2)}) collective-permute-start(bf16[64,512]{1,0:T(8,128)(2,1)} %bitcast.18), channel_id=1, source_target_pairs={{0,4},{4,0},{8,12},{12,8},{1,5},{5,1},{9,13},{13,9},{2,6},{6,2},{1... | collective-permute-start | bytes 196616 | tf_op jit(solution)/shard_map/ppermute | solution.py:539
  10.7 20.6 %collective-permute-start.11 = (bf16[2,128,256]{2,1,0:T(8,128)(2,1)S(1)}, bf16[2,128,256]{2,1,0:T(8,128)(2,1)S(1)}, u32[]{:S(2)}, u32[]{:S(2)}) collective-permute-start(bf16[2,128,256]{2,1,0:T(8,128)(2,1)S(1)} %get-tuple-element.43), channel_id=1, source_target_pairs={{0,4},{4,0},{8,12},{12,8},{1,5},{5,1},{9,13},{13,9},{2,6},{6,2},{1... | collective-permute-start | bytes 393224 | tf_op jit(solution)/shard_map/ppermute | solution.py:539
  12.2 19.1 %collective-permute-start.12 = (bf16[2,128,256]{2,1,0:T(8,128)(2,1)S(1)}, bf16[2,128,256]{2,1,0:T(8,128)(2,1)S(1)}, u32[]{:S(2)}, u32[]{:S(2)}) collective-permute-start(bf16[2,128,256]{2,1,0:T(8,128)(2,1)S(1)} %get-tuple-element.44), channel_id=1, source_target_pairs={{0,8},{4,12},{8,0},{12,4},{1,9},{5,13},{9,1},{13,5},{2,10},{6,14},... | collective-permute-start | bytes 393224 | tf_op jit(solution)/shard_map/ppermute | solution.py:539
  15.1 16.2 %collective-permute-start.13 = (bf16[2,128,256]{2,1,0:T(8,128)(2,1)S(1)}, bf16[2,128,256]{2,1,0:T(8,128)(2,1)S(1)}, u32[]{:S(2)}, u32[]{:S(2)}) collective-permute-start(bf16[2,128,256]{2,1,0:T(8,128)(2,1)S(1)} %get-tuple-element.45), channel_id=1, source_target_pairs={{0,12},{4,8},{8,4},{12,0},{1,13},{5,9},{9,5},{13,1},{2,14},{6,10},... | collective-permute-start | bytes 393224 | tf_op jit(solution)/shard_map/ppermute | solution.py:539
  15.2 6.7 %collective-permute-start.3 = (bf16[4,64,512]{2,1,0:T(8,128)(2,1)S(1)}, bf16[4,64,512]{2,1,0:T(8,128)(2,1)S(1)}, u32[]{:S(2)}, u32[]{:S(2)}) collective-permute-start(bf16[4,64,512]{2,1,0:T(8,128)(2,1)S(1)} %pack.1.refs_2_.refs_0_.rows_ref), channel_id=1, source_target_pairs={{0,2},{2,0},{1,3},{3,1},{4,6},{6,4},{5,7},{7,5},{8,10},{10,8},{9,1... | collective-permute-start | bytes 786440 | tf_op jit(solution)/shard_map/ppermute | solution.py:539
  17.6 4.5 %collective-permute-start.4 = (bf16[4,64,512]{2,1,0:T(8,128)(2,1)S(1)}, bf16[4,64,512]{2,1,0:T(8,128)(2,1)S(1)}, u32[]{:S(2)}, u32[]{:S(2)}) collective-permute-start(bf16[4,64,512]{2,1,0:T(8,128)(2,1)S(1)} %pack.1.refs_2_.refs_0_.rows_ref), channel_id=1, source_target_pairs={{0,1},{1,0},{2,3},{3,2},{4,5},{5,4},{6,7},{7,6},{8,9},{9,8},{10,11... | collective-permute-start | bytes 786440 | tf_op jit(solution)/shard_map/ppermute | solution.py:539
  21.9 1.5 %collective-permute-start.5 = (bf16[4,64,512]{2,1,0:T(8,128)(2,1)S(1)}, bf16[4,64,512]{2,1,0:T(8,128)(2,1)S(1)}, u32[]{:S(2)}, u32[]{:S(2)}) collective-permute-start(bf16[4,64,512]{2,1,0:T(8,128)(2,1)S(1)} %gate.2.refs_1_), channel_id=1, source_target_pairs={{0,1},{1,0},{2,3},{3,2},{4,5},{5,4},{6,7},{7,6},{8,9},{9,8},{10,11... | collective-permute-start | bytes 786440 | tf_op jit(solution)/shard_map/ppermute | solution.py:539
  24.8 6.3 %collective-permute-start.6 = (s16[528,128]{1,0:T(8,128)(2,1)S(1)}, s16[528,128]{1,0:T(8,128)(2,1)S(1)}, u32[]{:S(2)}, u32[]{:S(2)}) collective-permute-start(s16[528,128]{1,0:T(8,128)(2,1)S(1)} %get-tuple-element.36), channel_id=1, source_target_pairs={{0,2},{2,0},{1,3},{3,1},{4,6},{6,4},{5,7},{7,5},{8,10},{10,8},{9,1... | collective-permute-start | bytes 405512 | tf_op jit(solution)/shard_map/ppermute | solution.py:539
  31.3 10.8 %collective-permute-start.14 = (bf16[4,128,256]{2,1,0:T(8,128)(2,1)S(1)}, bf16[4,128,256]{2,1,0:T(8,128)(2,1)S(1)}, u32[]{:S(2)}, u32[]{:S(2)}) collective-permute-start(bf16[4,128,256]{2,1,0:T(8,128)(2,1)S(1)} %get-tuple-element.47), channel_id=1, source_target_pairs={{0,2},{2,0},{1,3},{3,1},{4,6},{6,4},{5,7},{7,5},{8,10},{10,8},{9,1... | collective-permute-start | bytes 786440 | tf_op jit(solution)/shard_map/ppermute | solution.py:539
  32.3 5.1 %collective-permute-start.7 = (s16[144,128]{1,0:T(8,128)(2,1)S(1)}, s16[144,128]{1,0:T(8,128)(2,1)S(1)}, u32[]{:S(2)}, u32[]{:S(2)}) collective-permute-start(s16[144,128]{1,0:T(8,128)(2,1)S(1)} %get-tuple-element.38), channel_id=1, source_target_pairs={{0,4},{4,0},{8,12},{12,8},{1,5},{5,1},{9,13},{13,9},{2,6},{6,2},{1... | collective-permute-start | bytes 110600 | tf_op jit(solution)/shard_map/ppermute | solution.py:539
  32.8 5.9 %collective-permute-start.8 = (s16[144,128]{1,0:T(8,128)(2,1)S(1)}, s16[144,128]{1,0:T(8,128)(2,1)S(1)}, u32[]{:S(2)}, u32[]{:S(2)}) collective-permute-start(s16[144,128]{1,0:T(8,128)(2,1)S(1)} %get-tuple-element.39), channel_id=1, source_target_pairs={{0,8},{4,12},{8,0},{12,4},{1,9},{5,13},{9,1},{13,5},{2,10},{6,14},... | collective-permute-start | bytes 110600 | tf_op jit(solution)/shard_map/ppermute | solution.py:539
  36.3 5.8 %collective-permute-start.9 = (s16[144,128]{1,0:T(8,128)(2,1)S(1)}, s16[144,128]{1,0:T(8,128)(2,1)S(1)}, u32[]{:S(2)}, u32[]{:S(2)}) collective-permute-start(s16[144,128]{1,0:T(8,128)(2,1)S(1)} %get-tuple-element.40), channel_id=1, source_target_pairs={{0,12},{4,8},{8,4},{12,0},{1,13},{5,9},{9,5},{13,1},{2,14},{6,10},... | collective-permute-start | bytes 110600 | tf_op jit(solution)/shard_map/ppermute | solution.py:539
  37.2 6.6 %collective-permute-start.15 = (bf16[4,128,256]{2,1,0:T(8,128)(2,1)S(1)}, bf16[4,128,256]{2,1,0:T(8,128)(2,1)S(1)}, u32[]{:S(2)}, u32[]{:S(2)}) collective-permute-start(bf16[4,128,256]{2,1,0:T(8,128)(2,1)S(1)} %get-tuple-element.46.refs_0_), channel_id=1, source_target_pairs={{0,1},{1,0},{2,3},{3,2},{4,5},{5,4},{6,7},{7,6},{8,9},{9,8},{10,11... | collective-permute-start | bytes 786440 | tf_op jit(solution)/shard_map/ppermute | solution.py:539
  42.2 1.7 %collective-permute-start.16 = (bf16[4,128,256]{2,1,0:T(8,128)(2,1)S(1)}, bf16[4,128,256]{2,1,0:T(8,128)(2,1)S(1)}, u32[]{:S(2)}, u32[]{:S(2)}) collective-permute-start(bf16[4,128,256]{2,1,0:T(8,128)(2,1)S(1)} %gate.3.refs_1_), channel_id=1, source_target_pairs={{0,1},{1,0},{2,3},{3,2},{4,5},{5,4},{6,7},{7,6},{8,9},{9,8},{10,11... | collective-permute-start | bytes 786440 | tf_op jit(solution)/shard_map/ppermute | solution.py:539
  42.2 1.6 %collective-permute-start.10 = (f32[64,256]{1,0:T(8,128)S(1)}, f32[64,256]{1,0:T(8,128)S(1)}, u32[]{:S(2)}, u32[]{:S(2)}) collective-permute-start(f32[64,256]{1,0:T(8,128)S(1)} %fold_pairs.1.refs_1_.mine_ref), channel_id=1, source_target_pairs={{0,1},{1,0},{2,3},{3,2},{4,5},{5,4},{6,7},{7,6},{8,9},{9,8},{10,11... | collective-permute-start | bytes 196616 | tf_op jit(solution)/shard_map/ppermute | solution.py:539
  47.1 2.7 %collective-permute-start.17 = (f32[4,64,512]{2,1,0:T(8,128)S(1)}, f32[4,64,512]{2,1,0:T(8,128)S(1)}, u32[]{:S(2)}, u32[]{:S(2)}) collective-permute-start(f32[4,64,512]{2,1,0:T(8,128)S(1)} %outputs.4.refs_0_), channel_id=1, source_target_pairs={{0,1},{1,0},{2,3},{3,2},{4,5},{5,4},{6,7},{7,6},{8,9},{9,8},{10,11... | collective-permute-start | bytes 1572872 | tf_op jit(solution)/shard_map/ppermute | solution.py:539
  48.3 4.8 %collective-permute-start.18 = (f32[4,64,512]{2,1,0:T(8,128)S(1)}, f32[4,64,512]{2,1,0:T(8,128)S(1)}, u32[]{:S(2)}, u32[]{:S(2)}) collective-permute-start(f32[4,64,512]{2,1,0:T(8,128)S(1)} %outputs.5.refs_0_), channel_id=1, source_target_pairs={{0,1},{1,0},{2,3},{3,2},{4,5},{5,4},{6,7},{7,6},{8,9},{9,8},{10,11... | collective-permute-start | bytes 1572872 | tf_op jit(solution)/shard_map/ppermute | solution.py:539
  50.1 6.5 %collective-permute-start.20 = (s16[528,128]{1,0:T(8,128)(2,1)S(1)}, s16[528,128]{1,0:T(8,128)(2,1)S(1)}, u32[]{:S(2)}, u32[]{:S(2)}) collective-permute-start(s16[528,128]{1,0:T(8,128)(2,1)S(1)} %get-tuple-element.51), channel_id=1, source_target_pairs={{0,2},{2,0},{1,3},{3,1},{4,6},{6,4},{5,7},{7,5},{8,10},{10,8},{9,1... | collective-permute-start | bytes 405512 | tf_op jit(solution)/shard_map/ppermute | solution.py:539
  51.3 7.4 %collective-permute-start.19 = (s16[528,128]{1,0:T(8,128)(2,1)S(1)}, s16[528,128]{1,0:T(8,128)(2,1)S(1)}, u32[]{:S(2)}, u32[]{:S(2)}) collective-permute-start(s16[528,128]{1,0:T(8,128)(2,1)S(1)} %get-tuple-element.49.refs_0_), channel_id=1, source_target_pairs={{0,2},{2,0},{1,3},{3,1},{4,6},{6,4},{5,7},{7,5},{8,10},{10,8},{9,1... | collective-permute-start | bytes 405512 | tf_op jit(solution)/shard_map/ppermute | solution.py:539
  56.7 4.6 %collective-permute-start.21 = (s16[272,128]{1,0:T(8,128)(2,1)S(1)}, s16[272,128]{1,0:T(8,128)(2,1)S(1)}, u32[]{:S(2)}, u32[]{:S(2)}) collective-permute-start(s16[272,128]{1,0:T(8,128)(2,1)S(1)} %get-tuple-element.52), channel_id=1, source_target_pairs={{0,4},{4,0},{8,12},{12,8},{1,5},{5,1},{9,13},{13,9},{2,6},{6,2},{1... | collective-permute-start | bytes 208904 | tf_op jit(solution)/shard_map/ppermute | solution.py:539
  56.8 5.3 %collective-permute-start.22 = (s16[272,128]{1,0:T(8,128)(2,1)S(1)}, s16[272,128]{1,0:T(8,128)(2,1)S(1)}, u32[]{:S(2)}, u32[]{:S(2)}) collective-permute-start(s16[272,128]{1,0:T(8,128)(2,1)S(1)} %get-tuple-element.53), channel_id=1, source_target_pairs={{0,8},{4,12},{8,0},{12,4},{1,9},{5,13},{9,1},{13,5},{2,10},{6,14},... | collective-permute-start | bytes 208904 | tf_op jit(solution)/shard_map/ppermute | solution.py:539
  58.8 6.2 %collective-permute-start.23 = (s16[272,128]{1,0:T(8,128)(2,1)S(1)}, s16[272,128]{1,0:T(8,128)(2,1)S(1)}, u32[]{:S(2)}, u32[]{:S(2)}) collective-permute-start(s16[272,128]{1,0:T(8,128)(2,1)S(1)} %get-tuple-element.54), channel_id=1, source_target_pairs={{0,12},{4,8},{8,4},{12,0},{1,13},{5,9},{9,5},{13,1},{2,14},{6,10},... | collective-permute-start | bytes 208904 | tf_op jit(solution)/shard_map/ppermute | solution.py:539
  (8 other events, 49.4 us)

commit v8 on v7

--- a/solution.py
+++ b/solution.py
@@ -18,7 +18,6 @@
 ROWS = STEPS * SAMPLES
 PAIR = 2 * HEAD_SIZE
 LANES = 128
-HALVES = ((0, 3), (1, 2))
 TAIL = 16
 DEVICES = ("req", "sub", "section")
 
@@ -26,6 +25,7 @@
 eps_norm = 1e-05
 VMEM = 16 * 2**20
 LARGE_VMEM = 51 * 2**20
+IN_FLIGHT = 4
 
 
 def params(**more):
@@ -45,29 +45,57 @@
     return vectors * cosine + pltpu.roll(vectors, HEAD_SIZE // 2, vectors.ndim - 1) * sine
 
 
-def stage_kernel(count, *refs):
-    ins, outs, sems = refs[:count], refs[-2 - count : -1], refs[-1]
-    copies = [pltpu.make_async_copy(ins[i], outs[i], sems.at[i]) for i in range(count)]
+def stage_kernel(order, count, place, block_ref, *refs):
+    out_ref, token_ref, *outs, sems = refs[-3 - count :]
+    width = out_ref.shape[2]
+    copies = [
+        pltpu.make_async_copy(refs[i], outs[i], sems.at[len(order) + i]) for i in range(count)
+    ]
+    for i, block in enumerate(order):
+        columns = pl.ds(pl.multiple_of(block(place) * width, width), width)
+        copies.append(pltpu.make_async_copy(block_ref.at[:, columns], out_ref.at[i], sems.at[i]))
     for copy in copies:
         copy.start()
-    outs[-1][...] = jnp.zeros_like(outs[-1])
+    token_ref[...] = jnp.zeros_like(token_ref)
     for copy in copies:
         copy.wait()
 
 
-def staged(arrays, after=()):
-    count = len(arrays)
-    token = jax.ShapeDtypeStruct((8, LANES), jnp.float32)
-    return pl.pallas_call(
-        functools.partial(stage_kernel, count),
-        in_specs=[pl.BlockSpec(memory_space=pltpu.HBM)] * count + unread(after),
-        out_specs=[pl.BlockSpec(memory_space=pltpu.VMEM)] * (count + 1),
-        out_shape=[jax.ShapeDtypeStruct(array.shape, array.dtype) for array in arrays] + [token],
-        scratch_shapes=[pltpu.SemaphoreType.DMA((count,))],
-        compiler_params=params(),
-        cost_estimate=cost(arrays, arrays),
+def staged(place, array, width, order, more=(), after=()):
+    rows, count = array.shape[0], len(order)
+    return pl.pallas_call(
+        functools.partial(stage_kernel, order, len(more)),
+        in_specs=[pl.BlockSpec(memory_space=pltpu.SMEM)]
+        + [pl.BlockSpec(memory_space=pltpu.HBM)] * (1 + len(more))
+        + unread(after),
+        out_specs=[pl.BlockSpec(memory_space=pltpu.VMEM)] * (2 + len(more)),
+        out_shape=[
+            jax.ShapeDtypeStruct((count, rows, width), array.dtype),
+            jax.ShapeDtypeStruct((8, LANES), jnp.float32),
+        ]
+        + [jax.ShapeDtypeStruct(other.shape, other.dtype) for other in more],
+        scratch_shapes=[pltpu.SemaphoreType.DMA((count + len(more),))],
+        compiler_params=params(),
+        cost_estimate=cost([array], [array]),
         name="staged",
-    )(*arrays, *after)
+    )(place, array, *more, *after)
+
+
+def pair_order(subs):
+    return [
+        lambda place, j=j, z=z: 2 * (place[0] ^ z) + (place[1] ^ j) // (subs // 2)
+        for j in range(subs)
+        for z in range(GROUP_REQUESTS)
+    ]
+
+
+def output_order(subs):
+    return [
+        lambda place, c=c, j=j, z=z: ((place[0] ^ z) * subs + (place[1] ^ j)) * 2 + (place[2] ^ c)
+        for c in range(2)
+        for j in range(subs)
+        for z in range(GROUP_REQUESTS)
+    ]
 
 
 def gate_kernel(*refs):
@@ -208,12 +236,10 @@
     x = x_refs[0][0].astype(jnp.float32)
     mine = (x * scale * gain_ref[device]).astype(jnp.bfloat16)
     for shift in range(subs):
-        half = (sub ^ shift) // (subs // 2)
         pieces = []
         for z in range(GROUP_REQUESTS):
-            head = 2 * (request ^ z) + half
-            columns = pl.ds(pl.multiple_of(head * PAIR, PAIR), PAIR)
-            part = jnp.dot(mine, weight_ref[:, columns], preferred_element_type=jnp.float32)
+            block = weight_ref[shift * GROUP_REQUESTS + z]
+            part = jnp.dot(mine, block, preferred_element_type=jnp.float32)
             if shift == 0:
                 kept_ref[z] = part
             pieces += pieces_of(part)
@@ -250,7 +276,7 @@
     for i, (_, _, block) in enumerate(blocks):
         depth = pl.ds(pl.multiple_of(block * width, width), width)
         copies.append(pltpu.make_async_copy(weight_ref.at[depth], held.at[i], sems.at[i]))
-    for copy in copies:
+    for copy in copies[:IN_FLIGHT]:
         copy.start()
     scale = scale_ref[:, :1]
     total = jnp.zeros((rows, columns), jnp.float32)
@@ -258,6 +284,8 @@
         x = ref[z].astype(jnp.float32)
         x = (x * scale * gain_ref[block]).astype(jnp.bfloat16)
         copies[i].wait()
+        if i + IN_FLIGHT < len(copies):
+            copies[i + IN_FLIGHT].start()
         total += jnp.dot(x, held[i], preferred_element_type=jnp.float32)
     for head in range(columns // HEAD_SIZE):
         part = slice(head * HEAD_SIZE, (head + 1) * HEAD_SIZE)
@@ -363,16 +391,12 @@
     )(place, lengths, query, mine, other, cosine, sine, *caches)
 
 
-def output_kernel(away, subs, shifts, place, x_ref, weight_ref, *refs):
+def output_kernel(first, x_ref, weight_ref, *refs):
     out_ref = refs[-1]
     blocks, rows, width = out_ref.shape
-    core = 1 - place[2] if away else place[2]
     x = x_ref[...].reshape(rows, -1)
     for i in range(blocks):
-        z, shift = i % GROUP_REQUESTS, shifts[i // GROUP_REQUESTS]
-        block = ((place[0] ^ z) * subs + (place[1] ^ shift)) * 2 + core
-        columns = pl.ds(pl.multiple_of(block * width, width), width)
-        part = jnp.dot(x, weight_ref[:, columns], preferred_element_type=jnp.float32)
+        part = jnp.dot(x, weight_ref[first + i], preferred_element_type=jnp.float32)
         for r in range(GROUP_REQUESTS):
             for step in range(STEPS):
                 source = r * ROWS + step * SAMPLES
@@ -380,21 +404,17 @@
                 out_ref[i, target : target + SAMPLES] = part[source : source + SAMPLES]
 
 
-def outputs(place, mixed, weight, away, subs, shifts, after=()):
-    rows = GROUP_REQUESTS * ROWS
-    width = weight.shape[1] // (2 * GROUP_REQUESTS * subs)
-    blocks = GROUP_REQUESTS * len(shifts)
-    return pl.pallas_call(
-        functools.partial(output_kernel, away, subs, shifts),
-        in_specs=[pl.BlockSpec(memory_space=pltpu.SMEM)]
-        + [pl.BlockSpec(memory_space=pltpu.VMEM)] * 2
-        + unread(after),
+def outputs(mixed, weight, first, blocks, after=()):
+    rows, width = GROUP_REQUESTS * ROWS, weight.shape[2]
+    return pl.pallas_call(
+        functools.partial(output_kernel, first),
+        in_specs=[pl.BlockSpec(memory_space=pltpu.VMEM)] * 2 + unread(after),
         out_specs=pl.BlockSpec(memory_space=pltpu.VMEM),
         out_shape=jax.ShapeDtypeStruct((blocks, rows, width), jnp.float32),
         compiler_params=params(),
         cost_estimate=cost([mixed], flops=2 * rows * mixed.shape[2] * blocks * width),
         name="outputs",
-    )(place, mixed, weight, *after)
+    )(mixed, weight, *after)
 
 
 def pieces_of(block):
@@ -429,16 +449,18 @@
 def fold_core_kernel(mine_ref, got_ref, *out_refs):
     for i, out_ref in enumerate(out_refs):
         pieces = []
-        for z in HALVES[i % 2]:
-            block = i // 2 * GROUP_REQUESTS + z
+        for z in range(GROUP_REQUESTS):
+            block = i * GROUP_REQUESTS + z
             pieces += pieces_of(mine_ref[block] + got_ref[block])
         encode(out_ref, pieces)
 
 
 def fold_core(mine, got):
     blocks, rows, width = mine.shape
-    count = 2 * (blocks // GROUP_REQUESTS)
-    sent = jax.ShapeDtypeStruct((2 * width // LANES * rows + TAIL, LANES), jnp.int16)
+    count = blocks // GROUP_REQUESTS
+    sent = jax.ShapeDtypeStruct(
+        (GROUP_REQUESTS * width // LANES * rows + TAIL, LANES), jnp.int16
+    )
     return pl.pallas_call(
         fold_core_kernel,
         in_specs=[pl.BlockSpec(memory_space=pltpu.VMEM)] * 2,
@@ -450,18 +472,18 @@
     )(mine, got)
 
 
-def fold_sub_kernel(order, count, own, *refs):
-    own_refs, in_refs, out_refs = refs[:own], refs[own : own + count], refs[-len(order) :]
+def fold_sub_kernel(count, own, *refs):
+    own_refs, in_refs, out_refs = refs[:own], refs[own : own + count], refs[-GROUP_REQUESTS:]
     _, rows, width = own_refs[0].shape
     steps = [step_of(ref) for ref in in_refs]
-    for i, (z, out_ref) in enumerate(zip(order, out_refs)):
+    for z, out_ref in enumerate(out_refs):
         block = own_refs[0][z]
         for ref in own_refs[1:]:
             block = block + ref[z]
         pieces = pieces_of(block)
         for c in range(len(pieces)):
             for ref, step in zip(in_refs, steps):
-                first = (i * len(pieces) + c) * rows
+                first = (z * len(pieces) + c) * rows
                 pieces[c] = pieces[c] + decoded(ref, first, rows, step)
         if z:
             encode(out_ref, pieces)
@@ -470,16 +492,16 @@
                 out_ref[:, c * LANES : (c + 1) * LANES] = piece
 
 
-def fold_sub(order, own, parts, after=()):
+def fold_sub(own, parts, after=()):
     _, rows, width = own[0].shape
     total = jax.ShapeDtypeStruct((rows, width), jnp.float32)
     sent = jax.ShapeDtypeStruct((width // LANES * rows + TAIL, LANES), jnp.int16)
     return pl.pallas_call(
-        functools.partial(fold_sub_kernel, order, len(parts), len(own)),
+        functools.partial(fold_sub_kernel, len(parts), len(own)),
         in_specs=[pl.BlockSpec(memory_space=pltpu.VMEM)] * (len(own) + len(parts))
         + unread(after),
-        out_specs=[pl.BlockSpec(memory_space=pltpu.VMEM)] * len(order),
-        out_shape=[sent if z else total for z in order],
+        out_specs=[pl.BlockSpec(memory_space=pltpu.VMEM)] * GROUP_REQUESTS,
+        out_shape=[total] + [sent] * (GROUP_REQUESTS - 1),
         compiler_params=params(),
         cost_estimate=cost(own, parts),
         name="fold_sub",
@@ -572,8 +594,13 @@
     column = pack([rows] + column)
     gathered = [passed(column, "sub", s) for s in range(1, subs)]
     pages[1:] = [passed(pages[s], "req", s) for s in range(1, GROUP_REQUESTS)]
-    gain, key_value_weight, ready = staged(
-        [norm_gain.reshape(devices, 1, width), key_value_weight], after=[column]
+    key_value_weight, ready, gain = staged(
+        place,
+        key_value_weight,
+        PAIR,
+        pair_order(subs),
+        more=[norm_gain.reshape(devices, 1, width)],
+        after=[column],
     )
     gathered = [column] + list(gate(gathered, after=[ready]))
     gathered = gathered + [passed(part, "section", 1) for part in gathered]
@@ -593,11 +620,11 @@
     scale, kept, *parts = scale_and_pairs(place, gain, key_value_weight, gathered)
     parts = [passed(part, "sub", s + 1) for s, part in enumerate(parts)]
     query = queries(place, scale, gain, w_query, cosine, sine, gathered)
-    total, *parts = fold_sub((0, 1, 2, 3), [kept], parts, after=[query])
+    total, *parts = fold_sub([kept], parts, after=[query])
     parts = [passed(part, "req", s + 1) for s, part in enumerate(parts)]
     pages = regroup(pages, after=[total])
     caches = [passed(pages[s], "sub", s) for s in range(1, subs)]
-    w_output, ready = staged([w_output], after=[query])
+    w_output, ready = staged(place, w_output, width, output_order(subs), after=[query])
     mine = fold_pairs(total, parts, after=[ready])
     caches = list(pages[:1]) + list(gate(caches, after=[mine]))
     caches = caches + [passed(part, "section", 1) for part in caches]
@@ -607,20 +634,18 @@
         place, lengths.astype(jnp.int32), query, mine, other, cosine, sine, caches
     )
 
-    others = tuple(range(1, subs))
-    first = outputs(place, mixed, w_output, True, subs, others)
+    mid, end = GROUP_REQUESTS, GROUP_REQUESTS * subs
+    first = outputs(mixed, w_output, end + mid, end - mid)
     got_first = passed(first, "section", 1)
-    second = outputs(place, mixed, w_output, True, subs, (0,), after=[first])
+    second = outputs(mixed, w_output, end, mid, after=[first])
     got_second = passed(second, "section", 1)
-    kept = outputs(place, mixed, w_output, False, subs, others, after=[second])
+    kept = outputs(mixed, w_output, mid, end - mid, after=[second])
     parts = fold_core(kept, got_first)
-    kept = outputs(place, mixed, w_output, False, subs, (0,), after=parts[:1])
-    parts = [passed(part, "sub", i // 2 + 1) for i, part in enumerate(parts)]
-    last = {}
-    for half, order in enumerate(HALVES):
-        last.update(zip(order, fold_sub(order, [kept, got_second], parts[half::2])))
-    parts = [passed(last[s], "req", s) for s in range(1, GROUP_REQUESTS)]
-    return finish(gathered[0], last[0], parts).reshape(hidden.shape)
+    kept = outputs(mixed, w_output, 0, mid, after=parts[:1])
+    parts = [passed(part, "sub", s + 1) for s, part in enumerate(parts)]
+    total, *parts = fold_sub([kept, got_second], parts)
+    parts = [passed(part, "req", s + 1) for s, part in enumerate(parts)]
+    return finish(gathered[0], total, parts).reshape(hidden.shape)
 
 
 def solution(mesh):

time: 66.1 us -> 68 us (1.029)
  Pallas kernels: 16 us -> 17.4 us
  waiting for transfers between devices: 16.5 us -> 17.4 us
    pallas_call x1, Pallas kernels: 4.63 us -> 6.24 us  [queries(): pl.pallas_call(query_kernel, in_specs=[pl.BlockSpec(memory_space=pltpu.SM...]
    ppermute x24 -> x23, waiting for transfers between devices: 16.5 us -> 17.4 us  [passed(): lax.ppermute(array, axis, [(i, i ^ shift) for i in range(lax.axis_size(ax...]
    ppermute x24 -> x23, starting transfers between devices: 26.1 us -> 25.7 us  [passed(): lax.ppermute(array, axis, [(i, i ^ shift) for i in range(lax.axis_size(ax...]
    pallas_call x9 -> x8, Pallas kernels: 5.23 us -> 5.1 us  [the longest x2 2.85 us: staged(): pl.pallas_call(functools.partial(stage_kernel, order, len(more)), in_spec...]
  transfers between devices with their start and end apart: 24 -> 23, of which waited for: 9 -> 8; matrix products, arithmetic and copies ran while one was open for 3% -> 3% of each run, Pallas kernels for 18% -> 20%
where the time goes in v8:
time: 68 us; the launch traced here: 67.6 us
  starting transfers between devices  25.7 us (38%)
  Pallas kernels  17.4 us (26%)
  waiting for transfers between devices  17.4 us (26%)
  local copies, waits for them, and re-layouts  5.12 us (8%)
  other arithmetic  1.71 us (3%)
    ppermute x23, starting transfers between devices, passed(): lax.ppermute(array, axis, [(i, i ^ shift) for i in range(lax.axis_size(ax...  25.7 us
    ppermute x23, waiting for transfers between devices, passed(): lax.ppermute(array, axis, [(i, i ^ shift) for i in range(lax.axis_size(ax...  17.4 us
    pallas_call x1, Pallas kernels, queries(): pl.pallas_call(query_kernel, in_specs=[pl.BlockSpec(memory_space=pltpu.SM...  6.24 us
    unnamed x16, local copies, waits for them, and re-layouts  5.11 us
    pallas_call x2, Pallas kernels, staged(): pl.pallas_call(functools.partial(stage_kernel, order, len(more)), in_spec...  2.85 us
    pallas_call x1, Pallas kernels, attend(): pl.pallas_call(attend_kernel, in_specs=[pl.BlockSpec(memory_space=pltpu.S...  2.19 us
    pallas_call x4, Pallas kernels, outputs(): pl.pallas_call(functools.partial(output_kernel, first), in_specs=[pl.Bloc...  1.91 us
    pallas_call x1, Pallas kernels, used_pages(): pl.pallas_call(pages_kernel, grid_spec=pltpu.PrefetchScalarGridSpec(num_s...  1.51 us
  transfers between devices with their start and end apart: 23, of which 8 were waited for; matrix products, arithmetic and copies ran while one was open for 3% of the time, Pallas kernels for 20%

profile of v8, /device:TPU:0, one launch (start us, length us, event | category | flops | bytes accessed | tf_op | source)
XLA Modules:
  0.0 67.6 jit_solution(5504548078006569064)
XLA Ops:
  0.0 5.0 %collective-permute-start.2 = (bf16[64,512]{1,0:T(8,128)(2,1)}, bf16[64,512]{1,0:T(8,128)(2,1)S(1)}, u32[]{:S(2)}, u32[]{:S(2)}) collective-permute-start(bf16[64,512]{1,0:T(8,128)(2,1)} %bitcast.16), channel_id=1, source_target_pairs={{0,12},{4,8},{8,4},{12,0},{1,13},{5,9},{9,5},{13,1},{2,14},{6,10},... | collective-permute-start | bytes 196616 | tf_op jit(solution)/shard_map/ppermute | solution.py:561
  6.4 1.2 %copy-done.1 = bf16[16,16,2048]{2,1,0:T(8,128)(2,1)S(1)} copy-done((bf16[16,16,2048]{2,1,0:T(8,128)(2,1)S(1)}, bf16[16,16,2048]{2,1,0:T(8,128)(2,1)}, u32[]{:S(2)}) %copy-start.1) | copy-done | bytes 1048600
  7.6 0.8 %copy-done.2 = bf16[2,32,512]{2,1,0:T(8,128)(2,1)S(1)} copy-done((bf16[2,32,512]{2,1,0:T(8,128)(2,1)S(1)}, bf16[2,32,512]{2,1,0:T(8,128)(2,1)}, u32[]{:S(2)}) %copy-start.2) | copy-done | bytes 65560
  9.1 1.5 %used_pages.1 = (bf16[64,512]{1,0:T(8,128)(2,1)S(1)}, bf16[2,128,256]{2,1,0:T(8,128)(2,1)S(1)}, bf16[2,128,256]{2,1,0:T(8,128)(2,1)S(1)}, bf16[2,128,256]{2,1,0:T(8,128)(2,1)S(1)}, bf16[2,128,256]{2,1,0:T(8,128)(2,1)S(1)}) custom-call(s32[4,32]{1,0:T(4,128)S(1)} %copy-done.4, s32[3]{0:T(128)S(1)} %pad_add_fusion.place, ...), custom_call_target="tpu_custom_call" | custom-call | bytes 1048576 | tf_op jit(solution)/shard_map/used_pages/pallas_call | solution.py:141
  10.7 1.5 %collective-permute-start.11 = (bf16[2,128,256]{2,1,0:T(8,128)(2,1)S(1)}, bf16[2,128,256]{2,1,0:T(8,128)(2,1)S(1)}, u32[]{:S(2)}, u32[]{:S(2)}) collective-permute-start(bf16[2,128,256]{2,1,0:T(8,128)(2,1)S(1)} %get-tuple-element.41), channel_id=1, source_target_pairs={{0,4},{4,0},{8,12},{12,8},{1,5},{5,1},{9,13},{13,9},{2,6},{6,2},{1... | collective-permute-start | bytes 393224 | tf_op jit(solution)/shard_map/ppermute | solution.py:561
  12.2 2.9 %collective-permute-start.12 = (bf16[2,128,256]{2,1,0:T(8,128)(2,1)S(1)}, bf16[2,128,256]{2,1,0:T(8,128)(2,1)S(1)}, u32[]{:S(2)}, u32[]{:S(2)}) collective-permute-start(bf16[2,128,256]{2,1,0:T(8,128)(2,1)S(1)} %get-tuple-element.42), channel_id=1, source_target_pairs={{0,8},{4,12},{8,0},{12,4},{1,9},{5,13},{9,1},{13,5},{2,10},{6,14},... | collective-permute-start | bytes 393224 | tf_op jit(solution)/shard_map/ppermute | solution.py:561
  15.2 1.8 %collective-permute-start.3 = (bf16[4,64,512]{2,1,0:T(8,128)(2,1)S(1)}, bf16[4,64,512]{2,1,0:T(8,128)(2,1)S(1)}, u32[]{:S(2)}, u32[]{:S(2)}) collective-permute-start(bf16[4,64,512]{2,1,0:T(8,128)(2,1)S(1)} %pack.1.refs_1_.refs_0_.rows_ref), channel_id=1, source_target_pairs={{0,2},{2,0},{1,3},{3,1},{4,6},{6,4},{5,7},{7,5},{8,10},{10,8},{9,1... | collective-permute-start | bytes 786440 | tf_op jit(solution)/shard_map/ppermute | solution.py:561
  17.7 1.6 %copy-done = bf16[512,2048]{1,0:T(8,128)(2,1)S(1)} copy-done((bf16[512,2048]{1,0:T(8,128)(2,1)S(1)}, bf16[512,2048]{1,0:T(8,128)(2,1)}, u32[]{:S(2)}) %copy-start) | copy-done | bytes 2097176
  20.0 1.0 %staged.2 = (bf16[8,512,256]{2,1,0:T(8,128)(2,1)S(1)}, f32[8,128]{1,0:T(8,128)S(1)}, f32[16,1,512]{2,1,0:T(1,128)S(1)}) custom-call(s32[3]{0:T(128)S(1)} %pad_add_fusion.1.place, bf16[512,2048]{1,0:T(8,128)(2,1)S(1)} %copy-done, f32[16,1,512]{2,1,0:T(1,128)S(1)} %bitcast.20, bf16[4,64,512]{2,1,0:T(8,128)(2,1)S(1)} %pack.1.refs_1_.refs_0_.rows_ref), custom_call_target="tpu_custom_call" | custom-call | bytes 4194304 | tf_op jit(solution)/shard_map/staged/pallas_call | solution.py:66
  21.0 0.8 %collective-permute-done.3.refs_0_ = bf16[4,64,512]{2,1,0:T(8,128)(2,1)S(1)} collective-permute-done((bf16[4,64,512]{2,1,0:T(8,128)(2,1)S(1)}, bf16[4,64,512]{2,1,0:T(8,128)(2,1)S(1)}, u32[]{:S(2)}, u32[]{:S(2)}) %collective-permute-start.3) | collective-permute-done | bytes 262176 | tf_op jit(solution)/shard_map/ppermute | solution.py:561
  22.0 1.4 %collective-permute-done.5.refs_3_ = bf16[4,64,512]{2,1,0:T(8,128)(2,1)S(1)} collective-permute-done((bf16[4,64,512]{2,1,0:T(8,128)(2,1)S(1)}, bf16[4,64,512]{2,1,0:T(8,128)(2,1)S(1)}, u32[]{:S(2)}, u32[]{:S(2)}) %collective-permute-start.5) | collective-permute-done | bytes 262176 | tf_op jit(solution)/shard_map/ppermute | solution.py:561
  23.4 1.4 %scale_and_pairs.1 = (f32[64,128]{1,0:T(8,128)S(1)}, f32[4,64,256]{2,1,0:T(8,128)S(1)}, s16[528,128]{1,0:T(8,128)(2,1)S(1)}) custom-call(s32[3]{0:T(128)S(1)} %pad_add_fusion.1.place, f32[16,1,512]{2,1,0:T(1,128)S(1)} %get-tuple-element.29.gain_ref, bf16[8,512,256]{2,1,0:T(8,128)(2,1)S(1)} %get-tuple-element.30.weight_ref, ...), custom_call_target="tpu_custom_call" | custom-call | flops 134217728 | bytes 3145728 | tf_op jit(solution)/shard_map/scale_and_pairs/pallas_call | solution.py:258
  24.8 1.6 %collective-permute-start.6 = (s16[528,128]{1,0:T(8,128)(2,1)S(1)}, s16[528,128]{1,0:T(8,128)(2,1)S(1)}, u32[]{:S(2)}, u32[]{:S(2)}) collective-permute-start(s16[528,128]{1,0:T(8,128)(2,1)S(1)} %get-tuple-element.34), channel_id=1, source_target_pairs={{0,2},{2,0},{1,3},{3,1},{4,6},{6,4},{5,7},{7,5},{8,10},{10,8},{9,1... | collective-permute-start | bytes 405512 | tf_op jit(solution)/shard_map/ppermute | solution.py:561
  26.5 6.2 %queries.1.refs_2_.refs_0_.q_ref = bf16[4,16,512]{2,1,0:T(8,128)(2,1)S(1)} custom-call(s32[3]{0:T(128)S(1)} %pad_add_fusion.1.place, f32[64,128]{1,0:T(8,128)S(1)} %get-tuple-element.32.scale_ref, f32[16,1,512]{2,1,0:T(1,128)S(1)} %get-tuple-element.29.gain_ref, bf16[8192,512]{1,0:T(8,128)(2,1)} %weight_ref.1, f32[64,128]{1,0:T(8,128)S(1)} %bitcast.12, ...), custom_call_target="tpu_custom_call" | custom-call | flops 536870912 | bytes 8388608 | tf_op jit(solution)/shard_map/queries/pallas_call | solution.py:304
  34.1 3.5 %collective-permute-start.8 = (s16[144,128]{1,0:T(8,128)(2,1)S(1)}, s16[144,128]{1,0:T(8,128)(2,1)S(1)}, u32[]{:S(2)}, u32[]{:S(2)}) collective-permute-start(s16[144,128]{1,0:T(8,128)(2,1)S(1)} %get-tuple-element.37), channel_id=1, source_target_pairs={{0,8},{4,12},{8,0},{12,4},{1,9},{5,13},{9,1},{13,5},{2,10},{6,14},... | collective-permute-start | bytes 110600 | tf_op jit(solution)/shard_map/ppermute | solution.py:561
  37.9 1.9 %staged.3 = (bf16[16,512,512]{2,1,0:T(8,128)(2,1)S(1)}, f32[8,128]{1,0:T(8,128)S(1)}) custom-call(s32[3]{0:T(128)S(1)} %pad_add_fusion.1.place, bf16[512,8192]{1,0:T(8,128)(2,1)S(1)} %bitcast.11, bf16[4,16,512]{2,1,0:T(8,128)(2,1)S(1)} %queries.1.refs_2_.refs_0_.q_ref), custom_call_target="tpu_custom_call" | custom-call | bytes 16777216 | tf_op jit(solution)/shard_map/staged/pallas_call | solution.py:66
  40.1 3.2 %collective-permute-done.9.refs_2_ = s16[144,128]{1,0:T(8,128)(2,1)S(1)} collective-permute-done((s16[144,128]{1,0:T(8,128)(2,1)S(1)}, s16[144,128]{1,0:T(8,128)(2,1)S(1)}, u32[]{:S(2)}, u32[]{:S(2)}) %collective-permute-start.9) | collective-permute-done | bytes 36896 | tf_op jit(solution)/shard_map/ppermute | solution.py:561
  44.0 1.1 %collective-permute-done.10.other_ref = f32[64,256]{1,0:T(8,128)S(1)} collective-permute-done((f32[64,256]{1,0:T(8,128)S(1)}, f32[64,256]{1,0:T(8,128)S(1)}, u32[]{:S(2)}, u32[]{:S(2)}) %collective-permute-start.10) | collective-permute-done | bytes 65568 | tf_op jit(solution)/shard_map/ppermute | solution.py:561
  45.1 2.2 %attend.1.x_ref = bf16[4,16,512]{2,1,0:T(8,128)(2,1)S(1)} custom-call(s32[3]{0:T(128)S(1)} %pad_add_fusion.1.place, s32[4]{0:T(128)S(1)} %copy-done.5, bf16[4,16,512]{2,1,0:T(8,128)(2,1)S(1)} %queries.1.refs_2_.refs_0_.q_ref, f32[64,256]{1,0:T(8,128)S(1)} %fold_pairs.1.refs_1_.mine_ref, f32[64,256]{1,0:T(8,128)S(1)} %collective-permute-done.10.other_ref, ...), custom_call_target="tpu_custom_call" | custom-call | flops 268435456 | bytes 3145728 | tf_op jit(solution)/shard_map/attend/pallas_call | solution.py:381
  50.0 1.6 %collective-permute-start.19 = (s16[1040,128]{1,0:T(8,128)(2,1)S(1)}, s16[1040,128]{1,0:T(8,128)(2,1)S(1)}, u32[]{:S(2)}, u32[]{:S(2)}) collective-permute-start(s16[1040,128]{1,0:T(8,128)(2,1)S(1)} %fold_core.1.refs_0_), channel_id=1, source_target_pairs={{0,2},{2,0},{1,3},{3,1},{4,6},{6,4},{5,7},{7,5},{8,10},{10,8},{9,1... | collective-permute-start | bytes 798728 | tf_op jit(solution)/shard_map/ppermute | solution.py:561
  52.1 6.4 %collective-permute-done.19.refs_2_ = s16[1040,128]{1,0:T(8,128)(2,1)S(1)} collective-permute-done((s16[1040,128]{1,0:T(8,128)(2,1)S(1)}, s16[1040,128]{1,0:T(8,128)(2,1)S(1)}, u32[]{:S(2)}, u32[]{:S(2)}) %collective-permute-start.19) | collective-permute-done | bytes 266272 | tf_op jit(solution)/shard_map/ppermute | solution.py:561
  58.8 1.7 %collective-permute-start.21 = (s16[272,128]{1,0:T(8,128)(2,1)S(1)}, s16[272,128]{1,0:T(8,128)(2,1)S(1)}, u32[]{:S(2)}, u32[]{:S(2)}) collective-permute-start(s16[272,128]{1,0:T(8,128)(2,1)S(1)} %get-tuple-element.49), channel_id=1, source_target_pairs={{0,8},{4,12},{8,0},{12,4},{1,9},{5,13},{9,1},{13,5},{2,10},{6,14},... | collective-permute-start | bytes 208904 | tf_op jit(solution)/shard_map/ppermute | solution.py:561
  60.5 2.7 %collective-permute-start.22 = (s16[272,128]{1,0:T(8,128)(2,1)S(1)}, s16[272,128]{1,0:T(8,128)(2,1)S(1)}, u32[]{:S(2)}, u32[]{:S(2)}) collective-permute-start(s16[272,128]{1,0:T(8,128)(2,1)S(1)} %get-tuple-element.50), channel_id=1, source_target_pairs={{0,12},{4,8},{8,4},{12,0},{1,13},{5,9},{9,5},{13,1},{2,14},{6,10},... | collective-permute-start | bytes 208904 | tf_op jit(solution)/shard_map/ppermute | solution.py:561
  63.2 3.7 %collective-permute-done.21.refs_1_ = s16[272,128]{1,0:T(8,128)(2,1)S(1)} collective-permute-done((s16[272,128]{1,0:T(8,128)(2,1)S(1)}, s16[272,128]{1,0:T(8,128)(2,1)S(1)}, u32[]{:S(2)}, u32[]{:S(2)}) %collective-permute-start.21) | collective-permute-done | bytes 69664 | tf_op jit(solution)/shard_map/ppermute | solution.py:561
  (67 shorter events, 10.4 us)
Async XLA Ops:
  0.0 15.1 %collective-permute-start.2 = (bf16[64,512]{1,0:T(8,128)(2,1)}, bf16[64,512]{1,0:T(8,128)(2,1)S(1)}, u32[]{:S(2)}, u32[]{:S(2)}) collective-permute-start(bf16[64,512]{1,0:T(8,128)(2,1)} %bitcast.16), channel_id=1, source_target_pairs={{0,12},{4,8},{8,4},{12,0},{1,13},{5,9},{9,5},{13,1},{2,14},{6,10},... | collective-permute-start | bytes 196616 | tf_op jit(solution)/shard_map/ppermute | solution.py:561
  5.0 10.1 %collective-permute-start.1 = (bf16[64,512]{1,0:T(8,128)(2,1)}, bf16[64,512]{1,0:T(8,128)(2,1)S(1)}, u32[]{:S(2)}, u32[]{:S(2)}) collective-permute-start(bf16[64,512]{1,0:T(8,128)(2,1)} %bitcast.17), channel_id=1, source_target_pairs={{0,8},{4,12},{8,0},{12,4},{1,9},{5,13},{9,1},{13,5},{2,10},{6,14},... | collective-permute-start | bytes 196616 | tf_op jit(solution)/shard_map/ppermute | solution.py:561
  5.1 10.1 %collective-permute-start = (bf16[64,512]{1,0:T(8,128)(2,1)}, bf16[64,512]{1,0:T(8,128)(2,1)S(1)}, u32[]{:S(2)}, u32[]{:S(2)}) collective-permute-start(bf16[64,512]{1,0:T(8,128)(2,1)} %bitcast.18), channel_id=1, source_target_pairs={{0,4},{4,0},{8,12},{12,8},{1,5},{5,1},{9,13},{13,9},{2,6},{6,2},{1... | collective-permute-start | bytes 196616 | tf_op jit(solution)/shard_map/ppermute | solution.py:561
  10.7 22.2 %collective-permute-start.11 = (bf16[2,128,256]{2,1,0:T(8,128)(2,1)S(1)}, bf16[2,128,256]{2,1,0:T(8,128)(2,1)S(1)}, u32[]{:S(2)}, u32[]{:S(2)}) collective-permute-start(bf16[2,128,256]{2,1,0:T(8,128)(2,1)S(1)} %get-tuple-element.41), channel_id=1, source_target_pairs={{0,4},{4,0},{8,12},{12,8},{1,5},{5,1},{9,13},{13,9},{2,6},{6,2},{1... | collective-permute-start | bytes 393224 | tf_op jit(solution)/shard_map/ppermute | solution.py:561
  12.2 20.7 %collective-permute-start.12 = (bf16[2,128,256]{2,1,0:T(8,128)(2,1)S(1)}, bf16[2,128,256]{2,1,0:T(8,128)(2,1)S(1)}, u32[]{:S(2)}, u32[]{:S(2)}) collective-permute-start(bf16[2,128,256]{2,1,0:T(8,128)(2,1)S(1)} %get-tuple-element.42), channel_id=1, source_target_pairs={{0,8},{4,12},{8,0},{12,4},{1,9},{5,13},{9,1},{13,5},{2,10},{6,14},... | collective-permute-start | bytes 393224 | tf_op jit(solution)/shard_map/ppermute | solution.py:561
  15.1 17.8 %collective-permute-start.13 = (bf16[2,128,256]{2,1,0:T(8,128)(2,1)S(1)}, bf16[2,128,256]{2,1,0:T(8,128)(2,1)S(1)}, u32[]{:S(2)}, u32[]{:S(2)}) collective-permute-start(bf16[2,128,256]{2,1,0:T(8,128)(2,1)S(1)} %get-tuple-element.43), channel_id=1, source_target_pairs={{0,12},{4,8},{8,4},{12,0},{1,13},{5,9},{9,5},{13,1},{2,14},{6,10},... | collective-permute-start | bytes 393224 | tf_op jit(solution)/shard_map/ppermute | solution.py:561
  15.2 6.7 %collective-permute-start.3 = (bf16[4,64,512]{2,1,0:T(8,128)(2,1)S(1)}, bf16[4,64,512]{2,1,0:T(8,128)(2,1)S(1)}, u32[]{:S(2)}, u32[]{:S(2)}) collective-permute-start(bf16[4,64,512]{2,1,0:T(8,128)(2,1)S(1)} %pack.1.refs_1_.refs_0_.rows_ref), channel_id=1, source_target_pairs={{0,2},{2,0},{1,3},{3,1},{4,6},{6,4},{5,7},{7,5},{8,10},{10,8},{9,1... | collective-permute-start | bytes 786440 | tf_op jit(solution)/shard_map/ppermute | solution.py:561
  17.7 4.3 %collective-permute-start.4 = (bf16[4,64,512]{2,1,0:T(8,128)(2,1)S(1)}, bf16[4,64,512]{2,1,0:T(8,128)(2,1)S(1)}, u32[]{:S(2)}, u32[]{:S(2)}) collective-permute-start(bf16[4,64,512]{2,1,0:T(8,128)(2,1)S(1)} %pack.1.refs_1_.refs_0_.rows_ref), channel_id=1, source_target_pairs={{0,1},{1,0},{2,3},{3,2},{4,5},{5,4},{6,7},{7,6},{8,9},{9,8},{10,11... | collective-permute-start | bytes 786440 | tf_op jit(solution)/shard_map/ppermute | solution.py:561
  21.9 1.5 %collective-permute-start.5 = (bf16[4,64,512]{2,1,0:T(8,128)(2,1)S(1)}, bf16[4,64,512]{2,1,0:T(8,128)(2,1)S(1)}, u32[]{:S(2)}, u32[]{:S(2)}) collective-permute-start(bf16[4,64,512]{2,1,0:T(8,128)(2,1)S(1)} %gate.2.refs_1_), channel_id=1, source_target_pairs={{0,1},{1,0},{2,3},{3,2},{4,5},{5,4},{6,7},{7,6},{8,9},{9,8},{10,11... | collective-permute-start | bytes 786440 | tf_op jit(solution)/shard_map/ppermute | solution.py:561
  24.8 8.0 %collective-permute-start.6 = (s16[528,128]{1,0:T(8,128)(2,1)S(1)}, s16[528,128]{1,0:T(8,128)(2,1)S(1)}, u32[]{:S(2)}, u32[]{:S(2)}) collective-permute-start(s16[528,128]{1,0:T(8,128)(2,1)S(1)} %get-tuple-element.34), channel_id=1, source_target_pairs={{0,2},{2,0},{1,3},{3,1},{4,6},{6,4},{5,7},{7,5},{8,10},{10,8},{9,1... | collective-permute-start | bytes 405512 | tf_op jit(solution)/shard_map/ppermute | solution.py:561
  26.5 18.7 %copy-start.5 = (s32[4]{0:T(128)S(1)}, s32[4]{0:T(128)}, u32[]{:S(2)}) copy-start(s32[4]{0:T(128)} %lengths.1) | copy-start | bytes 52
  32.9 10.5 %collective-permute-start.14 = (bf16[4,128,256]{2,1,0:T(8,128)(2,1)S(1)}, bf16[4,128,256]{2,1,0:T(8,128)(2,1)S(1)}, u32[]{:S(2)}, u32[]{:S(2)}) collective-permute-start(bf16[4,128,256]{2,1,0:T(8,128)(2,1)S(1)} %get-tuple-element.45), channel_id=1, source_target_pairs={{0,2},{2,0},{1,3},{3,1},{4,6},{6,4},{5,7},{7,5},{8,10},{10,8},{9,1... | collective-permute-start | bytes 786440 | tf_op jit(solution)/shard_map/ppermute | solution.py:561
  33.5 6.4 %collective-permute-start.7 = (s16[144,128]{1,0:T(8,128)(2,1)S(1)}, s16[144,128]{1,0:T(8,128)(2,1)S(1)}, u32[]{:S(2)}, u32[]{:S(2)}) collective-permute-start(s16[144,128]{1,0:T(8,128)(2,1)S(1)} %get-tuple-element.36), channel_id=1, source_target_pairs={{0,4},{4,0},{8,12},{12,8},{1,5},{5,1},{9,13},{13,9},{2,6},{6,2},{1... | collective-permute-start | bytes 110600 | tf_op jit(solution)/shard_map/ppermute | solution.py:561
  34.1 6.1 %collective-permute-start.8 = (s16[144,128]{1,0:T(8,128)(2,1)S(1)}, s16[144,128]{1,0:T(8,128)(2,1)S(1)}, u32[]{:S(2)}, u32[]{:S(2)}) collective-permute-start(s16[144,128]{1,0:T(8,128)(2,1)S(1)} %get-tuple-element.37), channel_id=1, source_target_pairs={{0,8},{4,12},{8,0},{12,4},{1,9},{5,13},{9,1},{13,5},{2,10},{6,14},... | collective-permute-start | bytes 110600 | tf_op jit(solution)/shard_map/ppermute | solution.py:561
  37.6 5.8 %collective-permute-start.9 = (s16[144,128]{1,0:T(8,128)(2,1)S(1)}, s16[144,128]{1,0:T(8,128)(2,1)S(1)}, u32[]{:S(2)}, u32[]{:S(2)}) collective-permute-start(s16[144,128]{1,0:T(8,128)(2,1)S(1)} %get-tuple-element.38), channel_id=1, source_target_pairs={{0,12},{4,8},{8,4},{12,0},{1,13},{5,9},{9,5},{13,1},{2,14},{6,10},... | collective-permute-start | bytes 110600 | tf_op jit(solution)/shard_map/ppermute | solution.py:561
  39.8 5.3 %collective-permute-start.15 = (bf16[4,128,256]{2,1,0:T(8,128)(2,1)S(1)}, bf16[4,128,256]{2,1,0:T(8,128)(2,1)S(1)}, u32[]{:S(2)}, u32[]{:S(2)}) collective-permute-start(bf16[4,128,256]{2,1,0:T(8,128)(2,1)S(1)} %get-tuple-element.44.refs_0_), channel_id=1, source_target_pairs={{0,1},{1,0},{2,3},{3,2},{4,5},{5,4},{6,7},{7,6},{8,9},{9,8},{10,11... | collective-permute-start | bytes 786440 | tf_op jit(solution)/shard_map/ppermute | solution.py:561
  43.4 1.7 %collective-permute-start.16 = (bf16[4,128,256]{2,1,0:T(8,128)(2,1)S(1)}, bf16[4,128,256]{2,1,0:T(8,128)(2,1)S(1)}, u32[]{:S(2)}, u32[]{:S(2)}) collective-permute-start(bf16[4,128,256]{2,1,0:T(8,128)(2,1)S(1)} %gate.3.refs_1_), channel_id=1, source_target_pairs={{0,1},{1,0},{2,3},{3,2},{4,5},{5,4},{6,7},{7,6},{8,9},{9,8},{10,11... | collective-permute-start | bytes 786440 | tf_op jit(solution)/shard_map/ppermute | solution.py:561
  43.5 1.6 %collective-permute-start.10 = (f32[64,256]{1,0:T(8,128)S(1)}, f32[64,256]{1,0:T(8,128)S(1)}, u32[]{:S(2)}, u32[]{:S(2)}) collective-permute-start(f32[64,256]{1,0:T(8,128)S(1)} %fold_pairs.1.refs_1_.mine_ref), channel_id=1, source_target_pairs={{0,1},{1,0},{2,3},{3,2},{4,5},{5,4},{6,7},{7,6},{8,9},{9,8},{10,11... | collective-permute-start | bytes 196616 | tf_op jit(solution)/shard_map/ppermute | solution.py:561
  47.8 2.0 %collective-permute-start.17 = (f32[4,64,512]{2,1,0:T(8,128)S(1)}, f32[4,64,512]{2,1,0:T(8,128)S(1)}, u32[]{:S(2)}, u32[]{:S(2)}) collective-permute-start(f32[4,64,512]{2,1,0:T(8,128)S(1)} %outputs.4.refs_0_), channel_id=1, source_target_pairs={{0,1},{1,0},{2,3},{3,2},{4,5},{5,4},{6,7},{7,6},{8,9},{9,8},{10,11... | collective-permute-start | bytes 1572872 | tf_op jit(solution)/shard_map/ppermute | solution.py:561
  48.5 3.6 %collective-permute-start.18 = (f32[4,64,512]{2,1,0:T(8,128)S(1)}, f32[4,64,512]{2,1,0:T(8,128)S(1)}, u32[]{:S(2)}, u32[]{:S(2)}) collective-permute-start(f32[4,64,512]{2,1,0:T(8,128)S(1)} %outputs.5.refs_0_), channel_id=1, source_target_pairs={{0,1},{1,0},{2,3},{3,2},{4,5},{5,4},{6,7},{7,6},{8,9},{9,8},{10,11... | collective-permute-start | bytes 1572872 | tf_op jit(solution)/shard_map/ppermute | solution.py:561
  50.0 8.5 %collective-permute-start.19 = (s16[1040,128]{1,0:T(8,128)(2,1)S(1)}, s16[1040,128]{1,0:T(8,128)(2,1)S(1)}, u32[]{:S(2)}, u32[]{:S(2)}) collective-permute-start(s16[1040,128]{1,0:T(8,128)(2,1)S(1)} %fold_core.1.refs_0_), channel_id=1, source_target_pairs={{0,2},{2,0},{1,3},{3,1},{4,6},{6,4},{5,7},{7,5},{8,10},{10,8},{9,1... | collective-permute-start | bytes 798728 | tf_op jit(solution)/shard_map/ppermute | solution.py:561
  58.7 4.5 %collective-permute-start.20 = (s16[272,128]{1,0:T(8,128)(2,1)S(1)}, s16[272,128]{1,0:T(8,128)(2,1)S(1)}, u32[]{:S(2)}, u32[]{:S(2)}) collective-permute-start(s16[272,128]{1,0:T(8,128)(2,1)S(1)} %get-tuple-element.48), channel_id=1, source_target_pairs={{0,4},{4,0},{8,12},{12,8},{1,5},{5,1},{9,13},{13,9},{2,6},{6,2},{1... | collective-permute-start | bytes 208904 | tf_op jit(solution)/shard_map/ppermute | solution.py:561
  58.8 8.1 %collective-permute-start.21 = (s16[272,128]{1,0:T(8,128)(2,1)S(1)}, s16[272,128]{1,0:T(8,128)(2,1)S(1)}, u32[]{:S(2)}, u32[]{:S(2)}) collective-permute-start(s16[272,128]{1,0:T(8,128)(2,1)S(1)} %get-tuple-element.49), channel_id=1, source_target_pairs={{0,8},{4,12},{8,0},{12,4},{1,9},{5,13},{9,1},{13,5},{2,10},{6,14},... | collective-permute-start | bytes 208904 | tf_op jit(solution)/shard_map/ppermute | solution.py:561
  60.5 6.4 %collective-permute-start.22 = (s16[272,128]{1,0:T(8,128)(2,1)S(1)}, s16[272,128]{1,0:T(8,128)(2,1)S(1)}, u32[]{:S(2)}, u32[]{:S(2)}) collective-permute-start(s16[272,128]{1,0:T(8,128)(2,1)S(1)} %get-tuple-element.50), channel_id=1, source_target_pairs={{0,12},{4,8},{8,4},{12,0},{1,13},{5,9},{9,5},{13,1},{2,14},{6,10},... | collective-permute-start | bytes 208904 | tf_op jit(solution)/shard_map/ppermute | solution.py:561
  (7 other events, 34.4 us)

commit v9 on v8

--- a/solution.py
+++ b/solution.py
@@ -19,13 +19,13 @@
 PAIR = 2 * HEAD_SIZE
 LANES = 128
 TAIL = 16
+HALVES = ((0, 3), (1, 2))
 DEVICES = ("req", "sub", "section")
 
 theta_base = 500000.0
 eps_norm = 1e-05
 VMEM = 16 * 2**20
 LARGE_VMEM = 51 * 2**20
-IN_FLIGHT = 4
 
 
 def params(**more):
@@ -76,7 +76,7 @@
         + [jax.ShapeDtypeStruct(other.shape, other.dtype) for other in more],
         scratch_shapes=[pltpu.SemaphoreType.DMA((count + len(more),))],
         compiler_params=params(),
-        cost_estimate=cost([array], [array]),
+        cost_estimate=cost([array] * 2),
         name="staged",
     )(place, array, *more, *after)
 
@@ -262,7 +262,7 @@
         out_specs=[pl.BlockSpec(memory_space=pltpu.VMEM)] * len(shapes),
         out_shape=shapes,
         compiler_params=params(),
-        cost_estimate=cost(gathered, [weight], flops=2 * count * weight.size),
+        cost_estimate=cost(gathered * 1, [weight], flops=2 * count * weight.size),
         name="scale_and_pairs",
     )(place, gain, weight, *gathered)
 
@@ -276,7 +276,7 @@
     for i, (_, _, block) in enumerate(blocks):
         depth = pl.ds(pl.multiple_of(block * width, width), width)
         copies.append(pltpu.make_async_copy(weight_ref.at[depth], held.at[i], sems.at[i]))
-    for copy in copies[:IN_FLIGHT]:
+    for copy in copies:
         copy.start()
     scale = scale_ref[:, :1]
     total = jnp.zeros((rows, columns), jnp.float32)
@@ -284,8 +284,6 @@
         x = ref[z].astype(jnp.float32)
         x = (x * scale * gain_ref[block]).astype(jnp.bfloat16)
         copies[i].wait()
-        if i + IN_FLIGHT < len(copies):
-            copies[i + IN_FLIGHT].start()
         total += jnp.dot(x, held[i], preferred_element_type=jnp.float32)
     for head in range(columns // HEAD_SIZE):
         part = slice(head * HEAD_SIZE, (head + 1) * HEAD_SIZE)
@@ -449,18 +447,16 @@
 def fold_core_kernel(mine_ref, got_ref, *out_refs):
     for i, out_ref in enumerate(out_refs):
         pieces = []
-        for z in range(GROUP_REQUESTS):
-            block = i * GROUP_REQUESTS + z
+        for z in HALVES[i % 2]:
+            block = i // 2 * GROUP_REQUESTS + z
             pieces += pieces_of(mine_ref[block] + got_ref[block])
         encode(out_ref, pieces)
 
 
 def fold_core(mine, got):
     blocks, rows, width = mine.shape
-    count = blocks // GROUP_REQUESTS
-    sent = jax.ShapeDtypeStruct(
-        (GROUP_REQUESTS * width // LANES * rows + TAIL, LANES), jnp.int16
-    )
+    count = 2 * (blocks // GROUP_REQUESTS)
+    sent = jax.ShapeDtypeStruct((2 * width // LANES * rows + TAIL, LANES), jnp.int16)
     return pl.pallas_call(
         fold_core_kernel,
         in_specs=[pl.BlockSpec(memory_space=pltpu.VMEM)] * 2,
@@ -472,18 +468,18 @@
     )(mine, got)
 
 
-def fold_sub_kernel(count, own, *refs):
-    own_refs, in_refs, out_refs = refs[:own], refs[own : own + count], refs[-GROUP_REQUESTS:]
+def fold_sub_kernel(order, count, own, *refs):
+    own_refs, in_refs, out_refs = refs[:own], refs[own : own + count], refs[-len(order) :]
     _, rows, width = own_refs[0].shape
     steps = [step_of(ref) for ref in in_refs]
-    for z, out_ref in enumerate(out_refs):
+    for i, (z, out_ref) in enumerate(zip(order, out_refs)):
         block = own_refs[0][z]
         for ref in own_refs[1:]:
             block = block + ref[z]
         pieces = pieces_of(block)
         for c in range(len(pieces)):
             for ref, step in zip(in_refs, steps):
-                first = (z * len(pieces) + c) * rows
+                first = (i * len(pieces) + c) * rows
                 pieces[c] = pieces[c] + decoded(ref, first, rows, step)
         if z:
             encode(out_ref, pieces)
@@ -492,16 +488,16 @@
                 out_ref[:, c * LANES : (c + 1) * LANES] = piece
 
 
-def fold_sub(own, parts, after=()):
+def fold_sub(order, own, parts, after=()):
     _, rows, width = own[0].shape
     total = jax.ShapeDtypeStruct((rows, width), jnp.float32)
     sent = jax.ShapeDtypeStruct((width // LANES * rows + TAIL, LANES), jnp.int16)
     return pl.pallas_call(
-        functools.partial(fold_sub_kernel, len(parts), len(own)),
+        functools.partial(fold_sub_kernel, order, len(parts), len(own)),
         in_specs=[pl.BlockSpec(memory_space=pltpu.VMEM)] * (len(own) + len(parts))
         + unread(after),
-        out_specs=[pl.BlockSpec(memory_space=pltpu.VMEM)] * GROUP_REQUESTS,
-        out_shape=[total] + [sent] * (GROUP_REQUESTS - 1),
+        out_specs=[pl.BlockSpec(memory_space=pltpu.VMEM)] * len(order),
+        out_shape=[sent if z else total for z in order],
         compiler_params=params(),
         cost_estimate=cost(own, parts),
         name="fold_sub",
@@ -620,7 +616,7 @@
     scale, kept, *parts = scale_and_pairs(place, gain, key_value_weight, gathered)
     parts = [passed(part, "sub", s + 1) for s, part in enumerate(parts)]
     query = queries(place, scale, gain, w_query, cosine, sine, gathered)
-    total, *parts = fold_sub([kept], parts, after=[query])
+    total, *parts = fold_sub((0, 1, 2, 3), [kept], parts, after=[query])
     parts = [passed(part, "req", s + 1) for s, part in enumerate(parts)]
     pages = regroup(pages, after=[total])
     caches = [passed(pages[s], "sub", s) for s in range(1, subs)]
@@ -642,10 +638,12 @@
     kept = outputs(mixed, w_output, mid, end - mid, after=[second])
     parts = fold_core(kept, got_first)
     kept = outputs(mixed, w_output, 0, mid, after=parts[:1])
-    parts = [passed(part, "sub", s + 1) for s, part in enumerate(parts)]
-    total, *parts = fold_sub([kept, got_second], parts)
-    parts = [passed(part, "req", s + 1) for s, part in enumerate(parts)]
-    return finish(gathered[0], total, parts).reshape(hidden.shape)
+    parts = [passed(part, "sub", i // 2 + 1) for i, part in enumerate(parts)]
+    last = {}
+    for half, order in enumerate(HALVES):
+        last.update(zip(order, fold_sub(order, [kept, got_second], parts[half::2])))
+    parts = [passed(last[s], "req", s) for s in range(1, GROUP_REQUESTS)]
+    return finish(gathered[0], last[0], parts).reshape(hidden.shape)
 
 
 def solution(mesh):

time: 68 us -> 64.8 us (0.953)
  waiting for transfers between devices: 17.4 us -> 15.4 us
  Pallas kernels: 17.4 us -> 15.8 us
    ppermute x23 -> x24, waiting for transfers between devices: 17.4 us -> 15.4 us  [passed(): lax.ppermute(array, axis, [(i, i ^ shift) for i in range(lax.axis_size(ax...]
    pallas_call x1, Pallas kernels: 6.24 us -> 4.63 us  [queries(): pl.pallas_call(query_kernel, in_specs=[pl.BlockSpec(memory_space=pltpu.SM...]
    ppermute x23 -> x24, starting transfers between devices: 25.7 us -> 26.1 us  [passed(): lax.ppermute(array, axis, [(i, i ^ shift) for i in range(lax.axis_size(ax...]
  transfers between devices with their start and end apart: 23 -> 24, of which waited for: 8 -> 10; matrix products, arithmetic and copies ran while one was open for 3% -> 3% of each run, Pallas kernels for 20% -> 19%
where the time goes in v9:
time: 64.8 us; the launch traced here: 64.4 us
  starting transfers between devices  26.1 us (40%)
  Pallas kernels  15.8 us (24%)
  waiting for transfers between devices  15.4 us (24%)
  local copies, waits for them, and re-layouts  5.12 us (8%)
  other arithmetic  1.71 us (3%)
    ppermute x24, starting transfers between devices, passed(): lax.ppermute(array, axis, [(i, i ^ shift) for i in range(lax.axis_size(ax...  26.1 us
    ppermute x24, waiting for transfers between devices, passed(): lax.ppermute(array, axis, [(i, i ^ shift) for i in range(lax.axis_size(ax...  15.4 us
    unnamed x16, local copies, waits for them, and re-layouts  5.11 us
    pallas_call x1, Pallas kernels, queries(): pl.pallas_call(query_kernel, in_specs=[pl.BlockSpec(memory_space=pltpu.SM...  4.63 us
    pallas_call x2, Pallas kernels, staged(): pl.pallas_call(functools.partial(stage_kernel, order, len(more)), in_spec...  2.85 us
    pallas_call x1, Pallas kernels, attend(): pl.pallas_call(attend_kernel, in_specs=[pl.BlockSpec(memory_space=pltpu.S...  2.18 us
    pallas_call x4, Pallas kernels, outputs(): pl.pallas_call(functools.partial(output_kernel, first), in_specs=[pl.Bloc...  1.89 us
    pallas_call x1, Pallas kernels, used_pages(): pl.pallas_call(pages_kernel, grid_spec=pltpu.PrefetchScalarGridSpec(num_s...  1.51 us
  transfers between devices with their start and end apart: 24, of which 10 were waited for; matrix products, arithmetic and copies ran while one was open for 3% of the time, Pallas kernels for 19%

profile of v9, /device:TPU:0, one launch (start us, length us, event | category | flops | bytes accessed | tf_op | source)
XLA Modules:
  0.0 64.4 jit_solution(13571977088780206927)
XLA Ops:
  0.0 5.0 %collective-permute-start.2 = (bf16[64,512]{1,0:T(8,128)(2,1)}, bf16[64,512]{1,0:T(8,128)(2,1)S(1)}, u32[]{:S(2)}, u32[]{:S(2)}) collective-permute-start(bf16[64,512]{1,0:T(8,128)(2,1)} %bitcast.16), channel_id=1, source_target_pairs={{0,12},{4,8},{8,4},{12,0},{1,13},{5,9},{9,5},{13,1},{2,14},{6,10},... | collective-permute-start | bytes 196616 | tf_op jit(solution)/shard_map/ppermute | solution.py:557
  6.4 1.2 %copy-done.1 = bf16[16,16,2048]{2,1,0:T(8,128)(2,1)S(1)} copy-done((bf16[16,16,2048]{2,1,0:T(8,128)(2,1)S(1)}, bf16[16,16,2048]{2,1,0:T(8,128)(2,1)}, u32[]{:S(2)}) %copy-start.1) | copy-done | bytes 1048600
  9.1 1.5 %used_pages.1 = (bf16[64,512]{1,0:T(8,128)(2,1)S(1)}, bf16[2,128,256]{2,1,0:T(8,128)(2,1)S(1)}, bf16[2,128,256]{2,1,0:T(8,128)(2,1)S(1)}, bf16[2,128,256]{2,1,0:T(8,128)(2,1)S(1)}, bf16[2,128,256]{2,1,0:T(8,128)(2,1)S(1)}) custom-call(s32[4,32]{1,0:T(4,128)S(1)} %copy-done.4, s32[3]{0:T(128)S(1)} %pad_add_fusion.place, ...), custom_call_target="tpu_custom_call" | custom-call | bytes 1048576 | tf_op jit(solution)/shard_map/used_pages/pallas_call | solution.py:141
  10.7 1.5 %collective-permute-start.11 = (bf16[2,128,256]{2,1,0:T(8,128)(2,1)S(1)}, bf16[2,128,256]{2,1,0:T(8,128)(2,1)S(1)}, u32[]{:S(2)}, u32[]{:S(2)}) collective-permute-start(bf16[2,128,256]{2,1,0:T(8,128)(2,1)S(1)} %get-tuple-element.43), channel_id=1, source_target_pairs={{0,4},{4,0},{8,12},{12,8},{1,5},{5,1},{9,13},{13,9},{2,6},{6,2},{1... | collective-permute-start | bytes 393224 | tf_op jit(solution)/shard_map/ppermute | solution.py:557
  12.2 2.9 %collective-permute-start.12 = (bf16[2,128,256]{2,1,0:T(8,128)(2,1)S(1)}, bf16[2,128,256]{2,1,0:T(8,128)(2,1)S(1)}, u32[]{:S(2)}, u32[]{:S(2)}) collective-permute-start(bf16[2,128,256]{2,1,0:T(8,128)(2,1)S(1)} %get-tuple-element.44), channel_id=1, source_target_pairs={{0,8},{4,12},{8,0},{12,4},{1,9},{5,13},{9,1},{13,5},{2,10},{6,14},... | collective-permute-start | bytes 393224 | tf_op jit(solution)/shard_map/ppermute | solution.py:557
  15.2 1.8 %collective-permute-start.3 = (bf16[4,64,512]{2,1,0:T(8,128)(2,1)S(1)}, bf16[4,64,512]{2,1,0:T(8,128)(2,1)S(1)}, u32[]{:S(2)}, u32[]{:S(2)}) collective-permute-start(bf16[4,64,512]{2,1,0:T(8,128)(2,1)S(1)} %pack.1.refs_1_.refs_0_.rows_ref), channel_id=1, source_target_pairs={{0,2},{2,0},{1,3},{3,1},{4,6},{6,4},{5,7},{7,5},{8,10},{10,8},{9,1... | collective-permute-start | bytes 786440 | tf_op jit(solution)/shard_map/ppermute | solution.py:557
  17.7 1.6 %copy-done = bf16[512,2048]{1,0:T(8,128)(2,1)S(1)} copy-done((bf16[512,2048]{1,0:T(8,128)(2,1)S(1)}, bf16[512,2048]{1,0:T(8,128)(2,1)}, u32[]{:S(2)}) %copy-start) | copy-done | bytes 2097176
  20.0 1.0 %staged.2 = (bf16[8,512,256]{2,1,0:T(8,128)(2,1)S(1)}, f32[8,128]{1,0:T(8,128)S(1)}, f32[16,1,512]{2,1,0:T(1,128)S(1)}) custom-call(s32[3]{0:T(128)S(1)} %pad_add_fusion.1.place, bf16[512,2048]{1,0:T(8,128)(2,1)S(1)} %copy-done, f32[16,1,512]{2,1,0:T(1,128)S(1)} %bitcast.20, bf16[4,64,512]{2,1,0:T(8,128)(2,1)S(1)} %pack.1.refs_1_.refs_0_.rows_ref), custom_call_target="tpu_custom_call" | custom-call | bytes 4194304 | tf_op jit(solution)/shard_map/staged/pallas_call | solution.py:66
  22.0 1.4 %collective-permute-done.5.refs_3_ = bf16[4,64,512]{2,1,0:T(8,128)(2,1)S(1)} collective-permute-done((bf16[4,64,512]{2,1,0:T(8,128)(2,1)S(1)}, bf16[4,64,512]{2,1,0:T(8,128)(2,1)S(1)}, u32[]{:S(2)}, u32[]{:S(2)}) %collective-permute-start.5) | collective-permute-done | bytes 262176 | tf_op jit(solution)/shard_map/ppermute | solution.py:557
  23.4 1.4 %scale_and_pairs.1 = (f32[64,128]{1,0:T(8,128)S(1)}, f32[4,64,256]{2,1,0:T(8,128)S(1)}, s16[528,128]{1,0:T(8,128)(2,1)S(1)}) custom-call(s32[3]{0:T(128)S(1)} %pad_add_fusion.1.place, f32[16,1,512]{2,1,0:T(1,128)S(1)} %get-tuple-element.31.gain_ref, bf16[8,512,256]{2,1,0:T(8,128)(2,1)S(1)} %get-tuple-element.32.weight_ref, ...), custom_call_target="tpu_custom_call" | custom-call | flops 134217728 | bytes 3145728 | tf_op jit(solution)/shard_map/scale_and_pairs/pallas_call | solution.py:258
  24.8 1.6 %collective-permute-start.6 = (s16[528,128]{1,0:T(8,128)(2,1)S(1)}, s16[528,128]{1,0:T(8,128)(2,1)S(1)}, u32[]{:S(2)}, u32[]{:S(2)}) collective-permute-start(s16[528,128]{1,0:T(8,128)(2,1)S(1)} %get-tuple-element.36), channel_id=1, source_target_pairs={{0,2},{2,0},{1,3},{3,1},{4,6},{6,4},{5,7},{7,5},{8,10},{10,8},{9,1... | collective-permute-start | bytes 405512 | tf_op jit(solution)/shard_map/ppermute | solution.py:557
  26.5 4.6 %queries.1.refs_2_.refs_0_.q_ref = bf16[4,16,512]{2,1,0:T(8,128)(2,1)S(1)} custom-call(s32[3]{0:T(128)S(1)} %pad_add_fusion.1.place, f32[64,128]{1,0:T(8,128)S(1)} %get-tuple-element.34.scale_ref, f32[16,1,512]{2,1,0:T(1,128)S(1)} %get-tuple-element.31.gain_ref, bf16[8192,512]{1,0:T(8,128)(2,1)} %weight_ref.1, f32[64,128]{1,0:T(8,128)S(1)} %bitcast.12, ...), custom_call_target="tpu_custom_call" | custom-call | flops 536870912 | bytes 8388608 | tf_op jit(solution)/shard_map/queries/pallas_call | solution.py:302
  31.3 0.9 %collective-permute-start.14 = (bf16[4,128,256]{2,1,0:T(8,128)(2,1)S(1)}, bf16[4,128,256]{2,1,0:T(8,128)(2,1)S(1)}, u32[]{:S(2)}, u32[]{:S(2)}) collective-permute-start(bf16[4,128,256]{2,1,0:T(8,128)(2,1)S(1)} %get-tuple-element.47), channel_id=1, source_target_pairs={{0,2},{2,0},{1,3},{3,1},{4,6},{6,4},{5,7},{7,5},{8,10},{10,8},{9,1... | collective-permute-start | bytes 786440 | tf_op jit(solution)/shard_map/ppermute | solution.py:557
  32.8 3.5 %collective-permute-start.8 = (s16[144,128]{1,0:T(8,128)(2,1)S(1)}, s16[144,128]{1,0:T(8,128)(2,1)S(1)}, u32[]{:S(2)}, u32[]{:S(2)}) collective-permute-start(s16[144,128]{1,0:T(8,128)(2,1)S(1)} %get-tuple-element.39), channel_id=1, source_target_pairs={{0,8},{4,12},{8,0},{12,4},{1,9},{5,13},{9,1},{13,5},{2,10},{6,14},... | collective-permute-start | bytes 110600 | tf_op jit(solution)/shard_map/ppermute | solution.py:557
  36.6 1.9 %staged.3 = (bf16[16,512,512]{2,1,0:T(8,128)(2,1)S(1)}, f32[8,128]{1,0:T(8,128)S(1)}) custom-call(s32[3]{0:T(128)S(1)} %pad_add_fusion.1.place, bf16[512,8192]{1,0:T(8,128)(2,1)S(1)} %bitcast.11, bf16[4,16,512]{2,1,0:T(8,128)(2,1)S(1)} %queries.1.refs_2_.refs_0_.q_ref), custom_call_target="tpu_custom_call" | custom-call | bytes 16777216 | tf_op jit(solution)/shard_map/staged/pallas_call | solution.py:66
  38.7 3.4 %collective-permute-done.9.refs_2_ = s16[144,128]{1,0:T(8,128)(2,1)S(1)} collective-permute-done((s16[144,128]{1,0:T(8,128)(2,1)S(1)}, s16[144,128]{1,0:T(8,128)(2,1)S(1)}, u32[]{:S(2)}, u32[]{:S(2)}) %collective-permute-start.9) | collective-permute-done | bytes 36896 | tf_op jit(solution)/shard_map/ppermute | solution.py:557
  42.7 1.1 %collective-permute-done.10.other_ref = f32[64,256]{1,0:T(8,128)S(1)} collective-permute-done((f32[64,256]{1,0:T(8,128)S(1)}, f32[64,256]{1,0:T(8,128)S(1)}, u32[]{:S(2)}, u32[]{:S(2)}) %collective-permute-start.10) | collective-permute-done | bytes 65568 | tf_op jit(solution)/shard_map/ppermute | solution.py:557
  43.9 2.2 %attend.1.x_ref = bf16[4,16,512]{2,1,0:T(8,128)(2,1)S(1)} custom-call(s32[3]{0:T(128)S(1)} %pad_add_fusion.1.place, s32[4]{0:T(128)S(1)} %copy-done.5, bf16[4,16,512]{2,1,0:T(8,128)(2,1)S(1)} %queries.1.refs_2_.refs_0_.q_ref, f32[64,256]{1,0:T(8,128)S(1)} %fold_pairs.1.refs_1_.mine_ref, f32[64,256]{1,0:T(8,128)S(1)} %collective-permute-done.10.other_ref, ...), custom_call_target="tpu_custom_call" | custom-call | flops 268435456 | bytes 3145728 | tf_op jit(solution)/shard_map/attend/pallas_call | solution.py:379
  48.7 1.2 %collective-permute-start.20 = (s16[528,128]{1,0:T(8,128)(2,1)S(1)}, s16[528,128]{1,0:T(8,128)(2,1)S(1)}, u32[]{:S(2)}, u32[]{:S(2)}) collective-permute-start(s16[528,128]{1,0:T(8,128)(2,1)S(1)} %get-tuple-element.51), channel_id=1, source_target_pairs={{0,2},{2,0},{1,3},{3,1},{4,6},{6,4},{5,7},{7,5},{8,10},{10,8},{9,1... | collective-permute-start | bytes 405512 | tf_op jit(solution)/shard_map/ppermute | solution.py:557
  50.0 0.9 %collective-permute-start.19 = (s16[528,128]{1,0:T(8,128)(2,1)S(1)}, s16[528,128]{1,0:T(8,128)(2,1)S(1)}, u32[]{:S(2)}, u32[]{:S(2)}) collective-permute-start(s16[528,128]{1,0:T(8,128)(2,1)S(1)} %get-tuple-element.49.refs_0_), channel_id=1, source_target_pairs={{0,2},{2,0},{1,3},{3,1},{4,6},{6,4},{5,7},{7,5},{8,10},{10,8},{9,1... | collective-permute-start | bytes 405512 | tf_op jit(solution)/shard_map/ppermute | solution.py:557
  51.3 3.9 %collective-permute-done.20.refs_2_ = s16[528,128]{1,0:T(8,128)(2,1)S(1)} collective-permute-done((s16[528,128]{1,0:T(8,128)(2,1)S(1)}, s16[528,128]{1,0:T(8,128)(2,1)S(1)}, u32[]{:S(2)}, u32[]{:S(2)}) %collective-permute-start.20) | collective-permute-done | bytes 135200 | tf_op jit(solution)/shard_map/ppermute | solution.py:557
  55.5 1.3 %collective-permute-start.22 = (s16[272,128]{1,0:T(8,128)(2,1)S(1)}, s16[272,128]{1,0:T(8,128)(2,1)S(1)}, u32[]{:S(2)}, u32[]{:S(2)}) collective-permute-start(s16[272,128]{1,0:T(8,128)(2,1)S(1)} %get-tuple-element.53), channel_id=1, source_target_pairs={{0,8},{4,12},{8,0},{12,4},{1,9},{5,13},{9,1},{13,5},{2,10},{6,14},... | collective-permute-start | bytes 208904 | tf_op jit(solution)/shard_map/ppermute | solution.py:557
  57.5 2.6 %collective-permute-start.23 = (s16[272,128]{1,0:T(8,128)(2,1)S(1)}, s16[272,128]{1,0:T(8,128)(2,1)S(1)}, u32[]{:S(2)}, u32[]{:S(2)}) collective-permute-start(s16[272,128]{1,0:T(8,128)(2,1)S(1)} %get-tuple-element.54), channel_id=1, source_target_pairs={{0,12},{4,8},{8,4},{12,0},{1,13},{5,9},{9,5},{13,1},{2,14},{6,10},... | collective-permute-start | bytes 208904 | tf_op jit(solution)/shard_map/ppermute | solution.py:557
  60.7 3.0 %collective-permute-done.23.refs_2_ = s16[272,128]{1,0:T(8,128)(2,1)S(1)} collective-permute-done((s16[272,128]{1,0:T(8,128)(2,1)S(1)}, s16[272,128]{1,0:T(8,128)(2,1)S(1)}, u32[]{:S(2)}, u32[]{:S(2)}) %collective-permute-start.23) | collective-permute-done | bytes 69664 | tf_op jit(solution)/shard_map/ppermute | solution.py:557
  (70 shorter events, 12.6 us)
Async XLA Ops:
  0.0 15.1 %collective-permute-start.2 = (bf16[64,512]{1,0:T(8,128)(2,1)}, bf16[64,512]{1,0:T(8,128)(2,1)S(1)}, u32[]{:S(2)}, u32[]{:S(2)}) collective-permute-start(bf16[64,512]{1,0:T(8,128)(2,1)} %bitcast.16), channel_id=1, source_target_pairs={{0,12},{4,8},{8,4},{12,0},{1,13},{5,9},{9,5},{13,1},{2,14},{6,10},... | collective-permute-start | bytes 196616 | tf_op jit(solution)/shard_map/ppermute | solution.py:557
  5.0 10.1 %collective-permute-start.1 = (bf16[64,512]{1,0:T(8,128)(2,1)}, bf16[64,512]{1,0:T(8,128)(2,1)S(1)}, u32[]{:S(2)}, u32[]{:S(2)}) collective-permute-start(bf16[64,512]{1,0:T(8,128)(2,1)} %bitcast.17), channel_id=1, source_target_pairs={{0,8},{4,12},{8,0},{12,4},{1,9},{5,13},{9,1},{13,5},{2,10},{6,14},... | collective-permute-start | bytes 196616 | tf_op jit(solution)/shard_map/ppermute | solution.py:557
  5.1 10.1 %collective-permute-start = (bf16[64,512]{1,0:T(8,128)(2,1)}, bf16[64,512]{1,0:T(8,128)(2,1)S(1)}, u32[]{:S(2)}, u32[]{:S(2)}) collective-permute-start(bf16[64,512]{1,0:T(8,128)(2,1)} %bitcast.18), channel_id=1, source_target_pairs={{0,4},{4,0},{8,12},{12,8},{1,5},{5,1},{9,13},{13,9},{2,6},{6,2},{1... | collective-permute-start | bytes 196616 | tf_op jit(solution)/shard_map/ppermute | solution.py:557
  10.7 20.6 %collective-permute-start.11 = (bf16[2,128,256]{2,1,0:T(8,128)(2,1)S(1)}, bf16[2,128,256]{2,1,0:T(8,128)(2,1)S(1)}, u32[]{:S(2)}, u32[]{:S(2)}) collective-permute-start(bf16[2,128,256]{2,1,0:T(8,128)(2,1)S(1)} %get-tuple-element.43), channel_id=1, source_target_pairs={{0,4},{4,0},{8,12},{12,8},{1,5},{5,1},{9,13},{13,9},{2,6},{6,2},{1... | collective-permute-start | bytes 393224 | tf_op jit(solution)/shard_map/ppermute | solution.py:557
  12.2 19.1 %collective-permute-start.12 = (bf16[2,128,256]{2,1,0:T(8,128)(2,1)S(1)}, bf16[2,128,256]{2,1,0:T(8,128)(2,1)S(1)}, u32[]{:S(2)}, u32[]{:S(2)}) collective-permute-start(bf16[2,128,256]{2,1,0:T(8,128)(2,1)S(1)} %get-tuple-element.44), channel_id=1, source_target_pairs={{0,8},{4,12},{8,0},{12,4},{1,9},{5,13},{9,1},{13,5},{2,10},{6,14},... | collective-permute-start | bytes 393224 | tf_op jit(solution)/shard_map/ppermute | solution.py:557
  15.1 16.2 %collective-permute-start.13 = (bf16[2,128,256]{2,1,0:T(8,128)(2,1)S(1)}, bf16[2,128,256]{2,1,0:T(8,128)(2,1)S(1)}, u32[]{:S(2)}, u32[]{:S(2)}) collective-permute-start(bf16[2,128,256]{2,1,0:T(8,128)(2,1)S(1)} %get-tuple-element.45), channel_id=1, source_target_pairs={{0,12},{4,8},{8,4},{12,0},{1,13},{5,9},{9,5},{13,1},{2,14},{6,10},... | collective-permute-start | bytes 393224 | tf_op jit(solution)/shard_map/ppermute | solution.py:557
  15.2 6.7 %collective-permute-start.3 = (bf16[4,64,512]{2,1,0:T(8,128)(2,1)S(1)}, bf16[4,64,512]{2,1,0:T(8,128)(2,1)S(1)}, u32[]{:S(2)}, u32[]{:S(2)}) collective-permute-start(bf16[4,64,512]{2,1,0:T(8,128)(2,1)S(1)} %pack.1.refs_1_.refs_0_.rows_ref), channel_id=1, source_target_pairs={{0,2},{2,0},{1,3},{3,1},{4,6},{6,4},{5,7},{7,5},{8,10},{10,8},{9,1... | collective-permute-start | bytes 786440 | tf_op jit(solution)/shard_map/ppermute | solution.py:557
  17.7 4.3 %collective-permute-start.4 = (bf16[4,64,512]{2,1,0:T(8,128)(2,1)S(1)}, bf16[4,64,512]{2,1,0:T(8,128)(2,1)S(1)}, u32[]{:S(2)}, u32[]{:S(2)}) collective-permute-start(bf16[4,64,512]{2,1,0:T(8,128)(2,1)S(1)} %pack.1.refs_1_.refs_0_.rows_ref), channel_id=1, source_target_pairs={{0,1},{1,0},{2,3},{3,2},{4,5},{5,4},{6,7},{7,6},{8,9},{9,8},{10,11... | collective-permute-start | bytes 786440 | tf_op jit(solution)/shard_map/ppermute | solution.py:557
  21.9 1.5 %collective-permute-start.5 = (bf16[4,64,512]{2,1,0:T(8,128)(2,1)S(1)}, bf16[4,64,512]{2,1,0:T(8,128)(2,1)S(1)}, u32[]{:S(2)}, u32[]{:S(2)}) collective-permute-start(bf16[4,64,512]{2,1,0:T(8,128)(2,1)S(1)} %gate.2.refs_1_), channel_id=1, source_target_pairs={{0,1},{1,0},{2,3},{3,2},{4,5},{5,4},{6,7},{7,6},{8,9},{9,8},{10,11... | collective-permute-start | bytes 786440 | tf_op jit(solution)/shard_map/ppermute | solution.py:557
  24.8 6.3 %collective-permute-start.6 = (s16[528,128]{1,0:T(8,128)(2,1)S(1)}, s16[528,128]{1,0:T(8,128)(2,1)S(1)}, u32[]{:S(2)}, u32[]{:S(2)}) collective-permute-start(s16[528,128]{1,0:T(8,128)(2,1)S(1)} %get-tuple-element.36), channel_id=1, source_target_pairs={{0,2},{2,0},{1,3},{3,1},{4,6},{6,4},{5,7},{7,5},{8,10},{10,8},{9,1... | collective-permute-start | bytes 405512 | tf_op jit(solution)/shard_map/ppermute | solution.py:557
  31.3 10.8 %collective-permute-start.14 = (bf16[4,128,256]{2,1,0:T(8,128)(2,1)S(1)}, bf16[4,128,256]{2,1,0:T(8,128)(2,1)S(1)}, u32[]{:S(2)}, u32[]{:S(2)}) collective-permute-start(bf16[4,128,256]{2,1,0:T(8,128)(2,1)S(1)} %get-tuple-element.47), channel_id=1, source_target_pairs={{0,2},{2,0},{1,3},{3,1},{4,6},{6,4},{5,7},{7,5},{8,10},{10,8},{9,1... | collective-permute-start | bytes 786440 | tf_op jit(solution)/shard_map/ppermute | solution.py:557
  32.2 6.4 %collective-permute-start.7 = (s16[144,128]{1,0:T(8,128)(2,1)S(1)}, s16[144,128]{1,0:T(8,128)(2,1)S(1)}, u32[]{:S(2)}, u32[]{:S(2)}) collective-permute-start(s16[144,128]{1,0:T(8,128)(2,1)S(1)} %get-tuple-element.38), channel_id=1, source_target_pairs={{0,4},{4,0},{8,12},{12,8},{1,5},{5,1},{9,13},{13,9},{2,6},{6,2},{1... | collective-permute-start | bytes 110600 | tf_op jit(solution)/shard_map/ppermute | solution.py:557
  32.8 5.9 %collective-permute-start.8 = (s16[144,128]{1,0:T(8,128)(2,1)S(1)}, s16[144,128]{1,0:T(8,128)(2,1)S(1)}, u32[]{:S(2)}, u32[]{:S(2)}) collective-permute-start(s16[144,128]{1,0:T(8,128)(2,1)S(1)} %get-tuple-element.39), channel_id=1, source_target_pairs={{0,8},{4,12},{8,0},{12,4},{1,9},{5,13},{9,1},{13,5},{2,10},{6,14},... | collective-permute-start | bytes 110600 | tf_op jit(solution)/shard_map/ppermute | solution.py:557
  36.3 5.8 %collective-permute-start.9 = (s16[144,128]{1,0:T(8,128)(2,1)S(1)}, s16[144,128]{1,0:T(8,128)(2,1)S(1)}, u32[]{:S(2)}, u32[]{:S(2)}) collective-permute-start(s16[144,128]{1,0:T(8,128)(2,1)S(1)} %get-tuple-element.40), channel_id=1, source_target_pairs={{0,12},{4,8},{8,4},{12,0},{1,13},{5,9},{9,5},{13,1},{2,14},{6,10},... | collective-permute-start | bytes 110600 | tf_op jit(solution)/shard_map/ppermute | solution.py:557
  38.5 5.3 %collective-permute-start.15 = (bf16[4,128,256]{2,1,0:T(8,128)(2,1)S(1)}, bf16[4,128,256]{2,1,0:T(8,128)(2,1)S(1)}, u32[]{:S(2)}, u32[]{:S(2)}) collective-permute-start(bf16[4,128,256]{2,1,0:T(8,128)(2,1)S(1)} %get-tuple-element.46.refs_0_), channel_id=1, source_target_pairs={{0,1},{1,0},{2,3},{3,2},{4,5},{5,4},{6,7},{7,6},{8,9},{9,8},{10,11... | collective-permute-start | bytes 786440 | tf_op jit(solution)/shard_map/ppermute | solution.py:557
  42.2 1.7 %collective-permute-start.16 = (bf16[4,128,256]{2,1,0:T(8,128)(2,1)S(1)}, bf16[4,128,256]{2,1,0:T(8,128)(2,1)S(1)}, u32[]{:S(2)}, u32[]{:S(2)}) collective-permute-start(bf16[4,128,256]{2,1,0:T(8,128)(2,1)S(1)} %gate.3.refs_1_), channel_id=1, source_target_pairs={{0,1},{1,0},{2,3},{3,2},{4,5},{5,4},{6,7},{7,6},{8,9},{9,8},{10,11... | collective-permute-start | bytes 786440 | tf_op jit(solution)/shard_map/ppermute | solution.py:557
  42.2 1.6 %collective-permute-start.10 = (f32[64,256]{1,0:T(8,128)S(1)}, f32[64,256]{1,0:T(8,128)S(1)}, u32[]{:S(2)}, u32[]{:S(2)}) collective-permute-start(f32[64,256]{1,0:T(8,128)S(1)} %fold_pairs.1.refs_1_.mine_ref), channel_id=1, source_target_pairs={{0,1},{1,0},{2,3},{3,2},{4,5},{5,4},{6,7},{7,6},{8,9},{9,8},{10,11... | collective-permute-start | bytes 196616 | tf_op jit(solution)/shard_map/ppermute | solution.py:557
  46.5 2.0 %collective-permute-start.17 = (f32[4,64,512]{2,1,0:T(8,128)S(1)}, f32[4,64,512]{2,1,0:T(8,128)S(1)}, u32[]{:S(2)}, u32[]{:S(2)}) collective-permute-start(f32[4,64,512]{2,1,0:T(8,128)S(1)} %outputs.4.refs_0_), channel_id=1, source_target_pairs={{0,1},{1,0},{2,3},{3,2},{4,5},{5,4},{6,7},{7,6},{8,9},{9,8},{10,11... | collective-permute-start | bytes 1572872 | tf_op jit(solution)/shard_map/ppermute | solution.py:557
  47.2 4.1 %collective-permute-start.18 = (f32[4,64,512]{2,1,0:T(8,128)S(1)}, f32[4,64,512]{2,1,0:T(8,128)S(1)}, u32[]{:S(2)}, u32[]{:S(2)}) collective-permute-start(f32[4,64,512]{2,1,0:T(8,128)S(1)} %outputs.5.refs_0_), channel_id=1, source_target_pairs={{0,1},{1,0},{2,3},{3,2},{4,5},{5,4},{6,7},{7,6},{8,9},{9,8},{10,11... | collective-permute-start | bytes 1572872 | tf_op jit(solution)/shard_map/ppermute | solution.py:557
  48.7 6.5 %collective-permute-start.20 = (s16[528,128]{1,0:T(8,128)(2,1)S(1)}, s16[528,128]{1,0:T(8,128)(2,1)S(1)}, u32[]{:S(2)}, u32[]{:S(2)}) collective-permute-start(s16[528,128]{1,0:T(8,128)(2,1)S(1)} %get-tuple-element.51), channel_id=1, source_target_pairs={{0,2},{2,0},{1,3},{3,1},{4,6},{6,4},{5,7},{7,5},{8,10},{10,8},{9,1... | collective-permute-start | bytes 405512 | tf_op jit(solution)/shard_map/ppermute | solution.py:557
  50.0 7.4 %collective-permute-start.19 = (s16[528,128]{1,0:T(8,128)(2,1)S(1)}, s16[528,128]{1,0:T(8,128)(2,1)S(1)}, u32[]{:S(2)}, u32[]{:S(2)}) collective-permute-start(s16[528,128]{1,0:T(8,128)(2,1)S(1)} %get-tuple-element.49.refs_0_), channel_id=1, source_target_pairs={{0,2},{2,0},{1,3},{3,1},{4,6},{6,4},{5,7},{7,5},{8,10},{10,8},{9,1... | collective-permute-start | bytes 405512 | tf_op jit(solution)/shard_map/ppermute | solution.py:557
  55.4 4.6 %collective-permute-start.21 = (s16[272,128]{1,0:T(8,128)(2,1)S(1)}, s16[272,128]{1,0:T(8,128)(2,1)S(1)}, u32[]{:S(2)}, u32[]{:S(2)}) collective-permute-start(s16[272,128]{1,0:T(8,128)(2,1)S(1)} %get-tuple-element.52), channel_id=1, source_target_pairs={{0,4},{4,0},{8,12},{12,8},{1,5},{5,1},{9,13},{13,9},{2,6},{6,2},{1... | collective-permute-start | bytes 208904 | tf_op jit(solution)/shard_map/ppermute | solution.py:557
  55.5 5.3 %collective-permute-start.22 = (s16[272,128]{1,0:T(8,128)(2,1)S(1)}, s16[272,128]{1,0:T(8,128)(2,1)S(1)}, u32[]{:S(2)}, u32[]{:S(2)}) collective-permute-start(s16[272,128]{1,0:T(8,128)(2,1)S(1)} %get-tuple-element.53), channel_id=1, source_target_pairs={{0,8},{4,12},{8,0},{12,4},{1,9},{5,13},{9,1},{13,5},{2,10},{6,14},... | collective-permute-start | bytes 208904 | tf_op jit(solution)/shard_map/ppermute | solution.py:557
  57.5 6.2 %collective-permute-start.23 = (s16[272,128]{1,0:T(8,128)(2,1)S(1)}, s16[272,128]{1,0:T(8,128)(2,1)S(1)}, u32[]{:S(2)}, u32[]{:S(2)}) collective-permute-start(s16[272,128]{1,0:T(8,128)(2,1)S(1)} %get-tuple-element.54), channel_id=1, source_target_pairs={{0,12},{4,8},{8,4},{12,0},{1,13},{5,9},{9,5},{13,1},{2,14},{6,10},... | collective-permute-start | bytes 208904 | tf_op jit(solution)/shard_map/ppermute | solution.py:557
  (8 other events, 49.3 us)

commit v10 on v9

--- a/solution.py
+++ b/solution.py
@@ -19,7 +19,7 @@
 PAIR = 2 * HEAD_SIZE
 LANES = 128
 TAIL = 16
-HALVES = ((0, 3), (1, 2))
+HALVES = ((2, 3), (0, 1))
 DEVICES = ("req", "sub", "section")
 
 theta_base = 500000.0
@@ -45,15 +45,20 @@
     return vectors * cosine + pltpu.roll(vectors, HEAD_SIZE // 2, vectors.ndim - 1) * sine
 
 
-def stage_kernel(order, count, place, block_ref, *refs):
-    out_ref, token_ref, *outs, sems = refs[-3 - count :]
+def block_copies(order, place, block_ref, out_ref, sems):
     width = out_ref.shape[2]
-    copies = [
-        pltpu.make_async_copy(refs[i], outs[i], sems.at[len(order) + i]) for i in range(count)
-    ]
+    copies = []
     for i, block in enumerate(order):
         columns = pl.ds(pl.multiple_of(block(place) * width, width), width)
         copies.append(pltpu.make_async_copy(block_ref.at[:, columns], out_ref.at[i], sems.at[i]))
+    return copies
+
+
+def stage_kernel(order, count, place, block_ref, *refs):
+    out_ref, token_ref, *outs, sems = refs[-3 - count :]
+    copies = block_copies(order, place, block_ref, out_ref, sems)
+    for i in range(count):
+        copies.append(pltpu.make_async_copy(refs[i], outs[i], sems.at[len(order) + i]))
     for copy in copies:
         copy.start()
     token_ref[...] = jnp.zeros_like(token_ref)
@@ -76,7 +81,7 @@
         + [jax.ShapeDtypeStruct(other.shape, other.dtype) for other in more],
         scratch_shapes=[pltpu.SemaphoreType.DMA((count + len(more),))],
         compiler_params=params(),
-        cost_estimate=cost([array] * 2),
+        cost_estimate=cost([array], [array]),
         name="staged",
     )(place, array, *more, *after)
 
@@ -262,7 +267,7 @@
         out_specs=[pl.BlockSpec(memory_space=pltpu.VMEM)] * len(shapes),
         out_shape=shapes,
         compiler_params=params(),
-        cost_estimate=cost(gathered * 1, [weight], flops=2 * count * weight.size),
+        cost_estimate=cost(gathered, [weight], flops=2 * count * weight.size),
         name="scale_and_pairs",
     )(place, gain, weight, *gathered)
 
@@ -317,8 +322,13 @@
     )(place, scale, gain, weight, cosine, sine, *gathered)
 
 
-def attend_kernel(place, lengths, q_ref, mine_ref, other_ref, cos_ref, sin_ref, *refs):
-    caches, out_ref, key_ref, value_ref = refs[:-3], refs[-3], refs[-2], refs[-1]
+def attend_kernel(
+    order, place, lengths, q_ref, mine_ref, other_ref, cos_ref, sin_ref, block_ref, *refs
+):
+    caches, (out_ref, held_ref, key_ref, value_ref, sems) = refs[:-5], refs[-5:]
+    copies = block_copies(order, place, block_ref, held_ref, sems)
+    for copy in copies:
+        copy.start()
     request, sub, core = place[0], place[1], place[2]
     subs, span = len(caches) // 2, caches[0].shape[1]
     targets = 2 * subs
@@ -373,20 +383,29 @@
             out_ref[r, :, h * HEAD_SIZE : (h + 1) * HEAD_SIZE] = mixed[
                 h * ROWS : (h + 1) * ROWS
             ]
-
-
-def attend(place, lengths, query, mine, other, cosine, sine, caches):
-    return pl.pallas_call(
-        attend_kernel,
+    for copy in copies:
+        copy.wait()
+
+
+def attend(place, lengths, query, mine, other, cosine, sine, weight, width, order, caches):
+    count = len(order)
+    return pl.pallas_call(
+        functools.partial(attend_kernel, order),
         in_specs=[pl.BlockSpec(memory_space=pltpu.SMEM)] * 2
-        + [pl.BlockSpec(memory_space=pltpu.VMEM)] * (5 + len(caches)),
-        out_specs=pl.BlockSpec(memory_space=pltpu.VMEM),
-        out_shape=jax.ShapeDtypeStruct(query.shape, jnp.bfloat16),
-        scratch_shapes=[pltpu.VMEM(cosine.shape, jnp.float32)] * 2,
+        + [pl.BlockSpec(memory_space=pltpu.VMEM)] * 5
+        + [pl.BlockSpec(memory_space=pltpu.HBM)]
+        + [pl.BlockSpec(memory_space=pltpu.VMEM)] * len(caches),
+        out_specs=[pl.BlockSpec(memory_space=pltpu.VMEM)] * 2,
+        out_shape=[
+            jax.ShapeDtypeStruct(query.shape, jnp.bfloat16),
+            jax.ShapeDtypeStruct((count, weight.shape[0], width), weight.dtype),
+        ],
+        scratch_shapes=[pltpu.VMEM(cosine.shape, jnp.float32)] * 2
+        + [pltpu.SemaphoreType.DMA((count,))],
         compiler_params=params(),
         cost_estimate=cost(caches, caches, caches, flops=2**28),
         name="attend",
-    )(place, lengths, query, mine, other, cosine, sine, *caches)
+    )(place, lengths, query, mine, other, cosine, sine, weight, *caches)
 
 
 def output_kernel(first, x_ref, weight_ref, *refs):
@@ -620,14 +639,23 @@
     parts = [passed(part, "req", s + 1) for s, part in enumerate(parts)]
     pages = regroup(pages, after=[total])
     caches = [passed(pages[s], "sub", s) for s in range(1, subs)]
-    w_output, ready = staged(place, w_output, width, output_order(subs), after=[query])
-    mine = fold_pairs(total, parts, after=[ready])
+    mine = fold_pairs(total, parts)
     caches = list(pages[:1]) + list(gate(caches, after=[mine]))
     caches = caches + [passed(part, "section", 1) for part in caches]
     other = passed(mine, "section", 1)
 
-    mixed = attend(
-        place, lengths.astype(jnp.int32), query, mine, other, cosine, sine, caches
+    mixed, w_output = attend(
+        place,
+        lengths.astype(jnp.int32),
+        query,
+        mine,
+        other,
+        cosine,
+        sine,
+        w_output,
+        width,
+        output_order(subs),
+        caches,
     )
 
     mid, end = GROUP_REQUESTS, GROUP_REQUESTS * subs
@@ -638,10 +666,13 @@
     kept = outputs(mixed, w_output, mid, end - mid, after=[second])
     parts = fold_core(kept, got_first)
     kept = outputs(mixed, w_output, 0, mid, after=parts[:1])
-    parts = [passed(part, "sub", i // 2 + 1) for i, part in enumerate(parts)]
     last = {}
     for half, order in enumerate(HALVES):
-        last.update(zip(order, fold_sub(order, [kept, got_second], parts[half::2])))
+        sent = parts[half::2]
+        if half:
+            sent = gate(sent, after=[got[0], kept])
+        got = [passed(part, "sub", s + 1) for s, part in enumerate(sent)]
+        last.update(zip(order, fold_sub(order, [kept, got_second], got)))
     parts = [passed(last[s], "req", s) for s in range(1, GROUP_REQUESTS)]
     return finish(gathered[0], last[0], parts).reshape(hidden.shape)
 

time: 64.8 us -> 66.4 us (1.025)
  waiting for transfers between devices: 15.4 us -> 20.6 us
  starting transfers between devices: 26.1 us -> 23 us
    ppermute x24, waiting for transfers between devices: 15.4 us -> 20.6 us  [passed(): lax.ppermute(array, axis, [(i, i ^ shift) for i in range(lax.axis_size(ax...]
    ppermute x24, starting transfers between devices: 26.1 us -> 23 us  [passed(): lax.ppermute(array, axis, [(i, i ^ shift) for i in range(lax.axis_size(ax...]
    pallas_call x2 -> x1, Pallas kernels: 2.85 us -> 0.98 us  [staged(): pl.pallas_call(functools.partial(stage_kernel, order, len(more)), in_spec...]
    pallas_call x1, Pallas kernels: 2.18 us -> 3.53 us  [attend(): pl.pallas_call(functools.partial(attend_kernel, order), in_specs=[pl.Bloc...]
  transfers between devices with their start and end apart: 24 -> 24, of which waited for: 10 -> 10; matrix products, arithmetic and copies ran while one was open for 3% -> 3% of each run, Pallas kernels for 19% -> 16%
where the time goes in v10:
time: 66.4 us; the launch traced here: 66 us
  starting transfers between devices  23 us (35%)
  waiting for transfers between devices  20.6 us (31%)
  Pallas kernels  15.3 us (23%)
  local copies, waits for them, and re-layouts  5.12 us (8%)
  other arithmetic  1.71 us (3%)
    ppermute x24, starting transfers between devices, passed(): lax.ppermute(array, axis, [(i, i ^ shift) for i in range(lax.axis_size(ax...  23 us
    ppermute x24, waiting for transfers between devices, passed(): lax.ppermute(array, axis, [(i, i ^ shift) for i in range(lax.axis_size(ax...  20.6 us
    unnamed x16, local copies, waits for them, and re-layouts  5.11 us
    pallas_call x1, Pallas kernels, queries(): pl.pallas_call(query_kernel, in_specs=[pl.BlockSpec(memory_space=pltpu.SM...  4.64 us
    pallas_call x1, Pallas kernels, attend(): pl.pallas_call(functools.partial(attend_kernel, order), in_specs=[pl.Bloc...  3.53 us
    pallas_call x4, Pallas kernels, outputs(): pl.pallas_call(functools.partial(output_kernel, first), in_specs=[pl.Bloc...  1.89 us
    pallas_call x1, Pallas kernels, used_pages(): pl.pallas_call(pages_kernel, grid_spec=pltpu.PrefetchScalarGridSpec(num_s...  1.51 us
    pallas_call x1, Pallas kernels, scale_and_pairs(): pl.pallas_call(pairs_kernel, in_specs=[pl.BlockSpec(memory_space=pltpu.SM...  1.37 us
  transfers between devices with their start and end apart: 24, of which 10 were waited for; matrix products, arithmetic and copies ran while one was open for 3% of the time, Pallas kernels for 16%

profile of v10, /device:TPU:0, one launch (start us, length us, event | category | flops | bytes accessed | tf_op | source)
XLA Modules:
  0.0 66.0 jit_solution(12779741324290198791)
XLA Ops:
  0.0 5.0 %collective-permute-start.2 = (bf16[64,512]{1,0:T(8,128)(2,1)}, bf16[64,512]{1,0:T(8,128)(2,1)S(1)}, u32[]{:S(2)}, u32[]{:S(2)}) collective-permute-start(bf16[64,512]{1,0:T(8,128)(2,1)} %bitcast.16), channel_id=1, source_target_pairs={{0,12},{4,8},{8,4},{12,0},{1,13},{5,9},{9,5},{13,1},{2,14},{6,10},... | collective-permute-start | bytes 196616 | tf_op jit(solution)/shard_map/ppermute | solution.py:576
  6.4 1.2 %copy-done.1 = bf16[16,16,2048]{2,1,0:T(8,128)(2,1)S(1)} copy-done((bf16[16,16,2048]{2,1,0:T(8,128)(2,1)S(1)}, bf16[16,16,2048]{2,1,0:T(8,128)(2,1)}, u32[]{:S(2)}) %copy-start.1) | copy-done | bytes 1048600
  9.1 1.5 %used_pages.1 = (bf16[64,512]{1,0:T(8,128)(2,1)S(1)}, bf16[2,128,256]{2,1,0:T(8,128)(2,1)S(1)}, bf16[2,128,256]{2,1,0:T(8,128)(2,1)S(1)}, bf16[2,128,256]{2,1,0:T(8,128)(2,1)S(1)}, bf16[2,128,256]{2,1,0:T(8,128)(2,1)S(1)}) custom-call(s32[4,32]{1,0:T(4,128)S(1)} %copy-done.4, s32[3]{0:T(128)S(1)} %pad_add_fusion.place, ...), custom_call_target="tpu_custom_call" | custom-call | bytes 1048576 | tf_op jit(solution)/shard_map/used_pages/pallas_call | solution.py:146
  10.7 1.5 %collective-permute-start.11 = (bf16[2,128,256]{2,1,0:T(8,128)(2,1)S(1)}, bf16[2,128,256]{2,1,0:T(8,128)(2,1)S(1)}, u32[]{:S(2)}, u32[]{:S(2)}) collective-permute-start(bf16[2,128,256]{2,1,0:T(8,128)(2,1)S(1)} %get-tuple-element.42), channel_id=1, source_target_pairs={{0,4},{4,0},{8,12},{12,8},{1,5},{5,1},{9,13},{13,9},{2,6},{6,2},{1... | collective-permute-start | bytes 393224 | tf_op jit(solution)/shard_map/ppermute | solution.py:576
  12.2 2.9 %collective-permute-start.12 = (bf16[2,128,256]{2,1,0:T(8,128)(2,1)S(1)}, bf16[2,128,256]{2,1,0:T(8,128)(2,1)S(1)}, u32[]{:S(2)}, u32[]{:S(2)}) collective-permute-start(bf16[2,128,256]{2,1,0:T(8,128)(2,1)S(1)} %get-tuple-element.43), channel_id=1, source_target_pairs={{0,8},{4,12},{8,0},{12,4},{1,9},{5,13},{9,1},{13,5},{2,10},{6,14},... | collective-permute-start | bytes 393224 | tf_op jit(solution)/shard_map/ppermute | solution.py:576
  15.2 1.8 %collective-permute-start.3 = (bf16[4,64,512]{2,1,0:T(8,128)(2,1)S(1)}, bf16[4,64,512]{2,1,0:T(8,128)(2,1)S(1)}, u32[]{:S(2)}, u32[]{:S(2)}) collective-permute-start(bf16[4,64,512]{2,1,0:T(8,128)(2,1)S(1)} %pack.1.refs_1_.refs_0_.rows_ref), channel_id=1, source_target_pairs={{0,2},{2,0},{1,3},{3,1},{4,6},{6,4},{5,7},{7,5},{8,10},{10,8},{9,1... | collective-permute-start | bytes 786440 | tf_op jit(solution)/shard_map/ppermute | solution.py:576
  17.7 1.6 %copy-done = bf16[512,2048]{1,0:T(8,128)(2,1)S(1)} copy-done((bf16[512,2048]{1,0:T(8,128)(2,1)S(1)}, bf16[512,2048]{1,0:T(8,128)(2,1)}, u32[]{:S(2)}) %copy-start) | copy-done | bytes 2097176
  20.0 1.0 %staged.1 = (bf16[8,512,256]{2,1,0:T(8,128)(2,1)S(1)}, f32[8,128]{1,0:T(8,128)S(1)}, f32[16,1,512]{2,1,0:T(1,128)S(1)}) custom-call(s32[3]{0:T(128)S(1)} %pad_add_fusion.1.place, bf16[512,2048]{1,0:T(8,128)(2,1)S(1)} %copy-done, f32[16,1,512]{2,1,0:T(1,128)S(1)} %bitcast.20, bf16[4,64,512]{2,1,0:T(8,128)(2,1)S(1)} %pack.1.refs_1_.refs_0_.rows_ref), custom_call_target="tpu_custom_call" | custom-call | bytes 4194304 | tf_op jit(solution)/shard_map/staged/pallas_call | solution.py:71
  22.0 1.4 %collective-permute-done.5.refs_3_ = bf16[4,64,512]{2,1,0:T(8,128)(2,1)S(1)} collective-permute-done((bf16[4,64,512]{2,1,0:T(8,128)(2,1)S(1)}, bf16[4,64,512]{2,1,0:T(8,128)(2,1)S(1)}, u32[]{:S(2)}, u32[]{:S(2)}) %collective-permute-start.5) | collective-permute-done | bytes 262176 | tf_op jit(solution)/shard_map/ppermute | solution.py:576
  23.4 1.4 %scale_and_pairs.1 = (f32[64,128]{1,0:T(8,128)S(1)}, f32[4,64,256]{2,1,0:T(8,128)S(1)}, s16[528,128]{1,0:T(8,128)(2,1)S(1)}) custom-call(s32[3]{0:T(128)S(1)} %pad_add_fusion.1.place, f32[16,1,512]{2,1,0:T(1,128)S(1)} %get-tuple-element.31.gain_ref, bf16[8,512,256]{2,1,0:T(8,128)(2,1)S(1)} %get-tuple-element.32.weight_ref, ...), custom_call_target="tpu_custom_call" | custom-call | flops 134217728 | bytes 3145728 | tf_op jit(solution)/shard_map/scale_and_pairs/pallas_call | solution.py:263
  24.8 1.6 %collective-permute-start.6 = (s16[528,128]{1,0:T(8,128)(2,1)S(1)}, s16[528,128]{1,0:T(8,128)(2,1)S(1)}, u32[]{:S(2)}, u32[]{:S(2)}) collective-permute-start(s16[528,128]{1,0:T(8,128)(2,1)S(1)} %get-tuple-element.36), channel_id=1, source_target_pairs={{0,2},{2,0},{1,3},{3,1},{4,6},{6,4},{5,7},{7,5},{8,10},{10,8},{9,1... | collective-permute-start | bytes 405512 | tf_op jit(solution)/shard_map/ppermute | solution.py:576
  26.5 4.6 %queries.1.refs_2_.q_ref = bf16[4,16,512]{2,1,0:T(8,128)(2,1)S(1)} custom-call(s32[3]{0:T(128)S(1)} %pad_add_fusion.1.place, f32[64,128]{1,0:T(8,128)S(1)} %get-tuple-element.34.scale_ref, f32[16,1,512]{2,1,0:T(1,128)S(1)} %get-tuple-element.31.gain_ref, bf16[8192,512]{1,0:T(8,128)(2,1)} %weight_ref.1, f32[64,128]{1,0:T(8,128)S(1)} %bitcast.12, ...), custom_call_target="tpu_custom_call" | custom-call | flops 536870912 | bytes 8388608 | tf_op jit(solution)/shard_map/queries/pallas_call | solution.py:307
  31.3 0.9 %collective-permute-start.14 = (bf16[4,128,256]{2,1,0:T(8,128)(2,1)S(1)}, bf16[4,128,256]{2,1,0:T(8,128)(2,1)S(1)}, u32[]{:S(2)}, u32[]{:S(2)}) collective-permute-start(bf16[4,128,256]{2,1,0:T(8,128)(2,1)S(1)} %get-tuple-element.46), channel_id=1, source_target_pairs={{0,2},{2,0},{1,3},{3,1},{4,6},{6,4},{5,7},{7,5},{8,10},{10,8},{9,1... | collective-permute-start | bytes 786440 | tf_op jit(solution)/shard_map/ppermute | solution.py:576
  32.8 3.5 %collective-permute-start.8 = (s16[144,128]{1,0:T(8,128)(2,1)S(1)}, s16[144,128]{1,0:T(8,128)(2,1)S(1)}, u32[]{:S(2)}, u32[]{:S(2)}) collective-permute-start(s16[144,128]{1,0:T(8,128)(2,1)S(1)} %get-tuple-element.39), channel_id=1, source_target_pairs={{0,8},{4,12},{8,0},{12,4},{1,9},{5,13},{9,1},{13,5},{2,10},{6,14},... | collective-permute-start | bytes 110600 | tf_op jit(solution)/shard_map/ppermute | solution.py:576
  36.6 2.0 %collective-permute-done.8.refs_1_ = s16[144,128]{1,0:T(8,128)(2,1)S(1)} collective-permute-done((s16[144,128]{1,0:T(8,128)(2,1)S(1)}, s16[144,128]{1,0:T(8,128)(2,1)S(1)}, u32[]{:S(2)}, u32[]{:S(2)}) %collective-permute-start.8) | collective-permute-done | bytes 36896 | tf_op jit(solution)/shard_map/ppermute | solution.py:576
  38.7 3.4 %collective-permute-done.9.refs_2_ = s16[144,128]{1,0:T(8,128)(2,1)S(1)} collective-permute-done((s16[144,128]{1,0:T(8,128)(2,1)S(1)}, s16[144,128]{1,0:T(8,128)(2,1)S(1)}, u32[]{:S(2)}, u32[]{:S(2)}) %collective-permute-start.9) | collective-permute-done | bytes 36896 | tf_op jit(solution)/shard_map/ppermute | solution.py:576
  42.7 1.1 %collective-permute-done.10.other_ref = f32[64,256]{1,0:T(8,128)S(1)} collective-permute-done((f32[64,256]{1,0:T(8,128)S(1)}, f32[64,256]{1,0:T(8,128)S(1)}, u32[]{:S(2)}, u32[]{:S(2)}) %collective-permute-start.10) | collective-permute-done | bytes 65568 | tf_op jit(solution)/shard_map/ppermute | solution.py:576
  43.9 3.5 %attend.1 = (bf16[4,16,512]{2,1,0:T(8,128)(2,1)S(1)}, bf16[16,512,512]{2,1,0:T(8,128)(2,1)S(1)}) custom-call(s32[3]{0:T(128)S(1)} %pad_add_fusion.1.place, s32[4]{0:T(128)S(1)} %copy-done.5, bf16[4,16,512]{2,1,0:T(8,128)(2,1)S(1)} %queries.1.refs_2_.q_ref, f32[64,256]{1,0:T(8,128)S(1)} %fold_pairs.1.refs_1_.mine_ref, ...), custom_call_target="tpu_custom_call" | custom-call | flops 268435456 | bytes 3145728 | tf_op jit(solution)/shard_map/attend/pallas_call | solution.py:392
  50.1 1.2 %collective-permute-start.19 = (s16[528,128]{1,0:T(8,128)(2,1)S(1)}, s16[528,128]{1,0:T(8,128)(2,1)S(1)}, u32[]{:S(2)}, u32[]{:S(2)}) collective-permute-start(s16[528,128]{1,0:T(8,128)(2,1)S(1)} %get-tuple-element.49.refs_0_), channel_id=1, source_target_pairs={{0,2},{2,0},{1,3},{3,1},{4,6},{6,4},{5,7},{7,5},{8,10},{10,8},{9,1... | collective-permute-start | bytes 405512 | tf_op jit(solution)/shard_map/ppermute | solution.py:576
  51.8 4.0 %collective-permute-done.19.refs_1_.refs_2_ = s16[528,128]{1,0:T(8,128)(2,1)S(1)} collective-permute-done((s16[528,128]{1,0:T(8,128)(2,1)S(1)}, s16[528,128]{1,0:T(8,128)(2,1)S(1)}, u32[]{:S(2)}, u32[]{:S(2)}) %collective-permute-start.19) | collective-permute-done | bytes 135200 | tf_op jit(solution)/shard_map/ppermute | solution.py:576
  55.8 1.2 %collective-permute-start.20 = (s16[528,128]{1,0:T(8,128)(2,1)S(1)}, s16[528,128]{1,0:T(8,128)(2,1)S(1)}, u32[]{:S(2)}, u32[]{:S(2)}) collective-permute-start(s16[528,128]{1,0:T(8,128)(2,1)S(1)} %gate.5), channel_id=1, source_target_pairs={{0,2},{2,0},{1,3},{3,1},{4,6},{6,4},{5,7},{7,5},{8,10},{10,8},{9,1... | collective-permute-start | bytes 405512 | tf_op jit(solution)/shard_map/ppermute | solution.py:576
  57.8 3.1 %collective-permute-done.20.refs_2_ = s16[528,128]{1,0:T(8,128)(2,1)S(1)} collective-permute-done((s16[528,128]{1,0:T(8,128)(2,1)S(1)}, s16[528,128]{1,0:T(8,128)(2,1)S(1)}, u32[]{:S(2)}, u32[]{:S(2)}) %collective-permute-start.20) | collective-permute-done | bytes 135200 | tf_op jit(solution)/shard_map/ppermute | solution.py:576
  61.0 2.8 %collective-permute-done.22.refs_1_ = s16[272,128]{1,0:T(8,128)(2,1)S(1)} collective-permute-done((s16[272,128]{1,0:T(8,128)(2,1)S(1)}, s16[272,128]{1,0:T(8,128)(2,1)S(1)}, u32[]{:S(2)}, u32[]{:S(2)}) %collective-permute-start.22) | collective-permute-done | bytes 69664 | tf_op jit(solution)/shard_map/ppermute | solution.py:576
  63.8 1.5 %collective-permute-done.21.refs_0_ = s16[272,128]{1,0:T(8,128)(2,1)S(1)} collective-permute-done((s16[272,128]{1,0:T(8,128)(2,1)S(1)}, s16[272,128]{1,0:T(8,128)(2,1)S(1)}, u32[]{:S(2)}, u32[]{:S(2)}) %collective-permute-start.21) | collective-permute-done | bytes 69664 | tf_op jit(solution)/shard_map/ppermute | solution.py:576
  (70 shorter events, 11.9 us)
Async XLA Ops:
  0.0 15.1 %collective-permute-start.2 = (bf16[64,512]{1,0:T(8,128)(2,1)}, bf16[64,512]{1,0:T(8,128)(2,1)S(1)}, u32[]{:S(2)}, u32[]{:S(2)}) collective-permute-start(bf16[64,512]{1,0:T(8,128)(2,1)} %bitcast.16), channel_id=1, source_target_pairs={{0,12},{4,8},{8,4},{12,0},{1,13},{5,9},{9,5},{13,1},{2,14},{6,10},... | collective-permute-start | bytes 196616 | tf_op jit(solution)/shard_map/ppermute | solution.py:576
  5.0 10.1 %collective-permute-start.1 = (bf16[64,512]{1,0:T(8,128)(2,1)}, bf16[64,512]{1,0:T(8,128)(2,1)S(1)}, u32[]{:S(2)}, u32[]{:S(2)}) collective-permute-start(bf16[64,512]{1,0:T(8,128)(2,1)} %bitcast.17), channel_id=1, source_target_pairs={{0,8},{4,12},{8,0},{12,4},{1,9},{5,13},{9,1},{13,5},{2,10},{6,14},... | collective-permute-start | bytes 196616 | tf_op jit(solution)/shard_map/ppermute | solution.py:576
  5.1 10.1 %collective-permute-start = (bf16[64,512]{1,0:T(8,128)(2,1)}, bf16[64,512]{1,0:T(8,128)(2,1)S(1)}, u32[]{:S(2)}, u32[]{:S(2)}) collective-permute-start(bf16[64,512]{1,0:T(8,128)(2,1)} %bitcast.18), channel_id=1, source_target_pairs={{0,4},{4,0},{8,12},{12,8},{1,5},{5,1},{9,13},{13,9},{2,6},{6,2},{1... | collective-permute-start | bytes 196616 | tf_op jit(solution)/shard_map/ppermute | solution.py:576
  10.7 20.6 %collective-permute-start.11 = (bf16[2,128,256]{2,1,0:T(8,128)(2,1)S(1)}, bf16[2,128,256]{2,1,0:T(8,128)(2,1)S(1)}, u32[]{:S(2)}, u32[]{:S(2)}) collective-permute-start(bf16[2,128,256]{2,1,0:T(8,128)(2,1)S(1)} %get-tuple-element.42), channel_id=1, source_target_pairs={{0,4},{4,0},{8,12},{12,8},{1,5},{5,1},{9,13},{13,9},{2,6},{6,2},{1... | collective-permute-start | bytes 393224 | tf_op jit(solution)/shard_map/ppermute | solution.py:576
  12.2 19.1 %collective-permute-start.12 = (bf16[2,128,256]{2,1,0:T(8,128)(2,1)S(1)}, bf16[2,128,256]{2,1,0:T(8,128)(2,1)S(1)}, u32[]{:S(2)}, u32[]{:S(2)}) collective-permute-start(bf16[2,128,256]{2,1,0:T(8,128)(2,1)S(1)} %get-tuple-element.43), channel_id=1, source_target_pairs={{0,8},{4,12},{8,0},{12,4},{1,9},{5,13},{9,1},{13,5},{2,10},{6,14},... | collective-permute-start | bytes 393224 | tf_op jit(solution)/shard_map/ppermute | solution.py:576
  15.1 16.2 %collective-permute-start.13 = (bf16[2,128,256]{2,1,0:T(8,128)(2,1)S(1)}, bf16[2,128,256]{2,1,0:T(8,128)(2,1)S(1)}, u32[]{:S(2)}, u32[]{:S(2)}) collective-permute-start(bf16[2,128,256]{2,1,0:T(8,128)(2,1)S(1)} %get-tuple-element.44), channel_id=1, source_target_pairs={{0,12},{4,8},{8,4},{12,0},{1,13},{5,9},{9,5},{13,1},{2,14},{6,10},... | collective-permute-start | bytes 393224 | tf_op jit(solution)/shard_map/ppermute | solution.py:576
  15.2 6.7 %collective-permute-start.3 = (bf16[4,64,512]{2,1,0:T(8,128)(2,1)S(1)}, bf16[4,64,512]{2,1,0:T(8,128)(2,1)S(1)}, u32[]{:S(2)}, u32[]{:S(2)}) collective-permute-start(bf16[4,64,512]{2,1,0:T(8,128)(2,1)S(1)} %pack.1.refs_1_.refs_0_.rows_ref), channel_id=1, source_target_pairs={{0,2},{2,0},{1,3},{3,1},{4,6},{6,4},{5,7},{7,5},{8,10},{10,8},{9,1... | collective-permute-start | bytes 786440 | tf_op jit(solution)/shard_map/ppermute | solution.py:576
  17.7 4.3 %collective-permute-start.4 = (bf16[4,64,512]{2,1,0:T(8,128)(2,1)S(1)}, bf16[4,64,512]{2,1,0:T(8,128)(2,1)S(1)}, u32[]{:S(2)}, u32[]{:S(2)}) collective-permute-start(bf16[4,64,512]{2,1,0:T(8,128)(2,1)S(1)} %pack.1.refs_1_.refs_0_.rows_ref), channel_id=1, source_target_pairs={{0,1},{1,0},{2,3},{3,2},{4,5},{5,4},{6,7},{7,6},{8,9},{9,8},{10,11... | collective-permute-start | bytes 786440 | tf_op jit(solution)/shard_map/ppermute | solution.py:576
  21.9 1.5 %collective-permute-start.5 = (bf16[4,64,512]{2,1,0:T(8,128)(2,1)S(1)}, bf16[4,64,512]{2,1,0:T(8,128)(2,1)S(1)}, u32[]{:S(2)}, u32[]{:S(2)}) collective-permute-start(bf16[4,64,512]{2,1,0:T(8,128)(2,1)S(1)} %gate.3.refs_1_), channel_id=1, source_target_pairs={{0,1},{1,0},{2,3},{3,2},{4,5},{5,4},{6,7},{7,6},{8,9},{9,8},{10,11... | collective-permute-start | bytes 786440 | tf_op jit(solution)/shard_map/ppermute | solution.py:576
  24.8 6.3 %collective-permute-start.6 = (s16[528,128]{1,0:T(8,128)(2,1)S(1)}, s16[528,128]{1,0:T(8,128)(2,1)S(1)}, u32[]{:S(2)}, u32[]{:S(2)}) collective-permute-start(s16[528,128]{1,0:T(8,128)(2,1)S(1)} %get-tuple-element.36), channel_id=1, source_target_pairs={{0,2},{2,0},{1,3},{3,1},{4,6},{6,4},{5,7},{7,5},{8,10},{10,8},{9,1... | collective-permute-start | bytes 405512 | tf_op jit(solution)/shard_map/ppermute | solution.py:576
  31.3 10.8 %collective-permute-start.14 = (bf16[4,128,256]{2,1,0:T(8,128)(2,1)S(1)}, bf16[4,128,256]{2,1,0:T(8,128)(2,1)S(1)}, u32[]{:S(2)}, u32[]{:S(2)}) collective-permute-start(bf16[4,128,256]{2,1,0:T(8,128)(2,1)S(1)} %get-tuple-element.46), channel_id=1, source_target_pairs={{0,2},{2,0},{1,3},{3,1},{4,6},{6,4},{5,7},{7,5},{8,10},{10,8},{9,1... | collective-permute-start | bytes 786440 | tf_op jit(solution)/shard_map/ppermute | solution.py:576
  32.2 4.4 %collective-permute-start.7 = (s16[144,128]{1,0:T(8,128)(2,1)S(1)}, s16[144,128]{1,0:T(8,128)(2,1)S(1)}, u32[]{:S(2)}, u32[]{:S(2)}) collective-permute-start(s16[144,128]{1,0:T(8,128)(2,1)S(1)} %get-tuple-element.38), channel_id=1, source_target_pairs={{0,4},{4,0},{8,12},{12,8},{1,5},{5,1},{9,13},{13,9},{2,6},{6,2},{1... | collective-permute-start | bytes 110600 | tf_op jit(solution)/shard_map/ppermute | solution.py:576
  32.8 5.9 %collective-permute-start.8 = (s16[144,128]{1,0:T(8,128)(2,1)S(1)}, s16[144,128]{1,0:T(8,128)(2,1)S(1)}, u32[]{:S(2)}, u32[]{:S(2)}) collective-permute-start(s16[144,128]{1,0:T(8,128)(2,1)S(1)} %get-tuple-element.39), channel_id=1, source_target_pairs={{0,8},{4,12},{8,0},{12,4},{1,9},{5,13},{9,1},{13,5},{2,10},{6,14},... | collective-permute-start | bytes 110600 | tf_op jit(solution)/shard_map/ppermute | solution.py:576
  36.3 5.8 %collective-permute-start.9 = (s16[144,128]{1,0:T(8,128)(2,1)S(1)}, s16[144,128]{1,0:T(8,128)(2,1)S(1)}, u32[]{:S(2)}, u32[]{:S(2)}) collective-permute-start(s16[144,128]{1,0:T(8,128)(2,1)S(1)} %get-tuple-element.40), channel_id=1, source_target_pairs={{0,12},{4,8},{8,4},{12,0},{1,13},{5,9},{9,5},{13,1},{2,14},{6,10},... | collective-permute-start | bytes 110600 | tf_op jit(solution)/shard_map/ppermute | solution.py:576
  36.6 7.2 %collective-permute-start.15 = (bf16[4,128,256]{2,1,0:T(8,128)(2,1)S(1)}, bf16[4,128,256]{2,1,0:T(8,128)(2,1)S(1)}, u32[]{:S(2)}, u32[]{:S(2)}) collective-permute-start(bf16[4,128,256]{2,1,0:T(8,128)(2,1)S(1)} %get-tuple-element.45.refs_0_), channel_id=1, source_target_pairs={{0,1},{1,0},{2,3},{3,2},{4,5},{5,4},{6,7},{7,6},{8,9},{9,8},{10,11... | collective-permute-start | bytes 786440 | tf_op jit(solution)/shard_map/ppermute | solution.py:576
  42.2 1.7 %collective-permute-start.16 = (bf16[4,128,256]{2,1,0:T(8,128)(2,1)S(1)}, bf16[4,128,256]{2,1,0:T(8,128)(2,1)S(1)}, u32[]{:S(2)}, u32[]{:S(2)}) collective-permute-start(bf16[4,128,256]{2,1,0:T(8,128)(2,1)S(1)} %gate.4.refs_1_), channel_id=1, source_target_pairs={{0,1},{1,0},{2,3},{3,2},{4,5},{5,4},{6,7},{7,6},{8,9},{9,8},{10,11... | collective-permute-start | bytes 786440 | tf_op jit(solution)/shard_map/ppermute | solution.py:576
  42.2 1.6 %collective-permute-start.10 = (f32[64,256]{1,0:T(8,128)S(1)}, f32[64,256]{1,0:T(8,128)S(1)}, u32[]{:S(2)}, u32[]{:S(2)}) collective-permute-start(f32[64,256]{1,0:T(8,128)S(1)} %fold_pairs.1.refs_1_.mine_ref), channel_id=1, source_target_pairs={{0,1},{1,0},{2,3},{3,2},{4,5},{5,4},{6,7},{7,6},{8,9},{9,8},{10,11... | collective-permute-start | bytes 196616 | tf_op jit(solution)/shard_map/ppermute | solution.py:576
  47.9 2.0 %collective-permute-start.17 = (f32[4,64,512]{2,1,0:T(8,128)S(1)}, f32[4,64,512]{2,1,0:T(8,128)S(1)}, u32[]{:S(2)}, u32[]{:S(2)}) collective-permute-start(f32[4,64,512]{2,1,0:T(8,128)S(1)} %outputs.4.refs_0_), channel_id=1, source_target_pairs={{0,1},{1,0},{2,3},{3,2},{4,5},{5,4},{6,7},{7,6},{8,9},{9,8},{10,11... | collective-permute-start | bytes 1572872 | tf_op jit(solution)/shard_map/ppermute | solution.py:576
  48.6 8.4 %collective-permute-start.18 = (f32[4,64,512]{2,1,0:T(8,128)S(1)}, f32[4,64,512]{2,1,0:T(8,128)S(1)}, u32[]{:S(2)}, u32[]{:S(2)}) collective-permute-start(f32[4,64,512]{2,1,0:T(8,128)S(1)} %outputs.5.refs_0_), channel_id=1, source_target_pairs={{0,1},{1,0},{2,3},{3,2},{4,5},{5,4},{6,7},{7,6},{8,9},{9,8},{10,11... | collective-permute-start | bytes 1572872 | tf_op jit(solution)/shard_map/ppermute | solution.py:576
  50.1 5.7 %collective-permute-start.19 = (s16[528,128]{1,0:T(8,128)(2,1)S(1)}, s16[528,128]{1,0:T(8,128)(2,1)S(1)}, u32[]{:S(2)}, u32[]{:S(2)}) collective-permute-start(s16[528,128]{1,0:T(8,128)(2,1)S(1)} %get-tuple-element.49.refs_0_), channel_id=1, source_target_pairs={{0,2},{2,0},{1,3},{3,1},{4,6},{6,4},{5,7},{7,5},{8,10},{10,8},{9,1... | collective-permute-start | bytes 405512 | tf_op jit(solution)/shard_map/ppermute | solution.py:576
  55.8 5.0 %collective-permute-start.20 = (s16[528,128]{1,0:T(8,128)(2,1)S(1)}, s16[528,128]{1,0:T(8,128)(2,1)S(1)}, u32[]{:S(2)}, u32[]{:S(2)}) collective-permute-start(s16[528,128]{1,0:T(8,128)(2,1)S(1)} %gate.5), channel_id=1, source_target_pairs={{0,2},{2,0},{1,3},{3,1},{4,6},{6,4},{5,7},{7,5},{8,10},{10,8},{9,1... | collective-permute-start | bytes 405512 | tf_op jit(solution)/shard_map/ppermute | solution.py:576
  57.1 6.7 %collective-permute-start.22 = (s16[272,128]{1,0:T(8,128)(2,1)S(1)}, s16[272,128]{1,0:T(8,128)(2,1)S(1)}, u32[]{:S(2)}, u32[]{:S(2)}) collective-permute-start(s16[272,128]{1,0:T(8,128)(2,1)S(1)} %get-tuple-element.53), channel_id=1, source_target_pairs={{0,8},{4,12},{8,0},{12,4},{1,9},{5,13},{9,1},{13,5},{2,10},{6,14},... | collective-permute-start | bytes 208904 | tf_op jit(solution)/shard_map/ppermute | solution.py:576
  57.2 6.6 %collective-permute-start.23 = (s16[272,128]{1,0:T(8,128)(2,1)S(1)}, s16[272,128]{1,0:T(8,128)(2,1)S(1)}, u32[]{:S(2)}, u32[]{:S(2)}) collective-permute-start(s16[272,128]{1,0:T(8,128)(2,1)S(1)} %get-tuple-element.54), channel_id=1, source_target_pairs={{0,12},{4,8},{8,4},{12,0},{1,13},{5,9},{9,5},{13,1},{2,14},{6,10},... | collective-permute-start | bytes 208904 | tf_op jit(solution)/shard_map/ppermute | solution.py:576
  60.9 4.4 %collective-permute-start.21 = (s16[272,128]{1,0:T(8,128)(2,1)S(1)}, s16[272,128]{1,0:T(8,128)(2,1)S(1)}, u32[]{:S(2)}, u32[]{:S(2)}) collective-permute-start(s16[272,128]{1,0:T(8,128)(2,1)S(1)} %get-tuple-element.52), channel_id=1, source_target_pairs={{0,4},{4,0},{8,12},{12,8},{1,5},{5,1},{9,13},{13,9},{2,6},{6,2},{1... | collective-permute-start | bytes 208904 | tf_op jit(solution)/shard_map/ppermute | solution.py:576
  (8 other events, 70.2 us)

commit v11 on v9

--- a/solution.py
+++ b/solution.py
@@ -19,7 +19,7 @@
 PAIR = 2 * HEAD_SIZE
 LANES = 128
 TAIL = 16
-HALVES = ((0, 3), (1, 2))
+HALVES = ((1, 3), (0, 2))
 DEVICES = ("req", "sub", "section")
 
 theta_base = 500000.0
@@ -76,7 +76,7 @@
         + [jax.ShapeDtypeStruct(other.shape, other.dtype) for other in more],
         scratch_shapes=[pltpu.SemaphoreType.DMA((count + len(more),))],
         compiler_params=params(),
-        cost_estimate=cost([array] * 2),
+        cost_estimate=cost([array], [array]),
         name="staged",
     )(place, array, *more, *after)
 
@@ -262,7 +262,7 @@
         out_specs=[pl.BlockSpec(memory_space=pltpu.VMEM)] * len(shapes),
         out_shape=shapes,
         compiler_params=params(),
-        cost_estimate=cost(gathered * 1, [weight], flops=2 * count * weight.size),
+        cost_estimate=cost(gathered, [weight], flops=2 * count * weight.size),
         name="scale_and_pairs",
     )(place, gain, weight, *gathered)
 
@@ -468,40 +468,77 @@
     )(mine, got)
 
 
-def fold_sub_kernel(order, count, own, *refs):
-    own_refs, in_refs, out_refs = refs[:own], refs[own : own + count], refs[-len(order) :]
+def fold_sub_kernel(order, send, keep, own, count, *refs):
+    own_refs, in_refs = refs[:own], refs[own : own + count]
+    outs = list(refs[-(len(send) > 0) - (len(keep) > 0) :])
     _, rows, width = own_refs[0].shape
     steps = [step_of(ref) for ref in in_refs]
-    for i, (z, out_ref) in enumerate(zip(order, out_refs)):
+
+    def total(z):
         block = own_refs[0][z]
         for ref in own_refs[1:]:
             block = block + ref[z]
         pieces = pieces_of(block)
         for c in range(len(pieces)):
             for ref, step in zip(in_refs, steps):
-                first = (i * len(pieces) + c) * rows
+                first = (order.index(z) * len(pieces) + c) * rows
                 pieces[c] = pieces[c] + decoded(ref, first, rows, step)
-        if z:
-            encode(out_ref, pieces)
-        else:
-            for c, piece in enumerate(pieces):
-                out_ref[:, c * LANES : (c + 1) * LANES] = piece
-
-
-def fold_sub(order, own, parts, after=()):
+        return pieces
+
+    if send:
+        encode(outs.pop(0), [piece for z in send for piece in total(z)])
+    for i, z in enumerate(keep):
+        for c, piece in enumerate(total(z)):
+            outs[0][i, :, c * LANES : (c + 1) * LANES] = piece
+
+
+def fold_sub(order, send, keep, own, parts, after=()):
     _, rows, width = own[0].shape
-    total = jax.ShapeDtypeStruct((rows, width), jnp.float32)
-    sent = jax.ShapeDtypeStruct((width // LANES * rows + TAIL, LANES), jnp.int16)
-    return pl.pallas_call(
-        functools.partial(fold_sub_kernel, order, len(parts), len(own)),
+    shapes = []
+    if send:
+        length = len(send) * (width // LANES) * rows + TAIL
+        shapes.append(jax.ShapeDtypeStruct((length, LANES), jnp.int16))
+    if keep:
+        shapes.append(jax.ShapeDtypeStruct((len(keep), rows, width), jnp.float32))
+    return pl.pallas_call(
+        functools.partial(fold_sub_kernel, order, send, keep, len(own), len(parts)),
         in_specs=[pl.BlockSpec(memory_space=pltpu.VMEM)] * (len(own) + len(parts))
         + unread(after),
-        out_specs=[pl.BlockSpec(memory_space=pltpu.VMEM)] * len(order),
-        out_shape=[sent if z else total for z in order],
+        out_specs=[pl.BlockSpec(memory_space=pltpu.VMEM)] * len(shapes),
+        out_shape=shapes,
         compiler_params=params(),
         cost_estimate=cost(own, parts),
         name="fold_sub",
     )(*own, *parts, *after)
+
+
+def fold_near_kernel(kept_ref, got_ref, total_ref, out_ref):
+    _, rows, width = kept_ref.shape
+    step = step_of(got_ref)
+    count = width // LANES
+    sums = []
+    for i in range(2):
+        for c, piece in enumerate(pieces_of(kept_ref[i])):
+            sums.append(piece + decoded(got_ref, (i * count + c) * rows, rows, step))
+    for c in range(count):
+        total_ref[:, c * LANES : (c + 1) * LANES] = sums[c]
+    encode(out_ref, sums[count:])
+
+
+def fold_near(kept, got):
+    _, rows, width = kept.shape
+    return pl.pallas_call(
+        fold_near_kernel,
+        in_specs=[pl.BlockSpec(memory_space=pltpu.VMEM)] * 2,
+        out_specs=[pl.BlockSpec(memory_space=pltpu.VMEM)] * 2,
+        out_shape=[
+            jax.ShapeDtypeStruct((rows, width), jnp.float32),
+            jax.ShapeDtypeStruct((width // LANES * rows + TAIL, LANES), jnp.int16),
+        ],
+        compiler_params=params(),
+        cost_estimate=cost([kept], [got]),
+        name="fold_near",
+    )(kept, got)
 
 
 def fold_pairs_kernel(count, total_ref, *refs):
@@ -616,11 +653,13 @@
     scale, kept, *parts = scale_and_pairs(place, gain, key_value_weight, gathered)
     parts = [passed(part, "sub", s + 1) for s, part in enumerate(parts)]
     query = queries(place, scale, gain, w_query, cosine, sine, gathered)
-    total, *parts = fold_sub((0, 1, 2, 3), [kept], parts, after=[query])
-    parts = [passed(part, "req", s + 1) for s, part in enumerate(parts)]
-    pages = regroup(pages, after=[total])
+    near, kept = fold_sub((0, 1, 2, 3), (1, 3), (0, 2), [kept], parts, after=[query])
+    near = passed(near, "req", 1)
+    pages = regroup(pages, after=[kept])
     caches = [passed(pages[s], "sub", s) for s in range(1, subs)]
-    w_output, ready = staged(place, w_output, width, output_order(subs), after=[query])
+    w_output, ready = staged(place, w_output, width, output_order(subs), after=[kept])
+    total, far = fold_near(kept, near)
+    parts = [passed(far, "req", 2)]
     mine = fold_pairs(total, parts, after=[ready])
     caches = list(pages[:1]) + list(gate(caches, after=[mine]))
     caches = caches + [passed(part, "section", 1) for part in caches]
@@ -639,11 +678,12 @@
     parts = fold_core(kept, got_first)
     kept = outputs(mixed, w_output, 0, mid, after=parts[:1])
     parts = [passed(part, "sub", i // 2 + 1) for i, part in enumerate(parts)]
-    last = {}
-    for half, order in enumerate(HALVES):
-        last.update(zip(order, fold_sub(order, [kept, got_second], parts[half::2])))
-    parts = [passed(last[s], "req", s) for s in range(1, GROUP_REQUESTS)]
-    return finish(gathered[0], last[0], parts).reshape(hidden.shape)
+    (near,) = fold_sub((1, 3), (1, 3), (), [kept, got_second], parts[0::2])
+    near = passed(near, "req", 1)
+    (kept,) = fold_sub((0, 2), (), (0, 2), [kept, got_second], parts[1::2])
+    total, far = fold_near(kept, near)
+    parts = [passed(far, "req", 2)]
+    return finish(gathered[0], total, parts).reshape(hidden.shape)
 
 
 def solution(mesh):

time: 64.8 us -> 66.3 us (1.023)
  waiting for transfers between devices: 15.4 us -> 19.1 us
  starting transfers between devices: 26.1 us -> 23.8 us
    ppermute x24 -> x22, waiting for transfers between devices: 15.4 us -> 19.1 us  [passed(): lax.ppermute(array, axis, [(i, i ^ shift) for i in range(lax.axis_size(ax...]
    ppermute x24 -> x22, starting transfers between devices: 26.1 us -> 23.8 us  [passed(): lax.ppermute(array, axis, [(i, i ^ shift) for i in range(lax.axis_size(ax...]
  transfers between devices with their start and end apart: 24 -> 22, of which waited for: 10 -> 10; matrix products, arithmetic and copies ran while one was open for 3% -> 3% of each run, Pallas kernels for 19% -> 19%
where the time goes in v11:
time: 66.3 us; the launch traced here: 65.9 us
  starting transfers between devices  23.8 us (36%)
  waiting for transfers between devices  19.1 us (29%)
  Pallas kernels  15.9 us (24%)
  local copies, waits for them, and re-layouts  5.12 us (8%)
  other arithmetic  1.71 us (3%)
    ppermute x22, starting transfers between devices, passed(): lax.ppermute(array, axis, [(i, i ^ shift) for i in range(lax.axis_size(ax...  23.8 us
    ppermute x22, waiting for transfers between devices, passed(): lax.ppermute(array, axis, [(i, i ^ shift) for i in range(lax.axis_size(ax...  19.1 us
    unnamed x16, local copies, waits for them, and re-layouts  5.11 us
    pallas_call x1, Pallas kernels, queries(): pl.pallas_call(query_kernel, in_specs=[pl.BlockSpec(memory_space=pltpu.SM...  4.63 us
    pallas_call x2, Pallas kernels, staged(): pl.pallas_call(functools.partial(stage_kernel, order, len(more)), in_spec...  2.85 us
    pallas_call x1, Pallas kernels, attend(): pl.pallas_call(attend_kernel, in_specs=[pl.BlockSpec(memory_space=pltpu.S...  2.18 us
    pallas_call x4, Pallas kernels, outputs(): pl.pallas_call(functools.partial(output_kernel, first), in_specs=[pl.Bloc...  1.91 us
    pallas_call x1, Pallas kernels, used_pages(): pl.pallas_call(pages_kernel, grid_spec=pltpu.PrefetchScalarGridSpec(num_s...  1.51 us
  transfers between devices with their start and end apart: 22, of which 10 were waited for; matrix products, arithmetic and copies ran while one was open for 3% of the time, Pallas kernels for 19%

profile of v11, /device:TPU:0, one launch (start us, length us, event | category | flops | bytes accessed | tf_op | source)
XLA Modules:
  0.0 65.9 jit_solution(15168717770200458640)
XLA Ops:
  0.0 5.0 %collective-permute-start.2 = (bf16[64,512]{1,0:T(8,128)(2,1)}, bf16[64,512]{1,0:T(8,128)(2,1)S(1)}, u32[]{:S(2)}, u32[]{:S(2)}) collective-permute-start(bf16[64,512]{1,0:T(8,128)(2,1)} %bitcast.16), channel_id=1, source_target_pairs={{0,12},{4,8},{8,4},{12,0},{1,13},{5,9},{9,5},{13,1},{2,14},{6,10},... | collective-permute-start | bytes 196616 | tf_op jit(solution)/shard_map/ppermute | solution.py:594
  6.4 1.2 %copy-done.1 = bf16[16,16,2048]{2,1,0:T(8,128)(2,1)S(1)} copy-done((bf16[16,16,2048]{2,1,0:T(8,128)(2,1)S(1)}, bf16[16,16,2048]{2,1,0:T(8,128)(2,1)}, u32[]{:S(2)}) %copy-start.1) | copy-done | bytes 1048600
  9.1 1.5 %used_pages.1 = (bf16[64,512]{1,0:T(8,128)(2,1)S(1)}, bf16[2,128,256]{2,1,0:T(8,128)(2,1)S(1)}, bf16[2,128,256]{2,1,0:T(8,128)(2,1)S(1)}, bf16[2,128,256]{2,1,0:T(8,128)(2,1)S(1)}, bf16[2,128,256]{2,1,0:T(8,128)(2,1)S(1)}) custom-call(s32[4,32]{1,0:T(4,128)S(1)} %copy-done.4, s32[3]{0:T(128)S(1)} %pad_add_fusion.place, ...), custom_call_target="tpu_custom_call" | custom-call | bytes 1048576 | tf_op jit(solution)/shard_map/used_pages/pallas_call | solution.py:141
  10.7 1.5 %collective-permute-start.10 = (bf16[2,128,256]{2,1,0:T(8,128)(2,1)S(1)}, bf16[2,128,256]{2,1,0:T(8,128)(2,1)S(1)}, u32[]{:S(2)}, u32[]{:S(2)}) collective-permute-start(bf16[2,128,256]{2,1,0:T(8,128)(2,1)S(1)} %get-tuple-element.41), channel_id=1, source_target_pairs={{0,4},{4,0},{8,12},{12,8},{1,5},{5,1},{9,13},{13,9},{2,6},{6,2},{1... | collective-permute-start | bytes 393224 | tf_op jit(solution)/shard_map/ppermute | solution.py:594
  12.2 2.9 %collective-permute-start.11 = (bf16[2,128,256]{2,1,0:T(8,128)(2,1)S(1)}, bf16[2,128,256]{2,1,0:T(8,128)(2,1)S(1)}, u32[]{:S(2)}, u32[]{:S(2)}) collective-permute-start(bf16[2,128,256]{2,1,0:T(8,128)(2,1)S(1)} %get-tuple-element.42), channel_id=1, source_target_pairs={{0,8},{4,12},{8,0},{12,4},{1,9},{5,13},{9,1},{13,5},{2,10},{6,14},... | collective-permute-start | bytes 393224 | tf_op jit(solution)/shard_map/ppermute | solution.py:594
  15.2 1.8 %collective-permute-start.3 = (bf16[4,64,512]{2,1,0:T(8,128)(2,1)S(1)}, bf16[4,64,512]{2,1,0:T(8,128)(2,1)S(1)}, u32[]{:S(2)}, u32[]{:S(2)}) collective-permute-start(bf16[4,64,512]{2,1,0:T(8,128)(2,1)S(1)} %pack.1.refs_1_.refs_0_.rows_ref), channel_id=1, source_target_pairs={{0,2},{2,0},{1,3},{3,1},{4,6},{6,4},{5,7},{7,5},{8,10},{10,8},{9,1... | collective-permute-start | bytes 786440 | tf_op jit(solution)/shard_map/ppermute | solution.py:594
  17.7 1.6 %copy-done = bf16[512,2048]{1,0:T(8,128)(2,1)S(1)} copy-done((bf16[512,2048]{1,0:T(8,128)(2,1)S(1)}, bf16[512,2048]{1,0:T(8,128)(2,1)}, u32[]{:S(2)}) %copy-start) | copy-done | bytes 2097176
  20.0 1.0 %staged.2 = (bf16[8,512,256]{2,1,0:T(8,128)(2,1)S(1)}, f32[8,128]{1,0:T(8,128)S(1)}, f32[16,1,512]{2,1,0:T(1,128)S(1)}) custom-call(s32[3]{0:T(128)S(1)} %pad_add_fusion.1.place, bf16[512,2048]{1,0:T(8,128)(2,1)S(1)} %copy-done, f32[16,1,512]{2,1,0:T(1,128)S(1)} %bitcast.20, bf16[4,64,512]{2,1,0:T(8,128)(2,1)S(1)} %pack.1.refs_1_.refs_0_.rows_ref), custom_call_target="tpu_custom_call" | custom-call | bytes 4194304 | tf_op jit(solution)/shard_map/staged/pallas_call | solution.py:66
  22.0 1.4 %collective-permute-done.5.refs_3_ = bf16[4,64,512]{2,1,0:T(8,128)(2,1)S(1)} collective-permute-done((bf16[4,64,512]{2,1,0:T(8,128)(2,1)S(1)}, bf16[4,64,512]{2,1,0:T(8,128)(2,1)S(1)}, u32[]{:S(2)}, u32[]{:S(2)}) %collective-permute-start.5) | collective-permute-done | bytes 262176 | tf_op jit(solution)/shard_map/ppermute | solution.py:594
  23.4 1.4 %scale_and_pairs.1 = (f32[64,128]{1,0:T(8,128)S(1)}, f32[4,64,256]{2,1,0:T(8,128)S(1)}, s16[528,128]{1,0:T(8,128)(2,1)S(1)}) custom-call(s32[3]{0:T(128)S(1)} %pad_add_fusion.1.place, f32[16,1,512]{2,1,0:T(1,128)S(1)} %get-tuple-element.29.gain_ref, bf16[8,512,256]{2,1,0:T(8,128)(2,1)S(1)} %get-tuple-element.30.weight_ref, ...), custom_call_target="tpu_custom_call" | custom-call | flops 134217728 | bytes 3145728 | tf_op jit(solution)/shard_map/scale_and_pairs/pallas_call | solution.py:258
  24.8 1.6 %collective-permute-start.6 = (s16[528,128]{1,0:T(8,128)(2,1)S(1)}, s16[528,128]{1,0:T(8,128)(2,1)S(1)}, u32[]{:S(2)}, u32[]{:S(2)}) collective-permute-start(s16[528,128]{1,0:T(8,128)(2,1)S(1)} %get-tuple-element.34), channel_id=1, source_target_pairs={{0,2},{2,0},{1,3},{3,1},{4,6},{6,4},{5,7},{7,5},{8,10},{10,8},{9,1... | collective-permute-start | bytes 405512 | tf_op jit(solution)/shard_map/ppermute | solution.py:594
  26.5 4.6 %queries.1.refs_2_.q_ref = bf16[4,16,512]{2,1,0:T(8,128)(2,1)S(1)} custom-call(s32[3]{0:T(128)S(1)} %pad_add_fusion.1.place, f32[64,128]{1,0:T(8,128)S(1)} %get-tuple-element.32.scale_ref, f32[16,1,512]{2,1,0:T(1,128)S(1)} %get-tuple-element.29.gain_ref, bf16[8192,512]{1,0:T(8,128)(2,1)} %weight_ref.1, f32[64,128]{1,0:T(8,128)S(1)} %bitcast.12, ...), custom_call_target="tpu_custom_call" | custom-call | flops 536870912 | bytes 8388608 | tf_op jit(solution)/shard_map/queries/pallas_call | solution.py:302
  31.3 0.9 %collective-permute-start.13 = (bf16[4,128,256]{2,1,0:T(8,128)(2,1)S(1)}, bf16[4,128,256]{2,1,0:T(8,128)(2,1)S(1)}, u32[]{:S(2)}, u32[]{:S(2)}) collective-permute-start(bf16[4,128,256]{2,1,0:T(8,128)(2,1)S(1)} %get-tuple-element.45), channel_id=1, source_target_pairs={{0,2},{2,0},{1,3},{3,1},{4,6},{6,4},{5,7},{7,5},{8,10},{10,8},{9,1... | collective-permute-start | bytes 786440 | tf_op jit(solution)/shard_map/ppermute | solution.py:594
  32.8 3.8 %collective-permute-done.7.got_ref = s16[272,128]{1,0:T(8,128)(2,1)S(1)} collective-permute-done((s16[272,128]{1,0:T(8,128)(2,1)S(1)}, s16[272,128]{1,0:T(8,128)(2,1)S(1)}, u32[]{:S(2)}, u32[]{:S(2)}) %collective-permute-start.7) | collective-permute-done | bytes 69664 | tf_op jit(solution)/shard_map/ppermute | solution.py:594
  36.6 2.1 %collective-permute-start.8 = (s16[144,128]{1,0:T(8,128)(2,1)S(1)}, s16[144,128]{1,0:T(8,128)(2,1)S(1)}, u32[]{:S(2)}, u32[]{:S(2)}) collective-permute-start(s16[144,128]{1,0:T(8,128)(2,1)S(1)} %get-tuple-element.38), channel_id=1, source_target_pairs={{0,8},{4,12},{8,0},{12,4},{1,9},{5,13},{9,1},{13,5},{2,10},{6,14},... | collective-permute-start | bytes 110600 | tf_op jit(solution)/shard_map/ppermute | solution.py:594
  38.8 1.9 %staged.3 = (bf16[16,512,512]{2,1,0:T(8,128)(2,1)S(1)}, f32[8,128]{1,0:T(8,128)S(1)}) custom-call(s32[3]{0:T(128)S(1)} %pad_add_fusion.1.place, bf16[512,8192]{1,0:T(8,128)(2,1)S(1)} %bitcast.11, f32[2,64,256]{2,1,0:T(8,128)S(1)} %get-tuple-element.35.kept_ref.refs_0_.refs_4_), custom_call_target="tpu_custom_call" | custom-call | bytes 16777216 | tf_op jit(solution)/shard_map/staged/pallas_call | solution.py:66
  42.1 1.1 %collective-permute-done.9.other_ref = f32[64,256]{1,0:T(8,128)S(1)} collective-permute-done((f32[64,256]{1,0:T(8,128)S(1)}, f32[64,256]{1,0:T(8,128)S(1)}, u32[]{:S(2)}, u32[]{:S(2)}) %collective-permute-start.9) | collective-permute-done | bytes 65568 | tf_op jit(solution)/shard_map/ppermute | solution.py:594
  43.3 2.2 %attend.1.x_ref = bf16[4,16,512]{2,1,0:T(8,128)(2,1)S(1)} custom-call(s32[3]{0:T(128)S(1)} %pad_add_fusion.1.place, s32[4]{0:T(128)S(1)} %copy-done.5, bf16[4,16,512]{2,1,0:T(8,128)(2,1)S(1)} %queries.1.refs_2_.q_ref, f32[64,256]{1,0:T(8,128)S(1)} %fold_pairs.1.refs_1_.mine_ref, f32[64,256]{1,0:T(8,128)S(1)} %collective-permute-done.9.other_ref, ...), custom_call_target="tpu_custom_call" | custom-call | flops 268435456 | bytes 3145728 | tf_op jit(solution)/shard_map/attend/pallas_call | solution.py:379
  48.2 1.2 %collective-permute-start.19 = (s16[528,128]{1,0:T(8,128)(2,1)S(1)}, s16[528,128]{1,0:T(8,128)(2,1)S(1)}, u32[]{:S(2)}, u32[]{:S(2)}) collective-permute-start(s16[528,128]{1,0:T(8,128)(2,1)S(1)} %get-tuple-element.47.refs_0_), channel_id=1, source_target_pairs={{0,2},{2,0},{1,3},{3,1},{4,6},{6,4},{5,7},{7,5},{8,10},{10,8},{9,1... | collective-permute-start | bytes 405512 | tf_op jit(solution)/shard_map/ppermute | solution.py:594
  50.8 3.9 %collective-permute-done.19.refs_2_ = s16[528,128]{1,0:T(8,128)(2,1)S(1)} collective-permute-done((s16[528,128]{1,0:T(8,128)(2,1)S(1)}, s16[528,128]{1,0:T(8,128)(2,1)S(1)}, u32[]{:S(2)}, u32[]{:S(2)}) %collective-permute-start.19) | collective-permute-done | bytes 135200 | tf_op jit(solution)/shard_map/ppermute | solution.py:594
  54.8 1.3 %collective-permute-start.20 = (s16[528,128]{1,0:T(8,128)(2,1)S(1)}, s16[528,128]{1,0:T(8,128)(2,1)S(1)}, u32[]{:S(2)}, u32[]{:S(2)}) collective-permute-start(s16[528,128]{1,0:T(8,128)(2,1)S(1)} %fold_sub.5), channel_id=1, source_target_pairs={{0,4},{4,0},{8,12},{12,8},{1,5},{5,1},{9,13},{13,9},{2,6},{6,2},{1... | collective-permute-start | bytes 405512 | tf_op jit(solution)/shard_map/ppermute | solution.py:594
  56.8 3.1 %collective-permute-done.20.got_ref = s16[528,128]{1,0:T(8,128)(2,1)S(1)} collective-permute-done((s16[528,128]{1,0:T(8,128)(2,1)S(1)}, s16[528,128]{1,0:T(8,128)(2,1)S(1)}, u32[]{:S(2)}, u32[]{:S(2)}) %collective-permute-start.20) | collective-permute-done | bytes 135200 | tf_op jit(solution)/shard_map/ppermute | solution.py:594
  60.0 2.1 %collective-permute-start.21 = (s16[272,128]{1,0:T(8,128)(2,1)S(1)}, s16[272,128]{1,0:T(8,128)(2,1)S(1)}, u32[]{:S(2)}, u32[]{:S(2)}) collective-permute-start(s16[272,128]{1,0:T(8,128)(2,1)S(1)} %get-tuple-element.50), channel_id=1, source_target_pairs={{0,8},{4,12},{8,0},{12,4},{1,9},{5,13},{9,1},{13,5},{2,10},{6,14},... | collective-permute-start | bytes 208904 | tf_op jit(solution)/shard_map/ppermute | solution.py:594
  62.1 3.1 %collective-permute-done.21.refs_0_ = s16[272,128]{1,0:T(8,128)(2,1)S(1)} collective-permute-done((s16[272,128]{1,0:T(8,128)(2,1)S(1)}, s16[272,128]{1,0:T(8,128)(2,1)S(1)}, u32[]{:S(2)}, u32[]{:S(2)}) %collective-permute-start.21) | collective-permute-done | bytes 69664 | tf_op jit(solution)/shard_map/ppermute | solution.py:594
  (68 shorter events, 13.3 us)
Async XLA Ops:
  0.0 15.1 %collective-permute-start.2 = (bf16[64,512]{1,0:T(8,128)(2,1)}, bf16[64,512]{1,0:T(8,128)(2,1)S(1)}, u32[]{:S(2)}, u32[]{:S(2)}) collective-permute-start(bf16[64,512]{1,0:T(8,128)(2,1)} %bitcast.16), channel_id=1, source_target_pairs={{0,12},{4,8},{8,4},{12,0},{1,13},{5,9},{9,5},{13,1},{2,14},{6,10},... | collective-permute-start | bytes 196616 | tf_op jit(solution)/shard_map/ppermute | solution.py:594
  5.0 10.1 %collective-permute-start.1 = (bf16[64,512]{1,0:T(8,128)(2,1)}, bf16[64,512]{1,0:T(8,128)(2,1)S(1)}, u32[]{:S(2)}, u32[]{:S(2)}) collective-permute-start(bf16[64,512]{1,0:T(8,128)(2,1)} %bitcast.17), channel_id=1, source_target_pairs={{0,8},{4,12},{8,0},{12,4},{1,9},{5,13},{9,1},{13,5},{2,10},{6,14},... | collective-permute-start | bytes 196616 | tf_op jit(solution)/shard_map/ppermute | solution.py:594
  5.1 10.1 %collective-permute-start = (bf16[64,512]{1,0:T(8,128)(2,1)}, bf16[64,512]{1,0:T(8,128)(2,1)S(1)}, u32[]{:S(2)}, u32[]{:S(2)}) collective-permute-start(bf16[64,512]{1,0:T(8,128)(2,1)} %bitcast.18), channel_id=1, source_target_pairs={{0,4},{4,0},{8,12},{12,8},{1,5},{5,1},{9,13},{13,9},{2,6},{6,2},{1... | collective-permute-start | bytes 196616 | tf_op jit(solution)/shard_map/ppermute | solution.py:594
  10.7 20.6 %collective-permute-start.10 = (bf16[2,128,256]{2,1,0:T(8,128)(2,1)S(1)}, bf16[2,128,256]{2,1,0:T(8,128)(2,1)S(1)}, u32[]{:S(2)}, u32[]{:S(2)}) collective-permute-start(bf16[2,128,256]{2,1,0:T(8,128)(2,1)S(1)} %get-tuple-element.41), channel_id=1, source_target_pairs={{0,4},{4,0},{8,12},{12,8},{1,5},{5,1},{9,13},{13,9},{2,6},{6,2},{1... | collective-permute-start | bytes 393224 | tf_op jit(solution)/shard_map/ppermute | solution.py:594
  12.2 19.1 %collective-permute-start.11 = (bf16[2,128,256]{2,1,0:T(8,128)(2,1)S(1)}, bf16[2,128,256]{2,1,0:T(8,128)(2,1)S(1)}, u32[]{:S(2)}, u32[]{:S(2)}) collective-permute-start(bf16[2,128,256]{2,1,0:T(8,128)(2,1)S(1)} %get-tuple-element.42), channel_id=1, source_target_pairs={{0,8},{4,12},{8,0},{12,4},{1,9},{5,13},{9,1},{13,5},{2,10},{6,14},... | collective-permute-start | bytes 393224 | tf_op jit(solution)/shard_map/ppermute | solution.py:594
  15.1 16.1 %collective-permute-start.12 = (bf16[2,128,256]{2,1,0:T(8,128)(2,1)S(1)}, bf16[2,128,256]{2,1,0:T(8,128)(2,1)S(1)}, u32[]{:S(2)}, u32[]{:S(2)}) collective-permute-start(bf16[2,128,256]{2,1,0:T(8,128)(2,1)S(1)} %get-tuple-element.43), channel_id=1, source_target_pairs={{0,12},{4,8},{8,4},{12,0},{1,13},{5,9},{9,5},{13,1},{2,14},{6,10},... | collective-permute-start | bytes 393224 | tf_op jit(solution)/shard_map/ppermute | solution.py:594
  15.2 6.7 %collective-permute-start.3 = (bf16[4,64,512]{2,1,0:T(8,128)(2,1)S(1)}, bf16[4,64,512]{2,1,0:T(8,128)(2,1)S(1)}, u32[]{:S(2)}, u32[]{:S(2)}) collective-permute-start(bf16[4,64,512]{2,1,0:T(8,128)(2,1)S(1)} %pack.1.refs_1_.refs_0_.rows_ref), channel_id=1, source_target_pairs={{0,2},{2,0},{1,3},{3,1},{4,6},{6,4},{5,7},{7,5},{8,10},{10,8},{9,1... | collective-permute-start | bytes 786440 | tf_op jit(solution)/shard_map/ppermute | solution.py:594
  17.7 4.3 %collective-permute-start.4 = (bf16[4,64,512]{2,1,0:T(8,128)(2,1)S(1)}, bf16[4,64,512]{2,1,0:T(8,128)(2,1)S(1)}, u32[]{:S(2)}, u32[]{:S(2)}) collective-permute-start(bf16[4,64,512]{2,1,0:T(8,128)(2,1)S(1)} %pack.1.refs_1_.refs_0_.rows_ref), channel_id=1, source_target_pairs={{0,1},{1,0},{2,3},{3,2},{4,5},{5,4},{6,7},{7,6},{8,9},{9,8},{10,11... | collective-permute-start | bytes 786440 | tf_op jit(solution)/shard_map/ppermute | solution.py:594
  20.0 18.7 %slice-start = ((s8[8388608]{0:T(1024)(128)(4,1)}), s8[4194304]{0:T(1024)(128)(4,1)S(1)}, s32[]{:S(2)}) async-start(s8[8388608]{0:T(1024)(128)(4,1)} %bitcast.10), calls=%async_computation | async-start | bytes 8388608
  21.9 1.5 %collective-permute-start.5 = (bf16[4,64,512]{2,1,0:T(8,128)(2,1)S(1)}, bf16[4,64,512]{2,1,0:T(8,128)(2,1)S(1)}, u32[]{:S(2)}, u32[]{:S(2)}) collective-permute-start(bf16[4,64,512]{2,1,0:T(8,128)(2,1)S(1)} %gate.2.refs_1_), channel_id=1, source_target_pairs={{0,1},{1,0},{2,3},{3,2},{4,5},{5,4},{6,7},{7,6},{8,9},{9,8},{10,11... | collective-permute-start | bytes 786440 | tf_op jit(solution)/shard_map/ppermute | solution.py:594
  24.8 6.3 %collective-permute-start.6 = (s16[528,128]{1,0:T(8,128)(2,1)S(1)}, s16[528,128]{1,0:T(8,128)(2,1)S(1)}, u32[]{:S(2)}, u32[]{:S(2)}) collective-permute-start(s16[528,128]{1,0:T(8,128)(2,1)S(1)} %get-tuple-element.34), channel_id=1, source_target_pairs={{0,2},{2,0},{1,3},{3,1},{4,6},{6,4},{5,7},{7,5},{8,10},{10,8},{9,1... | collective-permute-start | bytes 405512 | tf_op jit(solution)/shard_map/ppermute | solution.py:594
  26.5 16.8 %copy-start.5 = (s32[4]{0:T(128)S(1)}, s32[4]{0:T(128)}, u32[]{:S(2)}) copy-start(s32[4]{0:T(128)} %lengths.1) | copy-start | bytes 52
  31.3 10.2 %collective-permute-start.13 = (bf16[4,128,256]{2,1,0:T(8,128)(2,1)S(1)}, bf16[4,128,256]{2,1,0:T(8,128)(2,1)S(1)}, u32[]{:S(2)}, u32[]{:S(2)}) collective-permute-start(bf16[4,128,256]{2,1,0:T(8,128)(2,1)S(1)} %get-tuple-element.45), channel_id=1, source_target_pairs={{0,2},{2,0},{1,3},{3,1},{4,6},{6,4},{5,7},{7,5},{8,10},{10,8},{9,1... | collective-permute-start | bytes 786440 | tf_op jit(solution)/shard_map/ppermute | solution.py:594
  32.2 4.3 %collective-permute-start.7 = (s16[272,128]{1,0:T(8,128)(2,1)S(1)}, s16[272,128]{1,0:T(8,128)(2,1)S(1)}, u32[]{:S(2)}, u32[]{:S(2)}) collective-permute-start(s16[272,128]{1,0:T(8,128)(2,1)S(1)} %get-tuple-element.36), channel_id=1, source_target_pairs={{0,4},{4,0},{8,12},{12,8},{1,5},{5,1},{9,13},{13,9},{2,6},{6,2},{1... | collective-permute-start | bytes 208904 | tf_op jit(solution)/shard_map/ppermute | solution.py:594
  36.6 4.9 %collective-permute-start.8 = (s16[144,128]{1,0:T(8,128)(2,1)S(1)}, s16[144,128]{1,0:T(8,128)(2,1)S(1)}, u32[]{:S(2)}, u32[]{:S(2)}) collective-permute-start(s16[144,128]{1,0:T(8,128)(2,1)S(1)} %get-tuple-element.38), channel_id=1, source_target_pairs={{0,8},{4,12},{8,0},{12,4},{1,9},{5,13},{9,1},{13,5},{2,10},{6,14},... | collective-permute-start | bytes 110600 | tf_op jit(solution)/shard_map/ppermute | solution.py:594
  38.8 4.5 %collective-permute-start.14 = (bf16[4,128,256]{2,1,0:T(8,128)(2,1)S(1)}, bf16[4,128,256]{2,1,0:T(8,128)(2,1)S(1)}, u32[]{:S(2)}, u32[]{:S(2)}) collective-permute-start(bf16[4,128,256]{2,1,0:T(8,128)(2,1)S(1)} %get-tuple-element.44.refs_0_), channel_id=1, source_target_pairs={{0,1},{1,0},{2,3},{3,2},{4,5},{5,4},{6,7},{7,6},{8,9},{9,8},{10,11... | collective-permute-start | bytes 786440 | tf_op jit(solution)/shard_map/ppermute | solution.py:594
  41.6 1.7 %collective-permute-start.15 = (bf16[4,128,256]{2,1,0:T(8,128)(2,1)S(1)}, bf16[4,128,256]{2,1,0:T(8,128)(2,1)S(1)}, u32[]{:S(2)}, u32[]{:S(2)}) collective-permute-start(bf16[4,128,256]{2,1,0:T(8,128)(2,1)S(1)} %gate.3.refs_1_), channel_id=1, source_target_pairs={{0,1},{1,0},{2,3},{3,2},{4,5},{5,4},{6,7},{7,6},{8,9},{9,8},{10,11... | collective-permute-start | bytes 786440 | tf_op jit(solution)/shard_map/ppermute | solution.py:594
  41.7 1.6 %collective-permute-start.9 = (f32[64,256]{1,0:T(8,128)S(1)}, f32[64,256]{1,0:T(8,128)S(1)}, u32[]{:S(2)}, u32[]{:S(2)}) collective-permute-start(f32[64,256]{1,0:T(8,128)S(1)} %fold_pairs.1.refs_1_.mine_ref), channel_id=1, source_target_pairs={{0,1},{1,0},{2,3},{3,2},{4,5},{5,4},{6,7},{7,6},{8,9},{9,8},{10,11... | collective-permute-start | bytes 196616 | tf_op jit(solution)/shard_map/ppermute | solution.py:594
  46.0 2.0 %collective-permute-start.16 = (f32[4,64,512]{2,1,0:T(8,128)S(1)}, f32[4,64,512]{2,1,0:T(8,128)S(1)}, u32[]{:S(2)}, u32[]{:S(2)}) collective-permute-start(f32[4,64,512]{2,1,0:T(8,128)S(1)} %outputs.4.refs_0_), channel_id=1, source_target_pairs={{0,1},{1,0},{2,3},{3,2},{4,5},{5,4},{6,7},{7,6},{8,9},{9,8},{10,11... | collective-permute-start | bytes 1572872 | tf_op jit(solution)/shard_map/ppermute | solution.py:594
  46.6 4.1 %collective-permute-start.17 = (f32[4,64,512]{2,1,0:T(8,128)S(1)}, f32[4,64,512]{2,1,0:T(8,128)S(1)}, u32[]{:S(2)}, u32[]{:S(2)}) collective-permute-start(f32[4,64,512]{2,1,0:T(8,128)S(1)} %outputs.5.refs_0_), channel_id=1, source_target_pairs={{0,1},{1,0},{2,3},{3,2},{4,5},{5,4},{6,7},{7,6},{8,9},{9,8},{10,11... | collective-permute-start | bytes 1572872 | tf_op jit(solution)/shard_map/ppermute | solution.py:594
  48.2 6.5 %collective-permute-start.19 = (s16[528,128]{1,0:T(8,128)(2,1)S(1)}, s16[528,128]{1,0:T(8,128)(2,1)S(1)}, u32[]{:S(2)}, u32[]{:S(2)}) collective-permute-start(s16[528,128]{1,0:T(8,128)(2,1)S(1)} %get-tuple-element.47.refs_0_), channel_id=1, source_target_pairs={{0,2},{2,0},{1,3},{3,1},{4,6},{6,4},{5,7},{7,5},{8,10},{10,8},{9,1... | collective-permute-start | bytes 405512 | tf_op jit(solution)/shard_map/ppermute | solution.py:594
  49.4 7.4 %collective-permute-start.18 = (s16[528,128]{1,0:T(8,128)(2,1)S(1)}, s16[528,128]{1,0:T(8,128)(2,1)S(1)}, u32[]{:S(2)}, u32[]{:S(2)}) collective-permute-start(s16[528,128]{1,0:T(8,128)(2,1)S(1)} %get-tuple-element.48), channel_id=1, source_target_pairs={{0,2},{2,0},{1,3},{3,1},{4,6},{6,4},{5,7},{7,5},{8,10},{10,8},{9,1... | collective-permute-start | bytes 405512 | tf_op jit(solution)/shard_map/ppermute | solution.py:594
  54.8 5.1 %collective-permute-start.20 = (s16[528,128]{1,0:T(8,128)(2,1)S(1)}, s16[528,128]{1,0:T(8,128)(2,1)S(1)}, u32[]{:S(2)}, u32[]{:S(2)}) collective-permute-start(s16[528,128]{1,0:T(8,128)(2,1)S(1)} %fold_sub.5), channel_id=1, source_target_pairs={{0,4},{4,0},{8,12},{12,8},{1,5},{5,1},{9,13},{13,9},{2,6},{6,2},{1... | collective-permute-start | bytes 405512 | tf_op jit(solution)/shard_map/ppermute | solution.py:594
  60.0 5.3 %collective-permute-start.21 = (s16[272,128]{1,0:T(8,128)(2,1)S(1)}, s16[272,128]{1,0:T(8,128)(2,1)S(1)}, u32[]{:S(2)}, u32[]{:S(2)}) collective-permute-start(s16[272,128]{1,0:T(8,128)(2,1)S(1)} %get-tuple-element.50), channel_id=1, source_target_pairs={{0,8},{4,12},{8,0},{12,4},{1,9},{5,13},{9,1},{13,5},{2,10},{6,14},... | collective-permute-start | bytes 208904 | tf_op jit(solution)/shard_map/ppermute | solution.py:594
  (6 other events, 17.4 us)

commit v12 on v9

--- a/solution.py
+++ b/solution.py
@@ -19,7 +19,6 @@
 PAIR = 2 * HEAD_SIZE
 LANES = 128
 TAIL = 16
-HALVES = ((0, 3), (1, 2))
 DEVICES = ("req", "sub", "section")
 
 theta_base = 500000.0
@@ -76,7 +75,7 @@
         + [jax.ShapeDtypeStruct(other.shape, other.dtype) for other in more],
         scratch_shapes=[pltpu.SemaphoreType.DMA((count + len(more),))],
         compiler_params=params(),
-        cost_estimate=cost([array] * 2),
+        cost_estimate=cost([array], [array]),
         name="staged",
     )(place, array, *more, *after)
 
@@ -262,7 +261,7 @@
         out_specs=[pl.BlockSpec(memory_space=pltpu.VMEM)] * len(shapes),
         out_shape=shapes,
         compiler_params=params(),
-        cost_estimate=cost(gathered * 1, [weight], flops=2 * count * weight.size),
+        cost_estimate=cost(gathered, [weight], flops=2 * count * weight.size),
         name="scale_and_pairs",
     )(place, gain, weight, *gathered)
 
@@ -363,10 +362,11 @@
         scores = jnp.exp(scores - highest)
         own = jnp.exp(own - highest)
         total = jnp.sum(scores, axis=-1, keepdims=True) + jnp.sum(own, axis=-1, keepdims=True)
+        share = 1.0 / total
         mixed = jnp.dot(
-            (scores / total).astype(jnp.bfloat16), values, preferred_element_type=jnp.float32
+            (scores * share).astype(jnp.bfloat16), values, preferred_element_type=jnp.float32
         ) + jnp.dot(
-            (own / total).astype(jnp.bfloat16), new_value, preferred_element_type=jnp.float32
+            (own * share).astype(jnp.bfloat16), new_value, preferred_element_type=jnp.float32
         )
         mixed = mixed.astype(jnp.bfloat16)
         for h in range(quarter):
@@ -444,24 +444,24 @@
     return ref[pl.ds(first, rows)].astype(jnp.int32).astype(jnp.float32) * step
 
 
-def fold_core_kernel(mine_ref, got_ref, *out_refs):
+def fold_core_kernel(keep, mine_ref, got_ref, *out_refs):
     for i, out_ref in enumerate(out_refs):
-        pieces = []
-        for z in HALVES[i % 2]:
-            block = i // 2 * GROUP_REQUESTS + z
-            pieces += pieces_of(mine_ref[block] + got_ref[block])
-        encode(out_ref, pieces)
-
-
-def fold_core(mine, got):
+        block = mine_ref[i] + got_ref[i]
+        if keep and i == 0:
+            out_ref[...] = block
+        else:
+            encode(out_ref, pieces_of(block))
+
+
+def fold_core(mine, got, keep):
     blocks, rows, width = mine.shape
-    count = 2 * (blocks // GROUP_REQUESTS)
-    sent = jax.ShapeDtypeStruct((2 * width // LANES * rows + TAIL, LANES), jnp.int16)
-    return pl.pallas_call(
-        fold_core_kernel,
+    sent = jax.ShapeDtypeStruct((width // LANES * rows + TAIL, LANES), jnp.int16)
+    kept = jax.ShapeDtypeStruct((rows, width), jnp.float32)
+    return pl.pallas_call(
+        functools.partial(fold_core_kernel, keep),
         in_specs=[pl.BlockSpec(memory_space=pltpu.VMEM)] * 2,
-        out_specs=[pl.BlockSpec(memory_space=pltpu.VMEM)] * count,
-        out_shape=[sent] * count,
+        out_specs=[pl.BlockSpec(memory_space=pltpu.VMEM)] * blocks,
+        out_shape=[kept if keep and i == 0 else sent for i in range(blocks)],
         compiler_params=params(),
         cost_estimate=cost([mine, got]),
         name="fold_core",
@@ -555,6 +555,13 @@
 
 def passed(array, axis, shift):
     return lax.ppermute(array, axis, [(i, i ^ shift) for i in range(lax.axis_size(axis))])
+
+
+def sent_to(array, step, shift):
+    subs = lax.axis_size("sub")
+    count = lax.axis_size("req") * subs
+    there = [(i, ((i // subs) ^ step) * subs + (i % subs ^ shift)) for i in range(count)]
+    return lax.ppermute(array, ("req", "sub"), there)
 
 
 def scalars(*values):
@@ -636,14 +643,13 @@
     second = outputs(mixed, w_output, end, mid, after=[first])
     got_second = passed(second, "section", 1)
     kept = outputs(mixed, w_output, mid, end - mid, after=[second])
-    parts = fold_core(kept, got_first)
+    parts = fold_core(kept, got_first, False)
     kept = outputs(mixed, w_output, 0, mid, after=parts[:1])
-    parts = [passed(part, "sub", i // 2 + 1) for i, part in enumerate(parts)]
-    last = {}
-    for half, order in enumerate(HALVES):
-        last.update(zip(order, fold_sub(order, [kept, got_second], parts[half::2])))
-    parts = [passed(last[s], "req", s) for s in range(1, GROUP_REQUESTS)]
-    return finish(gathered[0], last[0], parts).reshape(hidden.shape)
+    steps = [(z, j) for j in range(1, subs) for z in range(GROUP_REQUESTS)]
+    parts = [sent_to(part, *step) for part, step in zip(parts, steps)]
+    total, *near = fold_core(kept, got_second, True)
+    parts += [sent_to(part, z + 1, 0) for z, part in enumerate(near)]
+    return finish(gathered[0], total, parts).reshape(hidden.shape)
 
 
 def solution(mesh):

time: 64.8 us -> 65.4 us (level)
  starting transfers between devices: 26.1 us -> 31.3 us
  waiting for transfers between devices: 15.4 us -> 10.8 us
    ppermute x0 -> x7, starting transfers between devices: none -> 11.3 us  [sent_to(): return lax.ppermute(array, ('req', 'sub'), there)]
    ppermute x24 -> x19, waiting for transfers between devices: 15.4 us -> 7.25 us  [passed(): lax.ppermute(array, axis, [(i, i ^ shift) for i in range(lax.axis_size(ax...]
    ppermute x24 -> x19, starting transfers between devices: 26.1 us -> 20 us  [passed(): lax.ppermute(array, axis, [(i, i ^ shift) for i in range(lax.axis_size(ax...]
    ppermute x0 -> x7, waiting for transfers between devices: none -> 3.58 us  [sent_to(): return lax.ppermute(array, ('req', 'sub'), there)]
  transfers between devices with their start and end apart: 24 -> 26, of which waited for: 10 -> 7; matrix products, arithmetic and copies ran while one was open for 3% -> 3% of each run, Pallas kernels for 19% -> 19%
where the time goes in v12:
time: 65.4 us; the launch traced here: 65.1 us
  starting transfers between devices  31.3 us (48%)
  Pallas kernels  15.9 us (24%)
  waiting for transfers between devices  10.8 us (17%)
  local copies, waits for them, and re-layouts  5.12 us (8%)
  other arithmetic  1.71 us (3%)
    ppermute x19, starting transfers between devices, passed(): lax.ppermute(array, axis, [(i, i ^ shift) for i in range(lax.axis_size(ax...  20 us
    ppermute x7, starting transfers between devices, sent_to(): return lax.ppermute(array, ('req', 'sub'), there)  11.3 us
    ppermute x19, waiting for transfers between devices, passed(): lax.ppermute(array, axis, [(i, i ^ shift) for i in range(lax.axis_size(ax...  7.25 us
    unnamed x16, local copies, waits for them, and re-layouts  5.11 us
    pallas_call x1, Pallas kernels, queries(): pl.pallas_call(query_kernel, in_specs=[pl.BlockSpec(memory_space=pltpu.SM...  4.63 us
    ppermute x7, waiting for transfers between devices, sent_to(): return lax.ppermute(array, ('req', 'sub'), there)  3.58 us
    pallas_call x2, Pallas kernels, staged(): pl.pallas_call(functools.partial(stage_kernel, order, len(more)), in_spec...  2.85 us
    pallas_call x1, Pallas kernels, attend(): pl.pallas_call(attend_kernel, in_specs=[pl.BlockSpec(memory_space=pltpu.S...  2.18 us
  transfers between devices with their start and end apart: 26, of which 7 were waited for; matrix products, arithmetic and copies ran while one was open for 3% of the time, Pallas kernels for 19%

profile of v12, /device:TPU:0, one launch (start us, length us, event | category | flops | bytes accessed | tf_op | source)
XLA Modules:
  0.0 65.1 jit_solution(12480976617674300408)
XLA Ops:
  0.0 5.0 %collective-permute-start.2 = (bf16[64,512]{1,0:T(8,128)(2,1)}, bf16[64,512]{1,0:T(8,128)(2,1)S(1)}, u32[]{:S(2)}, u32[]{:S(2)}) collective-permute-start(bf16[64,512]{1,0:T(8,128)(2,1)} %bitcast.16), channel_id=1, source_target_pairs={{0,12},{4,8},{8,4},{12,0},{1,13},{5,9},{9,5},{13,1},{2,14},{6,10},... | collective-permute-start | bytes 196616 | tf_op jit(solution)/shard_map/ppermute | solution.py:557
  6.4 1.2 %copy-done.1 = bf16[16,16,2048]{2,1,0:T(8,128)(2,1)S(1)} copy-done((bf16[16,16,2048]{2,1,0:T(8,128)(2,1)S(1)}, bf16[16,16,2048]{2,1,0:T(8,128)(2,1)}, u32[]{:S(2)}) %copy-start.1) | copy-done | bytes 1048600
  9.1 1.5 %used_pages.1 = (bf16[64,512]{1,0:T(8,128)(2,1)S(1)}, bf16[2,128,256]{2,1,0:T(8,128)(2,1)S(1)}, bf16[2,128,256]{2,1,0:T(8,128)(2,1)S(1)}, bf16[2,128,256]{2,1,0:T(8,128)(2,1)S(1)}, bf16[2,128,256]{2,1,0:T(8,128)(2,1)S(1)}) custom-call(s32[4,32]{1,0:T(4,128)S(1)} %copy-done.4, s32[3]{0:T(128)S(1)} %pad_add_fusion.place, ...), custom_call_target="tpu_custom_call" | custom-call | bytes 1048576 | tf_op jit(solution)/shard_map/used_pages/pallas_call | solution.py:140
  10.7 1.5 %collective-permute-start.11 = (bf16[2,128,256]{2,1,0:T(8,128)(2,1)S(1)}, bf16[2,128,256]{2,1,0:T(8,128)(2,1)S(1)}, u32[]{:S(2)}, u32[]{:S(2)}) collective-permute-start(bf16[2,128,256]{2,1,0:T(8,128)(2,1)S(1)} %get-tuple-element.45), channel_id=1, source_target_pairs={{0,4},{4,0},{8,12},{12,8},{1,5},{5,1},{9,13},{13,9},{2,6},{6,2},{1... | collective-permute-start | bytes 393224 | tf_op jit(solution)/shard_map/ppermute | solution.py:557
  12.2 2.9 %collective-permute-start.12 = (bf16[2,128,256]{2,1,0:T(8,128)(2,1)S(1)}, bf16[2,128,256]{2,1,0:T(8,128)(2,1)S(1)}, u32[]{:S(2)}, u32[]{:S(2)}) collective-permute-start(bf16[2,128,256]{2,1,0:T(8,128)(2,1)S(1)} %get-tuple-element.46), channel_id=1, source_target_pairs={{0,8},{4,12},{8,0},{12,4},{1,9},{5,13},{9,1},{13,5},{2,10},{6,14},... | collective-permute-start | bytes 393224 | tf_op jit(solution)/shard_map/ppermute | solution.py:557
  15.2 1.8 %collective-permute-start.3 = (bf16[4,64,512]{2,1,0:T(8,128)(2,1)S(1)}, bf16[4,64,512]{2,1,0:T(8,128)(2,1)S(1)}, u32[]{:S(2)}, u32[]{:S(2)}) collective-permute-start(bf16[4,64,512]{2,1,0:T(8,128)(2,1)S(1)} %pack.1.refs_1_.refs_0_.rows_ref), channel_id=1, source_target_pairs={{0,2},{2,0},{1,3},{3,1},{4,6},{6,4},{5,7},{7,5},{8,10},{10,8},{9,1... | collective-permute-start | bytes 786440 | tf_op jit(solution)/shard_map/ppermute | solution.py:557
  17.7 1.6 %copy-done = bf16[512,2048]{1,0:T(8,128)(2,1)S(1)} copy-done((bf16[512,2048]{1,0:T(8,128)(2,1)S(1)}, bf16[512,2048]{1,0:T(8,128)(2,1)}, u32[]{:S(2)}) %copy-start) | copy-done | bytes 2097176
  20.0 1.0 %staged.2 = (bf16[8,512,256]{2,1,0:T(8,128)(2,1)S(1)}, f32[8,128]{1,0:T(8,128)S(1)}, f32[16,1,512]{2,1,0:T(1,128)S(1)}) custom-call(s32[3]{0:T(128)S(1)} %pad_add_fusion.1.place, bf16[512,2048]{1,0:T(8,128)(2,1)S(1)} %copy-done, f32[16,1,512]{2,1,0:T(1,128)S(1)} %bitcast.20, bf16[4,64,512]{2,1,0:T(8,128)(2,1)S(1)} %pack.1.refs_1_.refs_0_.rows_ref), custom_call_target="tpu_custom_call" | custom-call | bytes 4194304 | tf_op jit(solution)/shard_map/staged/pallas_call | solution.py:65
  22.0 1.4 %collective-permute-done.5.refs_3_ = bf16[4,64,512]{2,1,0:T(8,128)(2,1)S(1)} collective-permute-done((bf16[4,64,512]{2,1,0:T(8,128)(2,1)S(1)}, bf16[4,64,512]{2,1,0:T(8,128)(2,1)S(1)}, u32[]{:S(2)}, u32[]{:S(2)}) %collective-permute-start.5) | collective-permute-done | bytes 262176 | tf_op jit(solution)/shard_map/ppermute | solution.py:557
  23.4 1.4 %scale_and_pairs.1 = (f32[64,128]{1,0:T(8,128)S(1)}, f32[4,64,256]{2,1,0:T(8,128)S(1)}, s16[528,128]{1,0:T(8,128)(2,1)S(1)}) custom-call(s32[3]{0:T(128)S(1)} %pad_add_fusion.1.place, f32[16,1,512]{2,1,0:T(1,128)S(1)} %get-tuple-element.33.gain_ref, bf16[8,512,256]{2,1,0:T(8,128)(2,1)S(1)} %get-tuple-element.34.weight_ref, ...), custom_call_target="tpu_custom_call" | custom-call | flops 134217728 | bytes 3145728 | tf_op jit(solution)/shard_map/scale_and_pairs/pallas_call | solution.py:257
  24.8 1.6 %collective-permute-start.6 = (s16[528,128]{1,0:T(8,128)(2,1)S(1)}, s16[528,128]{1,0:T(8,128)(2,1)S(1)}, u32[]{:S(2)}, u32[]{:S(2)}) collective-permute-start(s16[528,128]{1,0:T(8,128)(2,1)S(1)} %get-tuple-element.38), channel_id=1, source_target_pairs={{0,2},{2,0},{1,3},{3,1},{4,6},{6,4},{5,7},{7,5},{8,10},{10,8},{9,1... | collective-permute-start | bytes 405512 | tf_op jit(solution)/shard_map/ppermute | solution.py:557
  26.5 4.6 %queries.1.refs_2_.refs_0_.q_ref = bf16[4,16,512]{2,1,0:T(8,128)(2,1)S(1)} custom-call(s32[3]{0:T(128)S(1)} %pad_add_fusion.1.place, f32[64,128]{1,0:T(8,128)S(1)} %get-tuple-element.36.scale_ref, f32[16,1,512]{2,1,0:T(1,128)S(1)} %get-tuple-element.33.gain_ref, bf16[8192,512]{1,0:T(8,128)(2,1)} %weight_ref.1, f32[64,128]{1,0:T(8,128)S(1)} %bitcast.12, ...), custom_call_target="tpu_custom_call" | custom-call | flops 536870912 | bytes 8388608 | tf_op jit(solution)/shard_map/queries/pallas_call | solution.py:301
  31.3 0.9 %collective-permute-start.14 = (bf16[4,128,256]{2,1,0:T(8,128)(2,1)S(1)}, bf16[4,128,256]{2,1,0:T(8,128)(2,1)S(1)}, u32[]{:S(2)}, u32[]{:S(2)}) collective-permute-start(bf16[4,128,256]{2,1,0:T(8,128)(2,1)S(1)} %get-tuple-element.49), channel_id=1, source_target_pairs={{0,2},{2,0},{1,3},{3,1},{4,6},{6,4},{5,7},{7,5},{8,10},{10,8},{9,1... | collective-permute-start | bytes 786440 | tf_op jit(solution)/shard_map/ppermute | solution.py:557
  32.8 3.5 %collective-permute-start.8 = (s16[144,128]{1,0:T(8,128)(2,1)S(1)}, s16[144,128]{1,0:T(8,128)(2,1)S(1)}, u32[]{:S(2)}, u32[]{:S(2)}) collective-permute-start(s16[144,128]{1,0:T(8,128)(2,1)S(1)} %get-tuple-element.41), channel_id=1, source_target_pairs={{0,8},{4,12},{8,0},{12,4},{1,9},{5,13},{9,1},{13,5},{2,10},{6,14},... | collective-permute-start | bytes 110600 | tf_op jit(solution)/shard_map/ppermute | solution.py:557
  36.6 1.9 %staged.3 = (bf16[16,512,512]{2,1,0:T(8,128)(2,1)S(1)}, f32[8,128]{1,0:T(8,128)S(1)}) custom-call(s32[3]{0:T(128)S(1)} %pad_add_fusion.1.place, bf16[512,8192]{1,0:T(8,128)(2,1)S(1)} %bitcast.11, bf16[4,16,512]{2,1,0:T(8,128)(2,1)S(1)} %queries.1.refs_2_.refs_0_.q_ref), custom_call_target="tpu_custom_call" | custom-call | bytes 16777216 | tf_op jit(solution)/shard_map/staged/pallas_call | solution.py:65
  38.7 3.4 %collective-permute-done.9.refs_2_ = s16[144,128]{1,0:T(8,128)(2,1)S(1)} collective-permute-done((s16[144,128]{1,0:T(8,128)(2,1)S(1)}, s16[144,128]{1,0:T(8,128)(2,1)S(1)}, u32[]{:S(2)}, u32[]{:S(2)}) %collective-permute-start.9) | collective-permute-done | bytes 36896 | tf_op jit(solution)/shard_map/ppermute | solution.py:557
  42.7 1.1 %collective-permute-done.10.other_ref = f32[64,256]{1,0:T(8,128)S(1)} collective-permute-done((f32[64,256]{1,0:T(8,128)S(1)}, f32[64,256]{1,0:T(8,128)S(1)}, u32[]{:S(2)}, u32[]{:S(2)}) %collective-permute-start.10) | collective-permute-done | bytes 65568 | tf_op jit(solution)/shard_map/ppermute | solution.py:557
  43.9 2.2 %attend.1.x_ref = bf16[4,16,512]{2,1,0:T(8,128)(2,1)S(1)} custom-call(s32[3]{0:T(128)S(1)} %pad_add_fusion.1.place, s32[4]{0:T(128)S(1)} %copy-done.5, bf16[4,16,512]{2,1,0:T(8,128)(2,1)S(1)} %queries.1.refs_2_.refs_0_.q_ref, f32[64,256]{1,0:T(8,128)S(1)} %fold_pairs.1.refs_1_.mine_ref, f32[64,256]{1,0:T(8,128)S(1)} %collective-permute-done.10.other_ref, ...), custom_call_target="tpu_custom_call" | custom-call | flops 268435456 | bytes 3145728 | tf_op jit(solution)/shard_map/attend/pallas_call | solution.py:379
  48.8 2.2 %collective-permute-start.21 = (s16[272,128]{1,0:T(8,128)(2,1)S(1)}, s16[272,128]{1,0:T(8,128)(2,1)S(1)}, u32[]{:S(2)}, u32[]{:S(2)}) collective-permute-start(s16[272,128]{1,0:T(8,128)(2,1)S(1)} %get-tuple-element.54), channel_id=1, source_target_pairs={{0,10},{2,8},{4,14},{6,12},{8,2},{10,0},{12,6},{14,4},{1,11},{3,9}... | collective-permute-start | bytes 208904 | tf_op jit(solution)/shard_map/ppermute | solution.py:564
  51.1 3.7 %collective-permute-start.22 = (s16[272,128]{1,0:T(8,128)(2,1)S(1)}, s16[272,128]{1,0:T(8,128)(2,1)S(1)}, u32[]{:S(2)}, u32[]{:S(2)}) collective-permute-start(s16[272,128]{1,0:T(8,128)(2,1)S(1)} %get-tuple-element.55), channel_id=1, source_target_pairs={{0,14},{2,12},{4,10},{6,8},{8,6},{10,4},{12,2},{14,0},{1,15},{3,13... | collective-permute-start | bytes 208904 | tf_op jit(solution)/shard_map/ppermute | solution.py:564
  55.5 0.9 %collective-permute-start.24 = (s16[272,128]{1,0:T(8,128)(2,1)S(1)}, s16[272,128]{1,0:T(8,128)(2,1)S(1)}, u32[]{:S(2)}, u32[]{:S(2)}) collective-permute-start(s16[272,128]{1,0:T(8,128)(2,1)S(1)} %get-tuple-element.57), channel_id=1, source_target_pairs={{0,8},{2,10},{4,12},{6,14},{8,0},{10,2},{12,4},{14,6},{1,9},{3,11}... | collective-permute-start | bytes 208904 | tf_op jit(solution)/shard_map/ppermute | solution.py:564
  56.4 3.4 %collective-permute-start.25 = (s16[272,128]{1,0:T(8,128)(2,1)S(1)}, s16[272,128]{1,0:T(8,128)(2,1)S(1)}, u32[]{:S(2)}, u32[]{:S(2)}) collective-permute-start(s16[272,128]{1,0:T(8,128)(2,1)S(1)} %get-tuple-element.58), channel_id=1, source_target_pairs={{0,12},{2,14},{4,8},{6,10},{8,4},{10,6},{12,0},{14,2},{1,13},{3,15... | collective-permute-start | bytes 208904 | tf_op jit(solution)/shard_map/ppermute | solution.py:564
  59.9 0.9 %collective-permute-start.19 = (s16[272,128]{1,0:T(8,128)(2,1)S(1)}, s16[272,128]{1,0:T(8,128)(2,1)S(1)}, u32[]{:S(2)}, u32[]{:S(2)}) collective-permute-start(s16[272,128]{1,0:T(8,128)(2,1)S(1)} %get-tuple-element.51.refs_0_), channel_id=1, source_target_pairs={{0,2},{2,0},{4,6},{6,4},{8,10},{10,8},{12,14},{14,12},{1,3},{3,1},... | collective-permute-start | bytes 208904 | tf_op jit(solution)/shard_map/ppermute | solution.py:564
  60.7 3.6 %collective-permute-done.24.refs_5_ = s16[272,128]{1,0:T(8,128)(2,1)S(1)} collective-permute-done((s16[272,128]{1,0:T(8,128)(2,1)S(1)}, s16[272,128]{1,0:T(8,128)(2,1)S(1)}, u32[]{:S(2)}, u32[]{:S(2)}) %collective-permute-start.24) | collective-permute-done | bytes 69664 | tf_op jit(solution)/shard_map/ppermute | solution.py:564
  (73 shorter events, 11.5 us)
Async XLA Ops:
  0.0 15.1 %collective-permute-start.2 = (bf16[64,512]{1,0:T(8,128)(2,1)}, bf16[64,512]{1,0:T(8,128)(2,1)S(1)}, u32[]{:S(2)}, u32[]{:S(2)}) collective-permute-start(bf16[64,512]{1,0:T(8,128)(2,1)} %bitcast.16), channel_id=1, source_target_pairs={{0,12},{4,8},{8,4},{12,0},{1,13},{5,9},{9,5},{13,1},{2,14},{6,10},... | collective-permute-start | bytes 196616 | tf_op jit(solution)/shard_map/ppermute | solution.py:557
  5.0 10.1 %collective-permute-start.1 = (bf16[64,512]{1,0:T(8,128)(2,1)}, bf16[64,512]{1,0:T(8,128)(2,1)S(1)}, u32[]{:S(2)}, u32[]{:S(2)}) collective-permute-start(bf16[64,512]{1,0:T(8,128)(2,1)} %bitcast.17), channel_id=1, source_target_pairs={{0,8},{4,12},{8,0},{12,4},{1,9},{5,13},{9,1},{13,5},{2,10},{6,14},... | collective-permute-start | bytes 196616 | tf_op jit(solution)/shard_map/ppermute | solution.py:557
  5.1 10.1 %collective-permute-start = (bf16[64,512]{1,0:T(8,128)(2,1)}, bf16[64,512]{1,0:T(8,128)(2,1)S(1)}, u32[]{:S(2)}, u32[]{:S(2)}) collective-permute-start(bf16[64,512]{1,0:T(8,128)(2,1)} %bitcast.18), channel_id=1, source_target_pairs={{0,4},{4,0},{8,12},{12,8},{1,5},{5,1},{9,13},{13,9},{2,6},{6,2},{1... | collective-permute-start | bytes 196616 | tf_op jit(solution)/shard_map/ppermute | solution.py:557
  10.7 20.6 %collective-permute-start.11 = (bf16[2,128,256]{2,1,0:T(8,128)(2,1)S(1)}, bf16[2,128,256]{2,1,0:T(8,128)(2,1)S(1)}, u32[]{:S(2)}, u32[]{:S(2)}) collective-permute-start(bf16[2,128,256]{2,1,0:T(8,128)(2,1)S(1)} %get-tuple-element.45), channel_id=1, source_target_pairs={{0,4},{4,0},{8,12},{12,8},{1,5},{5,1},{9,13},{13,9},{2,6},{6,2},{1... | collective-permute-start | bytes 393224 | tf_op jit(solution)/shard_map/ppermute | solution.py:557
  12.2 19.1 %collective-permute-start.12 = (bf16[2,128,256]{2,1,0:T(8,128)(2,1)S(1)}, bf16[2,128,256]{2,1,0:T(8,128)(2,1)S(1)}, u32[]{:S(2)}, u32[]{:S(2)}) collective-permute-start(bf16[2,128,256]{2,1,0:T(8,128)(2,1)S(1)} %get-tuple-element.46), channel_id=1, source_target_pairs={{0,8},{4,12},{8,0},{12,4},{1,9},{5,13},{9,1},{13,5},{2,10},{6,14},... | collective-permute-start | bytes 393224 | tf_op jit(solution)/shard_map/ppermute | solution.py:557
  15.1 16.2 %collective-permute-start.13 = (bf16[2,128,256]{2,1,0:T(8,128)(2,1)S(1)}, bf16[2,128,256]{2,1,0:T(8,128)(2,1)S(1)}, u32[]{:S(2)}, u32[]{:S(2)}) collective-permute-start(bf16[2,128,256]{2,1,0:T(8,128)(2,1)S(1)} %get-tuple-element.47), channel_id=1, source_target_pairs={{0,12},{4,8},{8,4},{12,0},{1,13},{5,9},{9,5},{13,1},{2,14},{6,10},... | collective-permute-start | bytes 393224 | tf_op jit(solution)/shard_map/ppermute | solution.py:557
  15.2 6.7 %collective-permute-start.3 = (bf16[4,64,512]{2,1,0:T(8,128)(2,1)S(1)}, bf16[4,64,512]{2,1,0:T(8,128)(2,1)S(1)}, u32[]{:S(2)}, u32[]{:S(2)}) collective-permute-start(bf16[4,64,512]{2,1,0:T(8,128)(2,1)S(1)} %pack.1.refs_1_.refs_0_.rows_ref), channel_id=1, source_target_pairs={{0,2},{2,0},{1,3},{3,1},{4,6},{6,4},{5,7},{7,5},{8,10},{10,8},{9,1... | collective-permute-start | bytes 786440 | tf_op jit(solution)/shard_map/ppermute | solution.py:557
  17.7 4.3 %collective-permute-start.4 = (bf16[4,64,512]{2,1,0:T(8,128)(2,1)S(1)}, bf16[4,64,512]{2,1,0:T(8,128)(2,1)S(1)}, u32[]{:S(2)}, u32[]{:S(2)}) collective-permute-start(bf16[4,64,512]{2,1,0:T(8,128)(2,1)S(1)} %pack.1.refs_1_.refs_0_.rows_ref), channel_id=1, source_target_pairs={{0,1},{1,0},{2,3},{3,2},{4,5},{5,4},{6,7},{7,6},{8,9},{9,8},{10,11... | collective-permute-start | bytes 786440 | tf_op jit(solution)/shard_map/ppermute | solution.py:557
  24.8 6.3 %collective-permute-start.6 = (s16[528,128]{1,0:T(8,128)(2,1)S(1)}, s16[528,128]{1,0:T(8,128)(2,1)S(1)}, u32[]{:S(2)}, u32[]{:S(2)}) collective-permute-start(s16[528,128]{1,0:T(8,128)(2,1)S(1)} %get-tuple-element.38), channel_id=1, source_target_pairs={{0,2},{2,0},{1,3},{3,1},{4,6},{6,4},{5,7},{7,5},{8,10},{10,8},{9,1... | collective-permute-start | bytes 405512 | tf_op jit(solution)/shard_map/ppermute | solution.py:557
  31.3 10.8 %collective-permute-start.14 = (bf16[4,128,256]{2,1,0:T(8,128)(2,1)S(1)}, bf16[4,128,256]{2,1,0:T(8,128)(2,1)S(1)}, u32[]{:S(2)}, u32[]{:S(2)}) collective-permute-start(bf16[4,128,256]{2,1,0:T(8,128)(2,1)S(1)} %get-tuple-element.49), channel_id=1, source_target_pairs={{0,2},{2,0},{1,3},{3,1},{4,6},{6,4},{5,7},{7,5},{8,10},{10,8},{9,1... | collective-permute-start | bytes 786440 | tf_op jit(solution)/shard_map/ppermute | solution.py:557
  32.2 6.4 %collective-permute-start.7 = (s16[144,128]{1,0:T(8,128)(2,1)S(1)}, s16[144,128]{1,0:T(8,128)(2,1)S(1)}, u32[]{:S(2)}, u32[]{:S(2)}) collective-permute-start(s16[144,128]{1,0:T(8,128)(2,1)S(1)} %get-tuple-element.40), channel_id=1, source_target_pairs={{0,4},{4,0},{8,12},{12,8},{1,5},{5,1},{9,13},{13,9},{2,6},{6,2},{1... | collective-permute-start | bytes 110600 | tf_op jit(solution)/shard_map/ppermute | solution.py:557
  32.8 5.9 %collective-permute-start.8 = (s16[144,128]{1,0:T(8,128)(2,1)S(1)}, s16[144,128]{1,0:T(8,128)(2,1)S(1)}, u32[]{:S(2)}, u32[]{:S(2)}) collective-permute-start(s16[144,128]{1,0:T(8,128)(2,1)S(1)} %get-tuple-element.41), channel_id=1, source_target_pairs={{0,8},{4,12},{8,0},{12,4},{1,9},{5,13},{9,1},{13,5},{2,10},{6,14},... | collective-permute-start | bytes 110600 | tf_op jit(solution)/shard_map/ppermute | solution.py:557
  36.3 5.8 %collective-permute-start.9 = (s16[144,128]{1,0:T(8,128)(2,1)S(1)}, s16[144,128]{1,0:T(8,128)(2,1)S(1)}, u32[]{:S(2)}, u32[]{:S(2)}) collective-permute-start(s16[144,128]{1,0:T(8,128)(2,1)S(1)} %get-tuple-element.42), channel_id=1, source_target_pairs={{0,12},{4,8},{8,4},{12,0},{1,13},{5,9},{9,5},{13,1},{2,14},{6,10},... | collective-permute-start | bytes 110600 | tf_op jit(solution)/shard_map/ppermute | solution.py:557
  38.5 5.3 %collective-permute-start.15 = (bf16[4,128,256]{2,1,0:T(8,128)(2,1)S(1)}, bf16[4,128,256]{2,1,0:T(8,128)(2,1)S(1)}, u32[]{:S(2)}, u32[]{:S(2)}) collective-permute-start(bf16[4,128,256]{2,1,0:T(8,128)(2,1)S(1)} %get-tuple-element.48.refs_0_), channel_id=1, source_target_pairs={{0,1},{1,0},{2,3},{3,2},{4,5},{5,4},{6,7},{7,6},{8,9},{9,8},{10,11... | collective-permute-start | bytes 786440 | tf_op jit(solution)/shard_map/ppermute | solution.py:557
  42.2 1.7 %collective-permute-start.16 = (bf16[4,128,256]{2,1,0:T(8,128)(2,1)S(1)}, bf16[4,128,256]{2,1,0:T(8,128)(2,1)S(1)}, u32[]{:S(2)}, u32[]{:S(2)}) collective-permute-start(bf16[4,128,256]{2,1,0:T(8,128)(2,1)S(1)} %gate.3.refs_1_), channel_id=1, source_target_pairs={{0,1},{1,0},{2,3},{3,2},{4,5},{5,4},{6,7},{7,6},{8,9},{9,8},{10,11... | collective-permute-start | bytes 786440 | tf_op jit(solution)/shard_map/ppermute | solution.py:557
  46.5 2.0 %collective-permute-start.17 = (f32[4,64,512]{2,1,0:T(8,128)S(1)}, f32[4,64,512]{2,1,0:T(8,128)S(1)}, u32[]{:S(2)}, u32[]{:S(2)}) collective-permute-start(f32[4,64,512]{2,1,0:T(8,128)S(1)} %outputs.4.refs_0_), channel_id=1, source_target_pairs={{0,1},{1,0},{2,3},{3,2},{4,5},{5,4},{6,7},{7,6},{8,9},{9,8},{10,11... | collective-permute-start | bytes 1572872 | tf_op jit(solution)/shard_map/ppermute | solution.py:557
  47.2 8.0 %collective-permute-start.18 = (f32[4,64,512]{2,1,0:T(8,128)S(1)}, f32[4,64,512]{2,1,0:T(8,128)S(1)}, u32[]{:S(2)}, u32[]{:S(2)}) collective-permute-start(f32[4,64,512]{2,1,0:T(8,128)S(1)} %outputs.5.refs_0_), channel_id=1, source_target_pairs={{0,1},{1,0},{2,3},{3,2},{4,5},{5,4},{6,7},{7,6},{8,9},{9,8},{10,11... | collective-permute-start | bytes 1572872 | tf_op jit(solution)/shard_map/ppermute | solution.py:557
  48.8 7.7 %collective-permute-start.20 = (s16[272,128]{1,0:T(8,128)(2,1)S(1)}, s16[272,128]{1,0:T(8,128)(2,1)S(1)}, u32[]{:S(2)}, u32[]{:S(2)}) collective-permute-start(s16[272,128]{1,0:T(8,128)(2,1)S(1)} %get-tuple-element.53), channel_id=1, source_target_pairs={{0,6},{2,4},{4,2},{6,0},{8,14},{10,12},{12,10},{14,8},{1,7},{3,5},... | collective-permute-start | bytes 208904 | tf_op jit(solution)/shard_map/ppermute | solution.py:564
  48.8 11.0 %collective-permute-start.21 = (s16[272,128]{1,0:T(8,128)(2,1)S(1)}, s16[272,128]{1,0:T(8,128)(2,1)S(1)}, u32[]{:S(2)}, u32[]{:S(2)}) collective-permute-start(s16[272,128]{1,0:T(8,128)(2,1)S(1)} %get-tuple-element.54), channel_id=1, source_target_pairs={{0,10},{2,8},{4,14},{6,12},{8,2},{10,0},{12,6},{14,4},{1,11},{3,9}... | collective-permute-start | bytes 208904 | tf_op jit(solution)/shard_map/ppermute | solution.py:564
  51.1 9.7 %collective-permute-start.22 = (s16[272,128]{1,0:T(8,128)(2,1)S(1)}, s16[272,128]{1,0:T(8,128)(2,1)S(1)}, u32[]{:S(2)}, u32[]{:S(2)}) collective-permute-start(s16[272,128]{1,0:T(8,128)(2,1)S(1)} %get-tuple-element.55), channel_id=1, source_target_pairs={{0,14},{2,12},{4,10},{6,8},{8,6},{10,4},{12,2},{14,0},{1,15},{3,13... | collective-permute-start | bytes 208904 | tf_op jit(solution)/shard_map/ppermute | solution.py:564
  55.4 5.3 %collective-permute-start.23 = (s16[272,128]{1,0:T(8,128)(2,1)S(1)}, s16[272,128]{1,0:T(8,128)(2,1)S(1)}, u32[]{:S(2)}, u32[]{:S(2)}) collective-permute-start(s16[272,128]{1,0:T(8,128)(2,1)S(1)} %get-tuple-element.56), channel_id=1, source_target_pairs={{0,4},{2,6},{4,0},{6,2},{8,12},{10,14},{12,8},{14,10},{1,5},{3,7},... | collective-permute-start | bytes 208904 | tf_op jit(solution)/shard_map/ppermute | solution.py:564
  55.5 8.8 %collective-permute-start.24 = (s16[272,128]{1,0:T(8,128)(2,1)S(1)}, s16[272,128]{1,0:T(8,128)(2,1)S(1)}, u32[]{:S(2)}, u32[]{:S(2)}) collective-permute-start(s16[272,128]{1,0:T(8,128)(2,1)S(1)} %get-tuple-element.57), channel_id=1, source_target_pairs={{0,8},{2,10},{4,12},{6,14},{8,0},{10,2},{12,4},{14,6},{1,9},{3,11}... | collective-permute-start | bytes 208904 | tf_op jit(solution)/shard_map/ppermute | solution.py:564
  56.4 7.9 %collective-permute-start.25 = (s16[272,128]{1,0:T(8,128)(2,1)S(1)}, s16[272,128]{1,0:T(8,128)(2,1)S(1)}, u32[]{:S(2)}, u32[]{:S(2)}) collective-permute-start(s16[272,128]{1,0:T(8,128)(2,1)S(1)} %get-tuple-element.58), channel_id=1, source_target_pairs={{0,12},{2,14},{4,8},{6,10},{8,4},{10,6},{12,0},{14,2},{1,13},{3,15... | collective-permute-start | bytes 208904 | tf_op jit(solution)/shard_map/ppermute | solution.py:564
  59.9 4.4 %collective-permute-start.19 = (s16[272,128]{1,0:T(8,128)(2,1)S(1)}, s16[272,128]{1,0:T(8,128)(2,1)S(1)}, u32[]{:S(2)}, u32[]{:S(2)}) collective-permute-start(s16[272,128]{1,0:T(8,128)(2,1)S(1)} %get-tuple-element.51.refs_0_), channel_id=1, source_target_pairs={{0,2},{2,0},{4,6},{6,4},{8,10},{10,8},{12,14},{14,12},{1,3},{3,1},... | collective-permute-start | bytes 208904 | tf_op jit(solution)/shard_map/ppermute | solution.py:564
  (10 other events, 52.4 us)

commit v13 on v9

--- a/solution.py
+++ b/solution.py
@@ -19,7 +19,7 @@
 PAIR = 2 * HEAD_SIZE
 LANES = 128
 TAIL = 16
-HALVES = ((0, 3), (1, 2))
+HALVES = ((2, 3), (0, 1))
 DEVICES = ("req", "sub", "section")
 
 theta_base = 500000.0
@@ -76,7 +76,7 @@
         + [jax.ShapeDtypeStruct(other.shape, other.dtype) for other in more],
         scratch_shapes=[pltpu.SemaphoreType.DMA((count + len(more),))],
         compiler_params=params(),
-        cost_estimate=cost([array] * 2),
+        cost_estimate=cost([array], [array]),
         name="staged",
     )(place, array, *more, *after)
 
@@ -115,12 +115,18 @@
     )(*arrays, *after)
 
 
-def pages_kernel(table, place, scales, page_ref, rows_ref, rows_out_ref, *out_refs):
+def page_of(length, targets, e, place, facts):
+    index = place[0] * length + e * targets + place[1]
+    return facts[index].astype(jnp.int32) - place[2]
+
+
+def pages_kernel(length, place, facts, page_ref, rows_ref, rows_out_ref, *out_refs):
     e = pl.program_id(0)
     rows_out_ref[...] = rows_ref[...]
     subs = out_refs[0].shape[0]
     targets = 2 * subs
-    page = table[place[0], e * targets + place[1]] - place[2]
+    page = page_of(length, targets, e, place, facts)
+    scales = GROUP_REQUESTS * length + page * (2 * KEY_VALUE_HEADS)
     for z, out_ref in enumerate(out_refs):
         for j in range(subs):
             half = (place[1] // 2 ^ j) // (subs // 2)
@@ -130,27 +136,27 @@
                 columns = pl.ds(pl.multiple_of(c * HEAD_SIZE, HEAD_SIZE), HEAD_SIZE)
                 block = page_ref[0, :, columns].astype(jnp.float32)
                 out_ref[j, :, part * HEAD_SIZE : (part + 1) * HEAD_SIZE] = (
-                    block * scales[page, c]
+                    block * facts[scales + c]
                 ).astype(jnp.bfloat16)
 
 
 def used_pages(pages, scales, table, place, subs, rows):
     targets = 2 * subs
-    entries = table.shape[1] // targets
+    length = table.shape[1]
+    entries = length // targets
+    facts = jnp.concatenate(
+        [table.astype(jnp.float32).reshape(-1), scales.astype(jnp.float32).reshape(-1)]
+    )
     shape = jax.ShapeDtypeStruct((subs, entries * PAGE_TOKENS, PAIR), jnp.bfloat16)
     return pl.pallas_call(
-        pages_kernel,
+        functools.partial(pages_kernel, length),
         grid_spec=pltpu.PrefetchScalarGridSpec(
-            num_scalar_prefetch=3,
+            num_scalar_prefetch=2,
             grid=(entries,),
             in_specs=[
                 pl.BlockSpec(
                     (1, PAGE_TOKENS, pages.shape[2]),
-                    lambda e, table, place, scales: (
-                        table[place[0], e * targets + place[1]] - place[2],
-                        0,
-                        0,
-                    ),
+                    lambda e, place, facts: (page_of(length, targets, e, place, facts), 0, 0),
                 ),
                 pl.BlockSpec(rows.shape, lambda e, *_: (0, 0)),
             ],
@@ -164,7 +170,7 @@
             flops=0, bytes_accessed=4 * entries * PAGE_TOKENS * pages.shape[2], transcendentals=0
         ),
         name="used_pages",
-    )(table, place, scales.astype(jnp.float32), pages, rows)
+    )(place, facts, pages, rows)
 
 
 def regroup_kernel(*refs):
@@ -262,7 +268,7 @@
         out_specs=[pl.BlockSpec(memory_space=pltpu.VMEM)] * len(shapes),
         out_shape=shapes,
         compiler_params=params(),
-        cost_estimate=cost(gathered * 1, [weight], flops=2 * count * weight.size),
+        cost_estimate=cost(gathered, [weight], flops=2 * count * weight.size),
         name="scale_and_pairs",
     )(place, gain, weight, *gathered)
 
@@ -348,12 +354,21 @@
         new_key = jnp.concatenate([key_ref[rows] for rows in fresh], axis=0)
         new_value = jnp.concatenate([value_ref[rows] for rows in fresh], axis=0)
         new_key, new_value = new_key.astype(jnp.bfloat16), new_value.astype(jnp.bfloat16)
-        keys = jnp.concatenate([ref[z, :, :HEAD_SIZE] for ref in caches], axis=0)
-        values = jnp.concatenate([ref[z, :, HEAD_SIZE:] for ref in caches], axis=0)
+        keys = [ref[z, :, :HEAD_SIZE] for ref in caches]
+        values = [ref[z, :, HEAD_SIZE:] for ref in caches]
+        if span % LANES:
+            keys = [jnp.concatenate(keys, axis=0)]
+            values = [jnp.concatenate(values, axis=0)]
         query = jnp.concatenate(
             [q_ref[r, :, h * HEAD_SIZE : (h + 1) * HEAD_SIZE] for h in range(quarter)], axis=0
         )
-        scores = lax.dot_general(query, keys, contract, preferred_element_type=jnp.float32)
+        scores = jnp.concatenate(
+            [
+                lax.dot_general(query, part, contract, preferred_element_type=jnp.float32)
+                for part in keys
+            ],
+            axis=1,
+        )
         scores = jnp.where(position < lengths[r], scores * factor, -jnp.inf)
         own = lax.dot_general(query, new_key, contract, preferred_element_type=jnp.float32)
         own = jnp.where(own_visible, own * factor, -jnp.inf)
@@ -363,11 +378,15 @@
         scores = jnp.exp(scores - highest)
         own = jnp.exp(own - highest)
         total = jnp.sum(scores, axis=-1, keepdims=True) + jnp.sum(own, axis=-1, keepdims=True)
-        mixed = jnp.dot(
-            (scores / total).astype(jnp.bfloat16), values, preferred_element_type=jnp.float32
-        ) + jnp.dot(
-            (own / total).astype(jnp.bfloat16), new_value, preferred_element_type=jnp.float32
-        )
+        share = 1.0 / total
+        scores = (scores * share).astype(jnp.bfloat16)
+        own = (own * share).astype(jnp.bfloat16)
+        mixed = jnp.dot(own, new_value, preferred_element_type=jnp.float32)
+        first = 0
+        for part in values:
+            weights = scores[:, first : first + part.shape[0]]
+            mixed += jnp.dot(weights, part, preferred_element_type=jnp.float32)
+            first += part.shape[0]
         mixed = mixed.astype(jnp.bfloat16)
         for h in range(quarter):
             out_ref[r, :, h * HEAD_SIZE : (h + 1) * HEAD_SIZE] = mixed[
@@ -638,10 +657,13 @@
     kept = outputs(mixed, w_output, mid, end - mid, after=[second])
     parts = fold_core(kept, got_first)
     kept = outputs(mixed, w_output, 0, mid, after=parts[:1])
-    parts = [passed(part, "sub", i // 2 + 1) for i, part in enumerate(parts)]
     last = {}
     for half, order in enumerate(HALVES):
-        last.update(zip(order, fold_sub(order, [kept, got_second], parts[half::2])))
+        sent = parts[half::2]
+        if half:
+            sent = gate(sent, after=[got[0], kept])
+        got = [passed(part, "sub", s + 1) for s, part in enumerate(sent)]
+        last.update(zip(order, fold_sub(order, [kept, got_second], got)))
     parts = [passed(last[s], "req", s) for s in range(1, GROUP_REQUESTS)]
     return finish(gathered[0], last[0], parts).reshape(hidden.shape)
 

time: 64.8 us -> 65.1 us (level)
  waiting for transfers between devices: 15.4 us -> 18.6 us
  starting transfers between devices: 26.1 us -> 23.1 us
    ppermute x24, waiting for transfers between devices: 15.4 us -> 18.6 us  [passed(): lax.ppermute(array, axis, [(i, i ^ shift) for i in range(lax.axis_size(ax...]
    ppermute x24, starting transfers between devices: 26.1 us -> 23.1 us  [passed(): lax.ppermute(array, axis, [(i, i ^ shift) for i in range(lax.axis_size(ax...]
    reshape x0 -> x2, local copies, waits for them, and re-layouts: none -> 0.85 us  [the longest x1 0.77 us: used_pages(): scales.astype(jnp.float32).reshape(-1)]
    unnamed x16 -> x14, local copies, waits for them, and re-layouts: 5.11 us -> 4.43 us
  transfers between devices with their start and end apart: 24 -> 24, of which waited for: 10 -> 10; matrix products, arithmetic and copies ran while one was open for 3% -> 4% of each run, Pallas kernels for 19% -> 19%
where the time goes in v13:
time: 65.1 us; the launch traced here: 64.7 us
  starting transfers between devices  23.1 us (35%)
  waiting for transfers between devices  18.6 us (29%)
  Pallas kernels  15.7 us (24%)
  local copies, waits for them, and re-layouts  5.3 us (8%)
  other arithmetic  1.72 us (3%)
    ppermute x24, starting transfers between devices, passed(): lax.ppermute(array, axis, [(i, i ^ shift) for i in range(lax.axis_size(ax...  23.1 us
    ppermute x24, waiting for transfers between devices, passed(): lax.ppermute(array, axis, [(i, i ^ shift) for i in range(lax.axis_size(ax...  18.6 us
    pallas_call x1, Pallas kernels, queries(): pl.pallas_call(query_kernel, in_specs=[pl.BlockSpec(memory_space=pltpu.SM...  4.63 us
    unnamed x14, local copies, waits for them, and re-layouts  4.43 us
    pallas_call x2, Pallas kernels, staged(): pl.pallas_call(functools.partial(stage_kernel, order, len(more)), in_spec...  2.85 us
    pallas_call x1, Pallas kernels, attend(): pl.pallas_call(attend_kernel, in_specs=[pl.BlockSpec(memory_space=pltpu.S...  2.34 us
    pallas_call x4, Pallas kernels, outputs(): pl.pallas_call(functools.partial(output_kernel, first), in_specs=[pl.Bloc...  1.91 us
    pallas_call x1, Pallas kernels, scale_and_pairs(): pl.pallas_call(pairs_kernel, in_specs=[pl.BlockSpec(memory_space=pltpu.SM...  1.37 us
  transfers between devices with their start and end apart: 24, of which 10 were waited for; matrix products, arithmetic and copies ran while one was open for 4% of the time, Pallas kernels for 19%

profile of v13, /device:TPU:0, one launch (start us, length us, event | category | flops | bytes accessed | tf_op | source)
XLA Modules:
  0.0 64.7 jit_solution(1698826316434540040)
XLA Ops:
  0.0 5.0 %collective-permute-start.2 = (bf16[64,512]{1,0:T(8,128)(2,1)}, bf16[64,512]{1,0:T(8,128)(2,1)S(1)}, u32[]{:S(2)}, u32[]{:S(2)}) collective-permute-start(bf16[64,512]{1,0:T(8,128)(2,1)} %bitcast.16), channel_id=1, source_target_pairs={{0,12},{4,8},{8,4},{12,0},{1,13},{5,9},{9,5},{13,1},{2,14},{6,10},... | collective-permute-start | bytes 196616 | tf_op jit(solution)/shard_map/ppermute | solution.py:576
  7.2 1.2 %copy-done.1 = bf16[16,16,2048]{2,1,0:T(8,128)(2,1)S(1)} copy-done((bf16[16,16,2048]{2,1,0:T(8,128)(2,1)S(1)}, bf16[16,16,2048]{2,1,0:T(8,128)(2,1)}, u32[]{:S(2)}) %copy-start.1) | copy-done | bytes 1048600
  9.3 1.2 %used_pages.1 = (bf16[64,512]{1,0:T(8,128)(2,1)S(1)}, bf16[2,128,256]{2,1,0:T(8,128)(2,1)S(1)}, bf16[2,128,256]{2,1,0:T(8,128)(2,1)S(1)}, bf16[2,128,256]{2,1,0:T(8,128)(2,1)S(1)}, bf16[2,128,256]{2,1,0:T(8,128)(2,1)S(1)}) custom-call(s32[3]{0:T(128)S(1)} %pad_add_fusion.place, f32[384]{0:T(512)S(1)} %pad_maximum_fusion.2.facts, ...), custom_call_target="tpu_custom_call" | custom-call | bytes 1048576 | tf_op jit(solution)/shard_map/used_pages/pallas_call | solution.py:151
  10.5 1.5 %collective-permute-start.11 = (bf16[2,128,256]{2,1,0:T(8,128)(2,1)S(1)}, bf16[2,128,256]{2,1,0:T(8,128)(2,1)S(1)}, u32[]{:S(2)}, u32[]{:S(2)}) collective-permute-start(bf16[2,128,256]{2,1,0:T(8,128)(2,1)S(1)} %get-tuple-element.43), channel_id=1, source_target_pairs={{0,4},{4,0},{8,12},{12,8},{1,5},{5,1},{9,13},{13,9},{2,6},{6,2},{1... | collective-permute-start | bytes 393224 | tf_op jit(solution)/shard_map/ppermute | solution.py:576
  12.1 2.9 %collective-permute-start.12 = (bf16[2,128,256]{2,1,0:T(8,128)(2,1)S(1)}, bf16[2,128,256]{2,1,0:T(8,128)(2,1)S(1)}, u32[]{:S(2)}, u32[]{:S(2)}) collective-permute-start(bf16[2,128,256]{2,1,0:T(8,128)(2,1)S(1)} %get-tuple-element.44), channel_id=1, source_target_pairs={{0,8},{4,12},{8,0},{12,4},{1,9},{5,13},{9,1},{13,5},{2,10},{6,14},... | collective-permute-start | bytes 393224 | tf_op jit(solution)/shard_map/ppermute | solution.py:576
  15.0 1.8 %collective-permute-start.3 = (bf16[4,64,512]{2,1,0:T(8,128)(2,1)S(1)}, bf16[4,64,512]{2,1,0:T(8,128)(2,1)S(1)}, u32[]{:S(2)}, u32[]{:S(2)}) collective-permute-start(bf16[4,64,512]{2,1,0:T(8,128)(2,1)S(1)} %pack.1.refs_1_.refs_0_.rows_ref), channel_id=1, source_target_pairs={{0,2},{2,0},{1,3},{3,1},{4,6},{6,4},{5,7},{7,5},{8,10},{10,8},{9,1... | collective-permute-start | bytes 786440 | tf_op jit(solution)/shard_map/ppermute | solution.py:576
  17.6 1.6 %copy-done = bf16[512,2048]{1,0:T(8,128)(2,1)S(1)} copy-done((bf16[512,2048]{1,0:T(8,128)(2,1)S(1)}, bf16[512,2048]{1,0:T(8,128)(2,1)}, u32[]{:S(2)}) %copy-start) | copy-done | bytes 2097176
  19.9 1.0 %staged.2 = (bf16[8,512,256]{2,1,0:T(8,128)(2,1)S(1)}, f32[8,128]{1,0:T(8,128)S(1)}, f32[16,1,512]{2,1,0:T(1,128)S(1)}) custom-call(s32[3]{0:T(128)S(1)} %pad_add_fusion.1.place, bf16[512,2048]{1,0:T(8,128)(2,1)S(1)} %copy-done, f32[16,1,512]{2,1,0:T(1,128)S(1)} %bitcast.20, bf16[4,64,512]{2,1,0:T(8,128)(2,1)S(1)} %pack.1.refs_1_.refs_0_.rows_ref), custom_call_target="tpu_custom_call" | custom-call | bytes 4194304 | tf_op jit(solution)/shard_map/staged/pallas_call | solution.py:66
  21.9 1.4 %collective-permute-done.5.refs_3_ = bf16[4,64,512]{2,1,0:T(8,128)(2,1)S(1)} collective-permute-done((bf16[4,64,512]{2,1,0:T(8,128)(2,1)S(1)}, bf16[4,64,512]{2,1,0:T(8,128)(2,1)S(1)}, u32[]{:S(2)}, u32[]{:S(2)}) %collective-permute-start.5) | collective-permute-done | bytes 262176 | tf_op jit(solution)/shard_map/ppermute | solution.py:576
  23.3 1.4 %scale_and_pairs.1 = (f32[64,128]{1,0:T(8,128)S(1)}, f32[4,64,256]{2,1,0:T(8,128)S(1)}, s16[528,128]{1,0:T(8,128)(2,1)S(1)}) custom-call(s32[3]{0:T(128)S(1)} %pad_add_fusion.1.place, f32[16,1,512]{2,1,0:T(1,128)S(1)} %get-tuple-element.31.gain_ref, bf16[8,512,256]{2,1,0:T(8,128)(2,1)S(1)} %get-tuple-element.32.weight_ref, ...), custom_call_target="tpu_custom_call" | custom-call | flops 134217728 | bytes 3145728 | tf_op jit(solution)/shard_map/scale_and_pairs/pallas_call | solution.py:264
  24.7 1.6 %collective-permute-start.6 = (s16[528,128]{1,0:T(8,128)(2,1)S(1)}, s16[528,128]{1,0:T(8,128)(2,1)S(1)}, u32[]{:S(2)}, u32[]{:S(2)}) collective-permute-start(s16[528,128]{1,0:T(8,128)(2,1)S(1)} %get-tuple-element.36), channel_id=1, source_target_pairs={{0,2},{2,0},{1,3},{3,1},{4,6},{6,4},{5,7},{7,5},{8,10},{10,8},{9,1... | collective-permute-start | bytes 405512 | tf_op jit(solution)/shard_map/ppermute | solution.py:576
  26.4 4.6 %queries.1.refs_2_.refs_0_.q_ref = bf16[4,16,512]{2,1,0:T(8,128)(2,1)S(1)} custom-call(s32[3]{0:T(128)S(1)} %pad_add_fusion.1.place, f32[64,128]{1,0:T(8,128)S(1)} %get-tuple-element.34.scale_ref, f32[16,1,512]{2,1,0:T(1,128)S(1)} %get-tuple-element.31.gain_ref, bf16[8192,512]{1,0:T(8,128)(2,1)} %weight_ref.1, f32[64,128]{1,0:T(8,128)S(1)} %bitcast.12, ...), custom_call_target="tpu_custom_call" | custom-call | flops 536870912 | bytes 8388608 | tf_op jit(solution)/shard_map/queries/pallas_call | solution.py:308
  31.2 0.9 %collective-permute-start.14 = (bf16[4,128,256]{2,1,0:T(8,128)(2,1)S(1)}, bf16[4,128,256]{2,1,0:T(8,128)(2,1)S(1)}, u32[]{:S(2)}, u32[]{:S(2)}) collective-permute-start(bf16[4,128,256]{2,1,0:T(8,128)(2,1)S(1)} %get-tuple-element.47), channel_id=1, source_target_pairs={{0,2},{2,0},{1,3},{3,1},{4,6},{6,4},{5,7},{7,5},{8,10},{10,8},{9,1... | collective-permute-start | bytes 786440 | tf_op jit(solution)/shard_map/ppermute | solution.py:576
  32.7 3.5 %collective-permute-start.8 = (s16[144,128]{1,0:T(8,128)(2,1)S(1)}, s16[144,128]{1,0:T(8,128)(2,1)S(1)}, u32[]{:S(2)}, u32[]{:S(2)}) collective-permute-start(s16[144,128]{1,0:T(8,128)(2,1)S(1)} %get-tuple-element.39), channel_id=1, source_target_pairs={{0,8},{4,12},{8,0},{12,4},{1,9},{5,13},{9,1},{13,5},{2,10},{6,14},... | collective-permute-start | bytes 110600 | tf_op jit(solution)/shard_map/ppermute | solution.py:576
  36.5 1.9 %staged.3 = (bf16[16,512,512]{2,1,0:T(8,128)(2,1)S(1)}, f32[8,128]{1,0:T(8,128)S(1)}) custom-call(s32[3]{0:T(128)S(1)} %pad_add_fusion.1.place, bf16[512,8192]{1,0:T(8,128)(2,1)S(1)} %bitcast.11, bf16[4,16,512]{2,1,0:T(8,128)(2,1)S(1)} %queries.1.refs_2_.refs_0_.q_ref), custom_call_target="tpu_custom_call" | custom-call | bytes 16777216 | tf_op jit(solution)/shard_map/staged/pallas_call | solution.py:66
  38.6 3.4 %collective-permute-done.9.refs_2_ = s16[144,128]{1,0:T(8,128)(2,1)S(1)} collective-permute-done((s16[144,128]{1,0:T(8,128)(2,1)S(1)}, s16[144,128]{1,0:T(8,128)(2,1)S(1)}, u32[]{:S(2)}, u32[]{:S(2)}) %collective-permute-start.9) | collective-permute-done | bytes 36896 | tf_op jit(solution)/shard_map/ppermute | solution.py:576
  42.6 1.1 %collective-permute-done.10.other_ref = f32[64,256]{1,0:T(8,128)S(1)} collective-permute-done((f32[64,256]{1,0:T(8,128)S(1)}, f32[64,256]{1,0:T(8,128)S(1)}, u32[]{:S(2)}, u32[]{:S(2)}) %collective-permute-start.10) | collective-permute-done | bytes 65568 | tf_op jit(solution)/shard_map/ppermute | solution.py:576
  43.7 2.3 %attend.1.x_ref = bf16[4,16,512]{2,1,0:T(8,128)(2,1)S(1)} custom-call(s32[3]{0:T(128)S(1)} %pad_add_fusion.1.place, s32[4]{0:T(128)S(1)} %copy-done.4, bf16[4,16,512]{2,1,0:T(8,128)(2,1)S(1)} %queries.1.refs_2_.refs_0_.q_ref, f32[64,256]{1,0:T(8,128)S(1)} %fold_pairs.1.refs_1_.mine_ref, f32[64,256]{1,0:T(8,128)S(1)} %collective-permute-done.10.other_ref, ...), custom_call_target="tpu_custom_call" | custom-call | flops 268435456 | bytes 3145728 | tf_op jit(solution)/shard_map/attend/pallas_call | solution.py:398
  48.8 1.2 %collective-permute-start.19 = (s16[528,128]{1,0:T(8,128)(2,1)S(1)}, s16[528,128]{1,0:T(8,128)(2,1)S(1)}, u32[]{:S(2)}, u32[]{:S(2)}) collective-permute-start(s16[528,128]{1,0:T(8,128)(2,1)S(1)} %get-tuple-element.49.refs_0_), channel_id=1, source_target_pairs={{0,2},{2,0},{1,3},{3,1},{4,6},{6,4},{5,7},{7,5},{8,10},{10,8},{9,1... | collective-permute-start | bytes 405512 | tf_op jit(solution)/shard_map/ppermute | solution.py:576
  50.5 4.0 %collective-permute-done.19.refs_1_.refs_2_ = s16[528,128]{1,0:T(8,128)(2,1)S(1)} collective-permute-done((s16[528,128]{1,0:T(8,128)(2,1)S(1)}, s16[528,128]{1,0:T(8,128)(2,1)S(1)}, u32[]{:S(2)}, u32[]{:S(2)}) %collective-permute-start.19) | collective-permute-done | bytes 135200 | tf_op jit(solution)/shard_map/ppermute | solution.py:576
  54.5 1.2 %collective-permute-start.20 = (s16[528,128]{1,0:T(8,128)(2,1)S(1)}, s16[528,128]{1,0:T(8,128)(2,1)S(1)}, u32[]{:S(2)}, u32[]{:S(2)}) collective-permute-start(s16[528,128]{1,0:T(8,128)(2,1)S(1)} %gate.5), channel_id=1, source_target_pairs={{0,2},{2,0},{1,3},{3,1},{4,6},{6,4},{5,7},{7,5},{8,10},{10,8},{9,1... | collective-permute-start | bytes 405512 | tf_op jit(solution)/shard_map/ppermute | solution.py:576
  56.4 3.1 %collective-permute-done.20.refs_2_ = s16[528,128]{1,0:T(8,128)(2,1)S(1)} collective-permute-done((s16[528,128]{1,0:T(8,128)(2,1)S(1)}, s16[528,128]{1,0:T(8,128)(2,1)S(1)}, u32[]{:S(2)}, u32[]{:S(2)}) %collective-permute-start.20) | collective-permute-done | bytes 135200 | tf_op jit(solution)/shard_map/ppermute | solution.py:576
  59.7 2.8 %collective-permute-done.22.refs_1_ = s16[272,128]{1,0:T(8,128)(2,1)S(1)} collective-permute-done((s16[272,128]{1,0:T(8,128)(2,1)S(1)}, s16[272,128]{1,0:T(8,128)(2,1)S(1)}, u32[]{:S(2)}, u32[]{:S(2)}) %collective-permute-start.22) | collective-permute-done | bytes 69664 | tf_op jit(solution)/shard_map/ppermute | solution.py:576
  62.5 1.5 %collective-permute-done.21.refs_0_ = s16[272,128]{1,0:T(8,128)(2,1)S(1)} collective-permute-done((s16[272,128]{1,0:T(8,128)(2,1)S(1)}, s16[272,128]{1,0:T(8,128)(2,1)S(1)}, u32[]{:S(2)}, u32[]{:S(2)}) %collective-permute-start.21) | collective-permute-done | bytes 69664 | tf_op jit(solution)/shard_map/ppermute | solution.py:576
  (72 shorter events, 12.2 us)
Async XLA Ops:
  0.0 15.0 %collective-permute-start.2 = (bf16[64,512]{1,0:T(8,128)(2,1)}, bf16[64,512]{1,0:T(8,128)(2,1)S(1)}, u32[]{:S(2)}, u32[]{:S(2)}) collective-permute-start(bf16[64,512]{1,0:T(8,128)(2,1)} %bitcast.16), channel_id=1, source_target_pairs={{0,12},{4,8},{8,4},{12,0},{1,13},{5,9},{9,5},{13,1},{2,14},{6,10},... | collective-permute-start | bytes 196616 | tf_op jit(solution)/shard_map/ppermute | solution.py:576
  5.0 9.9 %collective-permute-start.1 = (bf16[64,512]{1,0:T(8,128)(2,1)}, bf16[64,512]{1,0:T(8,128)(2,1)S(1)}, u32[]{:S(2)}, u32[]{:S(2)}) collective-permute-start(bf16[64,512]{1,0:T(8,128)(2,1)} %bitcast.17), channel_id=1, source_target_pairs={{0,8},{4,12},{8,0},{12,4},{1,9},{5,13},{9,1},{13,5},{2,10},{6,14},... | collective-permute-start | bytes 196616 | tf_op jit(solution)/shard_map/ppermute | solution.py:576
  5.1 9.9 %collective-permute-start = (bf16[64,512]{1,0:T(8,128)(2,1)}, bf16[64,512]{1,0:T(8,128)(2,1)S(1)}, u32[]{:S(2)}, u32[]{:S(2)}) collective-permute-start(bf16[64,512]{1,0:T(8,128)(2,1)} %bitcast.18), channel_id=1, source_target_pairs={{0,4},{4,0},{8,12},{12,8},{1,5},{5,1},{9,13},{13,9},{2,6},{6,2},{1... | collective-permute-start | bytes 196616 | tf_op jit(solution)/shard_map/ppermute | solution.py:576
  10.5 20.6 %collective-permute-start.11 = (bf16[2,128,256]{2,1,0:T(8,128)(2,1)S(1)}, bf16[2,128,256]{2,1,0:T(8,128)(2,1)S(1)}, u32[]{:S(2)}, u32[]{:S(2)}) collective-permute-start(bf16[2,128,256]{2,1,0:T(8,128)(2,1)S(1)} %get-tuple-element.43), channel_id=1, source_target_pairs={{0,4},{4,0},{8,12},{12,8},{1,5},{5,1},{9,13},{13,9},{2,6},{6,2},{1... | collective-permute-start | bytes 393224 | tf_op jit(solution)/shard_map/ppermute | solution.py:576
  12.1 19.1 %collective-permute-start.12 = (bf16[2,128,256]{2,1,0:T(8,128)(2,1)S(1)}, bf16[2,128,256]{2,1,0:T(8,128)(2,1)S(1)}, u32[]{:S(2)}, u32[]{:S(2)}) collective-permute-start(bf16[2,128,256]{2,1,0:T(8,128)(2,1)S(1)} %get-tuple-element.44), channel_id=1, source_target_pairs={{0,8},{4,12},{8,0},{12,4},{1,9},{5,13},{9,1},{13,5},{2,10},{6,14},... | collective-permute-start | bytes 393224 | tf_op jit(solution)/shard_map/ppermute | solution.py:576
  15.0 16.2 %collective-permute-start.13 = (bf16[2,128,256]{2,1,0:T(8,128)(2,1)S(1)}, bf16[2,128,256]{2,1,0:T(8,128)(2,1)S(1)}, u32[]{:S(2)}, u32[]{:S(2)}) collective-permute-start(bf16[2,128,256]{2,1,0:T(8,128)(2,1)S(1)} %get-tuple-element.45), channel_id=1, source_target_pairs={{0,12},{4,8},{8,4},{12,0},{1,13},{5,9},{9,5},{13,1},{2,14},{6,10},... | collective-permute-start | bytes 393224 | tf_op jit(solution)/shard_map/ppermute | solution.py:576
  15.0 6.7 %collective-permute-start.3 = (bf16[4,64,512]{2,1,0:T(8,128)(2,1)S(1)}, bf16[4,64,512]{2,1,0:T(8,128)(2,1)S(1)}, u32[]{:S(2)}, u32[]{:S(2)}) collective-permute-start(bf16[4,64,512]{2,1,0:T(8,128)(2,1)S(1)} %pack.1.refs_1_.refs_0_.rows_ref), channel_id=1, source_target_pairs={{0,2},{2,0},{1,3},{3,1},{4,6},{6,4},{5,7},{7,5},{8,10},{10,8},{9,1... | collective-permute-start | bytes 786440 | tf_op jit(solution)/shard_map/ppermute | solution.py:576
  17.6 4.3 %collective-permute-start.4 = (bf16[4,64,512]{2,1,0:T(8,128)(2,1)S(1)}, bf16[4,64,512]{2,1,0:T(8,128)(2,1)S(1)}, u32[]{:S(2)}, u32[]{:S(2)}) collective-permute-start(bf16[4,64,512]{2,1,0:T(8,128)(2,1)S(1)} %pack.1.refs_1_.refs_0_.rows_ref), channel_id=1, source_target_pairs={{0,1},{1,0},{2,3},{3,2},{4,5},{5,4},{6,7},{7,6},{8,9},{9,8},{10,11... | collective-permute-start | bytes 786440 | tf_op jit(solution)/shard_map/ppermute | solution.py:576
  21.7 1.5 %collective-permute-start.5 = (bf16[4,64,512]{2,1,0:T(8,128)(2,1)S(1)}, bf16[4,64,512]{2,1,0:T(8,128)(2,1)S(1)}, u32[]{:S(2)}, u32[]{:S(2)}) collective-permute-start(bf16[4,64,512]{2,1,0:T(8,128)(2,1)S(1)} %gate.3.refs_1_), channel_id=1, source_target_pairs={{0,1},{1,0},{2,3},{3,2},{4,5},{5,4},{6,7},{7,6},{8,9},{9,8},{10,11... | collective-permute-start | bytes 786440 | tf_op jit(solution)/shard_map/ppermute | solution.py:576
  24.7 6.3 %collective-permute-start.6 = (s16[528,128]{1,0:T(8,128)(2,1)S(1)}, s16[528,128]{1,0:T(8,128)(2,1)S(1)}, u32[]{:S(2)}, u32[]{:S(2)}) collective-permute-start(s16[528,128]{1,0:T(8,128)(2,1)S(1)} %get-tuple-element.36), channel_id=1, source_target_pairs={{0,2},{2,0},{1,3},{3,1},{4,6},{6,4},{5,7},{7,5},{8,10},{10,8},{9,1... | collective-permute-start | bytes 405512 | tf_op jit(solution)/shard_map/ppermute | solution.py:576
  31.2 10.8 %collective-permute-start.14 = (bf16[4,128,256]{2,1,0:T(8,128)(2,1)S(1)}, bf16[4,128,256]{2,1,0:T(8,128)(2,1)S(1)}, u32[]{:S(2)}, u32[]{:S(2)}) collective-permute-start(bf16[4,128,256]{2,1,0:T(8,128)(2,1)S(1)} %get-tuple-element.47), channel_id=1, source_target_pairs={{0,2},{2,0},{1,3},{3,1},{4,6},{6,4},{5,7},{7,5},{8,10},{10,8},{9,1... | collective-permute-start | bytes 786440 | tf_op jit(solution)/shard_map/ppermute | solution.py:576
  32.1 6.4 %collective-permute-start.7 = (s16[144,128]{1,0:T(8,128)(2,1)S(1)}, s16[144,128]{1,0:T(8,128)(2,1)S(1)}, u32[]{:S(2)}, u32[]{:S(2)}) collective-permute-start(s16[144,128]{1,0:T(8,128)(2,1)S(1)} %get-tuple-element.38), channel_id=1, source_target_pairs={{0,4},{4,0},{8,12},{12,8},{1,5},{5,1},{9,13},{13,9},{2,6},{6,2},{1... | collective-permute-start | bytes 110600 | tf_op jit(solution)/shard_map/ppermute | solution.py:576
  32.7 5.9 %collective-permute-start.8 = (s16[144,128]{1,0:T(8,128)(2,1)S(1)}, s16[144,128]{1,0:T(8,128)(2,1)S(1)}, u32[]{:S(2)}, u32[]{:S(2)}) collective-permute-start(s16[144,128]{1,0:T(8,128)(2,1)S(1)} %get-tuple-element.39), channel_id=1, source_target_pairs={{0,8},{4,12},{8,0},{12,4},{1,9},{5,13},{9,1},{13,5},{2,10},{6,14},... | collective-permute-start | bytes 110600 | tf_op jit(solution)/shard_map/ppermute | solution.py:576
  36.2 5.8 %collective-permute-start.9 = (s16[144,128]{1,0:T(8,128)(2,1)S(1)}, s16[144,128]{1,0:T(8,128)(2,1)S(1)}, u32[]{:S(2)}, u32[]{:S(2)}) collective-permute-start(s16[144,128]{1,0:T(8,128)(2,1)S(1)} %get-tuple-element.40), channel_id=1, source_target_pairs={{0,12},{4,8},{8,4},{12,0},{1,13},{5,9},{9,5},{13,1},{2,14},{6,10},... | collective-permute-start | bytes 110600 | tf_op jit(solution)/shard_map/ppermute | solution.py:576
  38.4 5.3 %collective-permute-start.15 = (bf16[4,128,256]{2,1,0:T(8,128)(2,1)S(1)}, bf16[4,128,256]{2,1,0:T(8,128)(2,1)S(1)}, u32[]{:S(2)}, u32[]{:S(2)}) collective-permute-start(bf16[4,128,256]{2,1,0:T(8,128)(2,1)S(1)} %get-tuple-element.46.refs_0_), channel_id=1, source_target_pairs={{0,1},{1,0},{2,3},{3,2},{4,5},{5,4},{6,7},{7,6},{8,9},{9,8},{10,11... | collective-permute-start | bytes 786440 | tf_op jit(solution)/shard_map/ppermute | solution.py:576
  42.0 1.7 %collective-permute-start.16 = (bf16[4,128,256]{2,1,0:T(8,128)(2,1)S(1)}, bf16[4,128,256]{2,1,0:T(8,128)(2,1)S(1)}, u32[]{:S(2)}, u32[]{:S(2)}) collective-permute-start(bf16[4,128,256]{2,1,0:T(8,128)(2,1)S(1)} %gate.4.refs_1_), channel_id=1, source_target_pairs={{0,1},{1,0},{2,3},{3,2},{4,5},{5,4},{6,7},{7,6},{8,9},{9,8},{10,11... | collective-permute-start | bytes 786440 | tf_op jit(solution)/shard_map/ppermute | solution.py:576
  42.1 1.6 %collective-permute-start.10 = (f32[64,256]{1,0:T(8,128)S(1)}, f32[64,256]{1,0:T(8,128)S(1)}, u32[]{:S(2)}, u32[]{:S(2)}) collective-permute-start(f32[64,256]{1,0:T(8,128)S(1)} %fold_pairs.1.refs_1_.mine_ref), channel_id=1, source_target_pairs={{0,1},{1,0},{2,3},{3,2},{4,5},{5,4},{6,7},{7,6},{8,9},{9,8},{10,11... | collective-permute-start | bytes 196616 | tf_op jit(solution)/shard_map/ppermute | solution.py:576
  46.6 2.0 %collective-permute-start.17 = (f32[4,64,512]{2,1,0:T(8,128)S(1)}, f32[4,64,512]{2,1,0:T(8,128)S(1)}, u32[]{:S(2)}, u32[]{:S(2)}) collective-permute-start(f32[4,64,512]{2,1,0:T(8,128)S(1)} %outputs.4.refs_0_), channel_id=1, source_target_pairs={{0,1},{1,0},{2,3},{3,2},{4,5},{5,4},{6,7},{7,6},{8,9},{9,8},{10,11... | collective-permute-start | bytes 1572872 | tf_op jit(solution)/shard_map/ppermute | solution.py:576
  47.3 8.4 %collective-permute-start.18 = (f32[4,64,512]{2,1,0:T(8,128)S(1)}, f32[4,64,512]{2,1,0:T(8,128)S(1)}, u32[]{:S(2)}, u32[]{:S(2)}) collective-permute-start(f32[4,64,512]{2,1,0:T(8,128)S(1)} %outputs.5.refs_0_), channel_id=1, source_target_pairs={{0,1},{1,0},{2,3},{3,2},{4,5},{5,4},{6,7},{7,6},{8,9},{9,8},{10,11... | collective-permute-start | bytes 1572872 | tf_op jit(solution)/shard_map/ppermute | solution.py:576
  48.8 5.7 %collective-permute-start.19 = (s16[528,128]{1,0:T(8,128)(2,1)S(1)}, s16[528,128]{1,0:T(8,128)(2,1)S(1)}, u32[]{:S(2)}, u32[]{:S(2)}) collective-permute-start(s16[528,128]{1,0:T(8,128)(2,1)S(1)} %get-tuple-element.49.refs_0_), channel_id=1, source_target_pairs={{0,2},{2,0},{1,3},{3,1},{4,6},{6,4},{5,7},{7,5},{8,10},{10,8},{9,1... | collective-permute-start | bytes 405512 | tf_op jit(solution)/shard_map/ppermute | solution.py:576
  54.5 5.0 %collective-permute-start.20 = (s16[528,128]{1,0:T(8,128)(2,1)S(1)}, s16[528,128]{1,0:T(8,128)(2,1)S(1)}, u32[]{:S(2)}, u32[]{:S(2)}) collective-permute-start(s16[528,128]{1,0:T(8,128)(2,1)S(1)} %gate.5), channel_id=1, source_target_pairs={{0,2},{2,0},{1,3},{3,1},{4,6},{6,4},{5,7},{7,5},{8,10},{10,8},{9,1... | collective-permute-start | bytes 405512 | tf_op jit(solution)/shard_map/ppermute | solution.py:576
  55.8 6.7 %collective-permute-start.22 = (s16[272,128]{1,0:T(8,128)(2,1)S(1)}, s16[272,128]{1,0:T(8,128)(2,1)S(1)}, u32[]{:S(2)}, u32[]{:S(2)}) collective-permute-start(s16[272,128]{1,0:T(8,128)(2,1)S(1)} %get-tuple-element.53), channel_id=1, source_target_pairs={{0,8},{4,12},{8,0},{12,4},{1,9},{5,13},{9,1},{13,5},{2,10},{6,14},... | collective-permute-start | bytes 208904 | tf_op jit(solution)/shard_map/ppermute | solution.py:576
  55.9 6.6 %collective-permute-start.23 = (s16[272,128]{1,0:T(8,128)(2,1)S(1)}, s16[272,128]{1,0:T(8,128)(2,1)S(1)}, u32[]{:S(2)}, u32[]{:S(2)}) collective-permute-start(s16[272,128]{1,0:T(8,128)(2,1)S(1)} %get-tuple-element.54), channel_id=1, source_target_pairs={{0,12},{4,8},{8,4},{12,0},{1,13},{5,9},{9,5},{13,1},{2,14},{6,10},... | collective-permute-start | bytes 208904 | tf_op jit(solution)/shard_map/ppermute | solution.py:576
  59.6 4.4 %collective-permute-start.21 = (s16[272,128]{1,0:T(8,128)(2,1)S(1)}, s16[272,128]{1,0:T(8,128)(2,1)S(1)}, u32[]{:S(2)}, u32[]{:S(2)}) collective-permute-start(s16[272,128]{1,0:T(8,128)(2,1)S(1)} %get-tuple-element.52), channel_id=1, source_target_pairs={{0,4},{4,0},{8,12},{12,8},{1,5},{5,1},{9,13},{13,9},{2,6},{6,2},{1... | collective-permute-start | bytes 208904 | tf_op jit(solution)/shard_map/ppermute | solution.py:576
  (7 other events, 48.6 us)

commit v14 on v9

--- a/solution.py
+++ b/solution.py
@@ -19,7 +19,7 @@
 PAIR = 2 * HEAD_SIZE
 LANES = 128
 TAIL = 16
-HALVES = ((0, 3), (1, 2))
+HALVES = ((2, 3), (0, 1))
 DEVICES = ("req", "sub", "section")
 
 theta_base = 500000.0
@@ -61,7 +61,7 @@
         copy.wait()
 
 
-def staged(place, array, width, order, more=(), after=()):
+def staged(place, array, width, order, more=(), after=(), limit=VMEM):
     rows, count = array.shape[0], len(order)
     return pl.pallas_call(
         functools.partial(stage_kernel, order, len(more)),
@@ -75,8 +75,8 @@
         ]
         + [jax.ShapeDtypeStruct(other.shape, other.dtype) for other in more],
         scratch_shapes=[pltpu.SemaphoreType.DMA((count + len(more),))],
-        compiler_params=params(),
-        cost_estimate=cost([array] * 2),
+        compiler_params=pltpu.CompilerParams(vmem_limit_bytes=limit),
+        cost_estimate=cost([array], [array]),
         name="staged",
     )(place, array, *more, *after)
 
@@ -262,7 +262,7 @@
         out_specs=[pl.BlockSpec(memory_space=pltpu.VMEM)] * len(shapes),
         out_shape=shapes,
         compiler_params=params(),
-        cost_estimate=cost(gathered * 1, [weight], flops=2 * count * weight.size),
+        cost_estimate=cost(gathered, [weight], flops=2 * count * weight.size),
         name="scale_and_pairs",
     )(place, gain, weight, *gathered)
 
@@ -589,6 +589,7 @@
     )
     column = pack([rows] + column)
     gathered = [passed(column, "sub", s) for s in range(1, subs)]
+    pages[1:] = gate(pages[1:], after=[column])
     pages[1:] = [passed(pages[s], "req", s) for s in range(1, GROUP_REQUESTS)]
     key_value_weight, ready, gain = staged(
         place,
@@ -597,8 +598,9 @@
         pair_order(subs),
         more=[norm_gain.reshape(devices, 1, width)],
         after=[column],
-    )
-    gathered = [column] + list(gate(gathered, after=[ready]))
+        limit=LARGE_VMEM,
+    )
+    gathered = [column] + list(gate(gathered, after=[ready, pages[1]]))
     gathered = gathered + [passed(part, "section", 1) for part in gathered]
 
     half = HEAD_SIZE // 2
@@ -638,10 +640,13 @@
     kept = outputs(mixed, w_output, mid, end - mid, after=[second])
     parts = fold_core(kept, got_first)
     kept = outputs(mixed, w_output, 0, mid, after=parts[:1])
-    parts = [passed(part, "sub", i // 2 + 1) for i, part in enumerate(parts)]
     last = {}
     for half, order in enumerate(HALVES):
-        last.update(zip(order, fold_sub(order, [kept, got_second], parts[half::2])))
+        sent = parts[half::2]
+        if half:
+            sent = gate(sent, after=[got[0], kept])
+        got = [passed(part, "sub", s + 1) for s, part in enumerate(sent)]
+        last.update(zip(order, fold_sub(order, [kept, got_second], got)))
     parts = [passed(last[s], "req", s) for s in range(1, GROUP_REQUESTS)]
     return finish(gathered[0], last[0], parts).reshape(hidden.shape)
 

time: 64.8 us -> 66.5 us (1.026)
  Pallas kernels: 15.8 us -> 17.5 us
  local copies, waits for them, and re-layouts: 5.12 us -> 3.52 us
  waiting for transfers between devices: 15.4 us -> 16.7 us
    pallas_call x2, Pallas kernels: 2.85 us -> 4.52 us  [staged(): pl.pallas_call(functools.partial(stage_kernel, order, len(more)), in_spec...]
    unnamed x16 -> x14, local copies, waits for them, and re-layouts: 5.11 us -> 3.52 us
    ppermute x24, waiting for transfers between devices: 15.4 us -> 16.7 us  [passed(): lax.ppermute(array, axis, [(i, i ^ shift) for i in range(lax.axis_size(ax...]
  transfers between devices with their start and end apart: 24 -> 24, of which waited for: 10 -> 12; matrix products, arithmetic and copies ran while one was open for 3% -> 3% of each run, Pallas kernels for 19% -> 21%
where the time goes in v14:
time: 66.5 us; the launch traced here: 66.1 us
  starting transfers between devices  26.5 us (40%)
  Pallas kernels  17.5 us (26%)
  waiting for transfers between devices  16.7 us (25%)
  local copies, waits for them, and re-layouts  3.52 us (5%)
  other arithmetic  1.71 us (3%)
    ppermute x24, starting transfers between devices, passed(): lax.ppermute(array, axis, [(i, i ^ shift) for i in range(lax.axis_size(ax...  26.5 us
    ppermute x24, waiting for transfers between devices, passed(): lax.ppermute(array, axis, [(i, i ^ shift) for i in range(lax.axis_size(ax...  16.7 us
    pallas_call x1, Pallas kernels, queries(): pl.pallas_call(query_kernel, in_specs=[pl.BlockSpec(memory_space=pltpu.SM...  4.63 us
    pallas_call x2, Pallas kernels, staged(): pl.pallas_call(functools.partial(stage_kernel, order, len(more)), in_spec...  4.52 us
    unnamed x14, local copies, waits for them, and re-layouts  3.52 us
    pallas_call x1, Pallas kernels, attend(): pl.pallas_call(attend_kernel, in_specs=[pl.BlockSpec(memory_space=pltpu.S...  2.18 us
    pallas_call x4, Pallas kernels, outputs(): pl.pallas_call(functools.partial(output_kernel, first), in_specs=[pl.Bloc...  1.89 us
    pallas_call x1, Pallas kernels, used_pages(): pl.pallas_call(pages_kernel, grid_spec=pltpu.PrefetchScalarGridSpec(num_s...  1.51 us
  transfers between devices with their start and end apart: 24, of which 12 were waited for; matrix products, arithmetic and copies ran while one was open for 3% of the time, Pallas kernels for 21%

profile of v14, /device:TPU:0, one launch (start us, length us, event | category | flops | bytes accessed | tf_op | source)
XLA Modules:
  0.0 66.1 jit_solution(18328909731275130565)
XLA Ops:
  0.0 5.0 %collective-permute-start.2 = (bf16[64,512]{1,0:T(8,128)(2,1)}, bf16[64,512]{1,0:T(8,128)(2,1)S(1)}, u32[]{:S(2)}, u32[]{:S(2)}) collective-permute-start(bf16[64,512]{1,0:T(8,128)(2,1)} %bitcast.16), channel_id=1, source_target_pairs={{0,12},{4,8},{8,4},{12,0},{1,13},{5,9},{9,5},{13,1},{2,14},{6,10},... | collective-permute-start | bytes 196616 | tf_op jit(solution)/shard_map/ppermute | solution.py:557
  6.4 1.2 %copy-done = bf16[16,16,2048]{2,1,0:T(8,128)(2,1)S(1)} copy-done((bf16[16,16,2048]{2,1,0:T(8,128)(2,1)S(1)}, bf16[16,16,2048]{2,1,0:T(8,128)(2,1)}, u32[]{:S(2)}) %copy-start) | copy-done | bytes 1048600
  9.1 1.5 %used_pages.1 = (bf16[64,512]{1,0:T(8,128)(2,1)S(1)}, bf16[2,128,256]{2,1,0:T(8,128)(2,1)S(1)}, bf16[2,128,256]{2,1,0:T(8,128)(2,1)S(1)}, bf16[2,128,256]{2,1,0:T(8,128)(2,1)S(1)}, bf16[2,128,256]{2,1,0:T(8,128)(2,1)S(1)}) custom-call(s32[4,32]{1,0:T(4,128)S(1)} %copy-done.3, s32[3]{0:T(128)S(1)} %pad_add_fusion.place, ...), custom_call_target="tpu_custom_call" | custom-call | bytes 1048576 | tf_op jit(solution)/shard_map/used_pages/pallas_call | solution.py:141
  10.9 1.6 %collective-permute-start.3 = (bf16[4,64,512]{2,1,0:T(8,128)(2,1)S(1)}, bf16[4,64,512]{2,1,0:T(8,128)(2,1)S(1)}, u32[]{:S(2)}, u32[]{:S(2)}) collective-permute-start(bf16[4,64,512]{2,1,0:T(8,128)(2,1)S(1)} %pack.1.refs_1_.refs_3_.refs_0_.rows_ref), channel_id=1, source_target_pairs={{0,2},{2,0},{1,3},{3,1},{4,6},{6,4},{5,7},{7,5},{8,10},{10,8},{9,1... | collective-permute-start | bytes 786440 | tf_op jit(solution)/shard_map/ppermute | solution.py:557
  12.5 1.2 %collective-permute-start.4 = (bf16[2,128,256]{2,1,0:T(8,128)(2,1)S(1)}, bf16[2,128,256]{2,1,0:T(8,128)(2,1)S(1)}, u32[]{:S(2)}, u32[]{:S(2)}) collective-permute-start(bf16[2,128,256]{2,1,0:T(8,128)(2,1)S(1)} %get-tuple-element.40), channel_id=1, source_target_pairs={{0,4},{4,0},{8,12},{12,8},{1,5},{5,1},{9,13},{13,9},{2,6},{6,2},{1... | collective-permute-start | bytes 393224 | tf_op jit(solution)/shard_map/ppermute | solution.py:557
  15.3 2.5 %staged.2 = (bf16[8,512,256]{2,1,0:T(8,128)(2,1)S(1)}, f32[8,128]{1,0:T(8,128)S(1)}, f32[16,1,512]{2,1,0:T(1,128)S(1)}) custom-call(s32[3]{0:T(128)S(1)} %pad_add_fusion.1.place, bf16[512,2048]{1,0:T(8,128)(2,1)} %block_ref.2, f32[16,1,512]{2,1,0:T(1,128)S(1)} %bitcast.20, bf16[4,64,512]{2,1,0:T(8,128)(2,1)S(1)} %pack.1.refs_1_.refs_3_.refs_0_.rows_ref), custom_call_target="tpu_custom_call" | custom-call | bytes 4194304 | tf_op jit(solution)/shard_map/staged/pallas_call | solution.py:66
  19.0 2.5 %collective-permute-start.12 = (bf16[2,128,256]{2,1,0:T(8,128)(2,1)S(1)}, bf16[2,128,256]{2,1,0:T(8,128)(2,1)S(1)}, u32[]{:S(2)}, u32[]{:S(2)}) collective-permute-start(bf16[2,128,256]{2,1,0:T(8,128)(2,1)S(1)} %get-tuple-element.50), channel_id=1, source_target_pairs={{0,8},{4,12},{8,0},{12,4},{1,9},{5,13},{9,1},{13,5},{2,10},{6,14},... | collective-permute-start | bytes 393224 | tf_op jit(solution)/shard_map/ppermute | solution.py:557
  22.3 1.4 %scale_and_pairs.1 = (f32[64,128]{1,0:T(8,128)S(1)}, f32[4,64,256]{2,1,0:T(8,128)S(1)}, s16[528,128]{1,0:T(8,128)(2,1)S(1)}) custom-call(s32[3]{0:T(128)S(1)} %pad_add_fusion.1.place, f32[16,1,512]{2,1,0:T(1,128)S(1)} %get-tuple-element.34.gain_ref, bf16[8,512,256]{2,1,0:T(8,128)(2,1)S(1)} %get-tuple-element.35.weight_ref, ...), custom_call_target="tpu_custom_call" | custom-call | flops 134217728 | bytes 3145728 | tf_op jit(solution)/shard_map/scale_and_pairs/pallas_call | solution.py:258
  23.7 1.6 %collective-permute-start.7 = (s16[528,128]{1,0:T(8,128)(2,1)S(1)}, s16[528,128]{1,0:T(8,128)(2,1)S(1)}, u32[]{:S(2)}, u32[]{:S(2)}) collective-permute-start(s16[528,128]{1,0:T(8,128)(2,1)S(1)} %get-tuple-element.43), channel_id=1, source_target_pairs={{0,2},{2,0},{1,3},{3,1},{4,6},{6,4},{5,7},{7,5},{8,10},{10,8},{9,1... | collective-permute-start | bytes 405512 | tf_op jit(solution)/shard_map/ppermute | solution.py:557
  25.4 4.6 %queries.1.refs_2_.refs_0_.q_ref = bf16[4,16,512]{2,1,0:T(8,128)(2,1)S(1)} custom-call(s32[3]{0:T(128)S(1)} %pad_add_fusion.1.place, f32[64,128]{1,0:T(8,128)S(1)} %get-tuple-element.41.scale_ref, f32[16,1,512]{2,1,0:T(1,128)S(1)} %get-tuple-element.34.gain_ref, bf16[8192,512]{1,0:T(8,128)(2,1)} %weight_ref.1, f32[64,128]{1,0:T(8,128)S(1)} %bitcast.12, ...), custom_call_target="tpu_custom_call" | custom-call | flops 536870912 | bytes 8388608 | tf_op jit(solution)/shard_map/queries/pallas_call | solution.py:302
  30.2 1.7 %collective-permute-done.12.refs_2_ = bf16[2,128,256]{2,1,0:T(8,128)(2,1)S(1)} collective-permute-done((bf16[2,128,256]{2,1,0:T(8,128)(2,1)S(1)}, bf16[2,128,256]{2,1,0:T(8,128)(2,1)S(1)}, u32[]{:S(2)}, u32[]{:S(2)}) %collective-permute-start.12) | collective-permute-done | bytes 131104 | tf_op jit(solution)/shard_map/ppermute | solution.py:557
  31.9 1.7 %collective-permute-start.14 = (bf16[4,128,256]{2,1,0:T(8,128)(2,1)S(1)}, bf16[4,128,256]{2,1,0:T(8,128)(2,1)S(1)}, u32[]{:S(2)}, u32[]{:S(2)}) collective-permute-start(bf16[4,128,256]{2,1,0:T(8,128)(2,1)S(1)} %get-tuple-element.53), channel_id=1, source_target_pairs={{0,2},{2,0},{1,3},{3,1},{4,6},{6,4},{5,7},{7,5},{8,10},{10,8},{9,1... | collective-permute-start | bytes 786440 | tf_op jit(solution)/shard_map/ppermute | solution.py:557
  33.5 3.1 %collective-permute-start.8 = (s16[144,128]{1,0:T(8,128)(2,1)S(1)}, s16[144,128]{1,0:T(8,128)(2,1)S(1)}, u32[]{:S(2)}, u32[]{:S(2)}) collective-permute-start(s16[144,128]{1,0:T(8,128)(2,1)S(1)} %get-tuple-element.45), channel_id=1, source_target_pairs={{0,4},{4,0},{8,12},{12,8},{1,5},{5,1},{9,13},{13,9},{2,6},{6,2},{1... | collective-permute-start | bytes 110600 | tf_op jit(solution)/shard_map/ppermute | solution.py:557
  36.6 1.1 %collective-permute-start.9 = (s16[144,128]{1,0:T(8,128)(2,1)S(1)}, s16[144,128]{1,0:T(8,128)(2,1)S(1)}, u32[]{:S(2)}, u32[]{:S(2)}) collective-permute-start(s16[144,128]{1,0:T(8,128)(2,1)S(1)} %get-tuple-element.46), channel_id=1, source_target_pairs={{0,8},{4,12},{8,0},{12,4},{1,9},{5,13},{9,1},{13,5},{2,10},{6,14},... | collective-permute-start | bytes 110600 | tf_op jit(solution)/shard_map/ppermute | solution.py:557
  37.7 1.5 %collective-permute-start.10 = (s16[144,128]{1,0:T(8,128)(2,1)S(1)}, s16[144,128]{1,0:T(8,128)(2,1)S(1)}, u32[]{:S(2)}, u32[]{:S(2)}) collective-permute-start(s16[144,128]{1,0:T(8,128)(2,1)S(1)} %get-tuple-element.47), channel_id=1, source_target_pairs={{0,12},{4,8},{8,4},{12,0},{1,13},{5,9},{9,5},{13,1},{2,14},{6,10},... | collective-permute-start | bytes 110600 | tf_op jit(solution)/shard_map/ppermute | solution.py:557
  39.2 2.0 %staged.3 = (bf16[16,512,512]{2,1,0:T(8,128)(2,1)S(1)}, f32[8,128]{1,0:T(8,128)S(1)}) custom-call(s32[3]{0:T(128)S(1)} %pad_add_fusion.1.place, bf16[512,8192]{1,0:T(8,128)(2,1)S(1)} %bitcast.11, bf16[4,16,512]{2,1,0:T(8,128)(2,1)S(1)} %queries.1.refs_2_.refs_0_.q_ref), custom_call_target="tpu_custom_call" | custom-call | bytes 16777216 | tf_op jit(solution)/shard_map/staged/pallas_call | solution.py:66
  41.3 1.3 %collective-permute-done.9.refs_1_ = s16[144,128]{1,0:T(8,128)(2,1)S(1)} collective-permute-done((s16[144,128]{1,0:T(8,128)(2,1)S(1)}, s16[144,128]{1,0:T(8,128)(2,1)S(1)}, u32[]{:S(2)}, u32[]{:S(2)}) %collective-permute-start.9) | collective-permute-done | bytes 36896 | tf_op jit(solution)/shard_map/ppermute | solution.py:557
  44.1 1.1 %collective-permute-done.11.other_ref = f32[64,256]{1,0:T(8,128)S(1)} collective-permute-done((f32[64,256]{1,0:T(8,128)S(1)}, f32[64,256]{1,0:T(8,128)S(1)}, u32[]{:S(2)}, u32[]{:S(2)}) %collective-permute-start.11) | collective-permute-done | bytes 65568 | tf_op jit(solution)/shard_map/ppermute | solution.py:557
  45.3 2.2 %attend.1.x_ref = bf16[4,16,512]{2,1,0:T(8,128)(2,1)S(1)} custom-call(s32[3]{0:T(128)S(1)} %pad_add_fusion.1.place, s32[4]{0:T(128)S(1)} %copy-done.4, bf16[4,16,512]{2,1,0:T(8,128)(2,1)S(1)} %queries.1.refs_2_.refs_0_.q_ref, f32[64,256]{1,0:T(8,128)S(1)} %fold_pairs.1.refs_1_.mine_ref, f32[64,256]{1,0:T(8,128)S(1)} %collective-permute-done.11.other_ref, ...), custom_call_target="tpu_custom_call" | custom-call | flops 268435456 | bytes 3145728 | tf_op jit(solution)/shard_map/attend/pallas_call | solution.py:379
  51.4 4.5 %collective-permute-done.19.refs_1_.refs_2_ = s16[528,128]{1,0:T(8,128)(2,1)S(1)} collective-permute-done((s16[528,128]{1,0:T(8,128)(2,1)S(1)}, s16[528,128]{1,0:T(8,128)(2,1)S(1)}, u32[]{:S(2)}, u32[]{:S(2)}) %collective-permute-start.19) | collective-permute-done | bytes 135200 | tf_op jit(solution)/shard_map/ppermute | solution.py:557
  56.7 1.7 %collective-permute-start.22 = (s16[272,128]{1,0:T(8,128)(2,1)S(1)}, s16[272,128]{1,0:T(8,128)(2,1)S(1)}, u32[]{:S(2)}, u32[]{:S(2)}) collective-permute-start(s16[272,128]{1,0:T(8,128)(2,1)S(1)} %get-tuple-element.59), channel_id=1, source_target_pairs={{0,8},{4,12},{8,0},{12,4},{1,9},{5,13},{9,1},{13,5},{2,10},{6,14},... | collective-permute-start | bytes 208904 | tf_op jit(solution)/shard_map/ppermute | solution.py:557
  58.4 1.1 %collective-permute-start.23 = (s16[272,128]{1,0:T(8,128)(2,1)S(1)}, s16[272,128]{1,0:T(8,128)(2,1)S(1)}, u32[]{:S(2)}, u32[]{:S(2)}) collective-permute-start(s16[272,128]{1,0:T(8,128)(2,1)S(1)} %get-tuple-element.60), channel_id=1, source_target_pairs={{0,12},{4,8},{8,4},{12,0},{1,13},{5,9},{9,5},{13,1},{2,14},{6,10},... | collective-permute-start | bytes 208904 | tf_op jit(solution)/shard_map/ppermute | solution.py:557
  59.5 1.4 %collective-permute-done.20.refs_2_ = s16[528,128]{1,0:T(8,128)(2,1)S(1)} collective-permute-done((s16[528,128]{1,0:T(8,128)(2,1)S(1)}, s16[528,128]{1,0:T(8,128)(2,1)S(1)}, u32[]{:S(2)}, u32[]{:S(2)}) %collective-permute-start.20) | collective-permute-done | bytes 135200 | tf_op jit(solution)/shard_map/ppermute | solution.py:557
  61.2 2.4 %collective-permute-done.22.refs_1_ = s16[272,128]{1,0:T(8,128)(2,1)S(1)} collective-permute-done((s16[272,128]{1,0:T(8,128)(2,1)S(1)}, s16[272,128]{1,0:T(8,128)(2,1)S(1)}, u32[]{:S(2)}, u32[]{:S(2)}) %collective-permute-start.22) | collective-permute-done | bytes 69664 | tf_op jit(solution)/shard_map/ppermute | solution.py:557
  (70 shorter events, 16.0 us)
Async XLA Ops:
  0.0 10.7 %collective-permute-start.2 = (bf16[64,512]{1,0:T(8,128)(2,1)}, bf16[64,512]{1,0:T(8,128)(2,1)S(1)}, u32[]{:S(2)}, u32[]{:S(2)}) collective-permute-start(bf16[64,512]{1,0:T(8,128)(2,1)} %bitcast.16), channel_id=1, source_target_pairs={{0,12},{4,8},{8,4},{12,0},{1,13},{5,9},{9,5},{13,1},{2,14},{6,10},... | collective-permute-start | bytes 196616 | tf_op jit(solution)/shard_map/ppermute | solution.py:557
  5.0 5.8 %collective-permute-start.1 = (bf16[64,512]{1,0:T(8,128)(2,1)}, bf16[64,512]{1,0:T(8,128)(2,1)S(1)}, u32[]{:S(2)}, u32[]{:S(2)}) collective-permute-start(bf16[64,512]{1,0:T(8,128)(2,1)} %bitcast.17), channel_id=1, source_target_pairs={{0,8},{4,12},{8,0},{12,4},{1,9},{5,13},{9,1},{13,5},{2,10},{6,14},... | collective-permute-start | bytes 196616 | tf_op jit(solution)/shard_map/ppermute | solution.py:557
  5.1 5.8 %collective-permute-start = (bf16[64,512]{1,0:T(8,128)(2,1)}, bf16[64,512]{1,0:T(8,128)(2,1)S(1)}, u32[]{:S(2)}, u32[]{:S(2)}) collective-permute-start(bf16[64,512]{1,0:T(8,128)(2,1)} %bitcast.18), channel_id=1, source_target_pairs={{0,4},{4,0},{8,12},{12,8},{1,5},{5,1},{9,13},{13,9},{2,6},{6,2},{1... | collective-permute-start | bytes 196616 | tf_op jit(solution)/shard_map/ppermute | solution.py:557
  10.9 7.9 %collective-permute-start.3 = (bf16[4,64,512]{2,1,0:T(8,128)(2,1)S(1)}, bf16[4,64,512]{2,1,0:T(8,128)(2,1)S(1)}, u32[]{:S(2)}, u32[]{:S(2)}) collective-permute-start(bf16[4,64,512]{2,1,0:T(8,128)(2,1)S(1)} %pack.1.refs_1_.refs_3_.refs_0_.rows_ref), channel_id=1, source_target_pairs={{0,2},{2,0},{1,3},{3,1},{4,6},{6,4},{5,7},{7,5},{8,10},{10,8},{9,1... | collective-permute-start | bytes 786440 | tf_op jit(solution)/shard_map/ppermute | solution.py:557
  12.5 5.3 %collective-permute-start.4 = (bf16[2,128,256]{2,1,0:T(8,128)(2,1)S(1)}, bf16[2,128,256]{2,1,0:T(8,128)(2,1)S(1)}, u32[]{:S(2)}, u32[]{:S(2)}) collective-permute-start(bf16[2,128,256]{2,1,0:T(8,128)(2,1)S(1)} %get-tuple-element.40), channel_id=1, source_target_pairs={{0,4},{4,0},{8,12},{12,8},{1,5},{5,1},{9,13},{13,9},{2,6},{6,2},{1... | collective-permute-start | bytes 393224 | tf_op jit(solution)/shard_map/ppermute | solution.py:557
  14.5 7.8 %collective-permute-start.5 = (bf16[4,64,512]{2,1,0:T(8,128)(2,1)S(1)}, bf16[4,64,512]{2,1,0:T(8,128)(2,1)S(1)}, u32[]{:S(2)}, u32[]{:S(2)}) collective-permute-start(bf16[4,64,512]{2,1,0:T(8,128)(2,1)S(1)} %pack.1.refs_1_.refs_3_.refs_0_.rows_ref), channel_id=1, source_target_pairs={{0,1},{1,0},{2,3},{3,2},{4,5},{5,4},{6,7},{7,6},{8,9},{9,8},{10,11... | collective-permute-start | bytes 786440 | tf_op jit(solution)/shard_map/ppermute | solution.py:557
  18.8 3.5 %collective-permute-start.6 = (bf16[4,64,512]{2,1,0:T(8,128)(2,1)S(1)}, bf16[4,64,512]{2,1,0:T(8,128)(2,1)S(1)}, u32[]{:S(2)}, u32[]{:S(2)}) collective-permute-start(bf16[4,64,512]{2,1,0:T(8,128)(2,1)S(1)} %gate.5.refs_1_), channel_id=1, source_target_pairs={{0,1},{1,0},{2,3},{3,2},{4,5},{5,4},{6,7},{7,6},{8,9},{9,8},{10,11... | collective-permute-start | bytes 786440 | tf_op jit(solution)/shard_map/ppermute | solution.py:557
  19.0 12.8 %collective-permute-start.12 = (bf16[2,128,256]{2,1,0:T(8,128)(2,1)S(1)}, bf16[2,128,256]{2,1,0:T(8,128)(2,1)S(1)}, u32[]{:S(2)}, u32[]{:S(2)}) collective-permute-start(bf16[2,128,256]{2,1,0:T(8,128)(2,1)S(1)} %get-tuple-element.50), channel_id=1, source_target_pairs={{0,8},{4,12},{8,0},{12,4},{1,9},{5,13},{9,1},{13,5},{2,10},{6,14},... | collective-permute-start | bytes 393224 | tf_op jit(solution)/shard_map/ppermute | solution.py:557
  21.5 10.3 %collective-permute-start.13 = (bf16[2,128,256]{2,1,0:T(8,128)(2,1)S(1)}, bf16[2,128,256]{2,1,0:T(8,128)(2,1)S(1)}, u32[]{:S(2)}, u32[]{:S(2)}) collective-permute-start(bf16[2,128,256]{2,1,0:T(8,128)(2,1)S(1)} %get-tuple-element.51), channel_id=1, source_target_pairs={{0,12},{4,8},{8,4},{12,0},{1,13},{5,9},{9,5},{13,1},{2,14},{6,10},... | collective-permute-start | bytes 393224 | tf_op jit(solution)/shard_map/ppermute | solution.py:557
  23.7 6.3 %collective-permute-start.7 = (s16[528,128]{1,0:T(8,128)(2,1)S(1)}, s16[528,128]{1,0:T(8,128)(2,1)S(1)}, u32[]{:S(2)}, u32[]{:S(2)}) collective-permute-start(s16[528,128]{1,0:T(8,128)(2,1)S(1)} %get-tuple-element.43), channel_id=1, source_target_pairs={{0,2},{2,0},{1,3},{3,1},{4,6},{6,4},{5,7},{7,5},{8,10},{10,8},{9,1... | collective-permute-start | bytes 405512 | tf_op jit(solution)/shard_map/ppermute | solution.py:557
  31.9 11.7 %collective-permute-start.14 = (bf16[4,128,256]{2,1,0:T(8,128)(2,1)S(1)}, bf16[4,128,256]{2,1,0:T(8,128)(2,1)S(1)}, u32[]{:S(2)}, u32[]{:S(2)}) collective-permute-start(bf16[4,128,256]{2,1,0:T(8,128)(2,1)S(1)} %get-tuple-element.53), channel_id=1, source_target_pairs={{0,2},{2,0},{1,3},{3,1},{4,6},{6,4},{5,7},{7,5},{8,10},{10,8},{9,1... | collective-permute-start | bytes 786440 | tf_op jit(solution)/shard_map/ppermute | solution.py:557
  33.5 7.7 %collective-permute-start.8 = (s16[144,128]{1,0:T(8,128)(2,1)S(1)}, s16[144,128]{1,0:T(8,128)(2,1)S(1)}, u32[]{:S(2)}, u32[]{:S(2)}) collective-permute-start(s16[144,128]{1,0:T(8,128)(2,1)S(1)} %get-tuple-element.45), channel_id=1, source_target_pairs={{0,4},{4,0},{8,12},{12,8},{1,5},{5,1},{9,13},{13,9},{2,6},{6,2},{1... | collective-permute-start | bytes 110600 | tf_op jit(solution)/shard_map/ppermute | solution.py:557
  36.6 5.9 %collective-permute-start.9 = (s16[144,128]{1,0:T(8,128)(2,1)S(1)}, s16[144,128]{1,0:T(8,128)(2,1)S(1)}, u32[]{:S(2)}, u32[]{:S(2)}) collective-permute-start(s16[144,128]{1,0:T(8,128)(2,1)S(1)} %get-tuple-element.46), channel_id=1, source_target_pairs={{0,8},{4,12},{8,0},{12,4},{1,9},{5,13},{9,1},{13,5},{2,10},{6,14},... | collective-permute-start | bytes 110600 | tf_op jit(solution)/shard_map/ppermute | solution.py:557
  37.7 5.8 %collective-permute-start.10 = (s16[144,128]{1,0:T(8,128)(2,1)S(1)}, s16[144,128]{1,0:T(8,128)(2,1)S(1)}, u32[]{:S(2)}, u32[]{:S(2)}) collective-permute-start(s16[144,128]{1,0:T(8,128)(2,1)S(1)} %get-tuple-element.47), channel_id=1, source_target_pairs={{0,12},{4,8},{8,4},{12,0},{1,13},{5,9},{9,5},{13,1},{2,14},{6,10},... | collective-permute-start | bytes 110600 | tf_op jit(solution)/shard_map/ppermute | solution.py:557
  41.2 4.1 %collective-permute-start.15 = (bf16[4,128,256]{2,1,0:T(8,128)(2,1)S(1)}, bf16[4,128,256]{2,1,0:T(8,128)(2,1)S(1)}, u32[]{:S(2)}, u32[]{:S(2)}) collective-permute-start(bf16[4,128,256]{2,1,0:T(8,128)(2,1)S(1)} %get-tuple-element.52.refs_0_), channel_id=1, source_target_pairs={{0,1},{1,0},{2,3},{3,2},{4,5},{5,4},{6,7},{7,6},{8,9},{9,8},{10,11... | collective-permute-start | bytes 786440 | tf_op jit(solution)/shard_map/ppermute | solution.py:557
  43.6 1.7 %collective-permute-start.16 = (bf16[4,128,256]{2,1,0:T(8,128)(2,1)S(1)}, bf16[4,128,256]{2,1,0:T(8,128)(2,1)S(1)}, u32[]{:S(2)}, u32[]{:S(2)}) collective-permute-start(bf16[4,128,256]{2,1,0:T(8,128)(2,1)S(1)} %gate.6.refs_1_), channel_id=1, source_target_pairs={{0,1},{1,0},{2,3},{3,2},{4,5},{5,4},{6,7},{7,6},{8,9},{9,8},{10,11... | collective-permute-start | bytes 786440 | tf_op jit(solution)/shard_map/ppermute | solution.py:557
  43.6 1.6 %collective-permute-start.11 = (f32[64,256]{1,0:T(8,128)S(1)}, f32[64,256]{1,0:T(8,128)S(1)}, u32[]{:S(2)}, u32[]{:S(2)}) collective-permute-start(f32[64,256]{1,0:T(8,128)S(1)} %fold_pairs.1.refs_1_.mine_ref), channel_id=1, source_target_pairs={{0,1},{1,0},{2,3},{3,2},{4,5},{5,4},{6,7},{7,6},{8,9},{9,8},{10,11... | collective-permute-start | bytes 196616 | tf_op jit(solution)/shard_map/ppermute | solution.py:557
  47.9 2.0 %collective-permute-start.17 = (f32[4,64,512]{2,1,0:T(8,128)S(1)}, f32[4,64,512]{2,1,0:T(8,128)S(1)}, u32[]{:S(2)}, u32[]{:S(2)}) collective-permute-start(f32[4,64,512]{2,1,0:T(8,128)S(1)} %outputs.4.refs_0_), channel_id=1, source_target_pairs={{0,1},{1,0},{2,3},{3,2},{4,5},{5,4},{6,7},{7,6},{8,9},{9,8},{10,11... | collective-permute-start | bytes 1572872 | tf_op jit(solution)/shard_map/ppermute | solution.py:557
  48.6 7.9 %collective-permute-start.18 = (f32[4,64,512]{2,1,0:T(8,128)S(1)}, f32[4,64,512]{2,1,0:T(8,128)S(1)}, u32[]{:S(2)}, u32[]{:S(2)}) collective-permute-start(f32[4,64,512]{2,1,0:T(8,128)S(1)} %outputs.5.refs_0_), channel_id=1, source_target_pairs={{0,1},{1,0},{2,3},{3,2},{4,5},{5,4},{6,7},{7,6},{8,9},{9,8},{10,11... | collective-permute-start | bytes 1572872 | tf_op jit(solution)/shard_map/ppermute | solution.py:557
  50.2 5.7 %collective-permute-start.19 = (s16[528,128]{1,0:T(8,128)(2,1)S(1)}, s16[528,128]{1,0:T(8,128)(2,1)S(1)}, u32[]{:S(2)}, u32[]{:S(2)}) collective-permute-start(s16[528,128]{1,0:T(8,128)(2,1)S(1)} %get-tuple-element.55.refs_0_), channel_id=1, source_target_pairs={{0,2},{2,0},{1,3},{3,1},{4,6},{6,4},{5,7},{7,5},{8,10},{10,8},{9,1... | collective-permute-start | bytes 405512 | tf_op jit(solution)/shard_map/ppermute | solution.py:557
  55.9 5.0 %collective-permute-start.20 = (s16[528,128]{1,0:T(8,128)(2,1)S(1)}, s16[528,128]{1,0:T(8,128)(2,1)S(1)}, u32[]{:S(2)}, u32[]{:S(2)}) collective-permute-start(s16[528,128]{1,0:T(8,128)(2,1)S(1)} %gate.7), channel_id=1, source_target_pairs={{0,2},{2,0},{1,3},{3,1},{4,6},{6,4},{5,7},{7,5},{8,10},{10,8},{9,1... | collective-permute-start | bytes 405512 | tf_op jit(solution)/shard_map/ppermute | solution.py:557
  56.7 7.0 %collective-permute-start.22 = (s16[272,128]{1,0:T(8,128)(2,1)S(1)}, s16[272,128]{1,0:T(8,128)(2,1)S(1)}, u32[]{:S(2)}, u32[]{:S(2)}) collective-permute-start(s16[272,128]{1,0:T(8,128)(2,1)S(1)} %get-tuple-element.59), channel_id=1, source_target_pairs={{0,8},{4,12},{8,0},{12,4},{1,9},{5,13},{9,1},{13,5},{2,10},{6,14},... | collective-permute-start | bytes 208904 | tf_op jit(solution)/shard_map/ppermute | solution.py:557
  58.4 6.3 %collective-permute-start.23 = (s16[272,128]{1,0:T(8,128)(2,1)S(1)}, s16[272,128]{1,0:T(8,128)(2,1)S(1)}, u32[]{:S(2)}, u32[]{:S(2)}) collective-permute-start(s16[272,128]{1,0:T(8,128)(2,1)S(1)} %get-tuple-element.60), channel_id=1, source_target_pairs={{0,12},{4,8},{8,4},{12,0},{1,13},{5,9},{9,5},{13,1},{2,14},{6,10},... | collective-permute-start | bytes 208904 | tf_op jit(solution)/shard_map/ppermute | solution.py:557
  61.0 4.4 %collective-permute-start.21 = (s16[272,128]{1,0:T(8,128)(2,1)S(1)}, s16[272,128]{1,0:T(8,128)(2,1)S(1)}, u32[]{:S(2)}, u32[]{:S(2)}) collective-permute-start(s16[272,128]{1,0:T(8,128)(2,1)S(1)} %get-tuple-element.58), channel_id=1, source_target_pairs={{0,4},{4,0},{8,12},{12,8},{1,5},{5,1},{9,13},{13,9},{2,6},{6,2},{1... | collective-permute-start | bytes 208904 | tf_op jit(solution)/shard_map/ppermute | solution.py:557
  (7 other events, 61.1 us)

commit v15 on v14

--- a/solution.py
+++ b/solution.py
@@ -589,7 +589,7 @@
     )
     column = pack([rows] + column)
     gathered = [passed(column, "sub", s) for s in range(1, subs)]
-    pages[1:] = gate(pages[1:], after=[column])
+    pages[3:] = gate(pages[3:], after=[column])
     pages[1:] = [passed(pages[s], "req", s) for s in range(1, GROUP_REQUESTS)]
     key_value_weight, ready, gain = staged(
         place,
@@ -600,7 +600,7 @@
         after=[column],
         limit=LARGE_VMEM,
     )
-    gathered = [column] + list(gate(gathered, after=[ready, pages[1]]))
+    gathered = [column] + list(gate(gathered, after=[ready]))
     gathered = gathered + [passed(part, "section", 1) for part in gathered]
 
     half = HEAD_SIZE // 2

time: 66.5 us -> 64.1 us (0.964)
  starting transfers between devices: 26.5 us -> 23.9 us
    ppermute x24, starting transfers between devices: 26.5 us -> 23.9 us  [passed(): lax.ppermute(array, axis, [(i, i ^ shift) for i in range(lax.axis_size(ax...]
  transfers between devices with their start and end apart: 24 -> 24, of which waited for: 12 -> 9; matrix products, arithmetic and copies ran while one was open for 3% -> 3% of each run, Pallas kernels for 21% -> 22%
where the time goes in v15:
time: 64.1 us; the launch traced here: 63.7 us
  starting transfers between devices  23.9 us (37%)
  Pallas kernels  17.5 us (27%)
  waiting for transfers between devices  16.8 us (26%)
  local copies, waits for them, and re-layouts  3.53 us (6%)
  other arithmetic  1.71 us (3%)
    ppermute x24, starting transfers between devices, passed(): lax.ppermute(array, axis, [(i, i ^ shift) for i in range(lax.axis_size(ax...  23.9 us
    ppermute x24, waiting for transfers between devices, passed(): lax.ppermute(array, axis, [(i, i ^ shift) for i in range(lax.axis_size(ax...  16.8 us
    pallas_call x1, Pallas kernels, queries(): pl.pallas_call(query_kernel, in_specs=[pl.BlockSpec(memory_space=pltpu.SM...  4.63 us
    pallas_call x2, Pallas kernels, staged(): pl.pallas_call(functools.partial(stage_kernel, order, len(more)), in_spec...  4.52 us
    unnamed x14, local copies, waits for them, and re-layouts  3.52 us
    pallas_call x1, Pallas kernels, attend(): pl.pallas_call(attend_kernel, in_specs=[pl.BlockSpec(memory_space=pltpu.S...  2.19 us
    pallas_call x4, Pallas kernels, outputs(): pl.pallas_call(functools.partial(output_kernel, first), in_specs=[pl.Bloc...  1.89 us
    pallas_call x1, Pallas kernels, used_pages(): pl.pallas_call(pages_kernel, grid_spec=pltpu.PrefetchScalarGridSpec(num_s...  1.51 us
  transfers between devices with their start and end apart: 24, of which 9 were waited for; matrix products, arithmetic and copies ran while one was open for 3% of the time, Pallas kernels for 22%

profile of v15, /device:TPU:0, one launch (start us, length us, event | category | flops | bytes accessed | tf_op | source)
XLA Modules:
  0.0 63.7 jit_solution(10299437428075165266)
XLA Ops:
  0.0 5.0 %collective-permute-start.2 = (bf16[64,512]{1,0:T(8,128)(2,1)}, bf16[64,512]{1,0:T(8,128)(2,1)S(1)}, u32[]{:S(2)}, u32[]{:S(2)}) collective-permute-start(bf16[64,512]{1,0:T(8,128)(2,1)} %bitcast.16), channel_id=1, source_target_pairs={{0,12},{4,8},{8,4},{12,0},{1,13},{5,9},{9,5},{13,1},{2,14},{6,10},... | collective-permute-start | bytes 196616 | tf_op jit(solution)/shard_map/ppermute | solution.py:557
  6.4 1.2 %copy-done = bf16[16,16,2048]{2,1,0:T(8,128)(2,1)S(1)} copy-done((bf16[16,16,2048]{2,1,0:T(8,128)(2,1)S(1)}, bf16[16,16,2048]{2,1,0:T(8,128)(2,1)}, u32[]{:S(2)}) %copy-start) | copy-done | bytes 1048600
  9.1 1.5 %used_pages.1 = (bf16[64,512]{1,0:T(8,128)(2,1)S(1)}, bf16[2,128,256]{2,1,0:T(8,128)(2,1)S(1)}, bf16[2,128,256]{2,1,0:T(8,128)(2,1)S(1)}, bf16[2,128,256]{2,1,0:T(8,128)(2,1)S(1)}, bf16[2,128,256]{2,1,0:T(8,128)(2,1)S(1)}) custom-call(s32[4,32]{1,0:T(4,128)S(1)} %copy-done.3, s32[3]{0:T(128)S(1)} %pad_add_fusion.place, ...), custom_call_target="tpu_custom_call" | custom-call | bytes 1048576 | tf_op jit(solution)/shard_map/used_pages/pallas_call | solution.py:141
  10.7 1.5 %collective-permute-start.11 = (bf16[2,128,256]{2,1,0:T(8,128)(2,1)S(1)}, bf16[2,128,256]{2,1,0:T(8,128)(2,1)S(1)}, u32[]{:S(2)}, u32[]{:S(2)}) collective-permute-start(bf16[2,128,256]{2,1,0:T(8,128)(2,1)S(1)} %get-tuple-element.43), channel_id=1, source_target_pairs={{0,4},{4,0},{8,12},{12,8},{1,5},{5,1},{9,13},{13,9},{2,6},{6,2},{1... | collective-permute-start | bytes 393224 | tf_op jit(solution)/shard_map/ppermute | solution.py:557
  12.2 2.9 %collective-permute-start.12 = (bf16[2,128,256]{2,1,0:T(8,128)(2,1)S(1)}, bf16[2,128,256]{2,1,0:T(8,128)(2,1)S(1)}, u32[]{:S(2)}, u32[]{:S(2)}) collective-permute-start(bf16[2,128,256]{2,1,0:T(8,128)(2,1)S(1)} %get-tuple-element.44), channel_id=1, source_target_pairs={{0,8},{4,12},{8,0},{12,4},{1,9},{5,13},{9,1},{13,5},{2,10},{6,14},... | collective-permute-start | bytes 393224 | tf_op jit(solution)/shard_map/ppermute | solution.py:557
  15.1 1.6 %collective-permute-start.3 = (bf16[4,64,512]{2,1,0:T(8,128)(2,1)S(1)}, bf16[4,64,512]{2,1,0:T(8,128)(2,1)S(1)}, u32[]{:S(2)}, u32[]{:S(2)}) collective-permute-start(bf16[4,64,512]{2,1,0:T(8,128)(2,1)S(1)} %pack.1.refs_1_.refs_0_.rows_ref), channel_id=1, source_target_pairs={{0,2},{2,0},{1,3},{3,1},{4,6},{6,4},{5,7},{7,5},{8,10},{10,8},{9,1... | collective-permute-start | bytes 786440 | tf_op jit(solution)/shard_map/ppermute | solution.py:557
  18.2 2.5 %staged.2 = (bf16[8,512,256]{2,1,0:T(8,128)(2,1)S(1)}, f32[8,128]{1,0:T(8,128)S(1)}, f32[16,1,512]{2,1,0:T(1,128)S(1)}) custom-call(s32[3]{0:T(128)S(1)} %pad_add_fusion.1.place, bf16[512,2048]{1,0:T(8,128)(2,1)} %block_ref.2, f32[16,1,512]{2,1,0:T(1,128)S(1)} %bitcast.20, bf16[4,64,512]{2,1,0:T(8,128)(2,1)S(1)} %pack.1.refs_1_.refs_0_.rows_ref), custom_call_target="tpu_custom_call" | custom-call | bytes 4194304 | tf_op jit(solution)/shard_map/staged/pallas_call | solution.py:66
  20.7 1.1 %collective-permute-done.3.refs_0_ = bf16[4,64,512]{2,1,0:T(8,128)(2,1)S(1)} collective-permute-done((bf16[4,64,512]{2,1,0:T(8,128)(2,1)S(1)}, bf16[4,64,512]{2,1,0:T(8,128)(2,1)S(1)}, u32[]{:S(2)}, u32[]{:S(2)}) %collective-permute-start.3) | collective-permute-done | bytes 262176 | tf_op jit(solution)/shard_map/ppermute | solution.py:557
  23.4 1.4 %scale_and_pairs.1 = (f32[64,128]{1,0:T(8,128)S(1)}, f32[4,64,256]{2,1,0:T(8,128)S(1)}, s16[528,128]{1,0:T(8,128)(2,1)S(1)}) custom-call(s32[3]{0:T(128)S(1)} %pad_add_fusion.1.place, f32[16,1,512]{2,1,0:T(1,128)S(1)} %get-tuple-element.31.gain_ref, bf16[8,512,256]{2,1,0:T(8,128)(2,1)S(1)} %get-tuple-element.32.weight_ref, ...), custom_call_target="tpu_custom_call" | custom-call | flops 134217728 | bytes 3145728 | tf_op jit(solution)/shard_map/scale_and_pairs/pallas_call | solution.py:258
  24.8 1.6 %collective-permute-start.6 = (s16[528,128]{1,0:T(8,128)(2,1)S(1)}, s16[528,128]{1,0:T(8,128)(2,1)S(1)}, u32[]{:S(2)}, u32[]{:S(2)}) collective-permute-start(s16[528,128]{1,0:T(8,128)(2,1)S(1)} %get-tuple-element.36), channel_id=1, source_target_pairs={{0,2},{2,0},{1,3},{3,1},{4,6},{6,4},{5,7},{7,5},{8,10},{10,8},{9,1... | collective-permute-start | bytes 405512 | tf_op jit(solution)/shard_map/ppermute | solution.py:557
  26.5 4.6 %queries.1.refs_2_.refs_0_.q_ref = bf16[4,16,512]{2,1,0:T(8,128)(2,1)S(1)} custom-call(s32[3]{0:T(128)S(1)} %pad_add_fusion.1.place, f32[64,128]{1,0:T(8,128)S(1)} %get-tuple-element.34.scale_ref, f32[16,1,512]{2,1,0:T(1,128)S(1)} %get-tuple-element.31.gain_ref, bf16[8192,512]{1,0:T(8,128)(2,1)} %weight_ref.1, f32[64,128]{1,0:T(8,128)S(1)} %bitcast.12, ...), custom_call_target="tpu_custom_call" | custom-call | flops 536870912 | bytes 8388608 | tf_op jit(solution)/shard_map/queries/pallas_call | solution.py:302
  32.8 2.6 %collective-permute-start.8 = (s16[144,128]{1,0:T(8,128)(2,1)S(1)}, s16[144,128]{1,0:T(8,128)(2,1)S(1)}, u32[]{:S(2)}, u32[]{:S(2)}) collective-permute-start(s16[144,128]{1,0:T(8,128)(2,1)S(1)} %get-tuple-element.39), channel_id=1, source_target_pairs={{0,8},{4,12},{8,0},{12,4},{1,9},{5,13},{9,1},{13,5},{2,10},{6,14},... | collective-permute-start | bytes 110600 | tf_op jit(solution)/shard_map/ppermute | solution.py:557
  35.4 1.2 %collective-permute-start.9 = (s16[144,128]{1,0:T(8,128)(2,1)S(1)}, s16[144,128]{1,0:T(8,128)(2,1)S(1)}, u32[]{:S(2)}, u32[]{:S(2)}) collective-permute-start(s16[144,128]{1,0:T(8,128)(2,1)S(1)} %get-tuple-element.40), channel_id=1, source_target_pairs={{0,12},{4,8},{8,4},{12,0},{1,13},{5,9},{9,5},{13,1},{2,14},{6,10},... | collective-permute-start | bytes 110600 | tf_op jit(solution)/shard_map/ppermute | solution.py:557
  36.6 2.0 %staged.3 = (bf16[16,512,512]{2,1,0:T(8,128)(2,1)S(1)}, f32[8,128]{1,0:T(8,128)S(1)}) custom-call(s32[3]{0:T(128)S(1)} %pad_add_fusion.1.place, bf16[512,8192]{1,0:T(8,128)(2,1)S(1)} %bitcast.11, bf16[4,16,512]{2,1,0:T(8,128)(2,1)S(1)} %queries.1.refs_2_.refs_0_.q_ref), custom_call_target="tpu_custom_call" | custom-call | bytes 16777216 | tf_op jit(solution)/shard_map/staged/pallas_call | solution.py:66
  38.8 2.4 %collective-permute-done.9.refs_2_ = s16[144,128]{1,0:T(8,128)(2,1)S(1)} collective-permute-done((s16[144,128]{1,0:T(8,128)(2,1)S(1)}, s16[144,128]{1,0:T(8,128)(2,1)S(1)}, u32[]{:S(2)}, u32[]{:S(2)}) %collective-permute-start.9) | collective-permute-done | bytes 36896 | tf_op jit(solution)/shard_map/ppermute | solution.py:557
  41.8 1.1 %collective-permute-done.10.other_ref = f32[64,256]{1,0:T(8,128)S(1)} collective-permute-done((f32[64,256]{1,0:T(8,128)S(1)}, f32[64,256]{1,0:T(8,128)S(1)}, u32[]{:S(2)}, u32[]{:S(2)}) %collective-permute-start.10) | collective-permute-done | bytes 65568 | tf_op jit(solution)/shard_map/ppermute | solution.py:557
  42.9 2.2 %attend.1.x_ref = bf16[4,16,512]{2,1,0:T(8,128)(2,1)S(1)} custom-call(s32[3]{0:T(128)S(1)} %pad_add_fusion.1.place, s32[4]{0:T(128)S(1)} %copy-done.4, bf16[4,16,512]{2,1,0:T(8,128)(2,1)S(1)} %queries.1.refs_2_.refs_0_.q_ref, f32[64,256]{1,0:T(8,128)S(1)} %fold_pairs.1.refs_1_.mine_ref, f32[64,256]{1,0:T(8,128)S(1)} %collective-permute-done.10.other_ref, ...), custom_call_target="tpu_custom_call" | custom-call | flops 268435456 | bytes 3145728 | tf_op jit(solution)/shard_map/attend/pallas_call | solution.py:379
  47.8 1.1 %collective-permute-start.19 = (s16[528,128]{1,0:T(8,128)(2,1)S(1)}, s16[528,128]{1,0:T(8,128)(2,1)S(1)}, u32[]{:S(2)}, u32[]{:S(2)}) collective-permute-start(s16[528,128]{1,0:T(8,128)(2,1)S(1)} %get-tuple-element.49.refs_0_), channel_id=1, source_target_pairs={{0,2},{2,0},{1,3},{3,1},{4,6},{6,4},{5,7},{7,5},{8,10},{10,8},{9,1... | collective-permute-start | bytes 405512 | tf_op jit(solution)/shard_map/ppermute | solution.py:557
  49.4 4.1 %collective-permute-done.19.refs_1_.refs_2_ = s16[528,128]{1,0:T(8,128)(2,1)S(1)} collective-permute-done((s16[528,128]{1,0:T(8,128)(2,1)S(1)}, s16[528,128]{1,0:T(8,128)(2,1)S(1)}, u32[]{:S(2)}, u32[]{:S(2)}) %collective-permute-start.19) | collective-permute-done | bytes 135200 | tf_op jit(solution)/shard_map/ppermute | solution.py:557
  53.5 1.1 %collective-permute-start.20 = (s16[528,128]{1,0:T(8,128)(2,1)S(1)}, s16[528,128]{1,0:T(8,128)(2,1)S(1)}, u32[]{:S(2)}, u32[]{:S(2)}) collective-permute-start(s16[528,128]{1,0:T(8,128)(2,1)S(1)} %gate.7), channel_id=1, source_target_pairs={{0,2},{2,0},{1,3},{3,1},{4,6},{6,4},{5,7},{7,5},{8,10},{10,8},{9,1... | collective-permute-start | bytes 405512 | tf_op jit(solution)/shard_map/ppermute | solution.py:557
  54.8 1.4 %collective-permute-start.23 = (s16[272,128]{1,0:T(8,128)(2,1)S(1)}, s16[272,128]{1,0:T(8,128)(2,1)S(1)}, u32[]{:S(2)}, u32[]{:S(2)}) collective-permute-start(s16[272,128]{1,0:T(8,128)(2,1)S(1)} %get-tuple-element.54), channel_id=1, source_target_pairs={{0,12},{4,8},{8,4},{12,0},{1,13},{5,9},{9,5},{13,1},{2,14},{6,10},... | collective-permute-start | bytes 208904 | tf_op jit(solution)/shard_map/ppermute | solution.py:557
  56.2 2.3 %collective-permute-done.20.refs_2_ = s16[528,128]{1,0:T(8,128)(2,1)S(1)} collective-permute-done((s16[528,128]{1,0:T(8,128)(2,1)S(1)}, s16[528,128]{1,0:T(8,128)(2,1)S(1)}, u32[]{:S(2)}, u32[]{:S(2)}) %collective-permute-start.20) | collective-permute-done | bytes 135200 | tf_op jit(solution)/shard_map/ppermute | solution.py:557
  58.7 2.8 %collective-permute-done.22.refs_1_ = s16[272,128]{1,0:T(8,128)(2,1)S(1)} collective-permute-done((s16[272,128]{1,0:T(8,128)(2,1)S(1)}, s16[272,128]{1,0:T(8,128)(2,1)S(1)}, u32[]{:S(2)}, u32[]{:S(2)}) %collective-permute-start.22) | collective-permute-done | bytes 69664 | tf_op jit(solution)/shard_map/ppermute | solution.py:557
  61.6 1.4 %collective-permute-done.21.refs_0_ = s16[272,128]{1,0:T(8,128)(2,1)S(1)} collective-permute-done((s16[272,128]{1,0:T(8,128)(2,1)S(1)}, s16[272,128]{1,0:T(8,128)(2,1)S(1)}, u32[]{:S(2)}, u32[]{:S(2)}) %collective-permute-start.21) | collective-permute-done | bytes 69664 | tf_op jit(solution)/shard_map/ppermute | solution.py:557
  (70 shorter events, 12.5 us)
Async XLA Ops:
  0.0 15.1 %collective-permute-start.2 = (bf16[64,512]{1,0:T(8,128)(2,1)}, bf16[64,512]{1,0:T(8,128)(2,1)S(1)}, u32[]{:S(2)}, u32[]{:S(2)}) collective-permute-start(bf16[64,512]{1,0:T(8,128)(2,1)} %bitcast.16), channel_id=1, source_target_pairs={{0,12},{4,8},{8,4},{12,0},{1,13},{5,9},{9,5},{13,1},{2,14},{6,10},... | collective-permute-start | bytes 196616 | tf_op jit(solution)/shard_map/ppermute | solution.py:557
  5.0 10.1 %collective-permute-start.1 = (bf16[64,512]{1,0:T(8,128)(2,1)}, bf16[64,512]{1,0:T(8,128)(2,1)S(1)}, u32[]{:S(2)}, u32[]{:S(2)}) collective-permute-start(bf16[64,512]{1,0:T(8,128)(2,1)} %bitcast.17), channel_id=1, source_target_pairs={{0,8},{4,12},{8,0},{12,4},{1,9},{5,13},{9,1},{13,5},{2,10},{6,14},... | collective-permute-start | bytes 196616 | tf_op jit(solution)/shard_map/ppermute | solution.py:557
  5.1 10.1 %collective-permute-start = (bf16[64,512]{1,0:T(8,128)(2,1)}, bf16[64,512]{1,0:T(8,128)(2,1)S(1)}, u32[]{:S(2)}, u32[]{:S(2)}) collective-permute-start(bf16[64,512]{1,0:T(8,128)(2,1)} %bitcast.18), channel_id=1, source_target_pairs={{0,4},{4,0},{8,12},{12,8},{1,5},{5,1},{9,13},{13,9},{2,6},{6,2},{1... | collective-permute-start | bytes 196616 | tf_op jit(solution)/shard_map/ppermute | solution.py:557
  10.7 20.6 %collective-permute-start.11 = (bf16[2,128,256]{2,1,0:T(8,128)(2,1)S(1)}, bf16[2,128,256]{2,1,0:T(8,128)(2,1)S(1)}, u32[]{:S(2)}, u32[]{:S(2)}) collective-permute-start(bf16[2,128,256]{2,1,0:T(8,128)(2,1)S(1)} %get-tuple-element.43), channel_id=1, source_target_pairs={{0,4},{4,0},{8,12},{12,8},{1,5},{5,1},{9,13},{13,9},{2,6},{6,2},{1... | collective-permute-start | bytes 393224 | tf_op jit(solution)/shard_map/ppermute | solution.py:557
  12.2 19.1 %collective-permute-start.12 = (bf16[2,128,256]{2,1,0:T(8,128)(2,1)S(1)}, bf16[2,128,256]{2,1,0:T(8,128)(2,1)S(1)}, u32[]{:S(2)}, u32[]{:S(2)}) collective-permute-start(bf16[2,128,256]{2,1,0:T(8,128)(2,1)S(1)} %get-tuple-element.44), channel_id=1, source_target_pairs={{0,8},{4,12},{8,0},{12,4},{1,9},{5,13},{9,1},{13,5},{2,10},{6,14},... | collective-permute-start | bytes 393224 | tf_op jit(solution)/shard_map/ppermute | solution.py:557
  15.1 6.7 %collective-permute-start.3 = (bf16[4,64,512]{2,1,0:T(8,128)(2,1)S(1)}, bf16[4,64,512]{2,1,0:T(8,128)(2,1)S(1)}, u32[]{:S(2)}, u32[]{:S(2)}) collective-permute-start(bf16[4,64,512]{2,1,0:T(8,128)(2,1)S(1)} %pack.1.refs_1_.refs_0_.rows_ref), channel_id=1, source_target_pairs={{0,2},{2,0},{1,3},{3,1},{4,6},{6,4},{5,7},{7,5},{8,10},{10,8},{9,1... | collective-permute-start | bytes 786440 | tf_op jit(solution)/shard_map/ppermute | solution.py:557
  17.5 4.9 %collective-permute-start.4 = (bf16[4,64,512]{2,1,0:T(8,128)(2,1)S(1)}, bf16[4,64,512]{2,1,0:T(8,128)(2,1)S(1)}, u32[]{:S(2)}, u32[]{:S(2)}) collective-permute-start(bf16[4,64,512]{2,1,0:T(8,128)(2,1)S(1)} %pack.1.refs_1_.refs_0_.rows_ref), channel_id=1, source_target_pairs={{0,1},{1,0},{2,3},{3,2},{4,5},{5,4},{6,7},{7,6},{8,9},{9,8},{10,11... | collective-permute-start | bytes 786440 | tf_op jit(solution)/shard_map/ppermute | solution.py:557
  21.9 1.5 %collective-permute-start.5 = (bf16[4,64,512]{2,1,0:T(8,128)(2,1)S(1)}, bf16[4,64,512]{2,1,0:T(8,128)(2,1)S(1)}, u32[]{:S(2)}, u32[]{:S(2)}) collective-permute-start(bf16[4,64,512]{2,1,0:T(8,128)(2,1)S(1)} %gate.4.refs_1_), channel_id=1, source_target_pairs={{0,1},{1,0},{2,3},{3,2},{4,5},{5,4},{6,7},{7,6},{8,9},{9,8},{10,11... | collective-permute-start | bytes 786440 | tf_op jit(solution)/shard_map/ppermute | solution.py:557
  22.0 9.3 %collective-permute-start.13 = (bf16[2,128,256]{2,1,0:T(8,128)(2,1)S(1)}, bf16[2,128,256]{2,1,0:T(8,128)(2,1)S(1)}, u32[]{:S(2)}, u32[]{:S(2)}) collective-permute-start(bf16[2,128,256]{2,1,0:T(8,128)(2,1)S(1)} %gate.5), channel_id=1, source_target_pairs={{0,12},{4,8},{8,4},{12,0},{1,13},{5,9},{9,5},{13,1},{2,14},{6,10},... | collective-permute-start | bytes 393224 | tf_op jit(solution)/shard_map/ppermute | solution.py:557
  24.8 6.3 %collective-permute-start.6 = (s16[528,128]{1,0:T(8,128)(2,1)S(1)}, s16[528,128]{1,0:T(8,128)(2,1)S(1)}, u32[]{:S(2)}, u32[]{:S(2)}) collective-permute-start(s16[528,128]{1,0:T(8,128)(2,1)S(1)} %get-tuple-element.36), channel_id=1, source_target_pairs={{0,2},{2,0},{1,3},{3,1},{4,6},{6,4},{5,7},{7,5},{8,10},{10,8},{9,1... | collective-permute-start | bytes 405512 | tf_op jit(solution)/shard_map/ppermute | solution.py:557
  31.3 9.9 %collective-permute-start.14 = (bf16[4,128,256]{2,1,0:T(8,128)(2,1)S(1)}, bf16[4,128,256]{2,1,0:T(8,128)(2,1)S(1)}, u32[]{:S(2)}, u32[]{:S(2)}) collective-permute-start(bf16[4,128,256]{2,1,0:T(8,128)(2,1)S(1)} %get-tuple-element.47), channel_id=1, source_target_pairs={{0,2},{2,0},{1,3},{3,1},{4,6},{6,4},{5,7},{7,5},{8,10},{10,8},{9,1... | collective-permute-start | bytes 786440 | tf_op jit(solution)/shard_map/ppermute | solution.py:557
  32.2 6.5 %collective-permute-start.7 = (s16[144,128]{1,0:T(8,128)(2,1)S(1)}, s16[144,128]{1,0:T(8,128)(2,1)S(1)}, u32[]{:S(2)}, u32[]{:S(2)}) collective-permute-start(s16[144,128]{1,0:T(8,128)(2,1)S(1)} %get-tuple-element.38), channel_id=1, source_target_pairs={{0,4},{4,0},{8,12},{12,8},{1,5},{5,1},{9,13},{13,9},{2,6},{6,2},{1... | collective-permute-start | bytes 110600 | tf_op jit(solution)/shard_map/ppermute | solution.py:557
  32.8 6.0 %collective-permute-start.8 = (s16[144,128]{1,0:T(8,128)(2,1)S(1)}, s16[144,128]{1,0:T(8,128)(2,1)S(1)}, u32[]{:S(2)}, u32[]{:S(2)}) collective-permute-start(s16[144,128]{1,0:T(8,128)(2,1)S(1)} %get-tuple-element.39), channel_id=1, source_target_pairs={{0,8},{4,12},{8,0},{12,4},{1,9},{5,13},{9,1},{13,5},{2,10},{6,14},... | collective-permute-start | bytes 110600 | tf_op jit(solution)/shard_map/ppermute | solution.py:557
  35.4 5.8 %collective-permute-start.9 = (s16[144,128]{1,0:T(8,128)(2,1)S(1)}, s16[144,128]{1,0:T(8,128)(2,1)S(1)}, u32[]{:S(2)}, u32[]{:S(2)}) collective-permute-start(s16[144,128]{1,0:T(8,128)(2,1)S(1)} %get-tuple-element.40), channel_id=1, source_target_pairs={{0,12},{4,8},{8,4},{12,0},{1,13},{5,9},{9,5},{13,1},{2,14},{6,10},... | collective-permute-start | bytes 110600 | tf_op jit(solution)/shard_map/ppermute | solution.py:557
  38.7 4.3 %collective-permute-start.15 = (bf16[4,128,256]{2,1,0:T(8,128)(2,1)S(1)}, bf16[4,128,256]{2,1,0:T(8,128)(2,1)S(1)}, u32[]{:S(2)}, u32[]{:S(2)}) collective-permute-start(bf16[4,128,256]{2,1,0:T(8,128)(2,1)S(1)} %get-tuple-element.46.refs_0_), channel_id=1, source_target_pairs={{0,1},{1,0},{2,3},{3,2},{4,5},{5,4},{6,7},{7,6},{8,9},{9,8},{10,11... | collective-permute-start | bytes 786440 | tf_op jit(solution)/shard_map/ppermute | solution.py:557
  41.2 1.7 %collective-permute-start.16 = (bf16[4,128,256]{2,1,0:T(8,128)(2,1)S(1)}, bf16[4,128,256]{2,1,0:T(8,128)(2,1)S(1)}, u32[]{:S(2)}, u32[]{:S(2)}) collective-permute-start(bf16[4,128,256]{2,1,0:T(8,128)(2,1)S(1)} %gate.6.refs_1_), channel_id=1, source_target_pairs={{0,1},{1,0},{2,3},{3,2},{4,5},{5,4},{6,7},{7,6},{8,9},{9,8},{10,11... | collective-permute-start | bytes 786440 | tf_op jit(solution)/shard_map/ppermute | solution.py:557
  41.3 1.6 %collective-permute-start.10 = (f32[64,256]{1,0:T(8,128)S(1)}, f32[64,256]{1,0:T(8,128)S(1)}, u32[]{:S(2)}, u32[]{:S(2)}) collective-permute-start(f32[64,256]{1,0:T(8,128)S(1)} %fold_pairs.1.refs_1_.mine_ref), channel_id=1, source_target_pairs={{0,1},{1,0},{2,3},{3,2},{4,5},{5,4},{6,7},{7,6},{8,9},{9,8},{10,11... | collective-permute-start | bytes 196616 | tf_op jit(solution)/shard_map/ppermute | solution.py:557
  45.6 2.0 %collective-permute-start.17 = (f32[4,64,512]{2,1,0:T(8,128)S(1)}, f32[4,64,512]{2,1,0:T(8,128)S(1)}, u32[]{:S(2)}, u32[]{:S(2)}) collective-permute-start(f32[4,64,512]{2,1,0:T(8,128)S(1)} %outputs.4.refs_0_), channel_id=1, source_target_pairs={{0,1},{1,0},{2,3},{3,2},{4,5},{5,4},{6,7},{7,6},{8,9},{9,8},{10,11... | collective-permute-start | bytes 1572872 | tf_op jit(solution)/shard_map/ppermute | solution.py:557
  46.3 8.3 %collective-permute-start.18 = (f32[4,64,512]{2,1,0:T(8,128)S(1)}, f32[4,64,512]{2,1,0:T(8,128)S(1)}, u32[]{:S(2)}, u32[]{:S(2)}) collective-permute-start(f32[4,64,512]{2,1,0:T(8,128)S(1)} %outputs.5.refs_0_), channel_id=1, source_target_pairs={{0,1},{1,0},{2,3},{3,2},{4,5},{5,4},{6,7},{7,6},{8,9},{9,8},{10,11... | collective-permute-start | bytes 1572872 | tf_op jit(solution)/shard_map/ppermute | solution.py:557
  47.8 5.7 %collective-permute-start.19 = (s16[528,128]{1,0:T(8,128)(2,1)S(1)}, s16[528,128]{1,0:T(8,128)(2,1)S(1)}, u32[]{:S(2)}, u32[]{:S(2)}) collective-permute-start(s16[528,128]{1,0:T(8,128)(2,1)S(1)} %get-tuple-element.49.refs_0_), channel_id=1, source_target_pairs={{0,2},{2,0},{1,3},{3,1},{4,6},{6,4},{5,7},{7,5},{8,10},{10,8},{9,1... | collective-permute-start | bytes 405512 | tf_op jit(solution)/shard_map/ppermute | solution.py:557
  53.5 5.0 %collective-permute-start.20 = (s16[528,128]{1,0:T(8,128)(2,1)S(1)}, s16[528,128]{1,0:T(8,128)(2,1)S(1)}, u32[]{:S(2)}, u32[]{:S(2)}) collective-permute-start(s16[528,128]{1,0:T(8,128)(2,1)S(1)} %gate.7), channel_id=1, source_target_pairs={{0,2},{2,0},{1,3},{3,1},{4,6},{6,4},{5,7},{7,5},{8,10},{10,8},{9,1... | collective-permute-start | bytes 405512 | tf_op jit(solution)/shard_map/ppermute | solution.py:557
  54.7 6.8 %collective-permute-start.22 = (s16[272,128]{1,0:T(8,128)(2,1)S(1)}, s16[272,128]{1,0:T(8,128)(2,1)S(1)}, u32[]{:S(2)}, u32[]{:S(2)}) collective-permute-start(s16[272,128]{1,0:T(8,128)(2,1)S(1)} %get-tuple-element.53), channel_id=1, source_target_pairs={{0,8},{4,12},{8,0},{12,4},{1,9},{5,13},{9,1},{13,5},{2,10},{6,14},... | collective-permute-start | bytes 208904 | tf_op jit(solution)/shard_map/ppermute | solution.py:557
  54.8 6.8 %collective-permute-start.23 = (s16[272,128]{1,0:T(8,128)(2,1)S(1)}, s16[272,128]{1,0:T(8,128)(2,1)S(1)}, u32[]{:S(2)}, u32[]{:S(2)}) collective-permute-start(s16[272,128]{1,0:T(8,128)(2,1)S(1)} %get-tuple-element.54), channel_id=1, source_target_pairs={{0,12},{4,8},{8,4},{12,0},{1,13},{5,9},{9,5},{13,1},{2,14},{6,10},... | collective-permute-start | bytes 208904 | tf_op jit(solution)/shard_map/ppermute | solution.py:557
  58.7 4.4 %collective-permute-start.21 = (s16[272,128]{1,0:T(8,128)(2,1)S(1)}, s16[272,128]{1,0:T(8,128)(2,1)S(1)}, u32[]{:S(2)}, u32[]{:S(2)}) collective-permute-start(s16[272,128]{1,0:T(8,128)(2,1)S(1)} %get-tuple-element.52), channel_id=1, source_target_pairs={{0,4},{4,0},{8,12},{12,8},{1,5},{5,1},{9,13},{13,9},{2,6},{6,2},{1... | collective-permute-start | bytes 208904 | tf_op jit(solution)/shard_map/ppermute | solution.py:557
  (7 other events, 48.6 us)
